TPU v7x, 32 devices: a whole 2x2x4 slice. The times are simulated.
32 devices in a mesh: parts: 2 (over x), blk: 16 (over z, y, core).
Axes of the slice: x: 2, y: 2, z: 4, core: 2. Of those that a mesh axis runs over, the one named last changes fastest.
Arguments:
- activations: bfloat16 [32, 160, 4096], P(('parts', 'blk')), parts along dimension 0, may hold values from -6 to 6
- output_grads: bfloat16 [32, 160, 14336], P(('parts', 'blk')), parts along dimension 0, may hold values from -6 to 6
- basis_in: bfloat16 [4096, 4096], P('blk'), may hold values from -0.09375 to 0.09375
- basis_out: bfloat16 [14336, 14336], P('blk'), may hold values from -0.046875 to 0.046875
- query_left: bfloat16 [16, 32, 4096], P('blk'), may hold values from -0.09375 to 0.09375
- query_right: bfloat16 [16, 32, 14336], P('blk'), may hold values from -0.046875 to 0.046875
- owners: int32 [4], replicated, may hold values from 0 to 15, as said below
- lengths: int32 [32], P('parts'), parts along dimension 0, may hold values from 1 to 160, 1920 in all
- slot_plan: int32 [32], P('parts'), parts along dimension 0, may hold values from 0 to 15, each once
Outputs:
- scores: float32 [32, 4], P(('parts', 'blk')), parts along dimension 0
There are 2 independent parts, one for each index of `parts`. A program takes and returns all parts, laid end to end along the dimension named above; an argument that names none is the same for every part. Nothing has to cross between parts.
Inputs may be any that keep to these rules, and one draw needn't show every extreme that they name: `owners`: distinct slots of blk.
All inputs are finite; a program needn't handle non-finite values.
Results may differ from a plain program's by a relative error of at most 0.01.
Values may be sent and summed in bfloat16 or wider, within the bound.
No kernel may reach another device: no remote copies, remote signals or barrier semaphores. Data moves between devices by JAX's collectives and lax.ppermute only.
A program may use at most 128 MiB of HBM per device.

v0:
```python
import jax
import jax.numpy as jnp
from jax import lax
from jax.sharding import PartitionSpec as P


def spread(value, axis, source):
    kept = jnp.where(lax.axis_index(axis) == source, value, 0).astype(value.dtype)
    return lax.psum(kept, axis)


def shards(
    activations,
    output_grads,
    basis_in,
    basis_out,
    query_left,
    query_right,
    owners,
    lengths,
    slot_plan,
):
    num_blocks = lax.axis_size("blk")
    my_index = lax.axis_index("blk")
    seqs_here = activations.shape[0]
    max_length = activations.shape[1]
    width_in = activations.shape[2]
    width_out = output_grads.shape[2]
    num_queries = owners.shape[0]
    rank_count = query_left.shape[1]
    total_seqs = seqs_here * num_blocks
    total_cols = num_queries * rank_count
    pieces_in = []
    pieces_out = []
    for query_num in range(num_queries):
        block_in, block_out = (
            spread(query_left[0], "blk", owners[query_num]),
            spread(query_right[0], "blk", owners[query_num]),
        )
        pieces_in.append(block_in)
        pieces_out.append(block_out)
    picked_in = jnp.stack(pieces_in).reshape(total_cols, query_left.shape[2])
    picked_out = jnp.stack(pieces_out).reshape(total_cols, query_right.shape[2])
    contract = (((1,), (1,)), ((), ()))
    rotated_in = lax.dot_general(
        basis_in, picked_in, contract, preferred_element_type=jnp.float32
    ).astype(jnp.bfloat16)
    rotated_out = lax.dot_general(
        basis_out, picked_out, contract, preferred_element_type=jnp.float32
    ).astype(jnp.bfloat16)
    slot_match = slot_plan[:, None] == jnp.arange(total_seqs, dtype=jnp.int32)[None, :]
    slot_lengths = jnp.sum(jnp.where(slot_match, lengths[None, :], 0), axis=1)
    live_all = (jnp.arange(max_length, dtype=jnp.int32)[None, :] < slot_lengths[:, None]).astype(
        jnp.float32
    )
    my_live = lax.dynamic_slice_in_dim(live_all, my_index * seqs_here, seqs_here, 0)
    flat_in = activations.reshape(-1, width_in)
    flat_out = output_grads.reshape(-1, width_out)
    whole_in, whole_out = (
        lax.all_gather(rotated_in, "blk", axis=0, tiled=True),
        lax.all_gather(rotated_out, "blk", axis=0, tiled=True),
    )
    project_in = jnp.dot(flat_in, whole_in, preferred_element_type=jnp.float32)
    project_out = jnp.dot(flat_out, whole_out, preferred_element_type=jnp.float32)
    products = (project_in * project_out).reshape(-1, max_length, num_queries, rank_count)
    gathered = lax.all_gather(
        jnp.einsum("stqr,st->sq", products, my_live) / rank_count, "blk", axis=0, tiled=True
    )
    seq_ids = my_index * seqs_here + jnp.arange(seqs_here, dtype=jnp.int32)
    chooser = (slot_plan[None, :] == seq_ids[:, None]).astype(jnp.float32)
    return jnp.dot(chooser, gathered, precision=lax.Precision.HIGHEST)


def solution(mesh):
    placed = (
        P(("parts", "blk"), None, None),
        P(("parts", "blk"), None, None),
        P("blk", None),
        P("blk", None),
        P("blk", None, None),
        P("blk", None, None),
        P(),
        P("parts"),
        P("parts"),
    )
    return jax.shard_map(
        shards, mesh=mesh, in_specs=placed, out_specs=P(("parts", "blk"), None), check_vma=False
    )
```

profile of v0, /device:TPU:0, one launch (start us, length us, event | category | flops | bytes accessed | tf_op | source)
XLA Modules:
  0.0 284.4 jit_solution(5358135961362964753)
XLA Ops:
  6.5 0.0 copy-start
  6.5 0.0 copy-start.2
  6.5 0.0 all-reduce.4.cloned.1.call-start
  6.5 1.5 fusion.21
  10.5 3.0 %broadcast_select_fusion.3 = (bf16[1,32,14336]{2,1,0:T(8,128)(2,1)}, bf16[1,32,14336]{2,1,0:T(8,128)(2,1)}, bf16[1,32,14336]{2,1,0:T(8,128)(2,1)}, bf16[1,32,14336]{2,1,0:T(8,128)(2,1)}) fusion(bf16[1,32,14336]{2,1,0:T(8,128)(2,1)} %param.14, pred[]{:T(512)S(6)} %eq.40, pred[]{:T(512)S(6)} %eq.41, pred[]{:T(512)S(6)} %eq.43, pred[]{:T(512)S(6)} %eq.42), kind=kLoop, calls=%fused_computation.17 | loop fusion | flops 1835008 | bytes 4587524 | tf_op jit(solution)/shard_map/jit(_where)/select_n | solution.py:8
  13.6 0.0 copy-done.2
  13.6 1.1 broadcast_select_fusion.7
  14.6 0.0 all-reduce.4.cloned.1.call-update
  14.6 0.0 all-gather.6.cloned.1.call-start
  14.7 122.2 %all-reduce.4.cloned.1.call-done = (bf16[1,32,14336]{2,1,0:T(8,128)(2,1)}, bf16[1,32,14336]{2,1,0:T(8,128)(2,1)}, bf16[1,32,14336]{2,1,0:T(8,128)(2,1)}, bf16[1,...) async-done(((bf16[1,32,14336]{2,1,0:T(8,128)(2,1)}, ...) | async-done | bytes 4718608 | tf_op jit(solution)/shard_map/psum | solution.py:9
  136.9 3.5 %pad_maximum_fusion = bf16[4,32,14336]{2,1,0:T(8,128)(2,1)} fusion(bf16[1,32,14336]{2,1,0:T(8,128)(2,1)} %get-tuple-element.5, bf16[1,32,14336]{2,1,0:T(8,128)(2,1)} %get-tuple-element.6, bf16[1,32,14336]{2,1,0:T(8,128)(2,1)} %get-tuple-element.7, bf16[1,32,14336]{2,1,0:T(8,128)(2,1)} %get-tuple-element.8), kind=kLoop, calls=%fused_computation.2 | loop fusion | flops 5505024 | bytes 7340032 | tf_op jit(solution)/shard_map/stack | solution.py:43
  140.3 0.0 copy-start.3
  140.3 0.0 copy-start.4
  140.3 0.0 copy-start.5
  140.3 0.0 copy-start.6
  140.3 14.3 %fusion.4 = bf16[896,128]{0,1:T(8,128)(2,1)} fusion(bf16[128,14336]{1,0:T(8,128)(2,1)} %bitcast.44, bf16[896,14336]{1,0:T(8,128)(2,1)} %param.12), kind=kOutput, calls=%fused_computation.6 | convolution fusion | flops 3288449024 | bytes 29589504 | tf_op jit(solution)/shard_map/dot_general | solution.py:48
  154.7 0.0 copy-start.7
  154.7 0.0 copy-start.8
  154.7 0.0 copy-start.9
  154.7 0.0 all-gather.6.cloned.1.call-update
  154.7 0.0 all-gather.4.cloned.1.call-start
  154.7 0.0 copy-done.3
  154.7 0.0 copy-done.4
  154.8 0.0 copy-done.5
  154.8 0.0 copy-done.6
  154.8 0.1 pad_maximum_fusion.1
  154.9 0.0 copy-done
  154.9 1.5 fusion.11
  156.4 0.0 all-gather.4.cloned.1.call-update
  156.4 0.0 copy-done.7
  156.4 0.0 copy-done.8
  156.4 0.2 select_reduce_fusion
  156.6 0.6 dynamic-slice.1
  157.2 0.0 copy-done.9
  157.2 0.6 dynamic-slice
  158.5 0.0 copy-start.1
  158.5 44.6 %all-gather.6.cloned.1.call-done = bf16[14336,128]{0,1:T(8,128)(2,1)} async-done(((bf16[896,128]{0,1:T(8,128)(2,1)}), bf16[14336,128]{0,1:T(8,128)(2,1)}) %all-gather.6.cloned.1.call-update) | async-done | bytes 3670032 | tf_op jit(solution)/shard_map/all_gather | solution.py:61
  203.0 4.8 %fusion = f32[128,160]{0,1:T(8,128)S(1)} fusion(bf16[14336,128]{0,1:T(8,128)(2,1)} %all-gather.6.cloned.1.call-done, bf16[1,160,14336]{2,1,0:T(8,128)(2,1)} %param.10), kind=kOutput, calls=%fused_computation | convolution fusion | flops 587202560 | bytes 8339456 | tf_op jit(solution)/shard_map/dot_general | solution.py:64
  207.8 32.8 %all-gather.4.cloned.1.call-done = bf16[4096,128]{0,1:T(8,128)(2,1)} async-done(((bf16[256,128]{0,1:T(8,128)(2,1)}), bf16[4096,128]{0,1:T(8,128)(2,1)}) %all-gather.4.cloned.1.call-update) | async-done | bytes 1048592 | tf_op jit(solution)/shard_map/all_gather | solution.py:60
  240.7 0.0 copy-done.1
  240.7 2.4 fusion.8
  243.0 1.0 copy.12
  244.0 0.8 fusion.12
  244.8 0.2 dynamic-update-slice
  245.0 32.1 %all-reduce = f32[64]{0:T(128)S(1)} all-reduce(f32[64]{0:T(128)S(1)} %dynamic-update-slice), channel_id=2, replica_groups=mesh['parts'=2,'blk'=16] {'blk'}, use_global_device_ids=true, to_apply=%add | all-reduce | flops 64 | bytes 512
  277.1 0.1 reshape.71
  277.2 0.7 fusion.15
  (2 shorter events, 0.0 us)
Async XLA Ops:
  6.5 148.4 %copy-start = (bf16[256,4096]{1,0:T(8,128)(2,1)S(1)}, bf16[256,4096]{1,0:T(8,128)(2,1)}, u32[]{:S(2)}) copy-start(bf16[256,4096]{1,0:T(8,128)(2,1)} %param.11) | copy-start | bytes 6291460
  6.5 7.0 %copy-start.2 = (bf16[1,32,4096]{2,1,0:T(8,128)(2,1)S(1)}, bf16[1,32,4096]{2,1,0:T(8,128)(2,1)}, u32[]{:S(2)}) copy-start(bf16[1,32,4096]{2,1,0:T(8,128)(2,1)} %param.13) | copy-start | bytes 786436
  6.5 130.3 %all-reduce.4.cloned.1.call-start = ((), (), s32[]{:S(2)}) async-start(), calls=%async_computation.2 | async-start | bytes 9437184 | tf_op jit(solution)/shard_map/psum | solution.py:9
  14.6 188.4 %all-gather.6.cloned.1.call-start = ((), (), s32[]{:S(2)}) async-start(), calls=%async_computation.1 | async-start | bytes 3899392 | tf_op jit(solution)/shard_map/all_gather | solution.py:61
  140.3 14.4 %copy-start.3 = (bf16[1,32,4096]{2,1,0:T(8,128)(2,1)S(1)}, bf16[1,32,4096]{2,1,0:T(8,128)(2,1)}, u32[]{:S(2)}) copy-start(bf16[1,32,4096]{2,1,0:T(8,128)(2,1)} %get-tuple-element.9) | copy-start | bytes 786436
  140.3 14.4 %copy-start.4 = (bf16[1,32,4096]{2,1,0:T(8,128)(2,1)S(1)}, bf16[1,32,4096]{2,1,0:T(8,128)(2,1)}, u32[]{:S(2)}) copy-start(bf16[1,32,4096]{2,1,0:T(8,128)(2,1)} %get-tuple-element.10) | copy-start | bytes 786436
  140.3 14.4 %copy-start.5 = (bf16[1,32,4096]{2,1,0:T(8,128)(2,1)S(1)}, bf16[1,32,4096]{2,1,0:T(8,128)(2,1)}, u32[]{:S(2)}) copy-start(bf16[1,32,4096]{2,1,0:T(8,128)(2,1)} %get-tuple-element.11) | copy-start | bytes 786436
  140.3 14.4 %copy-start.6 = (bf16[1,32,4096]{2,1,0:T(8,128)(2,1)S(1)}, bf16[1,32,4096]{2,1,0:T(8,128)(2,1)}, u32[]{:S(2)}) copy-start(bf16[1,32,4096]{2,1,0:T(8,128)(2,1)} %get-tuple-element.12) | copy-start | bytes 786436
  154.7 1.8 copy-start.7
  154.7 1.8 copy-start.8
  154.7 2.6 copy-start.9
  154.7 86.0 %all-gather.4.cloned.1.call-start = ((), (), s32[]{:S(2)}) async-start(), calls=%async_computation | async-start | bytes 1114112 | tf_op jit(solution)/shard_map/all_gather | solution.py:60
  158.5 82.2 %copy-start.1 = (bf16[1,160,4096]{2,1,0:T(8,128)(2,1)S(1)}, bf16[1,160,4096]{2,1,0:T(8,128)(2,1)}, u32[]{:S(2)}) copy-start(bf16[1,160,4096]{2,1,0:T(8,128)(2,1)} %param.9) | copy-start | bytes 3932164
Sparse Core Ops, SparseCore 0:
  14.8 122.0 all-reduce.3
  154.8 48.1 all-gather.5
  205.2 35.4 all-gather.3
where the time goes:
time: 285 us; the launch traced here: 284 us
  waiting for transfers between devices  200 us (70%)
  blocking collectives  32.1 us (11%)
  matrix products  24.3 us (9%)
  between operations  16.3 us (6%)
  other arithmetic  7.9 us (3%)
  local copies, waits for them, and re-layouts  3.97 us (1%)
    psum x1, waiting for transfers between devices, spread(): return lax.psum(kept, axis)  122 us
    all_gather x1, waiting for transfers between devices, shards(): lax.all_gather(rotated_out, 'blk', axis=0, tiled=True)  44.6 us
    all_gather x1, waiting for transfers between devices, shards(): lax.all_gather(rotated_in, 'blk', axis=0, tiled=True)  32.8 us
    unnamed x1, blocking collectives  32.1 us
    dot_general x1, matrix products, shards(): lax.dot_general(basis_out, picked_out, contract, preferred_element_type=j...  14.3 us
  transfers between devices with their start and end apart: 3, of which 3 were waited for; matrix products, arithmetic and copies ran while one was open for 3% of the time, Pallas kernels for 0%

commit v1 on v0

v1 whole, which is shorter than its diff:
```python
import functools

import jax
import jax.numpy as jnp
from jax import lax
from jax.experimental import pallas as pl
from jax.experimental.pallas import tpu as pltpu
from jax.sharding import PartitionSpec as P

ROWS = (((1,), (1,)), ((), ()))


def rotate_kernel(part, own_at, sib_at, own, sib, basis_in, basis_out, out, acc):
    step = pl.program_id(0)
    wide_in = basis_in.shape[1]
    rows_in = basis_in.shape[0]

    @pl.when(step == 0)
    def _():
        acc[...] = jnp.zeros_like(acc)

    left = jnp.concatenate([own[0, :, :wide_in], sib[0, :, :wide_in]], axis=0)
    right = jnp.concatenate([own[0, :, wide_in:], sib[0, :, wide_in:]], axis=0)
    acc[:, :rows_in] += lax.dot_general(
        left, basis_in[...], ROWS, preferred_element_type=jnp.float32
    )
    acc[:, rows_in:] += lax.dot_general(
        right, basis_out[...], ROWS, preferred_element_type=jnp.float32
    )

    @pl.when(step == pl.num_programs(0) - 1)
    def _():
        out[...] = acc[...]


def rotate(part, own_at, sib_at, own, sib, basis_in, basis_out):
    chips, ranks, wide = own.shape
    wide_in = basis_in.shape[1] // 2 // chips
    wide_out = basis_out.shape[1] // 2 // chips
    rows_in, rows_out = basis_in.shape[0], basis_out.shape[0]
    if wide_in % 128 or wide_out % 128 or rows_in % 128 or rows_out % 128:
        both = jnp.concatenate([jnp.take(own, own_at, 0), jnp.take(sib, sib_at, 0)], axis=1)
        both = both.transpose(1, 0, 2)
        left = both[:, :, :wide_in].reshape(2 * ranks, -1)
        right = both[:, :, wide_in:].reshape(2 * ranks, -1)
        half_in = lax.dynamic_slice_in_dim(basis_in, part * left.shape[1], left.shape[1], 1)
        half_out = lax.dynamic_slice_in_dim(basis_out, part * right.shape[1], right.shape[1], 1)
        return jnp.concatenate(
            [
                lax.dot_general(left, half_in, ROWS, preferred_element_type=jnp.float32),
                lax.dot_general(right, half_out, ROWS, preferred_element_type=jnp.float32),
            ],
            axis=1,
        )
    return pl.pallas_call(
        rotate_kernel,
        grid_spec=pltpu.PrefetchScalarGridSpec(
            num_scalar_prefetch=3,
            grid=(chips,),
            in_specs=[
                pl.BlockSpec((1, ranks, wide), lambda g, part, a, b: (a[g], 0, 0)),
                pl.BlockSpec((1, ranks, wide), lambda g, part, a, b: (b[g], 0, 0)),
                pl.BlockSpec((rows_in, wide_in), lambda g, part, a, b: (0, part[0] * chips + g)),
                pl.BlockSpec((rows_out, wide_out), lambda g, part, a, b: (0, part[0] * chips + g)),
            ],
            out_specs=pl.BlockSpec((2 * ranks, rows_in + rows_out), lambda g, part, a, b: (0, 0)),
            scratch_shapes=[pltpu.VMEM((2 * ranks, rows_in + rows_out), jnp.float32)],
        ),
        out_shape=jax.ShapeDtypeStruct((2 * ranks, rows_in + rows_out), jnp.float32),
        compiler_params=pltpu.CompilerParams(vmem_limit_bytes=32 * 1024 * 1024),
        name="rotate",
    )(part[None], own_at, sib_at, own, sib, basis_in, basis_out)


def project_kernel(part, own_at, sib_at, own, sib, acts, grads, other, mine_out, other_out, acc):
    step = pl.program_id(0)
    wide_in = acts.shape[1]

    @pl.when(step == 0)
    def _():
        acc[...] = jnp.zeros_like(acc)

    left = jnp.concatenate([own[0, :, :wide_in], sib[0, :, :wide_in]], axis=0)
    right = jnp.concatenate([own[0, :, wide_in:], sib[0, :, wide_in:]], axis=0)
    pairs = (
        (acts[...], left),
        (grads[...], right),
        (other[:, :wide_in], left),
        (other[:, wide_in:], right),
    )
    for num, (tokens, factors) in enumerate(pairs):
        acc[num] += lax.dot_general(tokens, factors, ROWS, preferred_element_type=jnp.float32)

    @pl.when(step == pl.num_programs(0) - 1)
    def _():
        mine_out[...] = acc[:2]
        other_out[...] = acc[2:]


def project(part, own_at, sib_at, own, sib, acts, grads, other):
    chips, ranks, wide = own.shape
    tokens = acts.shape[0]
    wide_in, wide_out = acts.shape[1] // 2 // chips, grads.shape[1] // 2 // chips
    if wide_in % 128 or wide_out % 128:
        both = jnp.concatenate([jnp.take(own, own_at, 0), jnp.take(sib, sib_at, 0)], axis=1)

        def dots(left_tokens, right_tokens):
            return jnp.stack(
                [
                    jnp.einsum("tgf,gcf->tc", left_tokens, both[:, :, :wide_in], preferred_element_type=jnp.float32),
                    jnp.einsum("tgf,gcf->tc", right_tokens, both[:, :, wide_in:], preferred_element_type=jnp.float32),
                ]
            )

        left_own = jnp.take(acts.reshape(tokens, chips, 2, wide_in), part, axis=2)
        right_own = jnp.take(grads.reshape(tokens, chips, 2, wide_out), part, axis=2)
        theirs = other.reshape(tokens, chips, wide)
        return dots(left_own, right_own), dots(theirs[:, :, :wide_in], theirs[:, :, wide_in:])
    shape = jax.ShapeDtypeStruct((2, tokens, 2 * ranks), jnp.float32)
    whole = pl.BlockSpec((2, tokens, 2 * ranks), lambda g, part, a, b: (0, 0, 0))
    return pl.pallas_call(
        project_kernel,
        grid_spec=pltpu.PrefetchScalarGridSpec(
            num_scalar_prefetch=3,
            grid=(chips,),
            in_specs=[
                pl.BlockSpec((1, ranks, wide), lambda g, part, a, b: (a[g], 0, 0)),
                pl.BlockSpec((1, ranks, wide), lambda g, part, a, b: (b[g], 0, 0)),
                pl.BlockSpec((tokens, wide_in), lambda g, part, a, b: (0, 2 * g + part[0])),
                pl.BlockSpec((tokens, wide_out), lambda g, part, a, b: (0, 2 * g + part[0])),
                pl.BlockSpec((tokens, wide), lambda g, part, a, b: (0, g)),
            ],
            out_specs=[whole, whole],
            scratch_shapes=[pltpu.VMEM((4, tokens, 2 * ranks), jnp.float32)],
        ),
        out_shape=[shape, shape],
        compiler_params=pltpu.CompilerParams(vmem_limit_bytes=32 * 1024 * 1024),
        name="project",
    )(part[None], own_at, sib_at, own, sib, acts, grads, other)


def orders_of(bits):
    far = list(range(bits - 1, 0, -1))
    if len(far) < 3:
        return far, far[::-1]
    return far, [far[-1]] + far[:-1]


def place_of(order, chips):
    place = [0] * chips
    for spot in range(chips):
        mask = 0
        for level, bit in enumerate(order):
            if spot >> level & 1:
                mask |= 1 << (bit - 1)
        place[mask] = spot
    return place


def xor_gather(piece, orders, count):
    held = piece[None]
    for level in range(len(orders[0])):
        pairs = [(i, i ^ (1 << orders[i & 1][level])) for i in range(count)]
        held = jnp.concatenate([held, lax.ppermute(held, "blk", pairs)], axis=0)
    return held


def swap_cores(value, count):
    return lax.ppermute(value, "blk", [(i, i ^ 1) for i in range(count)])


def shards(
    activations,
    output_grads,
    basis_in,
    basis_out,
    query_left,
    query_right,
    owners,
    lengths,
    slot_plan,
):
    count = lax.axis_size("blk")
    chips = count // 2
    bits = count.bit_length() - 1
    me = lax.axis_index("blk")
    part = lax.axis_index("parts")
    core, chip = me % 2, me // 2
    seqs_here, max_length, width_in = activations.shape
    width_out = output_grads.shape[2]
    num_queries = owners.shape[0]
    rank_count = query_left.shape[1]
    half_rank = rank_count // 2
    tokens = seqs_here * max_length
    acts = activations.reshape(tokens, width_in)
    grads = output_grads.reshape(tokens, width_out)
    everyone = ("parts", "blk")

    orders = orders_of(bits)
    table = jnp.asarray([place_of(order, chips) for order in orders], jnp.int32)
    mask = jnp.arange(chips, dtype=jnp.int32) ^ chip
    own_at = jnp.take(table[core], mask)
    sib_at = jnp.take(table[1 - core], mask)

    away_in = jnp.take(acts.reshape(tokens, chips, 2, -1), 1 - part, axis=2)
    away_out = jnp.take(grads.reshape(tokens, chips, 2, -1), 1 - part, axis=2)
    away = jnp.concatenate([away_in, away_out], axis=2).reshape(tokens, -1)
    across = [(p * count + i, (1 - p) * count + i) for p in range(2) for i in range(count)]
    other = lax.ppermute(away, everyone, across)

    def half(factor):
        wide = factor.shape[2] // 2
        kept = lax.dynamic_slice_in_dim(factor[0], part * wide, wide, 1)
        return kept.reshape(2, half_rank, chips, wide // chips)

    packed = jnp.concatenate([half(query_left), half(query_right)], axis=3)
    packed = packed.transpose(2, 0, 1, 3).reshape(count, half_rank, -1)
    slots = lax.all_to_all(packed, "blk", 0, 0, tiled=True)
    chosen = jnp.take(slots, owners, axis=0).reshape(num_queries * half_rank, -1)
    own = xor_gather(chosen, orders, count)
    sib = swap_cores(own, count)

    partial = rotate(part, own_at, sib_at, own, sib, basis_in, basis_out)
    to_sum = [(p * count + i, (1 - p) * count + i) for p in range(2) for i in range(count) if i % 2 != p]
    arrived = lax.ppermute(partial.astype(jnp.bfloat16), everyone, to_sum)
    summed = (partial + arrived.astype(jnp.float32)).astype(jnp.bfloat16)
    ranks = num_queries * half_rank
    to_core = [(p * count + i, p * count + (i ^ 1)) for p in range(2) for i in range(count) if i % 2 == p]
    given = lax.ppermute(summed[ranks:], everyone, to_core)
    piece = jnp.where(core == part, summed[:ranks], given)
    own_rotated = xor_gather(piece, orders, count)
    sib_rotated = swap_cores(own_rotated, count)

    mine, theirs = project(part, own_at, sib_at, own_rotated, sib_rotated, acts, grads, other)
    mine = mine + lax.ppermute(theirs, everyone, across)

    seqs = me * seqs_here + jnp.arange(seqs_here, dtype=jnp.int32)
    live = jnp.arange(max_length, dtype=jnp.int32)[None, :] < lengths[slot_plan[seqs]][:, None]
    products = (mine[0] * mine[1]).reshape(seqs_here, max_length, -1)
    sums = jnp.sum(jnp.where(live[:, :, None], products, 0.0), axis=1)
    held = (jnp.sum(sums.reshape(seqs_here, 2, num_queries, half_rank), axis=(1, 3)) / rank_count)[None]
    for bit in range(bits):
        pairs = [(i, i ^ (1 << bit)) for i in range(count)]
        held = jnp.concatenate([held, lax.ppermute(held, "blk", pairs)], axis=0)
    from_device = jnp.arange(count, dtype=jnp.int32) ^ me
    planned = slot_plan.reshape(count, seqs_here)[from_device]
    chooser = planned[None, :, :] == seqs[:, None, None]
    return jnp.sum(jnp.where(chooser[..., None], held[None], 0.0), axis=(1, 2))


def solution(mesh):
    placed = (
        P(("parts", "blk"), None, None),
        P(("parts", "blk"), None, None),
        P("blk", None),
        P("blk", None),
        P("blk", None, None),
        P("blk", None, None),
        P(),
        P("parts"),
        P("parts"),
    )
    return jax.shard_map(
        shards, mesh=mesh, in_specs=placed, out_specs=P(("parts", "blk"), None), check_vma=False
    )
```

time: 285 us -> 201 us (0.71)
  waiting for transfers between devices: 200 us -> 119 us
  local copies, waits for them, and re-layouts: 3.97 us -> 38.3 us
  blocking collectives: 32.1 us -> 0 us
  matrix products: 24.3 us -> 0 us
  starting transfers between devices: 0.09 us -> 20.1 us
  Pallas kernels: 0 us -> 17.5 us
  between operations: 16.3 us -> 2.31 us
  other arithmetic: 7.9 us -> 3.09 us
    psum x1 -> x0, waiting for transfers between devices: 122 us -> none  [spread(): return lax.psum(kept, axis)]
    ppermute x0 -> x16, waiting for transfers between devices: none -> 103 us  [the longest x6 45.6 us: xor_gather(): held = jnp.concatenate([held, lax.ppermute(held, 'blk', pairs)], axis=0)]
    all_gather x2 -> x0, waiting for transfers between devices: 77.4 us -> none  [the longest x1 44.6 us: shards(): lax.all_gather(rotated_out, 'blk', axis=0, tiled=True)]
    unnamed x1 -> x0, blocking collectives: 32.1 us -> none
    another operation x0 -> x4, local copies, waits for them, and re-layouts: none -> 25.5 us  [the longest x2 19.9 us: shards(): away_out = jnp.take(grads.reshape(tokens, chips, 2, -1), 1 - part, axis=2)]
    dot_general x6 -> x0, matrix products: 24.3 us -> none  [the longest x1 14.3 us: shards(): lax.dot_general(basis_out, picked_out, contract, preferred_element_type=j...]
    pallas_call x0 -> x2, Pallas kernels: none -> 17.5 us  [the longest x1 10.4 us: rotate(): pl.pallas_call(rotate_kernel, grid_spec=pltpu.PrefetchScalarGridSpec(num_...]
    all_to_all x0 -> x1, waiting for transfers between devices: none -> 15.3 us  [shards(): slots = lax.all_to_all(packed, 'blk', 0, 0, tiled=True)]
  transfers between devices with their start and end apart: 3 -> 17, of which waited for: 3 -> 15; matrix products, arithmetic and copies ran while one was open for 3% -> 16% of each run, Pallas kernels for 0% -> 0%
where the time goes in v1:
time: 201 us; the launch traced here: 200 us
  waiting for transfers between devices  119 us (59%)
  local copies, waits for them, and re-layouts  38.3 us (19%)
  starting transfers between devices  20.1 us (10%)
  Pallas kernels  17.5 us (9%)
  other arithmetic  3.09 us (2%)
  between operations  2.31 us (1%)
    ppermute x6, waiting for transfers between devices, xor_gather(): held = jnp.concatenate([held, lax.ppermute(held, 'blk', pairs)], axis=0)  45.6 us
    ppermute x1, waiting for transfers between devices, shards(): other = lax.ppermute(away, everyone, across)  40.9 us
    another operation x2, local copies, waits for them, and re-layouts, shards(): away_out = jnp.take(grads.reshape(tokens, chips, 2, -1), 1 - part, axis=2)  19.9 us
    all_to_all x1, waiting for transfers between devices, shards(): slots = lax.all_to_all(packed, 'blk', 0, 0, tiled=True)  15.3 us
    pallas_call x1, Pallas kernels, rotate(): pl.pallas_call(rotate_kernel, grid_spec=pltpu.PrefetchScalarGridSpec(num_...  10.4 us
    ppermute x4, waiting for transfers between devices, shards(): held = jnp.concatenate([held, lax.ppermute(held, 'blk', pairs)], axis=0)  7.88 us
    all_to_all x1, starting transfers between devices, shards(): slots = lax.all_to_all(packed, 'blk', 0, 0, tiled=True)  7.39 us
    unnamed x27, local copies, waits for them, and re-layouts  7.3 us
  transfers between devices with their start and end apart: 17, of which 15 were waited for; matrix products, arithmetic and copies ran while one was open for 16% of the time, Pallas kernels for 0%

profile of v1, /device:TPU:0, one launch (start us, length us, event | category | flops | bytes accessed | tf_op | source)
XLA Modules:
  0.0 199.9 jit_solution(1278796755486826374)
XLA Ops:
  0.0 1.2 copy-done
  1.4 0.9 copy.21
  2.3 7.4 %all-to-all-start = ((bf16[16,16,1152]{2,1,0:T(8,128)(2,1)}), bf16[16,16,1152]{2,1,0:T(8,128)(2,1)S(1)}, u32[]{:S(2)}, u32[]{:S(2)}) async-start(bf16[16,16,1152]{2,1,0:T(8,128)(2,1)} %bitcast.9), calls=%async_computation | async-start | bytes 1179648 | tf_op jit(solution)/shard_map/all_to_all | solution.py:218
  9.9 15.3 %all-to-all-done = bf16[16,16,1152]{2,1,0:T(8,128)(2,1)S(1)} async-done(((bf16[16,16,1152]{2,1,0:T(8,128)(2,1)}), bf16[16,16,1152]{2,1,0:T(8,128)(2,1)S(1)}, u32[]{:S(2)}, u32[]{:S(2)}) %all-to-all-start) | async-done | bytes 589856 | tf_op jit(solution)/shard_map/all_to_all | solution.py:218
  25.2 0.6 gather_fusion.1
  25.9 2.6 %collective-permute-start = (bf16[1,64,1152]{2,1,0:T(8,128)(2,1)S(1)}, bf16[1,64,1152]{2,1,0:T(8,128)(2,1)S(1)}, u32[]{:S(2)}, u32[]{:S(2)}) collective-permute-start(bf16[1,64,1152]{2,1,0:T(8,128)(2,1)S(1)} %bitcast_select_fusion), channel_id=1, source_target_pairs={{0,8},{1,3},{2,10},{3,1},{4,12},{5,7},{6,14},{7,5},{8,0},{9,11},{1... | collective-permute-start | bytes 442376 | tf_op jit(solution)/shard_map/ppermute | solution.py:164
  28.6 5.0 %collective-permute-done = bf16[1,64,1152]{2,1,0:T(8,128)(2,1)S(1)} collective-permute-done((bf16[1,64,1152]{2,1,0:T(8,128)(2,1)S(1)}, bf16[1,64,1152]{2,1,0:T(8,128)(2,1)S(1)}, u32[]{:S(2)}, u32[]{:S(2)}) %collective-permute-start) | collective-permute-done | bytes 147488 | tf_op jit(solution)/shard_map/ppermute | solution.py:164
  33.7 8.0 %collective-permute-done.1 = bf16[2,64,1152]{2,1,0:T(8,128)(2,1)S(1)} collective-permute-done((bf16[2,64,1152]{2,1,0:T(8,128)(2,1)S(1)}, bf16[2,64,1152]{2,1,0:T(8,128)(2,1)S(1)}, u32[]{:S(2)}, u32[]{:S(2)}) %collective-permute-start.1) | collective-permute-done | bytes 294944 | tf_op jit(solution)/shard_map/ppermute | solution.py:164
  41.9 9.9 %collective-permute-done.2 = bf16[4,64,1152]{2,1,0:T(8,128)(2,1)S(1)} collective-permute-done((bf16[4,64,1152]{2,1,0:T(8,128)(2,1)S(1)}, bf16[4,64,1152]{2,1,0:T(8,128)(2,1)S(1)}, u32[]{:S(2)}, u32[]{:S(2)}) %collective-permute-start.2) | collective-permute-done | bytes 589856 | tf_op jit(solution)/shard_map/ppermute | solution.py:164
  51.8 0.1 pad_maximum_fusion.1.own
  52.1 0.6 gather_fusion.3
  52.7 0.6 gather_fusion.2
  53.4 10.8 %reshape_reshape.7 = bf16[160,8,2,896]{3,2,1,0:T(2,128)(2,1)} reshape(bf16[1,160,14336]{2,1,0:T(8,128)(2,1)} %param.13) | data formatting | bytes 9175040 | tf_op jit(solution)/shard_map/reshape;reshape | solution.py:206
  64.2 1.8 reshape_reshape.6
  66.0 3.7 %constant_dynamic-slice_fusion.1 = bf16[160,8,1,256]{3,2,1,0:T(2,128)(2,1)} fusion(bf16[160,8,2,256]{3,2,1,0:T(2,128)(2,1)} %reshape_reshape.6, s32[]{:T(128)S(6)} %select_n.115), kind=kLoop, calls=%fused_computation.36 | loop fusion | bytes 1310724 | solution.py:205
  69.7 9.2 %constant_dynamic-slice_fusion = bf16[160,8,1,896]{3,2,1,0:T(2,128)(2,1)} fusion(bf16[160,8,2,896]{3,2,1,0:T(2,128)(2,1)} %reshape_reshape.7, s32[]{:T(128)S(6)} %select_n.115), kind=kLoop, calls=%fused_computation.35 | loop fusion | bytes 4587524 | solution.py:206
  78.9 1.6 copy-done.4
  80.5 10.4 %rotate.1 = f32[128,1152]{1,0:T(8,128)S(1)} custom-call(s32[1]{0:T(128)} %bitcast.5.part, s32[8]{0:T(128)S(1)} %get-tuple-element.57.own_at, s32[8]{0:T(128)S(1)} %get-tuple-element.56.sib_at, bf16[8,64,1152]{2,1,0:T(8,128)(2,1)S(1)} %pad_maximum_fusion.1.own, bf16[8,64,1152]{2,1,0:T(8,128)(2,1)} %collective-permute-done.3.sib, ...), custom_call_target="tpu_custom_call" | custom-call | tf_op jit(solution)/shard_map/rotate/pallas_call | solution.py:55
  91.0 1.3 collective-permute-start.4
  92.3 0.4 fusion
  92.7 6.9 %collective-permute-done.4 = bf16[128,1152]{1,0:T(8,128)(2,1)S(1)} collective-permute-done((bf16[128,1152]{1,0:T(8,128)(2,1)S(1)}, bf16[128,1152]{1,0:T(8,128)(2,1)S(1)}, u32[]{:S(2)}, u32[]{:S(2)}) %collective-permute-start.4) | collective-permute-done | bytes 294944 | tf_op jit(solution)/shard_map/ppermute | solution.py:225
  99.7 1.5 collective-permute-start.5
  101.3 0.8 collective-permute-done.5
  102.2 1.1 collective-permute-start.6
  103.3 0.2 pad_maximum_fusion
  103.5 2.1 %copy.33 = bf16[20,8,8,1152]{3,1,2,0:T(8,128)(2,1)} copy(bf16[20,8,8,1152]{3,2,1,0:T(8,128)(2,1)S(1)} %bitcast.44) | data formatting | bytes 5898240
  105.6 0.6 collective-permute-start.10
  106.2 3.6 %collective-permute-done.6 = bf16[1,64,1152]{2,1,0:T(8,128)(2,1)S(1)} collective-permute-done((bf16[1,64,1152]{2,1,0:T(8,128)(2,1)S(1)}, bf16[1,64,1152]{2,1,0:T(8,128)(2,1)S(1)}, u32[]{:S(2)}, u32[]{:S(2)}) %collective-permute-start.6) | collective-permute-done | bytes 147488 | tf_op jit(solution)/shard_map/ppermute | solution.py:164
  110.0 9.2 %collective-permute-done.7 = bf16[2,64,1152]{2,1,0:T(8,128)(2,1)S(1)} collective-permute-done((bf16[2,64,1152]{2,1,0:T(8,128)(2,1)S(1)}, bf16[2,64,1152]{2,1,0:T(8,128)(2,1)S(1)}, u32[]{:S(2)}, u32[]{:S(2)}) %collective-permute-start.7) | collective-permute-done | bytes 294944 | tf_op jit(solution)/shard_map/ppermute | solution.py:164
  119.4 9.9 %collective-permute-done.8 = bf16[4,64,1152]{2,1,0:T(8,128)(2,1)S(1)} collective-permute-done((bf16[4,64,1152]{2,1,0:T(8,128)(2,1)S(1)}, bf16[4,64,1152]{2,1,0:T(8,128)(2,1)S(1)}, u32[]{:S(2)}, u32[]{:S(2)}) %collective-permute-start.8) | collective-permute-done | bytes 589856 | tf_op jit(solution)/shard_map/ppermute | solution.py:164
  129.2 0.1 pad_maximum_fusion.2.own
  129.5 0.7 gather_fusion
  130.2 40.9 %collective-permute-done.10.other = bf16[160,9216]{1,0:T(8,128)(2,1)} collective-permute-done((bf16[160,9216]{1,0:T(8,128)(2,1)}, bf16[160,9216]{1,0:T(8,128)(2,1)}, u32[]{:S(2)}, u32[]{:S(2)}) %collective-permute-start.10) | collective-permute-done | bytes 2949152 | tf_op jit(solution)/shard_map/ppermute | solution.py:209
  171.1 2.3 %copy-done.2 = bf16[1,160,14336]{2,1,0:T(8,128)(2,1)S(1)} copy-done((bf16[1,160,14336]{2,1,0:T(8,128)(2,1)S(1)}, bf16[1,160,14336]{2,1,0:T(8,128)(2,1)}, u32[]{:S(2)}) %copy-start.2) | copy-done | bytes 4587544
  173.4 7.0 %project.1 = (f32[2,160,128]{2,1,0:T(8,128)S(1)}, f32[2,160,128]{2,1,0:T(8,128)S(1)}) custom-call(s32[1]{0:T(128)} %bitcast.5.part, s32[8]{0:T(128)S(1)} %get-tuple-element.57.own_at, s32[8]{0:T(128)S(1)} %get-tuple-element.56.sib_at, bf16[8,64,1152]{2,1,0:T(8,128)(2,1)S(1)} %pad_maximum_fusion.2.own, bf16[8,64,1152]{2,1,0:T(8,128)(2,1)} %collective-permute-done.9.sib, ...), custom_call_target="tpu_custom_call" | custom-call | tf_op jit(solution)/shard_map/project/pallas_call | solution.py:121
  180.4 0.5 collective-permute-start.11
  180.9 0.6 dynamic-slice.12
  183.4 0.6 dynamic-slice.13
  184.0 0.6 iota_compare_fusion
  184.6 1.2 collective-permute-done.11
  186.0 0.1 reduce_sum.30
  186.3 1.1 collective-permute-done.12
  187.4 1.7 collective-permute-start.13
  189.1 1.8 collective-permute-done.13
  191.1 3.5 %collective-permute-done.14 = f32[4,1,4]{2,1,0:T(1,128)S(1)} collective-permute-done((f32[4,1,4]{2,1,0:T(1,128)S(1)}, f32[4,1,4]{2,1,0:T(1,128)S(1)}, u32[]{:S(2)}, u32[]{:S(2)}) %collective-permute-start.14) | collective-permute-done | bytes 96 | tf_op jit(solution)/shard_map/ppermute | solution.py:244
  194.6 3.0 %collective-permute-start.15 = (f32[8,1,4]{2,1,0:T(1,128)S(1)}, f32[8,1,4]{2,1,0:T(1,128)S(1)}, u32[]{:S(2)}, u32[]{:S(2)}) collective-permute-start(f32[8,1,4]{2,1,0:T(1,128)S(1)} %pad_maximum_fusion.7), channel_id=1, source_target_pairs={{0,8},{1,9},{2,10},{3,11},{4,12},{5,13},{6,14},{7,15},{8,0},{9,1},... | collective-permute-start | bytes 392 | tf_op jit(solution)/shard_map/ppermute | solution.py:244
  197.7 1.4 collective-permute-done.15
  199.3 0.6 fusion.5
  (71 shorter events, 2.2 us)
Async XLA Ops:
  0.0 1.2 copy-start
  0.0 1.3 copy-start.8
  1.4 8.3 %copy-start.10 = (s32[4]{0:T(128)S(1)}, s32[4]{0:T(128)}, u32[]{:S(2)}) copy-start(s32[4]{0:T(128)} %param.18) | copy-start | bytes 52
  2.3 22.9 %all-to-all-start = ((bf16[16,16,1152]{2,1,0:T(8,128)(2,1)}), bf16[16,16,1152]{2,1,0:T(8,128)(2,1)S(1)}, u32[]{:S(2)}, u32[]{:S(2)}) async-start(bf16[16,16,1152]{2,1,0:T(8,128)(2,1)} %bitcast.9), calls=%async_computation | async-start | bytes 1179648 | tf_op jit(solution)/shard_map/all_to_all | solution.py:218
  25.9 7.7 %collective-permute-start = (bf16[1,64,1152]{2,1,0:T(8,128)(2,1)S(1)}, bf16[1,64,1152]{2,1,0:T(8,128)(2,1)S(1)}, u32[]{:S(2)}, u32[]{:S(2)}) collective-permute-start(bf16[1,64,1152]{2,1,0:T(8,128)(2,1)S(1)} %bitcast_select_fusion), channel_id=1, source_target_pairs={{0,8},{1,3},{2,10},{3,1},{4,12},{5,7},{6,14},{7,5},{8,0},{9,11},{1... | collective-permute-start | bytes 442376 | tf_op jit(solution)/shard_map/ppermute | solution.py:164
  33.6 8.1 %collective-permute-start.1 = (bf16[2,64,1152]{2,1,0:T(8,128)(2,1)S(1)}, bf16[2,64,1152]{2,1,0:T(8,128)(2,1)S(1)}, u32[]{:S(2)}, u32[]{:S(2)}) collective-permute-start(bf16[2,64,1152]{2,1,0:T(8,128)(2,1)S(1)} %pad_maximum_fusion.5), channel_id=1, source_target_pairs={{0,4},{1,9},{2,6},{3,11},{4,0},{5,13},{6,2},{7,15},{8,12},{9,1},{1... | collective-permute-start | bytes 884744 | tf_op jit(solution)/shard_map/ppermute | solution.py:164
  41.8 10.2 %copy-start.9 = (s32[2,8]{1,0:T(2,128)S(1)}, s32[2,8]{1,0:T(2,128)}, u32[]{:S(2)}) copy-start(s32[2,8]{1,0:T(2,128)} %constant.111.clone) | copy-start | bytes 196
  41.8 9.9 %collective-permute-start.2 = (bf16[4,64,1152]{2,1,0:T(8,128)(2,1)S(1)}, bf16[4,64,1152]{2,1,0:T(8,128)(2,1)S(1)}, u32[]{:S(2)}, u32[]{:S(2)}) collective-permute-start(bf16[4,64,1152]{2,1,0:T(8,128)(2,1)S(1)} %pad_maximum_fusion.3), channel_id=1, source_target_pairs={{0,2},{1,5},{2,0},{3,7},{4,6},{5,1},{6,4},{7,3},{8,10},{9,13},{10,... | collective-permute-start | bytes 1769480 | tf_op jit(solution)/shard_map/ppermute | solution.py:164
  51.9 27.0 %collective-permute-start.3 = (bf16[8,64,1152]{2,1,0:T(8,128)(2,1)S(1)}, bf16[8,64,1152]{2,1,0:T(8,128)(2,1)}, u32[]{:S(2)}, u32[]{:S(2)}) collective-permute-start(bf16[8,64,1152]{2,1,0:T(8,128)(2,1)S(1)} %pad_maximum_fusion.1.own), channel_id=1, source_target_pairs={{0,1},{1,0},{2,3},{3,2},{4,5},{5,4},{6,7},{7,6},{8,9},{9,8},{10,11... | collective-permute-start | bytes 3538952 | tf_op jit(solution)/shard_map/ppermute | solution.py:169
  53.4 10.8 %copy-start.3 = (bf16[1,160,4096]{2,1,0:T(8,128)(2,1)S(1)}, bf16[1,160,4096]{2,1,0:T(8,128)(2,1)}, u32[]{:S(2)}) copy-start(bf16[1,160,4096]{2,1,0:T(8,128)(2,1)} %param.12) | copy-start | bytes 3932164
  78.9 1.6 copy-start.4
  80.5 11.8 %copy-start.6 = (bf16[160,8,1,896]{3,2,1,0:T(2,128)(2,1)S(1)}, bf16[160,8,1,896]{3,2,1,0:T(2,128)(2,1)}, u32[]{:S(2)}) copy-start(bf16[160,8,1,896]{3,2,1,0:T(2,128)(2,1)} %constant_dynamic-slice_fusion) | copy-start | bytes 6881284
  91.0 8.6 %collective-permute-start.4 = (bf16[128,1152]{1,0:T(8,128)(2,1)S(1)}, bf16[128,1152]{1,0:T(8,128)(2,1)S(1)}, u32[]{:S(2)}, u32[]{:S(2)}) collective-permute-start(bf16[128,1152]{1,0:T(8,128)(2,1)S(1)} %convert_element_type.9), channel_id=1, source_target_pairs={{1,17},{3,19},{5,21},{7,23},{9,25},{11,27},{13,29},{15,31},{16,0},... | collective-permute-start | bytes 884744 | tf_op jit(solution)/shard_map/ppermute | solution.py:225
  92.7 8.4 %copy-start.7 = (bf16[160,8,1,256]{3,2,1,0:T(2,128)(2,1)S(1)}, bf16[160,8,1,256]{3,2,1,0:T(2,128)(2,1)}, u32[]{:S(2)}) copy-start(bf16[160,8,1,256]{3,2,1,0:T(2,128)(2,1)} %constant_dynamic-slice_fusion.1) | copy-start | bytes 1966084
  99.7 2.5 %collective-permute-start.5 = (bf16[64,1152]{1,0:T(8,128)(2,1)S(1)}, bf16[64,1152]{1,0:T(8,128)(2,1)S(1)}, u32[]{:S(2)}, u32[]{:S(2)}) collective-permute-start(bf16[64,1152]{1,0:T(8,128)(2,1)S(1)} %slice.57), channel_id=1, source_target_pairs={{0,1},{2,3},{4,5},{6,7},{8,9},{10,11},{12,13},{14,15},{17,16},{19,... | collective-permute-start | bytes 442376 | tf_op jit(solution)/shard_map/ppermute | solution.py:229
  102.2 7.7 %collective-permute-start.6 = (bf16[1,64,1152]{2,1,0:T(8,128)(2,1)S(1)}, bf16[1,64,1152]{2,1,0:T(8,128)(2,1)S(1)}, u32[]{:S(2)}, u32[]{:S(2)}) collective-permute-start(bf16[1,64,1152]{2,1,0:T(8,128)(2,1)S(1)} %fusion.2), channel_id=1, source_target_pairs={{0,8},{1,3},{2,10},{3,1},{4,12},{5,7},{6,14},{7,5},{8,0},{9,11},{1... | collective-permute-start | bytes 442376 | tf_op jit(solution)/shard_map/ppermute | solution.py:164
  105.6 65.5 %collective-permute-start.10 = (bf16[160,9216]{1,0:T(8,128)(2,1)}, bf16[160,9216]{1,0:T(8,128)(2,1)}, u32[]{:S(2)}, u32[]{:S(2)}) collective-permute-start(bf16[160,9216]{1,0:T(8,128)(2,1)} %bitcast.28), channel_id=1, source_target_pairs={{0,16},{1,17},{2,18},{3,19},{4,20},{5,21},{6,22},{7,23},{8,24},{9,... | collective-permute-start | bytes 8847368 | tf_op jit(solution)/shard_map/ppermute | solution.py:209
  109.9 9.3 %collective-permute-start.7 = (bf16[2,64,1152]{2,1,0:T(8,128)(2,1)S(1)}, bf16[2,64,1152]{2,1,0:T(8,128)(2,1)S(1)}, u32[]{:S(2)}, u32[]{:S(2)}) collective-permute-start(bf16[2,64,1152]{2,1,0:T(8,128)(2,1)S(1)} %pad_maximum_fusion.6), channel_id=1, source_target_pairs={{0,4},{1,9},{2,6},{3,11},{4,0},{5,13},{6,2},{7,15},{8,12},{9,1},{1... | collective-permute-start | bytes 884744 | tf_op jit(solution)/shard_map/ppermute | solution.py:164
  119.3 10.2 %copy-start.5 = (s32[16]{0:T(128)S(1)}, s32[16]{0:T(128)}, u32[]{:S(2)}) copy-start(s32[16]{0:T(128)} %param.20) | copy-start | bytes 196
  119.3 9.9 %collective-permute-start.8 = (bf16[4,64,1152]{2,1,0:T(8,128)(2,1)S(1)}, bf16[4,64,1152]{2,1,0:T(8,128)(2,1)S(1)}, u32[]{:S(2)}, u32[]{:S(2)}) collective-permute-start(bf16[4,64,1152]{2,1,0:T(8,128)(2,1)S(1)} %pad_maximum_fusion.4), channel_id=1, source_target_pairs={{0,2},{1,5},{2,0},{3,7},{4,6},{5,1},{6,4},{7,3},{8,10},{9,13},{10,... | collective-permute-start | bytes 1769480 | tf_op jit(solution)/shard_map/ppermute | solution.py:164
  129.4 41.7 %collective-permute-start.9 = (bf16[8,64,1152]{2,1,0:T(8,128)(2,1)S(1)}, bf16[8,64,1152]{2,1,0:T(8,128)(2,1)}, u32[]{:S(2)}, u32[]{:S(2)}) collective-permute-start(bf16[8,64,1152]{2,1,0:T(8,128)(2,1)S(1)} %pad_maximum_fusion.2.own), channel_id=1, source_target_pairs={{0,1},{1,0},{2,3},{3,2},{4,5},{5,4},{6,7},{7,6},{8,9},{9,8},{10,11... | collective-permute-start | bytes 3538952 | tf_op jit(solution)/shard_map/ppermute | solution.py:169
  171.1 2.3 %copy-start.2 = (bf16[1,160,14336]{2,1,0:T(8,128)(2,1)S(1)}, bf16[1,160,14336]{2,1,0:T(8,128)(2,1)}, u32[]{:S(2)}) copy-start(bf16[1,160,14336]{2,1,0:T(8,128)(2,1)} %param.13) | copy-start | bytes 13762564
  173.4 10.0 %copy-start.11 = (s32[16]{0:T(128)S(1)}, s32[16]{0:T(128)}, u32[]{:S(2)}) copy-start(s32[16]{0:T(128)} %param.19) | copy-start | bytes 196
  173.4 26.5 %copy-start.1 = (bf16[1,32,14336]{2,1,0:T(8,128)(2,1)S(1)}, bf16[1,32,14336]{2,1,0:T(8,128)(2,1)}, u32[]{:S(2)}) copy-start(bf16[1,32,14336]{2,1,0:T(8,128)(2,1)} %param.17) | copy-start | bytes 2752516
  180.4 5.4 %collective-permute-start.11 = (f32[2,160,128]{2,1,0:T(8,128)S(1)}, f32[2,160,128]{2,1,0:T(8,128)S(1)}, u32[]{:S(2)}, u32[]{:S(2)}) collective-permute-start(f32[2,160,128]{2,1,0:T(8,128)S(1)} %get-tuple-element.9), channel_id=1, source_target_pairs={{0,16},{1,17},{2,18},{3,19},{4,20},{5,21},{6,22},{7,23},{8,24},{9,... | collective-permute-start | bytes 491528 | tf_op jit(solution)/shard_map/ppermute | solution.py:235
  186.3 1.1 collective-permute-start.12
  187.4 3.6 %collective-permute-start.13 = (f32[2,1,4]{2,1,0:T(1,128)S(1)}, f32[2,1,4]{2,1,0:T(1,128)S(1)}, u32[]{:S(2)}, u32[]{:S(2)}) collective-permute-start(f32[2,1,4]{2,1,0:T(1,128)S(1)} %pad_maximum_fusion.9), channel_id=1, source_target_pairs={{0,2},{1,3},{2,0},{3,1},{4,6},{5,7},{6,4},{7,5},{8,10},{9,11},{10,... | collective-permute-start | bytes 104 | tf_op jit(solution)/shard_map/ppermute | solution.py:244
  191.0 3.6 %collective-permute-start.14 = (f32[4,1,4]{2,1,0:T(1,128)S(1)}, f32[4,1,4]{2,1,0:T(1,128)S(1)}, u32[]{:S(2)}, u32[]{:S(2)}) collective-permute-start(f32[4,1,4]{2,1,0:T(1,128)S(1)} %pad_maximum_fusion.8), channel_id=1, source_target_pairs={{0,4},{1,5},{2,6},{3,7},{4,0},{5,1},{6,2},{7,3},{8,12},{9,13},{10,... | collective-permute-start | bytes 200 | tf_op jit(solution)/shard_map/ppermute | solution.py:244
  194.6 4.6 %collective-permute-start.15 = (f32[8,1,4]{2,1,0:T(1,128)S(1)}, f32[8,1,4]{2,1,0:T(1,128)S(1)}, u32[]{:S(2)}, u32[]{:S(2)}) collective-permute-start(f32[8,1,4]{2,1,0:T(1,128)S(1)} %pad_maximum_fusion.7), channel_id=1, source_target_pairs={{0,8},{1,9},{2,10},{3,11},{4,12},{5,13},{6,14},{7,15},{8,0},{9,1},... | collective-permute-start | bytes 392 | tf_op jit(solution)/shard_map/ppermute | solution.py:244

commit v2 on v0

v2 whole, which is shorter than its diff:
```python
import jax
import jax.numpy as jnp
from jax import lax
from jax.experimental import pallas as pl
from jax.experimental.pallas import tpu as pltpu
from jax.sharding import PartitionSpec as P

ROWS = (((1,), (1,)), ((), ()))
EVERYONE = ("parts", "blk")
NEAR = 4
CHAINS = 2
MIB = 1024 * 1024


def dot_rows(left, right):
    return lax.dot_general(left, right, ROWS, preferred_element_type=jnp.float32)


def swapped(spot, bits):
    top, second = 1 << (bits - 1), 1 << (bits - 2)
    rest = spot & (second - 1)
    return rest | (second if spot & top else 0) | (top if spot & second else 0)


def masks_of(bits):
    steps = list(range(bits - 1, 1, -1))
    walks = (steps + [1, 0], steps + [0, 1])
    return walks, [
        [sum(1 << bit for level, bit in enumerate(walk) if spot >> level & 1) for spot in range(1 << bits)]
        for walk in walks
    ]


def pick(low, high, spot):
    half = low.shape[0]
    return low[spot] if spot < half else high[spot - half]


def rotate(part, chunks, chain, factors, bases, rows, total, last):
    own_low, own_high, sib_low, sib_high = factors
    ranks, wide = own_low.shape[1:]
    wide_in = bases[0].shape[1] // (2 * CHAINS * NEAR)
    wide_out = wide - wide_in
    (in_from, in_to), (out_from, out_to) = rows
    count_in, count_out = in_to - in_from, out_to - out_from
    height = count_in + count_out
    if height % 128 or wide_in % 128 or wide_out % 128:
        own = jnp.concatenate([own_low, own_high], axis=0)
        sib = jnp.concatenate([sib_low, sib_high], axis=0)[jnp.array([swapped(s, 2) for s in range(NEAR)])]
        both = jnp.concatenate([own, sib], axis=1)
        both = jnp.take(both, jnp.argsort(chunks), axis=0).transpose(1, 0, 2)
        result = []
        for basis, begin, end, lanes in (
            (bases[0], in_from, in_to, both[:, :, :wide_in]),
            (bases[1], out_from, out_to, both[:, :, wide_in:]),
        ):
            flat = lanes.reshape(2 * ranks, -1)
            kept = lax.dynamic_slice_in_dim(basis[begin:end], (part * CHAINS + chain) * flat.shape[1], flat.shape[1], 1)
            result.append(dot_rows(flat, kept))
        result = jnp.concatenate(result, axis=1)
        if total is not None:
            result = result + total
        return (result, result.astype(jnp.bfloat16)) if last else result

    def kernel(where, low, high, slow, shigh, basis_in, basis_out, *rest):
        if total is not None:
            start, rest = rest[0], rest[1:]
        outs, (buf_in, buf_out, acc, sems) = rest[:-4], rest[-4:]
        base = where[0] * CHAINS + chain
        copies = []
        for spot in range(NEAR):
            column = base * NEAR + where[1 + spot]
            pair = []
            if count_in:
                lanes = pl.ds(pl.multiple_of(column * wide_in, 128), wide_in)
                pair.append(
                    pltpu.make_async_copy(
                        basis_in.at[pl.ds(in_from, count_in), lanes], buf_in.at[spot], sems.at[0, spot]
                    )
                )
            if count_out:
                lanes = pl.ds(pl.multiple_of(column * wide_out, 128), wide_out)
                pair.append(
                    pltpu.make_async_copy(
                        basis_out.at[pl.ds(out_from, count_out), lanes], buf_out.at[spot], sems.at[1, spot]
                    )
                )
            for copy in pair:
                copy.start()
            copies.append(pair)
        for spot in range(NEAR):
            factor = jnp.concatenate([pick(low, high, spot), pick(slow, shigh, swapped(spot, 2))], axis=0)
            for copy in copies[spot]:
                copy.wait()
            if count_in:
                value = dot_rows(buf_in[spot], factor[:, :wide_in])
                acc[:count_in] = value if spot == 0 else acc[:count_in] + value
            if count_out:
                value = dot_rows(buf_out[spot], factor[:, wide_in:])
                acc[count_in:] = value if spot == 0 else acc[count_in:] + value
        value = acc[...].T
        if total is not None:
            value = value + start[...]
        outs[0][...] = value
        if last:
            outs[1][...] = value.astype(jnp.bfloat16)

    vmem = pl.BlockSpec(memory_space=pltpu.VMEM)
    hbm = pl.BlockSpec(memory_space=pl.ANY)
    shapes = [jax.ShapeDtypeStruct((2 * ranks, height), jnp.float32)]
    if last:
        shapes.append(jax.ShapeDtypeStruct((2 * ranks, height), jnp.bfloat16))
    given = [] if total is None else [total]
    results = pl.pallas_call(
        kernel,
        in_specs=[pl.BlockSpec(memory_space=pltpu.SMEM)] + [vmem] * 4 + [hbm] * 2 + [vmem] * len(given),
        out_specs=[vmem] * len(shapes),
        out_shape=shapes,
        scratch_shapes=[
            pltpu.VMEM((NEAR, max(count_in, 16), wide_in), jnp.bfloat16),
            pltpu.VMEM((NEAR, max(count_out, 16), wide_out), jnp.bfloat16),
            pltpu.VMEM((height, 2 * ranks), jnp.float32),
            pltpu.SemaphoreType.DMA((2, NEAR)),
        ],
        compiler_params=pltpu.CompilerParams(vmem_limit_bytes=20 * MIB),
        cost_estimate=pl.CostEstimate(
            flops=4 * ranks * NEAR * (count_in * wide_in + count_out * wide_out),
            bytes_accessed=2 * NEAR * (count_in * wide_in + count_out * wide_out),
            transcendentals=0,
        ),
        name="rotate",
    )(jnp.concatenate([part[None], chunks]), *factors, *bases, *given)
    return tuple(results) if last else results[0]


def project(part, chip_at, factors, lanes, acts, grads, other, totals, bits):
    chips = 1 << bits
    own_low, own_high, sib_low, sib_high = factors
    ranks = own_low.shape[1]
    tokens = acts.shape[0]
    wide_in, wide_out = acts.shape[1] // 2 // chips, grads.shape[1] // 2 // chips
    wide = wide_in + wide_out
    begin, end = lanes
    cut = min(max(wide_in - begin, 0), end - begin)
    has_in, has_out = cut > 0, cut < end - begin
    out_from, out_to = max(begin - wide_in, 0), end - wide_in
    names = [num for num, used in enumerate((has_in, has_out)) if used]
    if wide_in % 128 or wide_out % 128:
        order = jnp.array([swapped(s, bits) for s in range(chips)])
        own = jnp.concatenate([own_low, own_high], axis=0)
        sib = jnp.concatenate([sib_low, sib_high], axis=0)[order]
        both = jnp.take(jnp.concatenate([own, sib], axis=1), jnp.argsort(chip_at), axis=0)
        sides = []
        theirs = other.reshape(tokens, chips, wide)
        mine = jnp.concatenate(
            [
                jnp.take(acts.reshape(tokens, chips, 2, wide_in), part, axis=2),
                jnp.take(grads.reshape(tokens, chips, 2, wide_out), part, axis=2),
            ],
            axis=2,
        )
        for held in (mine, theirs):
            for piece in (slice(0, wide_in), slice(wide_in, wide)):
                sides.append(
                    jnp.einsum("tgf,gcf->tc", held[:, :, piece], both[:, :, piece], preferred_element_type=jnp.float32)
                )
        return jnp.stack(sides).reshape(2, 2, tokens, 2 * ranks)

    def kernel(where, low, high, slow, shigh, acts, grads, other, *rest):
        if totals is not None:
            start, rest = rest[0], rest[1:]
        out = rest[0]
        step = pl.program_id(0)

        @pl.when(step == 0)
        def _():
            out[...] = jnp.zeros_like(out) if totals is None else start[...]

        for spot in range(chips):

            @pl.when(step == spot)
            def _():
                factor = jnp.concatenate([pick(low, high, spot), pick(slow, shigh, swapped(spot, bits))], axis=0)
                if has_in:
                    out[0, 0] += dot_rows(acts[...], factor[:, :cut])
                    out[1, 0] += dot_rows(other[:, begin : begin + cut], factor[:, :cut])
                if has_out:
                    out[0, 1] += dot_rows(grads[:, out_from:out_to], factor[:, cut:])
                    out[1, 1] += dot_rows(other[:, wide_in + out_from : wide_in + out_to], factor[:, cut:])

    shape = (2, 2, tokens, 2 * ranks)
    full = lambda array: pl.BlockSpec(array.shape, lambda s, w: (0,) * array.ndim)
    given = [] if totals is None else [totals]
    return pl.pallas_call(
        kernel,
        grid_spec=pltpu.PrefetchScalarGridSpec(
            num_scalar_prefetch=1,
            grid=(chips,),
            in_specs=[full(factor) for factor in factors]
            + [
                pl.BlockSpec((tokens, wide_in), lambda s, w: (0, 2 * w[1 + s] + w[0])),
                pl.BlockSpec((tokens, wide_out), lambda s, w: (0, 2 * w[1 + s] + w[0])),
                pl.BlockSpec((tokens, wide), lambda s, w: (0, w[1 + s])),
            ]
            + [full(total) for total in given],
            out_specs=pl.BlockSpec(shape, lambda s, w: (0, 0, 0, 0)),
        ),
        out_shape=jax.ShapeDtypeStruct(shape, jnp.float32),
        compiler_params=pltpu.CompilerParams(vmem_limit_bytes=20 * MIB),
        cost_estimate=pl.CostEstimate(
            flops=8 * tokens * ranks * chips * (end - begin),
            bytes_accessed=4 * tokens * chips * (end - begin),
            transcendentals=0,
        ),
        name="project",
    )(jnp.concatenate([part[None], chip_at]), *factors, acts, grads, other, *given)


def features_away(part, acts, grads, chips):
    tokens = acts.shape[0]
    wide_in, wide_out = acts.shape[1] // 2 // chips, grads.shape[1] // 2 // chips
    if wide_in % 128 or wide_out % 128:
        away_in = jnp.take(acts.reshape(tokens, chips, 2, wide_in), 1 - part, axis=2)
        away_out = jnp.take(grads.reshape(tokens, chips, 2, wide_out), 1 - part, axis=2)
        return jnp.concatenate([away_in, away_out], axis=2).reshape(tokens, -1)

    def kernel(where, acts, grads, out):
        out[:, :wide_in] = acts[...]
        out[:, wide_in:] = grads[...]

    wide = wide_in + wide_out
    return pl.pallas_call(
        kernel,
        grid_spec=pltpu.PrefetchScalarGridSpec(
            num_scalar_prefetch=1,
            grid=(chips,),
            in_specs=[
                pl.BlockSpec((tokens, wide_in), lambda g, w: (0, 2 * g + 1 - w[0])),
                pl.BlockSpec((tokens, wide_out), lambda g, w: (0, 2 * g + 1 - w[0])),
            ],
            out_specs=pl.BlockSpec((tokens, wide), lambda g, w: (0, g)),
        ),
        out_shape=jax.ShapeDtypeStruct((tokens, chips * wide), acts.dtype),
        cost_estimate=pl.CostEstimate(flops=0, bytes_accessed=4 * tokens * chips * wide, transcendentals=0),
        name="features_away",
    )(part[None], acts, grads)


def shards(
    activations,
    output_grads,
    basis_in,
    basis_out,
    query_left,
    query_right,
    owners,
    lengths,
    slot_plan,
):
    count = lax.axis_size("blk")
    chips = count // 2
    bits = chips.bit_length() - 1
    me = lax.axis_index("blk")
    part = lax.axis_index("parts")
    core, chip = me % 2, me // 2
    seqs_here, max_length, width_in = activations.shape
    num_queries = owners.shape[0]
    rank_count = query_left.shape[1]
    half_rank = rank_count // 2
    ranks = num_queries * half_rank
    tokens = seqs_here * max_length
    acts = activations.reshape(tokens, width_in)
    grads = output_grads.reshape(tokens, -1)
    across = [(p * count + i, (1 - p) * count + i) for p in range(2) for i in range(count)]

    def to_chip(value, mask):
        return lax.ppermute(value, "blk", [(i, i ^ (2 * mask)) for i in range(count)])

    def along(value, first, second):
        return lax.ppermute(value, "blk", [(i, i ^ (2 << (second if i % 2 else first))) for i in range(count)])

    def to_core(value):
        return lax.ppermute(value, "blk", [(i, i ^ 1) for i in range(count)])

    walks, masks = masks_of(bits)
    chip_at = jnp.where(core == 0, jnp.array(masks[0], jnp.int32), jnp.array(masks[1], jnp.int32)) ^ chip
    _, near_masks = masks_of(2)
    near_at = jnp.where(core == 0, jnp.array(near_masks[0], jnp.int32), jnp.array(near_masks[1], jnp.int32)) ^ (
        chip % NEAR
    )

    def half(factor):
        wide = factor.shape[2] // 2
        kept = lax.dynamic_slice_in_dim(factor[0], part * wide, wide, 1)
        return kept.reshape(2, half_rank, CHAINS, NEAR, wide // (CHAINS * NEAR))

    packed = jnp.concatenate([half(query_left), half(query_right)], axis=4).transpose(0, 3, 2, 1, 4)
    mine = jnp.take(packed, core, axis=0)
    slot_pair = jnp.stack([mine, to_core(jnp.take(packed, 1 - core, axis=0))], axis=1)
    messages = [jnp.take(slot_pair, (chip % NEAR) ^ mask, axis=0) for mask in range(NEAR)]
    found = [messages[0]] + [to_chip(messages[mask], mask) for mask in range(1, NEAR)]

    acts_late, grads_late, *_ = lax.optimization_barrier((acts, grads, *messages))
    other = lax.ppermute(features_away(part, acts_late, grads_late, chips), EVERYONE, across)

    source = (owners // 2) ^ chip
    spot = jnp.minimum(source, NEAR - 1) * 2 + ((owners % 2) ^ core)
    known = (source < NEAR)[:, None, None]
    slots = jnp.concatenate(found, axis=0)
    gathered = []
    for chain in range(CHAINS):
        dense = jnp.where(known, jnp.take(slots[:, chain], spot, axis=0), 0).reshape(1, ranks, -1)
        for bit in range(bits - 1, 1, -1):
            dense = dense + to_chip(dense, 1 << bit)
        low = jnp.concatenate([dense, along(dense, 1, 0)], axis=0)
        high = along(low, 0, 1)
        gathered.append((low, high, to_core(low), to_core(high)))

    rows_in, rows_out = basis_in.shape[0], basis_out.shape[0]
    wide = rows_in + rows_out
    first = (wide // 128 + 1) // 2 * 128
    splits = [(0, wide)] if rows_in % 128 or rows_out % 128 or first <= rows_in else [(0, first), (first, wide)]
    bases = (basis_in, basis_out)
    everything = ((0, rows_in), (0, rows_out))
    total = None
    for chain in range(CHAINS - 1):
        total = rotate(part, near_at, chain, gathered[chain], bases, everything, total, False)
    to_sum = [(p * count + i, (1 - p) * count + i) for p in range(2) for i in range(count) if i % 2 != p]
    to_half = [(p * count + i, p * count + (i ^ 1)) for p in range(2) for i in range(count) if i % 2 == p]
    projected = None
    for begin, end in splits:
        rows = (
            (min(begin, rows_in), min(end, rows_in)),
            (max(begin - rows_in, 0), max(end - rows_in, 0)),
        )
        so_far = None if total is None else total[:, begin:end]
        partial, sent = rotate(part, near_at, CHAINS - 1, gathered[-1], bases, rows, so_far, True)
        arrived = lax.ppermute(sent, EVERYONE, to_sum)
        summed = (partial + arrived.astype(jnp.float32)).astype(jnp.bfloat16)
        given = lax.ppermute(summed[ranks:], EVERYONE, to_half)
        low = jnp.where(core == part, summed[:ranks], given)[None]
        for level in range(bits - 1):
            low = jnp.concatenate([low, along(low, walks[0][level], walks[1][level])], axis=0)
        high = along(low, walks[0][-1], walks[1][-1])
        factors = (low, high, to_core(low), to_core(high))
        projected = project(part, chip_at, factors, (begin, end), acts, grads, other, projected, bits)

    mine = projected[0] + lax.ppermute(projected[1], EVERYONE, across)
    seqs = me * seqs_here + jnp.arange(seqs_here, dtype=jnp.int32)
    live = jnp.arange(max_length, dtype=jnp.int32)[None, :] < lengths[slot_plan[seqs]][:, None]
    products = (mine[0] * mine[1]).reshape(seqs_here, max_length, -1)
    sums = jnp.sum(jnp.where(live[:, :, None], products, 0.0), axis=1)
    held = (jnp.sum(sums.reshape(seqs_here, 2, num_queries, half_rank), axis=(1, 3)) / rank_count)[None]
    for bit in range(bits + 1):
        pairs = [(i, i ^ (1 << bit)) for i in range(count)]
        held = jnp.concatenate([held, lax.ppermute(held, "blk", pairs)], axis=0)
    from_device = jnp.arange(count, dtype=jnp.int32) ^ me
    planned = slot_plan.reshape(count, seqs_here)[from_device]
    chooser = planned[None, :, :] == seqs[:, None, None]
    return jnp.sum(jnp.where(chooser[..., None], held[None], 0.0), axis=(1, 2))


def solution(mesh):
    placed = (
        P(("parts", "blk"), None, None),
        P(("parts", "blk"), None, None),
        P("blk", None),
        P("blk", None),
        P("blk", None, None),
        P("blk", None, None),
        P(),
        P("parts"),
        P("parts"),
    )
    return jax.shard_map(
        shards, mesh=mesh, in_specs=placed, out_specs=P(("parts", "blk"), None), check_vma=False
    )
```

time: 285 us -> 168 us (0.59)
  waiting for transfers between devices: 200 us -> 52.7 us
  starting transfers between devices: 0.09 us -> 36.1 us
  local copies, waits for them, and re-layouts: 3.97 us -> 37.1 us
  Pallas kernels: 0 us -> 32.4 us
  blocking collectives: 32.1 us -> 0 us
  matrix products: 24.3 us -> 0 us
  between operations: 16.3 us -> 2.26 us
    psum x1 -> x0, waiting for transfers between devices: 122 us -> none  [spread(): return lax.psum(kept, axis)]
    all_gather x2 -> x0, waiting for transfers between devices: 77.4 us -> none  [the longest x1 44.6 us: shards(): lax.all_gather(rotated_out, 'blk', axis=0, tiled=True)]
    ppermute x0 -> x34, waiting for transfers between devices: none -> 52.7 us  [the longest x10 22.3 us: along(): lax.ppermute(value, 'blk', [(i, i ^ 2 << (second if i % 2 else first)) fo...]
    ppermute x0 -> x34, starting transfers between devices: none -> 36.1 us  [the longest x10 15.1 us: along(): lax.ppermute(value, 'blk', [(i, i ^ 2 << (second if i % 2 else first)) fo...]
    pallas_call x0 -> x6, Pallas kernels: none -> 32.4 us  [the longest x2 13.1 us: project(): pl.pallas_call(kernel, grid_spec=pltpu.PrefetchScalarGridSpec(num_scalar_...]
    unnamed x1 -> x0, blocking collectives: 32.1 us -> none
    unnamed x23 -> x40, local copies, waits for them, and re-layouts: 0.83 us -> 31 us
    dot_general x6 -> x0, matrix products: 24.3 us -> none  [the longest x1 14.3 us: shards(): lax.dot_general(basis_out, picked_out, contract, preferred_element_type=j...]
  transfers between devices with their start and end apart: 3 -> 34, of which waited for: 3 -> 18; matrix products, arithmetic and copies ran while one was open for 3% -> 4% of each run, Pallas kernels for 0% -> 16%
where the time goes in v2:
time: 168 us; the launch traced here: 167 us
  waiting for transfers between devices  52.7 us (31%)
  local copies, waits for them, and re-layouts  37.1 us (22%)
  starting transfers between devices  36.1 us (21%)
  Pallas kernels  32.4 us (19%)
  other arithmetic  6.47 us (4%)
  between operations  2.26 us (1%)
    unnamed x40, local copies, waits for them, and re-layouts  31 us
    ppermute x10, waiting for transfers between devices, along(): lax.ppermute(value, 'blk', [(i, i ^ 2 << (second if i % 2 else first)) fo...  22.3 us
    ppermute x10, starting transfers between devices, along(): lax.ppermute(value, 'blk', [(i, i ^ 2 << (second if i % 2 else first)) fo...  15.1 us
    ppermute x5, waiting for transfers between devices, to_chip(): return lax.ppermute(value, 'blk', [(i, i ^ 2 * mask) for i in range(count)])  13.8 us
    pallas_call x2, Pallas kernels, project(): pl.pallas_call(kernel, grid_spec=pltpu.PrefetchScalarGridSpec(num_scalar_...  13.1 us
    pallas_call x3, Pallas kernels, rotate(): pl.pallas_call(kernel, in_specs=[pl.BlockSpec(memory_space=pltpu.SMEM)] +...  13 us
    ppermute x4, waiting for transfers between devices, shards(): held = jnp.concatenate([held, lax.ppermute(held, 'blk', pairs)], axis=0)  10.4 us
    ppermute x5, starting transfers between devices, to_chip(): return lax.ppermute(value, 'blk', [(i, i ^ 2 * mask) for i in range(count)])  7.59 us
  transfers between devices with their start and end apart: 34, of which 18 were waited for; matrix products, arithmetic and copies ran while one was open for 4% of the time, Pallas kernels for 16%

profile of v2, /device:TPU:0, one launch (start us, length us, event | category | flops | bytes accessed | tf_op | source)
XLA Modules:
  0.0 167.1 jit_solution(11200401560923084432)
XLA Ops:
  0.0 1.0 constant_dynamic-slice_fusion.1
  2.7 1.2 collective-permute-done
  3.9 2.0 %broadcast_select_fusion.3 = (bf16[1,2,2,16,1152]{4,0,2,3,1:T(2,128)(2,1)S(1)}, bf16[1,2,2,16,1152]{4,0,2,3,1:T(2,128)(2,1)S(1)}, bf16[1,2,2,16,1152]{4,0,2,3,1:T(2,128)(2,1)S(1)}, bf16[1,2,2,16,1152]{4,0,2,3,1:T(2,128)(2,1)S(1)}) fusion(pred[]{:T(512)S(6)} %and.58, s32[]{:T(128)S(6)} %select_n.173, bf16[4,1,2,16,1152]{4,0,2,3,1:T(4,128)(2,1)S(1)} %bitcast.67, ...), kind=kLoop, calls=%fused_computation.16 | loop fusion | flops 1474560 | bytes 1179668 | tf_op jit(solution)/shard_map/jit(_take)/select_n | solution.py:300
  6.0 4.0 %collective-permute-start.3 = (bf16[2,2,16,1152]{3,2,1,0:T(8,128)(2,1)S(1)}, bf16[2,2,16,1152]{3,2,1,0:T(8,128)(2,1)S(1)}, u32[]{:S(2)}, u32[]{:S(2)}) collective-permute-start(bf16[2,2,16,1152]{3,2,1,0:T(8,128)(2,1)S(1)} %bitcast.70), channel_id=1, source_target_pairs={{0,6},{1,7},{2,4},{3,5},{4,2},{5,3},{6,0},{7,1},{8,14},{9,15},{10,... | collective-permute-start | bytes 442376 | tf_op jit(solution)/shard_map/ppermute | solution.py:277
  10.7 3.9 %collective-permute-done.3 = bf16[2,2,16,1152]{3,2,1,0:T(8,128)(2,1)S(1)} collective-permute-done((bf16[2,2,16,1152]{3,2,1,0:T(8,128)(2,1)S(1)}, bf16[2,2,16,1152]{3,2,1,0:T(8,128)(2,1)S(1)}, u32[]{:S(2)}, u32[]{:S(2)}) %collective-permute-start.3) | collective-permute-done | bytes 147488 | tf_op jit(solution)/shard_map/ppermute | solution.py:277
  14.6 2.9 %collective-permute-done.2 = bf16[2,2,16,1152]{3,2,1,0:T(8,128)(2,1)S(1)} collective-permute-done((bf16[2,2,16,1152]{3,2,1,0:T(8,128)(2,1)S(1)}, bf16[2,2,16,1152]{3,2,1,0:T(8,128)(2,1)S(1)}, u32[]{:S(2)}, u32[]{:S(2)}) %collective-permute-start.2) | collective-permute-done | bytes 147488 | tf_op jit(solution)/shard_map/ppermute | solution.py:277
  18.9 2.6 %collective-permute-start.9 = (bf16[1,64,1152]{2,1,0:T(8,128)(2,1)S(1)}, bf16[1,64,1152]{2,1,0:T(8,128)(2,1)S(1)}, u32[]{:S(2)}, u32[]{:S(2)}) collective-permute-start(bf16[1,64,1152]{2,1,0:T(8,128)(2,1)S(1)} %bitcast.65), channel_id=1, source_target_pairs={{0,8},{1,9},{2,10},{3,11},{4,12},{5,13},{6,14},{7,15},{8,0},{9,1},... | collective-permute-start | bytes 442376 | tf_op jit(solution)/shard_map/ppermute | solution.py:277
  21.6 6.3 %features_away.1 = bf16[160,9216]{1,0:T(8,128)(2,1)} custom-call(s32[1]{0:T(128)} %bitcast.5.where, bf16[160,4096]{1,0:T(8,128)(2,1)} %bitcast.59, bf16[160,14336]{1,0:T(8,128)(2,1)} %bitcast.56), custom_call_target="tpu_custom_call" | custom-call | bytes 5898240 | tf_op jit(solution)/shard_map/features_away/pallas_call | solution.py:232
  27.9 1.5 collective-permute-start.21
  29.8 1.6 collective-permute-start.10
  31.4 7.0 %collective-permute-done.4 = bf16[1,64,1152]{2,1,0:T(8,128)(2,1)S(1)} collective-permute-done((bf16[1,64,1152]{2,1,0:T(8,128)(2,1)S(1)}, bf16[1,64,1152]{2,1,0:T(8,128)(2,1)S(1)}, u32[]{:S(2)}, u32[]{:S(2)}) %collective-permute-start.4) | collective-permute-done | bytes 147488 | tf_op jit(solution)/shard_map/ppermute | solution.py:277
  39.3 1.7 %collective-permute-start.11 = (bf16[2,64,1152]{2,1,0:T(8,128)(2,1)}, bf16[2,64,1152]{2,1,0:T(8,128)(2,1)}, u32[]{:S(2)}, u32[]{:S(2)}) collective-permute-start(bf16[2,64,1152]{2,1,0:T(8,128)(2,1)} %pad_maximum_fusion.3.low), channel_id=1, source_target_pairs={{0,2},{1,5},{2,0},{3,7},{4,6},{5,1},{6,4},{7,3},{8,10},{9,13},{10,... | collective-permute-start | bytes 884744 | tf_op jit(solution)/shard_map/ppermute | solution.py:280
  41.0 4.0 %collective-permute-done.5 = bf16[1,64,1152]{2,1,0:T(8,128)(2,1)S(1)} collective-permute-done((bf16[1,64,1152]{2,1,0:T(8,128)(2,1)S(1)}, bf16[1,64,1152]{2,1,0:T(8,128)(2,1)S(1)}, u32[]{:S(2)}, u32[]{:S(2)}) %collective-permute-start.5) | collective-permute-done | bytes 147488 | tf_op jit(solution)/shard_map/ppermute | solution.py:280
  45.0 2.0 %collective-permute-start.6 = (bf16[2,64,1152]{2,1,0:T(8,128)(2,1)S(1)}, bf16[2,64,1152]{2,1,0:T(8,128)(2,1)}, u32[]{:S(2)}, u32[]{:S(2)}) collective-permute-start(bf16[2,64,1152]{2,1,0:T(8,128)(2,1)S(1)} %pad_maximum_fusion.2.low), channel_id=1, source_target_pairs={{0,2},{1,5},{2,0},{3,7},{4,6},{5,1},{6,4},{7,3},{8,10},{9,13},{10,... | collective-permute-start | bytes 884744 | tf_op jit(solution)/shard_map/ppermute | solution.py:280
  47.5 4.3 %collective-permute-done.6.high = bf16[2,64,1152]{2,1,0:T(8,128)(2,1)} collective-permute-done((bf16[2,64,1152]{2,1,0:T(8,128)(2,1)S(1)}, bf16[2,64,1152]{2,1,0:T(8,128)(2,1)}, u32[]{:S(2)}, u32[]{:S(2)}) %collective-permute-start.6) | collective-permute-done | bytes 294944 | tf_op jit(solution)/shard_map/ppermute | solution.py:280
  52.0 8.3 %copy-done.1 = bf16[896,14336]{1,0:T(8,128)(2,1)S(1)} copy-done((bf16[896,14336]{1,0:T(8,128)(2,1)S(1)}, bf16[896,14336]{1,0:T(8,128)(2,1)}, u32[]{:S(2)}) %copy-start.1) | copy-done | bytes 25690136
  60.3 5.7 %rotate.3 = f32[128,1152]{1,0:T(8,128)S(1)} custom-call(s32[5]{0:T(128)S(1)} %pad_add_fusion.1.where, bf16[2,64,1152]{2,1,0:T(8,128)(2,1)} %pad_maximum_fusion.3.low, bf16[2,64,1152]{2,1,0:T(8,128)(2,1)} %collective-permute-done.11.high, bf16[2,64,1152]{2,1,0:T(8,128)(2,1)S(1)} %collective-permute-done.12.slow, ...), custom_call_target="tpu_custom_call" | custom-call | flops 889192448 | bytes 6946816 | tf_op jit(solution)/shard_map/rotate/pallas_call | solution.py:114
  66.0 0.8 copy-done.7
  66.8 8.4 %copy-done.2 = bf16[896,14336]{1,0:T(8,128)(2,1)S(1)} copy-done((bf16[896,14336]{1,0:T(8,128)(2,1)S(1)}, bf16[896,14336]{1,0:T(8,128)(2,1)}, u32[]{:S(2)}) %copy-start.2) | copy-done | bytes 25690136
  75.2 3.4 %rotate.5 = (f32[128,640]{1,0:T(8,128)S(1)}, bf16[128,640]{1,0:T(8,128)(2,1)S(1)}) custom-call(s32[5]{0:T(128)S(1)} %pad_add_fusion.1.where, bf16[2,64,1152]{2,1,0:T(8,128)(2,1)S(1)} %pad_maximum_fusion.2.low, bf16[2,64,1152]{2,1,0:T(8,128)(2,1)} %collective-permute-done.6.high, bf16[2,64,1152]{2,1,0:T(8,128)(2,1)S(1)} %collective-permute-done.7.slow, ...), custom_call_target="tpu_custom_call" | custom-call | flops 419430400 | bytes 3276800 | tf_op jit(solution)/shard_map/rotate/pallas_call | solution.py:114
  79.4 1.3 collective-permute-start.22
  80.7 1.0 slice.92.rest_0_
  81.7 8.3 %copy-done.3 = bf16[896,14336]{1,0:T(8,128)(2,1)S(1)} copy-done((bf16[896,14336]{1,0:T(8,128)(2,1)S(1)}, bf16[896,14336]{1,0:T(8,128)(2,1)}, u32[]{:S(2)}) %copy-start.3) | copy-done | bytes 25690136
  90.0 1.0 copy-done.9
  90.9 1.0 copy-done.11
  91.9 3.9 %rotate.4 = (f32[128,512]{1,0:T(8,128)S(1)}, bf16[128,512]{1,0:T(8,128)(2,1)S(1)}) custom-call(s32[5]{0:T(128)S(1)} %pad_add_fusion.1.where, bf16[2,64,1152]{2,1,0:T(8,128)(2,1)S(1)} %pad_maximum_fusion.2.low, bf16[2,64,1152]{2,1,0:T(8,128)(2,1)} %collective-permute-done.6.high, bf16[2,64,1152]{2,1,0:T(8,128)(2,1)S(1)} %copy-done.9, ...), custom_call_target="tpu_custom_call" | custom-call | flops 469762048 | bytes 3670016 | tf_op jit(solution)/shard_map/rotate/pallas_call | solution.py:114
  95.8 1.4 collective-permute-start.14
  97.3 1.1 add_convert_fusion
  98.4 3.9 %collective-permute-start.23 = (bf16[64,640]{1,0:T(8,128)(2,1)S(1)}, bf16[64,640]{1,0:T(8,128)(2,1)S(1)}, u32[]{:S(2)}, u32[]{:S(2)}) collective-permute-start(bf16[64,640]{1,0:T(8,128)(2,1)S(1)} %slice.97), channel_id=1, source_target_pairs={{0,1},{2,3},{4,5},{6,7},{8,9},{10,11},{12,13},{14,15},{17,16},{19,... | collective-permute-start | bytes 245768 | tf_op jit(solution)/shard_map/ppermute | solution.py:340
  102.3 1.2 collective-permute-done.14
  103.6 1.5 collective-permute-start.15
  105.8 2.4 %collective-permute-start.16 = (bf16[1,64,512]{2,1,0:T(8,128)(2,1)S(1)}, bf16[1,64,512]{2,1,0:T(8,128)(2,1)S(1)}, u32[]{:S(2)}, u32[]{:S(2)}) collective-permute-start(bf16[1,64,512]{2,1,0:T(8,128)(2,1)S(1)} %fusion.8), channel_id=1, source_target_pairs={{0,8},{1,9},{2,10},{3,11},{4,12},{5,13},{6,14},{7,15},{8,0},{9,1},... | collective-permute-start | bytes 196616 | tf_op jit(solution)/shard_map/ppermute | solution.py:280
  108.1 4.7 %collective-permute-done.24 = bf16[1,64,640]{2,1,0:T(8,128)(2,1)S(1)} collective-permute-done((bf16[1,64,640]{2,1,0:T(8,128)(2,1)S(1)}, bf16[1,64,640]{2,1,0:T(8,128)(2,1)S(1)}, u32[]{:S(2)}, u32[]{:S(2)}) %collective-permute-start.24) | collective-permute-done | bytes 81952 | tf_op jit(solution)/shard_map/ppermute | solution.py:280
  113.5 1.5 collective-permute-start.17
  115.0 4.2 %collective-permute-done.25 = bf16[2,64,640]{2,1,0:T(8,128)(2,1)S(1)} collective-permute-done((bf16[2,64,640]{2,1,0:T(8,128)(2,1)S(1)}, bf16[2,64,640]{2,1,0:T(8,128)(2,1)S(1)}, u32[]{:S(2)}, u32[]{:S(2)}) %collective-permute-start.25) | collective-permute-done | bytes 163872 | tf_op jit(solution)/shard_map/ppermute | solution.py:280
  119.2 2.8 %collective-permute-start.26 = (bf16[4,64,640]{2,1,0:T(8,128)(2,1)S(1)}, bf16[4,64,640]{2,1,0:T(8,128)(2,1)S(1)}, u32[]{:S(2)}, u32[]{:S(2)}) collective-permute-start(bf16[4,64,640]{2,1,0:T(8,128)(2,1)S(1)} %pad_maximum_fusion.1.low), channel_id=1, source_target_pairs={{0,2},{1,5},{2,0},{3,7},{4,6},{5,1},{6,4},{7,3},{8,10},{9,13},{10,... | collective-permute-start | bytes 983048 | tf_op jit(solution)/shard_map/ppermute | solution.py:280
  122.1 2.8 %collective-permute-start.18 = (bf16[4,64,512]{2,1,0:T(8,128)(2,1)S(1)}, bf16[4,64,512]{2,1,0:T(8,128)(2,1)}, u32[]{:S(2)}, u32[]{:S(2)}) collective-permute-start(bf16[4,64,512]{2,1,0:T(8,128)(2,1)S(1)} %pad_maximum_fusion.4.low), channel_id=1, source_target_pairs={{0,2},{1,5},{2,0},{3,7},{4,6},{5,1},{6,4},{7,3},{8,10},{9,13},{10,... | collective-permute-start | bytes 786440 | tf_op jit(solution)/shard_map/ppermute | solution.py:280
  125.0 2.2 %collective-permute-done.26.high = bf16[4,64,640]{2,1,0:T(8,128)(2,1)S(1)} collective-permute-done((bf16[4,64,640]{2,1,0:T(8,128)(2,1)S(1)}, bf16[4,64,640]{2,1,0:T(8,128)(2,1)S(1)}, u32[]{:S(2)}, u32[]{:S(2)}) %collective-permute-start.26) | collective-permute-done | bytes 327712 | tf_op jit(solution)/shard_map/ppermute | solution.py:280
  127.7 2.4 %collective-permute-done.18.high = bf16[4,64,512]{2,1,0:T(8,128)(2,1)} collective-permute-done((bf16[4,64,512]{2,1,0:T(8,128)(2,1)S(1)}, bf16[4,64,512]{2,1,0:T(8,128)(2,1)}, u32[]{:S(2)}, u32[]{:S(2)}) %collective-permute-start.18) | collective-permute-done | bytes 262176 | tf_op jit(solution)/shard_map/ppermute | solution.py:280
  130.9 2.3 %copy-done.4 = bf16[1,160,14336]{2,1,0:T(8,128)(2,1)S(1)} copy-done((bf16[1,160,14336]{2,1,0:T(8,128)(2,1)S(1)}, bf16[1,160,14336]{2,1,0:T(8,128)(2,1)}, u32[]{:S(2)}) %copy-start.4) | copy-done | bytes 4587544
  133.1 6.6 %project.2.rest_0_ = f32[2,2,160,128]{3,2,1,0:T(8,128)S(1)} custom-call(s32[9]{0:T(128)S(1)} %pad_add_fusion.where, bf16[4,64,640]{2,1,0:T(8,128)(2,1)S(1)} %pad_maximum_fusion.1.low, bf16[4,64,640]{2,1,0:T(8,128)(2,1)S(1)} %collective-permute-done.26.high, bf16[4,64,640]{2,1,0:T(8,128)(2,1)S(1)} %collective-permute-done.27.slow, ...), custom_call_target="tpu_custom_call" | custom-call | flops 419430400 | bytes 3276800 | tf_op jit(solution)/shard_map/project/pallas_call | solution.py:194
  139.8 6.5 %project.3 = f32[2,2,160,128]{3,2,1,0:T(8,128)S(1)} custom-call(s32[9]{0:T(128)S(1)} %pad_add_fusion.where, bf16[4,64,512]{2,1,0:T(8,128)(2,1)S(1)} %pad_maximum_fusion.4.low, bf16[4,64,512]{2,1,0:T(8,128)(2,1)} %collective-permute-done.18.high, bf16[4,64,512]{2,1,0:T(8,128)(2,1)} %collective-permute-done.19.slow, ...), custom_call_target="tpu_custom_call" | custom-call | flops 335544320 | bytes 2621440 | tf_op jit(solution)/shard_map/project/pallas_call | solution.py:194
  149.8 3.2 %collective-permute-done.29 = f32[2,160,128]{2,1,0:T(8,128)S(1)} collective-permute-done((f32[2,160,128]{2,1,0:T(8,128)S(1)}, f32[2,160,128]{2,1,0:T(8,128)S(1)}, u32[]{:S(2)}, u32[]{:S(2)}) %collective-permute-start.29) | collective-permute-done | bytes 163872 | tf_op jit(solution)/shard_map/ppermute | solution.py:348
  153.5 1.1 collective-permute-done.30
  154.6 2.0 %collective-permute-start.31 = (f32[2,1,4]{2,1,0:T(1,128)S(1)}, f32[2,1,4]{2,1,0:T(1,128)S(1)}, u32[]{:S(2)}, u32[]{:S(2)}) collective-permute-start(f32[2,1,4]{2,1,0:T(1,128)S(1)} %pad_maximum_fusion.9), channel_id=1, source_target_pairs={{0,2},{1,3},{2,0},{3,1},{4,6},{5,7},{6,4},{7,5},{8,10},{9,11},{10,... | collective-permute-start | bytes 104 | tf_op jit(solution)/shard_map/ppermute | solution.py:356
  156.6 1.5 collective-permute-done.31
  158.3 3.5 %collective-permute-done.32 = f32[4,1,4]{2,1,0:T(1,128)S(1)} collective-permute-done((f32[4,1,4]{2,1,0:T(1,128)S(1)}, f32[4,1,4]{2,1,0:T(1,128)S(1)}, u32[]{:S(2)}, u32[]{:S(2)}) %collective-permute-start.32) | collective-permute-done | bytes 96 | tf_op jit(solution)/shard_map/ppermute | solution.py:356
  162.0 4.3 %collective-permute-done.33 = f32[8,1,4]{2,1,0:T(1,128)S(1)} collective-permute-done((f32[8,1,4]{2,1,0:T(1,128)S(1)}, f32[8,1,4]{2,1,0:T(1,128)S(1)}, u32[]{:S(2)}, u32[]{:S(2)}) %collective-permute-start.33) | collective-permute-done | bytes 160 | tf_op jit(solution)/shard_map/ppermute | solution.py:356
  (128 shorter events, 12.8 us)
Async XLA Ops:
  2.2 1.7 %collective-permute-start = (bf16[4,2,16,1152]{3,0,1,2:T(4,128)(2,1)S(1)}, bf16[4,2,16,1152]{3,0,1,2:T(4,128)(2,1)S(1)}, u32[]{:S(2)}, u32[]{:S(2)}) collective-permute-start(bf16[4,2,16,1152]{3,0,1,2:T(4,128)(2,1)S(1)} %get-tuple-element.75), channel_id=1, source_target_pairs={{0,1},{1,0},{2,3},{3,2},{4,5},{5,4},{6,7},{7,6},{8,9},{9,8},{10,11... | collective-permute-start | bytes 884744 | tf_op jit(solution)/shard_map/ppermute | solution.py:283
  6.0 8.6 %collective-permute-start.3 = (bf16[2,2,16,1152]{3,2,1,0:T(8,128)(2,1)S(1)}, bf16[2,2,16,1152]{3,2,1,0:T(8,128)(2,1)S(1)}, u32[]{:S(2)}, u32[]{:S(2)}) collective-permute-start(bf16[2,2,16,1152]{3,2,1,0:T(8,128)(2,1)S(1)} %bitcast.70), channel_id=1, source_target_pairs={{0,6},{1,7},{2,4},{3,5},{4,2},{5,3},{6,0},{7,1},{8,14},{9,15},{10,... | collective-permute-start | bytes 442376 | tf_op jit(solution)/shard_map/ppermute | solution.py:277
  10.0 7.5 %collective-permute-start.2 = (bf16[2,2,16,1152]{3,2,1,0:T(8,128)(2,1)S(1)}, bf16[2,2,16,1152]{3,2,1,0:T(8,128)(2,1)S(1)}, u32[]{:S(2)}, u32[]{:S(2)}) collective-permute-start(bf16[2,2,16,1152]{3,2,1,0:T(8,128)(2,1)S(1)} %bitcast.69), channel_id=1, source_target_pairs={{0,4},{1,5},{2,6},{3,7},{4,0},{5,1},{6,2},{7,3},{8,12},{9,13},{10,... | collective-permute-start | bytes 442376 | tf_op jit(solution)/shard_map/ppermute | solution.py:277
  10.4 7.1 %collective-permute-start.1 = (bf16[2,2,16,1152]{3,2,1,0:T(8,128)(2,1)S(1)}, bf16[2,2,16,1152]{3,2,1,0:T(8,128)(2,1)S(1)}, u32[]{:S(2)}, u32[]{:S(2)}) collective-permute-start(bf16[2,2,16,1152]{3,2,1,0:T(8,128)(2,1)S(1)} %bitcast.68), channel_id=1, source_target_pairs={{0,2},{1,3},{2,0},{3,1},{4,6},{5,7},{6,4},{7,5},{8,10},{9,11},{10,... | collective-permute-start | bytes 442376 | tf_op jit(solution)/shard_map/ppermute | solution.py:277
  18.9 10.8 %collective-permute-start.9 = (bf16[1,64,1152]{2,1,0:T(8,128)(2,1)S(1)}, bf16[1,64,1152]{2,1,0:T(8,128)(2,1)S(1)}, u32[]{:S(2)}, u32[]{:S(2)}) collective-permute-start(bf16[1,64,1152]{2,1,0:T(8,128)(2,1)S(1)} %bitcast.65), channel_id=1, source_target_pairs={{0,8},{1,9},{2,10},{3,11},{4,12},{5,13},{6,14},{7,15},{8,0},{9,1},... | collective-permute-start | bytes 442376 | tf_op jit(solution)/shard_map/ppermute | solution.py:277
  21.6 30.3 %copy-start.18 = (s32[4]{0:T(128)S(1)}, s32[4]{0:T(128)}, u32[]{:S(2)}) copy-start(s32[4]{0:T(128)} %constant.140.clone) | copy-start | bytes 52
  21.6 30.4 %copy-start.5 = (bf16[256,4096]{1,0:T(8,128)(2,1)S(1)}, bf16[256,4096]{1,0:T(8,128)(2,1)}, u32[]{:S(2)}) copy-start(bf16[256,4096]{1,0:T(8,128)(2,1)} %basis_in.5) | copy-start | bytes 6291460
  27.9 102.9 %collective-permute-start.21 = (bf16[160,9216]{1,0:T(8,128)(2,1)}, bf16[160,9216]{1,0:T(8,128)(2,1)}, u32[]{:S(2)}, u32[]{:S(2)}) collective-permute-start(bf16[160,9216]{1,0:T(8,128)(2,1)} %features_away.1), channel_id=1, source_target_pairs={{0,16},{1,17},{2,18},{3,19},{4,20},{5,21},{6,22},{7,23},{8,24},{9,... | collective-permute-start | bytes 8847368 | tf_op jit(solution)/shard_map/ppermute | solution.py:304
  29.4 9.0 %collective-permute-start.4 = (bf16[1,64,1152]{2,1,0:T(8,128)(2,1)S(1)}, bf16[1,64,1152]{2,1,0:T(8,128)(2,1)S(1)}, u32[]{:S(2)}, u32[]{:S(2)}) collective-permute-start(bf16[1,64,1152]{2,1,0:T(8,128)(2,1)S(1)} %bitcast.63), channel_id=1, source_target_pairs={{0,8},{1,9},{2,10},{3,11},{4,12},{5,13},{6,14},{7,15},{8,0},{9,1},... | collective-permute-start | bytes 442376 | tf_op jit(solution)/shard_map/ppermute | solution.py:277
  29.8 8.7 %collective-permute-start.10 = (bf16[1,64,1152]{2,1,0:T(8,128)(2,1)S(1)}, bf16[1,64,1152]{2,1,0:T(8,128)(2,1)S(1)}, u32[]{:S(2)}, u32[]{:S(2)}) collective-permute-start(bf16[1,64,1152]{2,1,0:T(8,128)(2,1)S(1)} %bitcast_add_fusion), channel_id=1, source_target_pairs={{0,4},{1,3},{2,6},{3,1},{4,0},{5,7},{6,2},{7,5},{8,12},{9,11},{10,... | collective-permute-start | bytes 442376 | tf_op jit(solution)/shard_map/ppermute | solution.py:280
  38.4 6.5 %collective-permute-start.5 = (bf16[1,64,1152]{2,1,0:T(8,128)(2,1)S(1)}, bf16[1,64,1152]{2,1,0:T(8,128)(2,1)S(1)}, u32[]{:S(2)}, u32[]{:S(2)}) collective-permute-start(bf16[1,64,1152]{2,1,0:T(8,128)(2,1)S(1)} %bitcast_add_fusion.1), channel_id=1, source_target_pairs={{0,4},{1,3},{2,6},{3,1},{4,0},{5,7},{6,2},{7,5},{8,12},{9,11},{10,... | collective-permute-start | bytes 442376 | tf_op jit(solution)/shard_map/ppermute | solution.py:280
  39.3 8.3 %collective-permute-start.11 = (bf16[2,64,1152]{2,1,0:T(8,128)(2,1)}, bf16[2,64,1152]{2,1,0:T(8,128)(2,1)}, u32[]{:S(2)}, u32[]{:S(2)}) collective-permute-start(bf16[2,64,1152]{2,1,0:T(8,128)(2,1)} %pad_maximum_fusion.3.low), channel_id=1, source_target_pairs={{0,2},{1,5},{2,0},{3,7},{4,6},{5,1},{6,4},{7,3},{8,10},{9,13},{10,... | collective-permute-start | bytes 884744 | tf_op jit(solution)/shard_map/ppermute | solution.py:280
  45.0 6.9 %collective-permute-start.6 = (bf16[2,64,1152]{2,1,0:T(8,128)(2,1)S(1)}, bf16[2,64,1152]{2,1,0:T(8,128)(2,1)}, u32[]{:S(2)}, u32[]{:S(2)}) collective-permute-start(bf16[2,64,1152]{2,1,0:T(8,128)(2,1)S(1)} %pad_maximum_fusion.2.low), channel_id=1, source_target_pairs={{0,2},{1,5},{2,0},{3,7},{4,6},{5,1},{6,4},{7,3},{8,10},{9,13},{10,... | collective-permute-start | bytes 884744 | tf_op jit(solution)/shard_map/ppermute | solution.py:280
  47.0 5.0 %collective-permute-start.12 = (bf16[2,64,1152]{2,1,0:T(8,128)(2,1)}, bf16[2,64,1152]{2,1,0:T(8,128)(2,1)S(1)}, u32[]{:S(2)}, u32[]{:S(2)}) collective-permute-start(bf16[2,64,1152]{2,1,0:T(8,128)(2,1)} %pad_maximum_fusion.3.low), channel_id=1, source_target_pairs={{0,1},{1,0},{2,3},{3,2},{4,5},{5,4},{6,7},{7,6},{8,9},{9,8},{10,11... | collective-permute-start | bytes 884744 | tf_op jit(solution)/shard_map/ppermute | solution.py:283
  47.0 19.0 %collective-permute-start.7 = (bf16[2,64,1152]{2,1,0:T(8,128)(2,1)S(1)}, bf16[2,64,1152]{2,1,0:T(8,128)(2,1)S(1)}, u32[]{:S(2)}, u32[]{:S(2)}) collective-permute-start(bf16[2,64,1152]{2,1,0:T(8,128)(2,1)S(1)} %pad_maximum_fusion.2.low), channel_id=1, source_target_pairs={{0,1},{1,0},{2,3},{3,2},{4,5},{5,4},{6,7},{7,6},{8,9},{9,8},{10,11... | collective-permute-start | bytes 884744 | tf_op jit(solution)/shard_map/ppermute | solution.py:283
  47.5 4.4 %collective-permute-start.13 = (bf16[2,64,1152]{2,1,0:T(8,128)(2,1)}, bf16[2,64,1152]{2,1,0:T(8,128)(2,1)S(1)}, u32[]{:S(2)}, u32[]{:S(2)}) collective-permute-start(bf16[2,64,1152]{2,1,0:T(8,128)(2,1)} %collective-permute-done.11.high), channel_id=1, source_target_pairs={{0,1},{1,0},{2,3},{3,2},{4,5},{5,4},{6,7},{7,6},{8,9},{9,8},{10,11... | collective-permute-start | bytes 884744 | tf_op jit(solution)/shard_map/ppermute | solution.py:283
  51.9 14.9 %collective-permute-start.8 = (bf16[2,64,1152]{2,1,0:T(8,128)(2,1)}, bf16[2,64,1152]{2,1,0:T(8,128)(2,1)S(1)}, u32[]{:S(2)}, u32[]{:S(2)}) collective-permute-start(bf16[2,64,1152]{2,1,0:T(8,128)(2,1)} %collective-permute-done.6.high), channel_id=1, source_target_pairs={{0,1},{1,0},{2,3},{3,2},{4,5},{5,4},{6,7},{7,6},{8,9},{9,8},{10,11... | collective-permute-start | bytes 884744 | tf_op jit(solution)/shard_map/ppermute | solution.py:283
  52.0 8.3 %copy-start.1 = (bf16[896,14336]{1,0:T(8,128)(2,1)S(1)}, bf16[896,14336]{1,0:T(8,128)(2,1)}, u32[]{:S(2)}) copy-start(bf16[896,14336]{1,0:T(8,128)(2,1)} %basis_out.5) | copy-start | bytes 77070336
  66.8 11.9 %copy-start.8 = (bf16[2,64,1152]{2,1,0:T(8,128)(2,1)}, bf16[2,64,1152]{2,1,0:T(8,128)(2,1)S(1)}, u32[]{:S(2)}) copy-start(bf16[2,64,1152]{2,1,0:T(8,128)(2,1)S(1)} %collective-permute-done.7.slow) | copy-start | bytes 884740
  66.8 8.4 %copy-start.2 = (bf16[896,14336]{1,0:T(8,128)(2,1)S(1)}, bf16[896,14336]{1,0:T(8,128)(2,1)}, u32[]{:S(2)}) copy-start(bf16[896,14336]{1,0:T(8,128)(2,1)} %basis_out.5) | copy-start | bytes 77070336
  75.2 3.5 %copy-start.10 = (bf16[2,64,1152]{2,1,0:T(8,128)(2,1)}, bf16[2,64,1152]{2,1,0:T(8,128)(2,1)S(1)}, u32[]{:S(2)}) copy-start(bf16[2,64,1152]{2,1,0:T(8,128)(2,1)S(1)} %collective-permute-done.8.shigh) | copy-start | bytes 884740
  79.4 17.9 %collective-permute-start.22 = (bf16[128,640]{1,0:T(8,128)(2,1)S(1)}, bf16[128,640]{1,0:T(8,128)(2,1)}, u32[]{:S(2)}, u32[]{:S(2)}) collective-permute-start(bf16[128,640]{1,0:T(8,128)(2,1)S(1)} %get-tuple-element.19), channel_id=1, source_target_pairs={{1,17},{3,19},{5,21},{7,23},{9,25},{11,27},{13,29},{15,31},{16,0},... | collective-permute-start | bytes 491528 | tf_op jit(solution)/shard_map/ppermute | solution.py:338
  81.7 8.3 %copy-start.3 = (bf16[896,14336]{1,0:T(8,128)(2,1)S(1)}, bf16[896,14336]{1,0:T(8,128)(2,1)}, u32[]{:S(2)}) copy-start(bf16[896,14336]{1,0:T(8,128)(2,1)} %basis_out.5) | copy-start | bytes 77070336
  91.9 5.4 %copy-start.13 = (f32[128,640]{1,0:T(8,128)S(1)}, f32[128,640]{1,0:T(8,128)}, u32[]{:S(2)}) copy-start(f32[128,640]{1,0:T(8,128)} %copy-done.12) | copy-start | bytes 983044
  95.8 29.1 %copy-start.16 = (s32[8]{0:T(128)S(1)}, s32[8]{0:T(128)}, u32[]{:S(2)}) copy-start(s32[8]{0:T(128)} %constant.139.clone) | copy-start | bytes 100
  95.8 29.1 %copy-start.17 = (s32[8]{0:T(128)S(1)}, s32[8]{0:T(128)}, u32[]{:S(2)}) copy-start(s32[8]{0:T(128)} %constant.138.clone) | copy-start | bytes 100
  95.8 34.2 %copy-start.14 = (s32[16]{0:T(128)S(1)}, s32[16]{0:T(128)}, u32[]{:S(2)}) copy-start(s32[16]{0:T(128)} %param.27) | copy-start | bytes 196
  95.8 7.7 %collective-permute-start.14 = (bf16[128,512]{1,0:T(8,128)(2,1)S(1)}, bf16[128,512]{1,0:T(8,128)(2,1)S(1)}, u32[]{:S(2)}, u32[]{:S(2)}) collective-permute-start(bf16[128,512]{1,0:T(8,128)(2,1)S(1)} %get-tuple-element.15), channel_id=1, source_target_pairs={{1,17},{3,19},{5,21},{7,23},{9,25},{11,27},{13,29},{15,31},{16,0},... | collective-permute-start | bytes 393224 | tf_op jit(solution)/shard_map/ppermute | solution.py:338
  97.3 33.5 %copy-start.6 = (bf16[1,160,4096]{2,1,0:T(8,128)(2,1)S(1)}, bf16[1,160,4096]{2,1,0:T(8,128)(2,1)}, u32[]{:S(2)}) copy-start(bf16[1,160,4096]{2,1,0:T(8,128)(2,1)} %param.19) | copy-start | bytes 3932164
  98.4 6.7 %collective-permute-start.23 = (bf16[64,640]{1,0:T(8,128)(2,1)S(1)}, bf16[64,640]{1,0:T(8,128)(2,1)S(1)}, u32[]{:S(2)}, u32[]{:S(2)}) collective-permute-start(bf16[64,640]{1,0:T(8,128)(2,1)S(1)} %slice.97), channel_id=1, source_target_pairs={{0,1},{2,3},{4,5},{6,7},{8,9},{10,11},{12,13},{14,15},{17,16},{19,... | collective-permute-start | bytes 245768 | tf_op jit(solution)/shard_map/ppermute | solution.py:340
  103.6 2.2 %collective-permute-start.15 = (bf16[64,512]{1,0:T(8,128)(2,1)S(1)}, bf16[64,512]{1,0:T(8,128)(2,1)S(1)}, u32[]{:S(2)}, u32[]{:S(2)}) collective-permute-start(bf16[64,512]{1,0:T(8,128)(2,1)S(1)} %slice.94), channel_id=1, source_target_pairs={{0,1},{2,3},{4,5},{6,7},{8,9},{10,11},{12,13},{14,15},{17,16},{19,... | collective-permute-start | bytes 196616 | tf_op jit(solution)/shard_map/ppermute | solution.py:340
  105.1 7.7 %collective-permute-start.24 = (bf16[1,64,640]{2,1,0:T(8,128)(2,1)S(1)}, bf16[1,64,640]{2,1,0:T(8,128)(2,1)S(1)}, u32[]{:S(2)}, u32[]{:S(2)}) collective-permute-start(bf16[1,64,640]{2,1,0:T(8,128)(2,1)S(1)} %fusion.7), channel_id=1, source_target_pairs={{0,8},{1,9},{2,10},{3,11},{4,12},{5,13},{6,14},{7,15},{8,0},{9,1},... | collective-permute-start | bytes 245768 | tf_op jit(solution)/shard_map/ppermute | solution.py:280
  105.8 7.8 %collective-permute-start.16 = (bf16[1,64,512]{2,1,0:T(8,128)(2,1)S(1)}, bf16[1,64,512]{2,1,0:T(8,128)(2,1)S(1)}, u32[]{:S(2)}, u32[]{:S(2)}) collective-permute-start(bf16[1,64,512]{2,1,0:T(8,128)(2,1)S(1)} %fusion.8), channel_id=1, source_target_pairs={{0,8},{1,9},{2,10},{3,11},{4,12},{5,13},{6,14},{7,15},{8,0},{9,1},... | collective-permute-start | bytes 196616 | tf_op jit(solution)/shard_map/ppermute | solution.py:280
  112.8 6.4 %collective-permute-start.25 = (bf16[2,64,640]{2,1,0:T(8,128)(2,1)S(1)}, bf16[2,64,640]{2,1,0:T(8,128)(2,1)S(1)}, u32[]{:S(2)}, u32[]{:S(2)}) collective-permute-start(bf16[2,64,640]{2,1,0:T(8,128)(2,1)S(1)} %pad_maximum_fusion.5), channel_id=1, source_target_pairs={{0,4},{1,3},{2,6},{3,1},{4,0},{5,7},{6,2},{7,5},{8,12},{9,11},{10,... | collective-permute-start | bytes 491528 | tf_op jit(solution)/shard_map/ppermute | solution.py:280
  113.5 8.6 %collective-permute-start.17 = (bf16[2,64,512]{2,1,0:T(8,128)(2,1)S(1)}, bf16[2,64,512]{2,1,0:T(8,128)(2,1)S(1)}, u32[]{:S(2)}, u32[]{:S(2)}) collective-permute-start(bf16[2,64,512]{2,1,0:T(8,128)(2,1)S(1)} %pad_maximum_fusion.6), channel_id=1, source_target_pairs={{0,4},{1,3},{2,6},{3,1},{4,0},{5,7},{6,2},{7,5},{8,12},{9,11},{10,... | collective-permute-start | bytes 393224 | tf_op jit(solution)/shard_map/ppermute | solution.py:280
  119.2 7.9 %collective-permute-start.26 = (bf16[4,64,640]{2,1,0:T(8,128)(2,1)S(1)}, bf16[4,64,640]{2,1,0:T(8,128)(2,1)S(1)}, u32[]{:S(2)}, u32[]{:S(2)}) collective-permute-start(bf16[4,64,640]{2,1,0:T(8,128)(2,1)S(1)} %pad_maximum_fusion.1.low), channel_id=1, source_target_pairs={{0,2},{1,5},{2,0},{3,7},{4,6},{5,1},{6,4},{7,3},{8,10},{9,13},{10,... | collective-permute-start | bytes 983048 | tf_op jit(solution)/shard_map/ppermute | solution.py:280
  122.1 7.9 %collective-permute-start.18 = (bf16[4,64,512]{2,1,0:T(8,128)(2,1)S(1)}, bf16[4,64,512]{2,1,0:T(8,128)(2,1)}, u32[]{:S(2)}, u32[]{:S(2)}) collective-permute-start(bf16[4,64,512]{2,1,0:T(8,128)(2,1)S(1)} %pad_maximum_fusion.4.low), channel_id=1, source_target_pairs={{0,2},{1,5},{2,0},{3,7},{4,6},{5,1},{6,4},{7,3},{8,10},{9,13},{10,... | collective-permute-start | bytes 786440 | tf_op jit(solution)/shard_map/ppermute | solution.py:280
  124.9 5.9 %collective-permute-start.27 = (bf16[4,64,640]{2,1,0:T(8,128)(2,1)S(1)}, bf16[4,64,640]{2,1,0:T(8,128)(2,1)S(1)}, u32[]{:S(2)}, u32[]{:S(2)}) collective-permute-start(bf16[4,64,640]{2,1,0:T(8,128)(2,1)S(1)} %pad_maximum_fusion.1.low), channel_id=1, source_target_pairs={{0,1},{1,0},{2,3},{3,2},{4,5},{5,4},{6,7},{7,6},{8,9},{9,8},{10,11... | collective-permute-start | bytes 983048 | tf_op jit(solution)/shard_map/ppermute | solution.py:283
  127.1 3.7 %collective-permute-start.28 = (bf16[4,64,640]{2,1,0:T(8,128)(2,1)S(1)}, bf16[4,64,640]{2,1,0:T(8,128)(2,1)}, u32[]{:S(2)}, u32[]{:S(2)}) collective-permute-start(bf16[4,64,640]{2,1,0:T(8,128)(2,1)S(1)} %collective-permute-done.26.high), channel_id=1, source_target_pairs={{0,1},{1,0},{2,3},{3,2},{4,5},{5,4},{6,7},{7,6},{8,9},{9,8},{10,11... | collective-permute-start | bytes 983048 | tf_op jit(solution)/shard_map/ppermute | solution.py:283
  127.2 12.6 %collective-permute-start.19 = (bf16[4,64,512]{2,1,0:T(8,128)(2,1)S(1)}, bf16[4,64,512]{2,1,0:T(8,128)(2,1)}, u32[]{:S(2)}, u32[]{:S(2)}) collective-permute-start(bf16[4,64,512]{2,1,0:T(8,128)(2,1)S(1)} %pad_maximum_fusion.4.low), channel_id=1, source_target_pairs={{0,1},{1,0},{2,3},{3,2},{4,5},{5,4},{6,7},{7,6},{8,9},{9,8},{10,11... | collective-permute-start | bytes 786440 | tf_op jit(solution)/shard_map/ppermute | solution.py:283
  130.1 9.7 %collective-permute-start.20 = (bf16[4,64,512]{2,1,0:T(8,128)(2,1)}, bf16[4,64,512]{2,1,0:T(8,128)(2,1)}, u32[]{:S(2)}, u32[]{:S(2)}) collective-permute-start(bf16[4,64,512]{2,1,0:T(8,128)(2,1)} %collective-permute-done.18.high), channel_id=1, source_target_pairs={{0,1},{1,0},{2,3},{3,2},{4,5},{5,4},{6,7},{7,6},{8,9},{9,8},{10,11... | collective-permute-start | bytes 786440 | tf_op jit(solution)/shard_map/ppermute | solution.py:283
  130.8 2.3 %copy-start.4 = (bf16[1,160,14336]{2,1,0:T(8,128)(2,1)S(1)}, bf16[1,160,14336]{2,1,0:T(8,128)(2,1)}, u32[]{:S(2)}) copy-start(bf16[1,160,14336]{2,1,0:T(8,128)(2,1)} %param.20) | copy-start | bytes 13762564
  139.7 8.9 %copy-start.19 = (s32[16]{0:T(128)S(1)}, s32[16]{0:T(128)}, u32[]{:S(2)}) copy-start(s32[16]{0:T(128)} %param.26) | copy-start | bytes 196
  146.3 6.7 %collective-permute-start.29 = (f32[2,160,128]{2,1,0:T(8,128)S(1)}, f32[2,160,128]{2,1,0:T(8,128)S(1)}, u32[]{:S(2)}, u32[]{:S(2)}) collective-permute-start(f32[2,160,128]{2,1,0:T(8,128)S(1)} %slice_bitcast_fusion.2), channel_id=1, source_target_pairs={{0,16},{1,17},{2,18},{3,19},{4,20},{5,21},{6,22},{7,23},{8,24},{9,... | collective-permute-start | bytes 491528 | tf_op jit(solution)/shard_map/ppermute | solution.py:348
  153.4 1.1 collective-permute-start.30
  154.6 3.6 %collective-permute-start.31 = (f32[2,1,4]{2,1,0:T(1,128)S(1)}, f32[2,1,4]{2,1,0:T(1,128)S(1)}, u32[]{:S(2)}, u32[]{:S(2)}) collective-permute-start(f32[2,1,4]{2,1,0:T(1,128)S(1)} %pad_maximum_fusion.9), channel_id=1, source_target_pairs={{0,2},{1,3},{2,0},{3,1},{4,6},{5,7},{6,4},{7,5},{8,10},{9,11},{10,... | collective-permute-start | bytes 104 | tf_op jit(solution)/shard_map/ppermute | solution.py:356
  158.2 3.6 %collective-permute-start.32 = (f32[4,1,4]{2,1,0:T(1,128)S(1)}, f32[4,1,4]{2,1,0:T(1,128)S(1)}, u32[]{:S(2)}, u32[]{:S(2)}) collective-permute-start(f32[4,1,4]{2,1,0:T(1,128)S(1)} %pad_maximum_fusion.8), channel_id=1, source_target_pairs={{0,4},{1,5},{2,6},{3,7},{4,0},{5,1},{6,2},{7,3},{8,12},{9,13},{10,... | collective-permute-start | bytes 200 | tf_op jit(solution)/shard_map/ppermute | solution.py:356
  161.8 4.6 %collective-permute-start.33 = (f32[8,1,4]{2,1,0:T(1,128)S(1)}, f32[8,1,4]{2,1,0:T(1,128)S(1)}, u32[]{:S(2)}, u32[]{:S(2)}) collective-permute-start(f32[8,1,4]{2,1,0:T(1,128)S(1)} %pad_maximum_fusion.7), channel_id=1, source_target_pairs={{0,8},{1,9},{2,10},{3,11},{4,12},{5,13},{6,14},{7,15},{8,0},{9,1},... | collective-permute-start | bytes 392 | tf_op jit(solution)/shard_map/ppermute | solution.py:356
  (6 other events, 6.2 us)

commit v3 on v0

v3 whole, which is shorter than its diff:
```python
import jax
import jax.numpy as jnp
from jax import lax
from jax.experimental import pallas as pl
from jax.experimental.pallas import tpu as pltpu
from jax.sharding import PartitionSpec as P

ROWS = (((1,), (1,)), ((), ()))
EVERYONE = ("parts", "blk")
NEAR = 4
CHAINS = 2
SHARES = (2, 3, 3)
MIB = 1024 * 1024


def dot_rows(left, right):
    return lax.dot_general(left, right, ROWS, preferred_element_type=jnp.float32)


NEAR_MASKS = ((0, 1, 2, 3), (0, 2, 1, 3))
SIBLING = (0, 2, 1, 3)


def after(values, other):
    return list(lax.optimization_barrier((*values, other)))[:-1]


VMEM = pl.BlockSpec(memory_space=pltpu.VMEM)
SMEM = pl.BlockSpec(memory_space=pltpu.SMEM)
HBM = pl.BlockSpec(memory_space=pltpu.HBM)


def in_hbm(value):
    return pltpu.with_memory_space_constraint(value, pltpu.HBM)


def in_vmem(value):
    return pltpu.with_memory_space_constraint(value, pltpu.VMEM)


def lanes_at(number, width):
    return pl.ds(pl.multiple_of(number * width, 128), width)


def copy_all(copies):
    for copy in copies:
        copy.start()
    for copy in copies:
        copy.wait()


def estimate(flops, moved):
    return pl.CostEstimate(flops=flops, bytes_accessed=moved, transcendentals=0)


def rank_halves(part, core, left, right):
    half_rank = left.shape[1] // 2
    widths = [factor.shape[2] // (2 * CHAINS * NEAR) for factor in (left, right)]
    wide = sum(widths)

    def kernel(where, left, right, away, kept, sems):
        copies = []
        for side, out in enumerate((away, kept)):
            rows = pl.ds(pl.multiple_of((where[1] if side else 1 - where[1]) * half_rank, half_rank), half_rank)
            for chunk in range(NEAR):
                for chain in range(CHAINS):
                    number = (where[0] * CHAINS + chain) * NEAR + chunk
                    target = out.at[chunk, chain]
                    copies.append(
                        pltpu.make_async_copy(
                            left.at[0, rows, lanes_at(number, widths[0])],
                            target.at[:, pl.ds(0, widths[0])],
                            sems.at[len(copies)],
                        )
                    )
                    copies.append(
                        pltpu.make_async_copy(
                            right.at[0, rows, lanes_at(number, widths[1])],
                            target.at[:, pl.ds(widths[0], widths[1])],
                            sems.at[len(copies)],
                        )
                    )
        copy_all(copies)

    shape = (NEAR, CHAINS, half_rank, wide)
    return pl.pallas_call(
        kernel,
        in_specs=[SMEM, HBM, HBM],
        out_specs=[VMEM] * 2,
        out_shape=[pltpu.VMEM(shape, left.dtype)] * 2,
        scratch_shapes=[pltpu.SemaphoreType.DMA((4 * NEAR * CHAINS,))],
        compiler_params=pltpu.CompilerParams(vmem_limit_bytes=4 * MIB),
        cost_estimate=estimate(0, 8 * NEAR * CHAINS * half_rank * wide),
        name="rank_halves",
    )(jnp.stack([part, core]), in_hbm(left), in_hbm(right))


def messages_of(spot, kept, received):
    def kernel(where, kept, received, *outs):
        for chain in range(CHAINS):
            for mask in range(NEAR):
                chunk = where[0] ^ mask
                outs[chain * NEAR + mask][0] = kept[chunk, chain]
                outs[chain * NEAR + mask][1] = received[chunk, chain]

    shape = jax.ShapeDtypeStruct((2,) + kept.shape[2:], kept.dtype)
    outs = pl.pallas_call(
        kernel,
        in_specs=[SMEM, VMEM, VMEM],
        out_specs=[VMEM] * (NEAR * CHAINS),
        out_shape=[shape] * (NEAR * CHAINS),
        compiler_params=pltpu.CompilerParams(vmem_limit_bytes=4 * MIB),
        cost_estimate=estimate(0, 4 * 2 * kept.size),
        name="messages",
    )(spot[None], kept, received)
    return [outs[chain * NEAR : (chain + 1) * NEAR] for chain in range(CHAINS)]


def chunk_copies(number, bases, targets, widths, rows, sems):
    copies = []
    for num, (basis, target, width, (begin, end)) in enumerate(zip(bases, targets, widths, rows)):
        if end > begin:
            source = basis.at[pl.ds(begin, end - begin), lanes_at(number, width)]
            copies.append(pltpu.make_async_copy(source, target, sems.at[num]))
    return copies


def stage_bases(part, bases):
    widths = [basis.shape[1] // (2 * CHAINS) for basis in bases]
    rows = [(0, basis.shape[0]) for basis in bases]

    def kernel(where, first, second, first_out, second_out, sems):
        number = where[0] * CHAINS + CHAINS - 1
        copy_all(chunk_copies(number, (first, second), (first_out, second_out), widths, rows, sems))

    shapes = [(basis.shape[0], width) for basis, width in zip(bases, widths)]
    return pl.pallas_call(
        kernel,
        in_specs=[SMEM, HBM, HBM],
        out_specs=[VMEM] * 2,
        out_shape=[pltpu.VMEM(shape, bases[0].dtype) for shape in shapes],
        scratch_shapes=[pltpu.SemaphoreType.DMA((2,))],
        compiler_params=pltpu.CompilerParams(vmem_limit_bytes=4 * MIB),
        cost_estimate=estimate(0, 2 * sum(shape[0] * shape[1] for shape in shapes)),
        name="stage_bases",
    )(part[None], *map(in_hbm, bases))


def choose(spot, found):
    queries = spot.shape[0]
    ranks, wide = found[0].shape[1:]

    def kernel(where, *rest):
        out = rest[-1]
        for query in range(queries):
            place = pl.ds(query * ranks, ranks)
            for mask in range(NEAR):

                @pl.when(where[query] // 2 == mask)
                def _():
                    out[0, place] = rest[mask][where[query] % 2]

            @pl.when(where[query] >= 2 * NEAR)
            def _():
                out[0, place] = jnp.zeros((ranks, wide), out.dtype)

    return pl.pallas_call(
        kernel,
        in_specs=[SMEM] + [VMEM] * NEAR,
        out_specs=VMEM,
        out_shape=jax.ShapeDtypeStruct((1, queries * ranks, wide), found[0].dtype),
        compiler_params=pltpu.CompilerParams(vmem_limit_bytes=4 * MIB),
        cost_estimate=estimate(0, 4 * queries * ranks * wide),
        name="choose",
    )(spot, *found)


def features_of(part, chip_at, acts, grads, pieces):
    tokens, chips = acts.shape[0], chip_at.shape[0]
    wide_in, wide_out = acts.shape[1] // 2 // chips, grads.shape[1] // 2 // chips
    wide = wide_in + wide_out
    if wide_in % 128 or wide_out % 128:
        some_in = jnp.take(jnp.take(acts.reshape(tokens, chips, 2, wide_in), part, axis=2), chip_at, axis=1)
        some_out = jnp.take(jnp.take(grads.reshape(tokens, chips, 2, wide_out), part, axis=2), chip_at, axis=1)
        some = jnp.concatenate([some_in, some_out], axis=2)
        return [some[:, begin:end].reshape(tokens, -1) for begin, end in pieces]
    total = sum(end - begin for begin, end in pieces)

    def kernel(where, acts, grads, *rest):
        outs, sems = rest[:-1], rest[-1]
        copies = []
        for out, (first, last) in zip(outs, pieces):
            for spot in range(first, last):
                number = 2 * where[1 + spot] + where[0]
                for source, width, begin in ((acts, wide_in, 0), (grads, wide_out, wide_in)):
                    copies.append(
                        pltpu.make_async_copy(
                            source.at[:, lanes_at(number, width)],
                            out.at[:, pl.ds((spot - first) * wide + begin, width)],
                            sems.at[len(copies)],
                        )
                    )
        copy_all(copies)

    return pl.pallas_call(
        kernel,
        in_specs=[SMEM, HBM, HBM],
        out_specs=[VMEM] * len(pieces),
        out_shape=[pltpu.VMEM((tokens, (end - begin) * wide), acts.dtype) for begin, end in pieces],
        scratch_shapes=[pltpu.SemaphoreType.DMA((2 * total,))],
        compiler_params=pltpu.CompilerParams(vmem_limit_bytes=4 * MIB),
        cost_estimate=estimate(0, 4 * tokens * total * wide),
        name="features",
    )(jnp.concatenate([part[None], chip_at]), in_hbm(acts), in_hbm(grads))


def rotate(part, chunks, chain, factors, bases, rows, total):
    last = chain == CHAINS - 1
    ranks, wide = factors[0].shape
    wide_in = bases[0].shape[1] // NEAR if last else bases[0].shape[1] // (2 * CHAINS * NEAR)
    widths = (wide_in, wide - wide_in)
    counts = [end - begin for begin, end in rows]
    height = sum(counts)
    spans = [(0, counts[0], 0, wide_in), (counts[0], height, wide_in, wide)]

    def kernel(where, *rest):
        own, sib, (basis_in, basis_out), rest = rest[:NEAR], rest[NEAR : 2 * NEAR], rest[2 * NEAR :][:2], rest[2 * NEAR + 2 :]
        if total is not None:
            start, rest = rest[0], rest[1:]
        if last:
            outs, acc = rest[:-1], rest[-1]
        else:
            outs, (buf_in, buf_out, acc, sems) = rest[:-4], rest[-4:]
            copies = []
            for spot in range(NEAR):
                number = (where[0] * CHAINS + chain) * NEAR + where[1 + spot]
                targets = (buf_in.at[spot], buf_out.at[spot])
                copies.append(
                    chunk_copies(number, (basis_in, basis_out), targets, widths, rows, sems.at[spot])
                )
                for copy in copies[spot]:
                    copy.start()
        for spot in range(NEAR):
            factor = jnp.concatenate([own[spot][...], sib[SIBLING[spot]][...]], axis=0)
            if not last:
                for copy in copies[spot]:
                    copy.wait()
            for num, (from_row, to_row, from_lane, to_lane) in enumerate(spans):
                if to_row == from_row:
                    continue
                if last:
                    basis = (basis_in, basis_out)[num]
                    block = basis[rows[num][0] : rows[num][1], lanes_at(where[1 + spot], widths[num])]
                else:
                    block = (buf_in, buf_out)[num][spot]
                value = dot_rows(block, factor[:, from_lane:to_lane])
                acc[from_row:to_row] = value if spot == 0 else acc[from_row:to_row] + value
        value = acc[...]
        if total is not None:
            value = value + start[...]
        if last:
            value = value.T
            outs[1][...] = value.astype(jnp.bfloat16)
        outs[0][...] = value

    if last:
        shapes = [jax.ShapeDtypeStruct((2 * ranks, height), kind) for kind in (jnp.float32, jnp.bfloat16)]
        scratch = []
        place, operands = VMEM, map(in_vmem, bases)
    else:
        shapes = [jax.ShapeDtypeStruct((height, 2 * ranks), jnp.float32)]
        scratch = [pltpu.VMEM((NEAR, count, width), jnp.bfloat16) for count, width in zip(counts, widths)]
        place, operands = HBM, map(in_hbm, bases)
    scratch.append(pltpu.VMEM((height, 2 * ranks), jnp.float32))
    if not last:
        scratch.append(pltpu.SemaphoreType.DMA((NEAR, 2)))
    given = [] if total is None else [total]
    moved = sum(count * width for count, width in zip(counts, widths))
    results = pl.pallas_call(
        kernel,
        in_specs=[SMEM] + [VMEM] * (2 * NEAR) + [place] * 2 + [VMEM] * len(given),
        out_specs=[VMEM] * len(shapes),
        out_shape=shapes,
        scratch_shapes=scratch,
        compiler_params=pltpu.CompilerParams(vmem_limit_bytes=(4 if last else 12) * MIB),
        cost_estimate=estimate(4 * ranks * NEAR * moved, 2 * NEAR * moved),
        name="rotate",
    )(jnp.concatenate([part[None], chunks]), *factors, *operands, *given)
    return tuple(results) if last else results[0]


def project(own, sib, wide_in, tokens_in, pieces, kind):
    chips = len(own)
    ranks, wide = own[0].shape
    tokens = tokens_in[0].shape[0]
    if wide_in % 128 or wide % 128:
        both = jnp.stack([jnp.concatenate(pair, axis=0) for pair in zip(own, sib)])
        held = jnp.concatenate(tokens_in, axis=1).reshape(tokens, chips, wide)
        return [
            jnp.einsum("tgf,gcf->tc", held[:, :, lanes], both[:, :, lanes], preferred_element_type=jnp.float32).astype(
                kind
            )
            for lanes in (slice(0, wide_in), slice(wide_in, wide))
        ]
    staged = len(tokens_in) == 1

    def kernel(*rest):
        factors, rest = rest[: 2 * chips], rest[2 * chips :]
        held, rest = rest[: len(tokens_in)], rest[len(tokens_in) :]
        outs, acc = rest[:2], rest[2]
        if not staged:
            buffer, sems = rest[3:]
            copies = []
            for source, (first, last) in zip(held, pieces):
                for spot in range(first, last):
                    block = source.at[:, pl.ds((spot - first) * wide, wide)]
                    copies.append(pltpu.make_async_copy(block, buffer.at[spot], sems.at[spot]))
                    copies[-1].start()
        for spot in range(chips):
            factor = jnp.concatenate([factors[spot][...], factors[chips + spot][...]], axis=0)
            if not staged:
                copies[spot].wait()
            for num, (begin, end) in enumerate(((0, wide_in), (wide_in, wide))):
                block = held[0][:, spot * wide + begin : spot * wide + end] if staged else buffer[spot, :, begin:end]
                value = dot_rows(block, factor[:, begin:end])
                acc[num] = value if spot == 0 else acc[num] + value
        for num, out in enumerate(outs):
            out[...] = acc[num].astype(kind)

    scratch = [pltpu.VMEM((2, tokens, 2 * ranks), jnp.float32)]
    if not staged:
        scratch += [pltpu.VMEM((chips, tokens, wide), own[0].dtype), pltpu.SemaphoreType.DMA((chips,))]
    return pl.pallas_call(
        kernel,
        in_specs=[VMEM] * (2 * chips) + [VMEM if staged else HBM] * len(tokens_in),
        out_specs=[VMEM] * 2,
        out_shape=[jax.ShapeDtypeStruct((tokens, 2 * ranks), kind)] * 2,
        scratch_shapes=scratch,
        compiler_params=pltpu.CompilerParams(vmem_limit_bytes=(4 if staged else 8) * MIB),
        cost_estimate=estimate(4 * tokens * ranks * chips * wide, 4 * ranks * chips * wide),
        name="project",
    )(*own, *sib, *map(in_vmem if staged else in_hbm, tokens_in))


def shards(
    activations,
    output_grads,
    basis_in,
    basis_out,
    query_left,
    query_right,
    owners,
    lengths,
    slot_plan,
):
    count = lax.axis_size("blk")
    chips = count // 2
    bits = chips.bit_length() - 1
    me = lax.axis_index("blk")
    part = lax.axis_index("parts")
    core, chip = me % 2, me // 2
    seqs_here, max_length, width_in = activations.shape
    num_queries = owners.shape[0]
    rank_count = query_left.shape[1]
    half_rank = rank_count // 2
    ranks = num_queries * half_rank
    tokens = seqs_here * max_length
    acts = activations.reshape(tokens, width_in)
    grads = output_grads.reshape(tokens, -1)
    across = [(p * count + i, (1 - p) * count + i) for p in range(2) for i in range(count)]

    def to_chip(value, mask):
        return lax.ppermute(value, "blk", [(i, i ^ (2 * mask)) for i in range(count)])

    def along(value, first, second):
        return lax.ppermute(value, "blk", [(i, i ^ (2 << (second if i % 2 else first))) for i in range(count)])

    def to_core(value):
        return lax.ppermute(value, "blk", [(i, i ^ 1) for i in range(count)])

    def near_gather(value):
        first = along(value, 0, 1)
        second = along(value, 1, 0)
        return [value, first, second, along(first, 1, 0)]

    near_at = jnp.where(core == 0, jnp.array(NEAR_MASKS[0], jnp.int32), jnp.array(NEAR_MASKS[1], jnp.int32)) ^ (
        chip % NEAR
    )
    sources = [[0]]
    for bit in range(2, bits):
        sources.append([mask | (1 << bit) for group in sources for mask in group])
    orders = [[far | near for group in sources for near in NEAR_MASKS[side] for far in group] for side in range(2)]
    chip_at = jnp.where(core == 0, jnp.array(orders[0], jnp.int32), jnp.array(orders[1], jnp.int32)) ^ chip

    away, kept = rank_halves(part, core, query_left, query_right)
    messages = messages_of(chip % NEAR, kept, to_core(away))
    shares = [chips * sum(SHARES[:num]) // sum(SHARES) for num in range(len(SHARES) + 1)]
    pieces = list(zip(shares[:-1], shares[1:]))

    def give_away(num, other):
        (piece,) = features_of(1 - part, chip_at, *after((acts, grads), other), pieces[num : num + 1])
        return piece

    others = [lax.ppermute(give_away(0, messages[0][0]), EVERYONE, across)]

    source = (owners // 2) ^ chip
    spot = jnp.where(source < NEAR, source * 2 + ((owners % 2) ^ core), 2 * NEAR)
    every = range(CHAINS)
    found = [[to_chip(group[mask], mask) if mask else group[0] for mask in range(NEAR)] for group in messages]
    dense = []
    for chain in every:
        if chain:
            found[chain] = after(found[chain], dense[chain - 1])
        dense.append(choose(spot, found[chain]))
    bases = stage_bases(part, after((basis_in, basis_out), dense[0]))
    for bit in range(bits - 1, 1, -1):
        arrived = [to_chip(dense[chain], 1 << bit) for chain in every]
        for chain in every:
            if chain:
                (arrived[chain],) = after((arrived[chain],), dense[chain - 1])
            dense[chain] = dense[chain] + arrived[chain]
    others.append(lax.ppermute(give_away(1, bases[0]), EVERYONE, across))
    others[0], dense[0], *bases = lax.optimization_barrier((others[0], dense[0], *bases))
    gathered = []
    for chain in every:
        own = near_gather(dense[chain][0])
        if chain:
            own[1:3] = after(own[1:3], gathered[0][0][1])
        if chain == CHAINS - 1:
            own[3], others[1] = lax.optimization_barrier((own[3], others[1]))
        gathered.append((own, [to_core(value) for value in own]))

    rows_in, rows_out = basis_in.shape[0], basis_out.shape[0]
    rows = ((0, rows_in), (0, rows_out))
    total = None
    for chain in range(CHAINS - 1):
        total = rotate(part, near_at, chain, sum(gathered[chain], []), (basis_in, basis_out), rows, total)
    partial, sent = rotate(part, near_at, CHAINS - 1, sum(gathered[-1], []), bases, rows, total)
    to_sum = [(p * count + i, (1 - p) * count + i) for p in range(2) for i in range(count) if i % 2 != p]
    to_half = [(p * count + i, p * count + (i ^ 1)) for p in range(2) for i in range(count) if i % 2 == p]
    own_tokens = features_of(part, chip_at, *after((acts, grads), sent), [(0, chips)])
    last_piece = give_away(2, sent)
    arrived, last_piece = lax.optimization_barrier((lax.ppermute(sent, EVERYONE, to_sum), last_piece))
    others.append(lax.ppermute(last_piece, EVERYONE, across))
    summed = (partial + arrived.astype(jnp.float32)).astype(jnp.bfloat16)
    given = lax.ppermute(summed[ranks:], EVERYONE, to_half)
    piece = jnp.where(core == part, summed[:ranks], given)

    held = [piece[None]]
    for bit in range(2, bits):
        held.append(to_chip(held[0] if len(held) == 1 else jnp.concatenate(held, axis=0), 1 << bit))
    held[1], *own_tokens = lax.optimization_barrier((held[1], *own_tokens))
    own, sib = [], []
    for source in held:
        group = near_gather(source)
        swapped = [to_core(value) for value in group]
        for step in range(NEAR):
            own += [group[step][entry] for entry in range(source.shape[0])]
            sib += [swapped[SIBLING[step]][entry] for entry in range(source.shape[0])]

    theirs = project(own, sib, rows_in, others, pieces, jnp.bfloat16)
    back = lax.ppermute(jnp.stack(theirs), EVERYONE, across).astype(jnp.float32)
    mine = project(own, sib, rows_in, own_tokens, [(0, chips)], jnp.float32)
    mine_in, mine_out = mine[0] + back[0], mine[1] + back[1]
    seqs = me * seqs_here + jnp.arange(seqs_here, dtype=jnp.int32)
    live = jnp.arange(max_length, dtype=jnp.int32)[None, :] < lengths[slot_plan[seqs]][:, None]
    products = (mine_in * mine_out).reshape(seqs_here, max_length, -1)
    sums = jnp.sum(jnp.where(live[:, :, None], products, 0.0), axis=1)
    held = (jnp.sum(sums.reshape(seqs_here, 2, num_queries, half_rank), axis=(1, 3)) / rank_count)[None]
    for bit in range(bits + 1):
        pairs = [(i, i ^ (1 << bit)) for i in range(count)]
        held = jnp.concatenate([held, lax.ppermute(held, "blk", pairs)], axis=0)
    from_device = jnp.arange(count, dtype=jnp.int32) ^ me
    planned = slot_plan.reshape(count, seqs_here)[from_device]
    chooser = planned[None, :, :] == seqs[:, None, None]
    return jnp.sum(jnp.where(chooser[..., None], held[None], 0.0), axis=(1, 2))


def solution(mesh):
    placed = (
        P(("parts", "blk"), None, None),
        P(("parts", "blk"), None, None),
        P("blk", None),
        P("blk", None),
        P("blk", None, None),
        P("blk", None, None),
        P(),
        P("parts"),
        P("parts"),
    )
    return jax.shard_map(
        shards, mesh=mesh, in_specs=placed, out_specs=P(("parts", "blk"), None), check_vma=False
    )
```

time: 285 us -> 125 us (0.44)
  waiting for transfers between devices: 200 us -> 42 us
  starting transfers between devices: 0.09 us -> 40.2 us
  blocking collectives: 32.1 us -> 0 us
  Pallas kernels: 0 us -> 30.7 us
  matrix products: 24.3 us -> 0 us
  between operations: 16.3 us -> 2.24 us
  other arithmetic: 7.9 us -> 1.95 us
  local copies, waits for them, and re-layouts: 3.97 us -> 7.68 us
    psum x1 -> x0, waiting for transfers between devices: 122 us -> none  [spread(): return lax.psum(kept, axis)]
    all_gather x2 -> x0, waiting for transfers between devices: 77.4 us -> none  [the longest x1 44.6 us: shards(): lax.all_gather(rotated_out, 'blk', axis=0, tiled=True)]
    ppermute x0 -> x48, waiting for transfers between devices: none -> 42 us  [the longest x12 11.9 us: along(): lax.ppermute(value, 'blk', [(i, i ^ 2 << (second if i % 2 else first)) fo...]
    ppermute x0 -> x48, starting transfers between devices: none -> 40.2 us  [the longest x9 14.5 us: to_chip(): return lax.ppermute(value, 'blk', [(i, i ^ 2 * mask) for i in range(count)])]
    unnamed x1 -> x0, blocking collectives: 32.1 us -> none
    pallas_call x0 -> x13, Pallas kernels: none -> 30.7 us  [the longest x4 8.93 us: features_of(): pl.pallas_call(kernel, in_specs=[SMEM, HBM, HBM], out_specs=[VMEM] * len(...]
    dot_general x6 -> x0, matrix products: 24.3 us -> none  [the longest x1 14.3 us: shards(): lax.dot_general(basis_out, picked_out, contract, preferred_element_type=j...]
    unnamed x23 -> x28, local copies, waits for them, and re-layouts: 0.83 us -> 5.11 us
  transfers between devices with their start and end apart: 3 -> 48, of which waited for: 3 -> 22; matrix products, arithmetic and copies ran while one was open for 3% -> 3% of each run, Pallas kernels for 0% -> 17%
where the time goes in v3:
time: 125 us
  waiting for transfers between devices  42 us (34%)
  starting transfers between devices  40.2 us (32%)
  Pallas kernels  30.7 us (25%)
  local copies, waits for them, and re-layouts  7.68 us (6%)
  between operations  2.24 us (2%)
  other arithmetic  1.95 us (2%)
    ppermute x9, starting transfers between devices, to_chip(): return lax.ppermute(value, 'blk', [(i, i ^ 2 * mask) for i in range(count)])  14.5 us
    ppermute x12, waiting for transfers between devices, along(): lax.ppermute(value, 'blk', [(i, i ^ 2 << (second if i % 2 else first)) fo...  11.9 us
    ppermute x12, starting transfers between devices, along(): lax.ppermute(value, 'blk', [(i, i ^ 2 << (second if i % 2 else first)) fo...  10.7 us
    pallas_call x4, Pallas kernels, features_of(): pl.pallas_call(kernel, in_specs=[SMEM, HBM, HBM], out_specs=[VMEM] * len(...  8.93 us
    pallas_call x2, Pallas kernels, rotate(): pl.pallas_call(kernel, in_specs=[SMEM] + [VMEM] * (2 * NEAR) + [place] *...  8.21 us
    ppermute x4, waiting for transfers between devices, shards(): held = jnp.concatenate([held, lax.ppermute(held, 'blk', pairs)], axis=0)  7.54 us
    ppermute x1, waiting for transfers between devices, shards(): others.append(lax.ppermute(give_away(1, bases[0]), EVERYONE, across))  7.42 us
    pallas_call x2, Pallas kernels, project(): pl.pallas_call(kernel, in_specs=[VMEM] * (2 * chips) + [VMEM if staged el...  6.91 us
  transfers between devices with their start and end apart: 48, of which 22 were waited for; matrix products, arithmetic and copies ran while one was open for 3% of the time, Pallas kernels for 17%

profile of v3, /device:TPU:0, one launch (start us, length us, event | category | flops | bytes accessed | tf_op | source)
XLA Modules:
  0.0 124.8 jit_solution(1374197955947109586)
XLA Ops:
  0.1 1.9 %rank_halves.1 = (bf16[4,2,16,1152]{3,2,1,0:T(8,128)(2,1)S(1)}, bf16[4,2,16,1152]{3,2,1,0:T(8,128)(2,1)S(1)}) custom-call(s32[2]{0:T(128)S(1)} %pad_add_fusion.1.where, bf16[1,32,4096]{2,1,0:T(8,128)(2,1)} %left.1, bf16[1,32,14336]{2,1,0:T(8,128)(2,1)} %right.1), custom_call_target="tpu_custom_call" | custom-call | bytes 1179648 | tf_op jit(solution)/shard_map/rank_halves/pallas_call | solution.py:86
  2.5 1.2 collective-permute-done.received
  3.8 3.0 %collective-permute-start.4 = (bf16[2,16,1152]{2,1,0:T(8,128)(2,1)S(1)}, bf16[2,16,1152]{2,1,0:T(8,128)(2,1)S(1)}, u32[]{:S(2)}, u32[]{:S(2)}) collective-permute-start(bf16[2,16,1152]{2,1,0:T(8,128)(2,1)S(1)} %get-tuple-element.55), channel_id=1, source_target_pairs={{0,2},{1,3},{2,0},{3,1},{4,6},{5,7},{6,4},{7,5},{8,10},{9,11},{10,... | collective-permute-start | bytes 221192 | tf_op jit(solution)/shard_map/ppermute | solution.py:373
  6.7 1.6 %collective-permute-start.5 = (bf16[2,16,1152]{2,1,0:T(8,128)(2,1)S(1)}, bf16[2,16,1152]{2,1,0:T(8,128)(2,1)S(1)}, u32[]{:S(2)}, u32[]{:S(2)}) collective-permute-start(bf16[2,16,1152]{2,1,0:T(8,128)(2,1)S(1)} %get-tuple-element.56), channel_id=1, source_target_pairs={{0,4},{1,5},{2,6},{3,7},{4,0},{5,1},{6,2},{7,3},{8,12},{9,13},{10,... | collective-permute-start | bytes 221192 | tf_op jit(solution)/shard_map/ppermute | solution.py:373
  8.4 1.7 %features.4 = bf16[160,2304]{1,0:T(8,128)(2,1)S(1)} custom-call(s32[9]{0:T(128)S(1)} %get-tuple-element.114.where, bf16[160,4096]{1,0:T(8,128)(2,1)} %bitcast.90, bf16[160,14336]{1,0:T(8,128)(2,1)} %bitcast.86), custom_call_target="tpu_custom_call" | custom-call | bytes 1474560 | tf_op jit(solution)/shard_map/features/pallas_call | solution.py:205
  10.1 1.9 %collective-permute-start.11 = (bf16[160,2304]{1,0:T(8,128)(2,1)S(1)}, bf16[160,2304]{1,0:T(8,128)(2,1)S(1)}, u32[]{:S(2)}, u32[]{:S(2)}) collective-permute-start(bf16[160,2304]{1,0:T(8,128)(2,1)S(1)} %features.4), channel_id=1, source_target_pairs={{0,16},{1,17},{2,18},{3,19},{4,20},{5,21},{6,22},{7,23},{8,24},{9,... | collective-permute-start | bytes 2211848 | tf_op jit(solution)/shard_map/ppermute | solution.py:404
  12.1 1.5 %collective-permute-start.1 = (bf16[2,16,1152]{2,1,0:T(8,128)(2,1)S(1)}, bf16[2,16,1152]{2,1,0:T(8,128)(2,1)S(1)}, u32[]{:S(2)}, u32[]{:S(2)}) collective-permute-start(bf16[2,16,1152]{2,1,0:T(8,128)(2,1)S(1)} %get-tuple-element.51), channel_id=1, source_target_pairs={{0,2},{1,3},{2,0},{3,1},{4,6},{5,7},{6,4},{7,5},{8,10},{9,11},{10,... | collective-permute-start | bytes 221192 | tf_op jit(solution)/shard_map/ppermute | solution.py:373
  13.6 1.6 %collective-permute-start.2 = (bf16[2,16,1152]{2,1,0:T(8,128)(2,1)S(1)}, bf16[2,16,1152]{2,1,0:T(8,128)(2,1)S(1)}, u32[]{:S(2)}, u32[]{:S(2)}) collective-permute-start(bf16[2,16,1152]{2,1,0:T(8,128)(2,1)S(1)} %get-tuple-element.52), channel_id=1, source_target_pairs={{0,4},{1,5},{2,6},{3,7},{4,0},{5,1},{6,2},{7,3},{8,12},{9,13},{10,... | collective-permute-start | bytes 221192 | tf_op jit(solution)/shard_map/ppermute | solution.py:373
  16.4 2.6 %collective-permute-start.8 = (bf16[1,64,1152]{2,1,0:T(8,128)(2,1)S(1)}, bf16[1,64,1152]{2,1,0:T(8,128)(2,1)S(1)}, u32[]{:S(2)}, u32[]{:S(2)}) collective-permute-start(bf16[1,64,1152]{2,1,0:T(8,128)(2,1)S(1)} %choose.2), channel_id=1, source_target_pairs={{0,8},{1,9},{2,10},{3,11},{4,12},{5,13},{6,14},{7,15},{8,0},{9,1},... | collective-permute-start | bytes 442376 | tf_op jit(solution)/shard_map/ppermute | solution.py:373
  19.1 2.4 %collective-permute-done.3.rest_3_ = bf16[2,16,1152]{2,1,0:T(8,128)(2,1)S(1)} collective-permute-done((bf16[2,16,1152]{2,1,0:T(8,128)(2,1)S(1)}, bf16[2,16,1152]{2,1,0:T(8,128)(2,1)S(1)}, u32[]{:S(2)}, u32[]{:S(2)}) %collective-permute-start.3) | collective-permute-done | bytes 73760 | tf_op jit(solution)/shard_map/ppermute | solution.py:373
  22.3 2.2 %collective-permute-start.7 = (bf16[1,64,1152]{2,1,0:T(8,128)(2,1)S(1)}, bf16[1,64,1152]{2,1,0:T(8,128)(2,1)S(1)}, u32[]{:S(2)}, u32[]{:S(2)}) collective-permute-start(bf16[1,64,1152]{2,1,0:T(8,128)(2,1)S(1)} %choose.3), channel_id=1, source_target_pairs={{0,8},{1,9},{2,10},{3,11},{4,12},{5,13},{6,14},{7,15},{8,0},{9,1},... | collective-permute-start | bytes 442376 | tf_op jit(solution)/shard_map/ppermute | solution.py:373
  24.5 3.0 %stage_bases.1 = (bf16[256,1024]{1,0:T(8,128)(2,1)S(1)}, bf16[896,3584]{1,0:T(8,128)(2,1)S(1)}) custom-call(s32[1]{0:T(128)} %bitcast.5.where, bf16[256,4096]{1,0:T(8,128)(2,1)} %rest_8_.1, bf16[896,14336]{1,0:T(8,128)(2,1)} %rest_9_.1), custom_call_target="tpu_custom_call" | custom-call | bytes 6946816 | tf_op jit(solution)/shard_map/stage_bases/pallas_call | solution.py:137
  27.6 1.8 %features.5 = bf16[160,3456]{1,0:T(8,128)(2,1)S(1)} custom-call(s32[9]{0:T(128)S(1)} %get-tuple-element.114.where, bf16[160,4096]{1,0:T(8,128)(2,1)} %bitcast.91, bf16[160,14336]{1,0:T(8,128)(2,1)} %bitcast.87), custom_call_target="tpu_custom_call" | custom-call | bytes 2211840 | tf_op jit(solution)/shard_map/features/pallas_call | solution.py:205
  30.1 1.1 collective-permute-done.7
  31.1 1.4 %collective-permute-start.9 = (bf16[64,1152]{1,0:T(8,128)(2,1)S(1)}, bf16[64,1152]{1,0:T(8,128)(2,1)S(1)}, u32[]{:S(2)}, u32[]{:S(2)}) collective-permute-start(bf16[64,1152]{1,0:T(8,128)(2,1)S(1)} %add_bitcast_fusion.rest_0_), channel_id=1, source_target_pairs={{0,2},{1,5},{2,0},{3,7},{4,6},{5,1},{6,4},{7,3},{8,10},{9,13},{10,... | collective-permute-start | bytes 442376 | tf_op jit(solution)/shard_map/ppermute | solution.py:376
  34.5 2.8 %collective-permute-done.9.rest_1_ = bf16[64,1152]{1,0:T(8,128)(2,1)S(1)} collective-permute-done((bf16[64,1152]{1,0:T(8,128)(2,1)S(1)}, bf16[64,1152]{1,0:T(8,128)(2,1)S(1)}, u32[]{:S(2)}, u32[]{:S(2)}) %collective-permute-start.9) | collective-permute-done | bytes 147488 | tf_op jit(solution)/shard_map/ppermute | solution.py:376
  37.8 1.5 %collective-permute-start.19 = (bf16[64,1152]{1,0:T(8,128)(2,1)S(1)}, bf16[64,1152]{1,0:T(8,128)(2,1)S(1)}, u32[]{:S(2)}, u32[]{:S(2)}) collective-permute-start(bf16[64,1152]{1,0:T(8,128)(2,1)S(1)} %bitcast.61), channel_id=1, source_target_pairs={{0,4},{1,3},{2,6},{3,1},{4,0},{5,7},{6,2},{7,5},{8,12},{9,11},{10,... | collective-permute-start | bytes 442376 | tf_op jit(solution)/shard_map/ppermute | solution.py:376
  39.3 1.1 collective-permute-done.12.rest_1_
  41.0 1.5 %collective-permute-done.13.rest_3_ = bf16[64,1152]{1,0:T(8,128)(2,1)S(1)} collective-permute-done((bf16[64,1152]{1,0:T(8,128)(2,1)S(1)}, bf16[64,1152]{1,0:T(8,128)(2,1)S(1)}, u32[]{:S(2)}, u32[]{:S(2)}) %collective-permute-start.13) | collective-permute-done | bytes 147488 | tf_op jit(solution)/shard_map/ppermute | solution.py:376
  42.5 1.6 %collective-permute-done.19.rest_2_ = bf16[64,1152]{1,0:T(8,128)(2,1)S(1)} collective-permute-done((bf16[64,1152]{1,0:T(8,128)(2,1)S(1)}, bf16[64,1152]{1,0:T(8,128)(2,1)S(1)}, u32[]{:S(2)}, u32[]{:S(2)}) %collective-permute-start.19) | collective-permute-done | bytes 147488 | tf_op jit(solution)/shard_map/ppermute | solution.py:376
  44.0 1.6 %collective-permute-done.20.rest_3_ = bf16[64,1152]{1,0:T(8,128)(2,1)S(1)} collective-permute-done((bf16[64,1152]{1,0:T(8,128)(2,1)S(1)}, bf16[64,1152]{1,0:T(8,128)(2,1)S(1)}, u32[]{:S(2)}, u32[]{:S(2)}) %collective-permute-start.20) | collective-permute-done | bytes 147488 | tf_op jit(solution)/shard_map/ppermute | solution.py:376
  45.6 7.4 %collective-permute-done.14.rest_17_ = bf16[160,3456]{1,0:T(8,128)(2,1)} collective-permute-done((bf16[160,3456]{1,0:T(8,128)(2,1)S(1)}, bf16[160,3456]{1,0:T(8,128)(2,1)}, u32[]{:S(2)}, u32[]{:S(2)}) %collective-permute-start.14) | collective-permute-done | bytes 1105952 | tf_op jit(solution)/shard_map/ppermute | solution.py:422
  54.2 5.6 %rotate.2.rest_10_ = f32[1152,128]{1,0:T(8,128)S(1)} custom-call(s32[5]{0:T(128)S(1)} %pad_add_fusion.where, bf16[64,1152]{1,0:T(8,128)(2,1)S(1)} %bitcast.63, bf16[64,1152]{1,0:T(8,128)(2,1)S(1)} %collective-permute-done.12.rest_1_, bf16[64,1152]{1,0:T(8,128)(2,1)S(1)} %collective-permute-done.19.rest_2_, ...), custom_call_target="tpu_custom_call" | custom-call | flops 889192448 | bytes 6946816 | tf_op jit(solution)/shard_map/rotate/pallas_call | solution.py:279
  59.8 2.6 %rotate.3 = (f32[128,1152]{1,0:T(8,128)S(1)}, bf16[128,1152]{1,0:T(8,128)(2,1)S(1)}) custom-call(s32[5]{0:T(128)S(1)} %pad_add_fusion.where, bf16[64,1152]{1,0:T(8,128)(2,1)S(1)} %add_bitcast_fusion.rest_0_, bf16[64,1152]{1,0:T(8,128)(2,1)S(1)} %collective-permute-done.9.rest_1_, bf16[64,1152]{1,0:T(8,128)(2,1)S(1)} %collective-permute-done.10.rest_2_, ...), custom_call_target="tpu_custom_call" | custom-call | flops 889192448 | bytes 6946816 | tf_op jit(solution)/shard_map/rotate/pallas_call | solution.py:279
  62.4 1.3 %collective-permute-start.25 = (bf16[128,1152]{1,0:T(8,128)(2,1)S(1)}, bf16[128,1152]{1,0:T(8,128)(2,1)S(1)}, u32[]{:S(2)}, u32[]{:S(2)}) collective-permute-start(bf16[128,1152]{1,0:T(8,128)(2,1)S(1)} %get-tuple-element.78), channel_id=1, source_target_pairs={{1,17},{3,19},{5,21},{7,23},{9,25},{11,27},{13,29},{15,31},{16,0},... | collective-permute-start | bytes 884744 | tf_op jit(solution)/shard_map/ppermute | solution.py:443
  63.7 2.9 %features.6 = bf16[160,3456]{1,0:T(8,128)(2,1)} custom-call(s32[9]{0:T(128)S(1)} %get-tuple-element.114.where, bf16[160,4096]{1,0:T(8,128)(2,1)} %bitcast.92, bf16[160,14336]{1,0:T(8,128)(2,1)} %bitcast.88), custom_call_target="tpu_custom_call" | custom-call | bytes 2211840 | tf_op jit(solution)/shard_map/features/pallas_call | solution.py:205
  66.6 4.4 %collective-permute-done.25 = bf16[128,1152]{1,0:T(8,128)(2,1)S(1)} collective-permute-done((bf16[128,1152]{1,0:T(8,128)(2,1)S(1)}, bf16[128,1152]{1,0:T(8,128)(2,1)S(1)}, u32[]{:S(2)}, u32[]{:S(2)}) %collective-permute-start.25) | collective-permute-done | bytes 294944 | tf_op jit(solution)/shard_map/ppermute | solution.py:443
  71.1 1.3 %collective-permute-start.26 = (bf16[64,1152]{1,0:T(8,128)(2,1)S(1)}, bf16[64,1152]{1,0:T(8,128)(2,1)S(1)}, u32[]{:S(2)}, u32[]{:S(2)}) collective-permute-start(bf16[64,1152]{1,0:T(8,128)(2,1)S(1)} %slice.29), channel_id=1, source_target_pairs={{0,1},{2,3},{4,5},{6,7},{8,9},{10,11},{12,13},{14,15},{17,16},{19,... | collective-permute-start | bytes 442376 | tf_op jit(solution)/shard_map/ppermute | solution.py:446
  73.4 1.7 %collective-permute-start.30 = (bf16[1,64,1152]{2,1,0:T(8,128)(2,1)S(1)}, bf16[1,64,1152]{2,1,0:T(8,128)(2,1)S(1)}, u32[]{:S(2)}, u32[]{:S(2)}) collective-permute-start(bf16[1,64,1152]{2,1,0:T(8,128)(2,1)S(1)} %bitcast.56), channel_id=1, source_target_pairs={{0,8},{1,9},{2,10},{3,11},{4,12},{5,13},{6,14},{7,15},{8,0},{9,1},... | collective-permute-start | bytes 442376 | tf_op jit(solution)/shard_map/ppermute | solution.py:373
  75.1 1.5 %collective-permute-start.27 = (bf16[1,64,1152]{2,1,0:T(8,128)(2,1)S(1)}, bf16[1,64,1152]{2,1,0:T(8,128)(2,1)S(1)}, u32[]{:S(2)}, u32[]{:S(2)}) collective-permute-start(bf16[1,64,1152]{2,1,0:T(8,128)(2,1)S(1)} %bitcast.57), channel_id=1, source_target_pairs={{0,2},{1,5},{2,0},{3,7},{4,6},{5,1},{6,4},{7,3},{8,10},{9,13},{10,... | collective-permute-start | bytes 442376 | tf_op jit(solution)/shard_map/ppermute | solution.py:376
  76.6 1.6 %collective-permute-start.28 = (bf16[1,64,1152]{2,1,0:T(8,128)(2,1)S(1)}, bf16[1,64,1152]{2,1,0:T(8,128)(2,1)S(1)}, u32[]{:S(2)}, u32[]{:S(2)}) collective-permute-start(bf16[1,64,1152]{2,1,0:T(8,128)(2,1)S(1)} %bitcast.58), channel_id=1, source_target_pairs={{0,4},{1,3},{2,6},{3,1},{4,0},{5,7},{6,2},{7,5},{8,12},{9,11},{10,... | collective-permute-start | bytes 442376 | tf_op jit(solution)/shard_map/ppermute | solution.py:376
  78.2 2.5 %features.7.rest_16_ = bf16[160,9216]{1,0:T(8,128)(2,1)S(1)} custom-call(s32[9]{0:T(128)S(1)} %get-tuple-element.113.where, bf16[160,4096]{1,0:T(8,128)(2,1)} %bitcast.93, bf16[160,14336]{1,0:T(8,128)(2,1)} %bitcast.89), custom_call_target="tpu_custom_call" | custom-call | bytes 5898240 | tf_op jit(solution)/shard_map/features/pallas_call | solution.py:205
  80.8 3.0 %collective-permute-done.30 = bf16[1,64,1152]{2,1,0:T(8,128)(2,1)S(1)} collective-permute-done((bf16[1,64,1152]{2,1,0:T(8,128)(2,1)S(1)}, bf16[1,64,1152]{2,1,0:T(8,128)(2,1)S(1)}, u32[]{:S(2)}, u32[]{:S(2)}) %collective-permute-start.30) | collective-permute-done | bytes 147488 | tf_op jit(solution)/shard_map/ppermute | solution.py:373
  85.6 1.4 %collective-permute-start.29 = (bf16[1,64,1152]{2,1,0:T(8,128)(2,1)S(1)}, bf16[1,64,1152]{2,1,0:T(8,128)(2,1)}, u32[]{:S(2)}, u32[]{:S(2)}) collective-permute-start(bf16[1,64,1152]{2,1,0:T(8,128)(2,1)S(1)} %collective-permute-done.27), channel_id=1, source_target_pairs={{0,4},{1,3},{2,6},{3,1},{4,0},{5,7},{6,2},{7,5},{8,12},{9,11},{10,... | collective-permute-start | bytes 442376 | tf_op jit(solution)/shard_map/ppermute | solution.py:376
  87.0 3.3 %collective-permute-done.31 = bf16[1,64,1152]{2,1,0:T(8,128)(2,1)} collective-permute-done((bf16[1,64,1152]{2,1,0:T(8,128)(2,1)S(1)}, bf16[1,64,1152]{2,1,0:T(8,128)(2,1)}, u32[]{:S(2)}, u32[]{:S(2)}) %collective-permute-start.31) | collective-permute-done | bytes 147488 | tf_op jit(solution)/shard_map/ppermute | solution.py:376
  95.5 1.0 collective-permute-start.40
  97.1 1.0 collective-permute-done.39
  98.7 0.9 copy-done.1
  101.4 4.7 %project.3 = (bf16[160,128]{1,0:T(8,128)(2,1)S(1)}, bf16[160,128]{1,0:T(8,128)(2,1)S(1)}) custom-call(bf16[64,1152]{1,0:T(8,128)(2,1)S(1)} %slice_select_fusion.rest_0_, bf16[64,1152]{1,0:T(8,128)(2,1)S(1)} %bitcast.66, bf16[64,1152]{1,0:T(8,128)(2,1)S(1)} %bitcast.68, bf16[64,1152]{1,0:T(8,128)(2,1)} %bitcast.16.rest_3_, bf16[64,1152]{1,0:T(8,128)(2,1)S(1)} %bitcast.64, ...), custom_call_target="tpu_custom_call" | custom-call | flops 377487360 | bytes 2359296 | tf_op jit(solution)/shard_map/project/pallas_call | solution.py:333
  106.2 1.2 collective-permute-start.43
  108.0 2.2 %project.2 = (f32[160,128]{1,0:T(8,128)S(1)}, f32[160,128]{1,0:T(8,128)S(1)}) custom-call(bf16[64,1152]{1,0:T(8,128)(2,1)S(1)} %slice_select_fusion.rest_0_, bf16[64,1152]{1,0:T(8,128)(2,1)S(1)} %bitcast.67, bf16[64,1152]{1,0:T(8,128)(2,1)S(1)} %bitcast.69, bf16[64,1152]{1,0:T(8,128)(2,1)} %bitcast.16.rest_3_, bf16[64,1152]{1,0:T(8,128)(2,1)S(1)} %bitcast.65, ...), custom_call_target="tpu_custom_call" | custom-call | flops 377487360 | bytes 2359296 | tf_op jit(solution)/shard_map/project/pallas_call | solution.py:333
  111.2 1.0 collective-permute-done.44
  112.3 1.2 collective-permute-start.45
  113.5 2.4 %collective-permute-done.45 = f32[2,1,4]{2,1,0:T(1,128)S(1)} collective-permute-done((f32[2,1,4]{2,1,0:T(1,128)S(1)}, f32[2,1,4]{2,1,0:T(1,128)S(1)}, u32[]{:S(2)}, u32[]{:S(2)}) %collective-permute-start.45) | collective-permute-done | bytes 64 | tf_op jit(solution)/shard_map/ppermute | solution.py:472
  115.8 1.3 %collective-permute-start.46 = (f32[4,1,4]{2,1,0:T(1,128)S(1)}, f32[4,1,4]{2,1,0:T(1,128)S(1)}, u32[]{:S(2)}, u32[]{:S(2)}) collective-permute-start(f32[4,1,4]{2,1,0:T(1,128)S(1)} %pad_maximum_fusion.2), channel_id=1, source_target_pairs={{0,4},{1,5},{2,6},{3,7},{4,0},{5,1},{6,2},{7,3},{8,12},{9,13},{10,... | collective-permute-start | bytes 200 | tf_op jit(solution)/shard_map/ppermute | solution.py:472
  117.2 2.2 %collective-permute-done.46 = f32[4,1,4]{2,1,0:T(1,128)S(1)} collective-permute-done((f32[4,1,4]{2,1,0:T(1,128)S(1)}, f32[4,1,4]{2,1,0:T(1,128)S(1)}, u32[]{:S(2)}, u32[]{:S(2)}) %collective-permute-start.46) | collective-permute-done | bytes 96 | tf_op jit(solution)/shard_map/ppermute | solution.py:472
  119.4 2.4 %collective-permute-start.47 = (f32[8,1,4]{2,1,0:T(1,128)S(1)}, f32[8,1,4]{2,1,0:T(1,128)S(1)}, u32[]{:S(2)}, u32[]{:S(2)}) collective-permute-start(f32[8,1,4]{2,1,0:T(1,128)S(1)} %pad_maximum_fusion.1), channel_id=1, source_target_pairs={{0,8},{1,9},{2,10},{3,11},{4,12},{5,13},{6,14},{7,15},{8,0},{9,1},... | collective-permute-start | bytes 392 | tf_op jit(solution)/shard_map/ppermute | solution.py:472
  122.0 2.0 %collective-permute-done.47 = f32[8,1,4]{2,1,0:T(1,128)S(1)} collective-permute-done((f32[8,1,4]{2,1,0:T(1,128)S(1)}, f32[8,1,4]{2,1,0:T(1,128)S(1)}, u32[]{:S(2)}, u32[]{:S(2)}) %collective-permute-start.47) | collective-permute-done | bytes 160 | tf_op jit(solution)/shard_map/ppermute | solution.py:472
  (123 shorter events, 19.7 us)
Async XLA Ops:
  2.0 1.7 %collective-permute-start = (bf16[4,2,16,1152]{3,2,1,0:T(8,128)(2,1)S(1)}, bf16[4,2,16,1152]{3,2,1,0:T(8,128)(2,1)S(1)}, u32[]{:S(2)}, u32[]{:S(2)}) collective-permute-start(bf16[4,2,16,1152]{3,2,1,0:T(8,128)(2,1)S(1)} %get-tuple-element.49), channel_id=1, source_target_pairs={{0,1},{1,0},{2,3},{3,2},{4,5},{5,4},{6,7},{7,6},{8,9},{9,8},{10,11... | collective-permute-start | bytes 884744 | tf_op jit(solution)/shard_map/ppermute | solution.py:379
  3.8 9.8 %collective-permute-start.4 = (bf16[2,16,1152]{2,1,0:T(8,128)(2,1)S(1)}, bf16[2,16,1152]{2,1,0:T(8,128)(2,1)S(1)}, u32[]{:S(2)}, u32[]{:S(2)}) collective-permute-start(bf16[2,16,1152]{2,1,0:T(8,128)(2,1)S(1)} %get-tuple-element.55), channel_id=1, source_target_pairs={{0,2},{1,3},{2,0},{3,1},{4,6},{5,7},{6,4},{7,5},{8,10},{9,11},{10,... | collective-permute-start | bytes 221192 | tf_op jit(solution)/shard_map/ppermute | solution.py:373
  6.7 8.4 %collective-permute-start.5 = (bf16[2,16,1152]{2,1,0:T(8,128)(2,1)S(1)}, bf16[2,16,1152]{2,1,0:T(8,128)(2,1)S(1)}, u32[]{:S(2)}, u32[]{:S(2)}) collective-permute-start(bf16[2,16,1152]{2,1,0:T(8,128)(2,1)S(1)} %get-tuple-element.56), channel_id=1, source_target_pairs={{0,4},{1,5},{2,6},{3,7},{4,0},{5,1},{6,2},{7,3},{8,12},{9,13},{10,... | collective-permute-start | bytes 221192 | tf_op jit(solution)/shard_map/ppermute | solution.py:373
  8.4 7.2 %collective-permute-start.6 = (bf16[2,16,1152]{2,1,0:T(8,128)(2,1)S(1)}, bf16[2,16,1152]{2,1,0:T(8,128)(2,1)S(1)}, u32[]{:S(2)}, u32[]{:S(2)}) collective-permute-start(bf16[2,16,1152]{2,1,0:T(8,128)(2,1)S(1)} %get-tuple-element.57), channel_id=1, source_target_pairs={{0,6},{1,7},{2,4},{3,5},{4,2},{5,3},{6,0},{7,1},{8,14},{9,15},{10,... | collective-permute-start | bytes 221192 | tf_op jit(solution)/shard_map/ppermute | solution.py:373
  10.1 22.4 %collective-permute-start.11 = (bf16[160,2304]{1,0:T(8,128)(2,1)S(1)}, bf16[160,2304]{1,0:T(8,128)(2,1)S(1)}, u32[]{:S(2)}, u32[]{:S(2)}) collective-permute-start(bf16[160,2304]{1,0:T(8,128)(2,1)S(1)} %features.4), channel_id=1, source_target_pairs={{0,16},{1,17},{2,18},{3,19},{4,20},{5,21},{6,22},{7,23},{8,24},{9,... | collective-permute-start | bytes 2211848 | tf_op jit(solution)/shard_map/ppermute | solution.py:404
  12.1 7.0 %collective-permute-start.1 = (bf16[2,16,1152]{2,1,0:T(8,128)(2,1)S(1)}, bf16[2,16,1152]{2,1,0:T(8,128)(2,1)S(1)}, u32[]{:S(2)}, u32[]{:S(2)}) collective-permute-start(bf16[2,16,1152]{2,1,0:T(8,128)(2,1)S(1)} %get-tuple-element.51), channel_id=1, source_target_pairs={{0,2},{1,3},{2,0},{3,1},{4,6},{5,7},{6,4},{7,5},{8,10},{9,11},{10,... | collective-permute-start | bytes 221192 | tf_op jit(solution)/shard_map/ppermute | solution.py:373
  13.6 5.5 %collective-permute-start.2 = (bf16[2,16,1152]{2,1,0:T(8,128)(2,1)S(1)}, bf16[2,16,1152]{2,1,0:T(8,128)(2,1)S(1)}, u32[]{:S(2)}, u32[]{:S(2)}) collective-permute-start(bf16[2,16,1152]{2,1,0:T(8,128)(2,1)S(1)} %get-tuple-element.52), channel_id=1, source_target_pairs={{0,4},{1,5},{2,6},{3,7},{4,0},{5,1},{6,2},{7,3},{8,12},{9,13},{10,... | collective-permute-start | bytes 221192 | tf_op jit(solution)/shard_map/ppermute | solution.py:373
  15.2 6.3 %collective-permute-start.3 = (bf16[2,16,1152]{2,1,0:T(8,128)(2,1)S(1)}, bf16[2,16,1152]{2,1,0:T(8,128)(2,1)S(1)}, u32[]{:S(2)}, u32[]{:S(2)}) collective-permute-start(bf16[2,16,1152]{2,1,0:T(8,128)(2,1)S(1)} %get-tuple-element.53), channel_id=1, source_target_pairs={{0,6},{1,7},{2,4},{3,5},{4,2},{5,3},{6,0},{7,1},{8,14},{9,15},{10,... | collective-permute-start | bytes 221192 | tf_op jit(solution)/shard_map/ppermute | solution.py:373
  16.4 13.6 %collective-permute-start.8 = (bf16[1,64,1152]{2,1,0:T(8,128)(2,1)S(1)}, bf16[1,64,1152]{2,1,0:T(8,128)(2,1)S(1)}, u32[]{:S(2)}, u32[]{:S(2)}) collective-permute-start(bf16[1,64,1152]{2,1,0:T(8,128)(2,1)S(1)} %choose.2), channel_id=1, source_target_pairs={{0,8},{1,9},{2,10},{3,11},{4,12},{5,13},{6,14},{7,15},{8,0},{9,1},... | collective-permute-start | bytes 442376 | tf_op jit(solution)/shard_map/ppermute | solution.py:373
  22.3 8.8 %collective-permute-start.7 = (bf16[1,64,1152]{2,1,0:T(8,128)(2,1)S(1)}, bf16[1,64,1152]{2,1,0:T(8,128)(2,1)S(1)}, u32[]{:S(2)}, u32[]{:S(2)}) collective-permute-start(bf16[1,64,1152]{2,1,0:T(8,128)(2,1)S(1)} %choose.3), channel_id=1, source_target_pairs={{0,8},{1,9},{2,10},{3,11},{4,12},{5,13},{6,14},{7,15},{8,0},{9,1},... | collective-permute-start | bytes 442376 | tf_op jit(solution)/shard_map/ppermute | solution.py:373
  29.4 23.6 %collective-permute-start.14 = (bf16[160,3456]{1,0:T(8,128)(2,1)S(1)}, bf16[160,3456]{1,0:T(8,128)(2,1)}, u32[]{:S(2)}, u32[]{:S(2)}) collective-permute-start(bf16[160,3456]{1,0:T(8,128)(2,1)S(1)} %features.5), channel_id=1, source_target_pairs={{0,16},{1,17},{2,18},{3,19},{4,20},{5,21},{6,22},{7,23},{8,24},{9,... | collective-permute-start | bytes 3317768 | tf_op jit(solution)/shard_map/ppermute | solution.py:422
  31.1 6.2 %collective-permute-start.9 = (bf16[64,1152]{1,0:T(8,128)(2,1)S(1)}, bf16[64,1152]{1,0:T(8,128)(2,1)S(1)}, u32[]{:S(2)}, u32[]{:S(2)}) collective-permute-start(bf16[64,1152]{1,0:T(8,128)(2,1)S(1)} %add_bitcast_fusion.rest_0_), channel_id=1, source_target_pairs={{0,2},{1,5},{2,0},{3,7},{4,6},{5,1},{6,4},{7,3},{8,10},{9,13},{10,... | collective-permute-start | bytes 442376 | tf_op jit(solution)/shard_map/ppermute | solution.py:376
  33.4 7.1 %collective-permute-start.12 = (bf16[64,1152]{1,0:T(8,128)(2,1)S(1)}, bf16[64,1152]{1,0:T(8,128)(2,1)S(1)}, u32[]{:S(2)}, u32[]{:S(2)}) collective-permute-start(bf16[64,1152]{1,0:T(8,128)(2,1)S(1)} %bitcast.60), channel_id=1, source_target_pairs={{0,2},{1,5},{2,0},{3,7},{4,6},{5,1},{6,4},{7,3},{8,10},{9,13},{10,... | collective-permute-start | bytes 442376 | tf_op jit(solution)/shard_map/ppermute | solution.py:376
  34.1 6.9 %collective-permute-start.10 = (bf16[64,1152]{1,0:T(8,128)(2,1)S(1)}, bf16[64,1152]{1,0:T(8,128)(2,1)S(1)}, u32[]{:S(2)}, u32[]{:S(2)}) collective-permute-start(bf16[64,1152]{1,0:T(8,128)(2,1)S(1)} %add_bitcast_fusion.rest_0_), channel_id=1, source_target_pairs={{0,4},{1,3},{2,6},{3,1},{4,0},{5,7},{6,2},{7,5},{8,12},{9,11},{10,... | collective-permute-start | bytes 442376 | tf_op jit(solution)/shard_map/ppermute | solution.py:376
  37.3 5.1 %collective-permute-start.13 = (bf16[64,1152]{1,0:T(8,128)(2,1)S(1)}, bf16[64,1152]{1,0:T(8,128)(2,1)S(1)}, u32[]{:S(2)}, u32[]{:S(2)}) collective-permute-start(bf16[64,1152]{1,0:T(8,128)(2,1)S(1)} %collective-permute-done.9.rest_1_), channel_id=1, source_target_pairs={{0,4},{1,3},{2,6},{3,1},{4,0},{5,7},{6,2},{7,5},{8,12},{9,11},{10,... | collective-permute-start | bytes 442376 | tf_op jit(solution)/shard_map/ppermute | solution.py:376
  37.8 6.2 %collective-permute-start.19 = (bf16[64,1152]{1,0:T(8,128)(2,1)S(1)}, bf16[64,1152]{1,0:T(8,128)(2,1)S(1)}, u32[]{:S(2)}, u32[]{:S(2)}) collective-permute-start(bf16[64,1152]{1,0:T(8,128)(2,1)S(1)} %bitcast.61), channel_id=1, source_target_pairs={{0,4},{1,3},{2,6},{3,1},{4,0},{5,7},{6,2},{7,5},{8,12},{9,11},{10,... | collective-permute-start | bytes 442376 | tf_op jit(solution)/shard_map/ppermute | solution.py:376
  40.5 5.1 %collective-permute-start.20 = (bf16[64,1152]{1,0:T(8,128)(2,1)S(1)}, bf16[64,1152]{1,0:T(8,128)(2,1)S(1)}, u32[]{:S(2)}, u32[]{:S(2)}) collective-permute-start(bf16[64,1152]{1,0:T(8,128)(2,1)S(1)} %collective-permute-done.12.rest_1_), channel_id=1, source_target_pairs={{0,4},{1,3},{2,6},{3,1},{4,0},{5,7},{6,2},{7,5},{8,12},{9,11},{10,... | collective-permute-start | bytes 442376 | tf_op jit(solution)/shard_map/ppermute | solution.py:376
  41.0 12.1 %collective-permute-start.21 = (bf16[64,1152]{1,0:T(8,128)(2,1)S(1)}, bf16[64,1152]{1,0:T(8,128)(2,1)S(1)}, u32[]{:S(2)}, u32[]{:S(2)}) collective-permute-start(bf16[64,1152]{1,0:T(8,128)(2,1)S(1)} %bitcast.62), channel_id=1, source_target_pairs={{0,1},{1,0},{2,3},{3,2},{4,5},{5,4},{6,7},{7,6},{8,9},{9,8},{10,11... | collective-permute-start | bytes 442376 | tf_op jit(solution)/shard_map/ppermute | solution.py:379
  42.5 11.1 %collective-permute-start.22 = (bf16[64,1152]{1,0:T(8,128)(2,1)S(1)}, bf16[64,1152]{1,0:T(8,128)(2,1)S(1)}, u32[]{:S(2)}, u32[]{:S(2)}) collective-permute-start(bf16[64,1152]{1,0:T(8,128)(2,1)S(1)} %collective-permute-done.12.rest_1_), channel_id=1, source_target_pairs={{0,1},{1,0},{2,3},{3,2},{4,5},{5,4},{6,7},{7,6},{8,9},{9,8},{10,11... | collective-permute-start | bytes 442376 | tf_op jit(solution)/shard_map/ppermute | solution.py:379
  44.0 9.6 %collective-permute-start.23 = (bf16[64,1152]{1,0:T(8,128)(2,1)S(1)}, bf16[64,1152]{1,0:T(8,128)(2,1)S(1)}, u32[]{:S(2)}, u32[]{:S(2)}) collective-permute-start(bf16[64,1152]{1,0:T(8,128)(2,1)S(1)} %collective-permute-done.19.rest_2_), channel_id=1, source_target_pairs={{0,1},{1,0},{2,3},{3,2},{4,5},{5,4},{6,7},{7,6},{8,9},{9,8},{10,11... | collective-permute-start | bytes 442376 | tf_op jit(solution)/shard_map/ppermute | solution.py:379
  45.6 8.5 %collective-permute-start.24 = (bf16[64,1152]{1,0:T(8,128)(2,1)S(1)}, bf16[64,1152]{1,0:T(8,128)(2,1)S(1)}, u32[]{:S(2)}, u32[]{:S(2)}) collective-permute-start(bf16[64,1152]{1,0:T(8,128)(2,1)S(1)} %collective-permute-done.20.rest_3_), channel_id=1, source_target_pairs={{0,1},{1,0},{2,3},{3,2},{4,5},{5,4},{6,7},{7,6},{8,9},{9,8},{10,11... | collective-permute-start | bytes 442376 | tf_op jit(solution)/shard_map/ppermute | solution.py:379
  53.1 6.7 %collective-permute-start.15 = (bf16[64,1152]{1,0:T(8,128)(2,1)S(1)}, bf16[64,1152]{1,0:T(8,128)(2,1)S(1)}, u32[]{:S(2)}, u32[]{:S(2)}) collective-permute-start(bf16[64,1152]{1,0:T(8,128)(2,1)S(1)} %add_bitcast_fusion.rest_0_), channel_id=1, source_target_pairs={{0,1},{1,0},{2,3},{3,2},{4,5},{5,4},{6,7},{7,6},{8,9},{9,8},{10,11... | collective-permute-start | bytes 442376 | tf_op jit(solution)/shard_map/ppermute | solution.py:379
  53.1 6.7 %collective-permute-start.16 = (bf16[64,1152]{1,0:T(8,128)(2,1)S(1)}, bf16[64,1152]{1,0:T(8,128)(2,1)S(1)}, u32[]{:S(2)}, u32[]{:S(2)}) collective-permute-start(bf16[64,1152]{1,0:T(8,128)(2,1)S(1)} %collective-permute-done.9.rest_1_), channel_id=1, source_target_pairs={{0,1},{1,0},{2,3},{3,2},{4,5},{5,4},{6,7},{7,6},{8,9},{9,8},{10,11... | collective-permute-start | bytes 442376 | tf_op jit(solution)/shard_map/ppermute | solution.py:379
  53.6 6.2 %collective-permute-start.17 = (bf16[64,1152]{1,0:T(8,128)(2,1)S(1)}, bf16[64,1152]{1,0:T(8,128)(2,1)S(1)}, u32[]{:S(2)}, u32[]{:S(2)}) collective-permute-start(bf16[64,1152]{1,0:T(8,128)(2,1)S(1)} %collective-permute-done.10.rest_2_), channel_id=1, source_target_pairs={{0,1},{1,0},{2,3},{3,2},{4,5},{5,4},{6,7},{7,6},{8,9},{9,8},{10,11... | collective-permute-start | bytes 442376 | tf_op jit(solution)/shard_map/ppermute | solution.py:379
  53.6 6.1 %collective-permute-start.18 = (bf16[64,1152]{1,0:T(8,128)(2,1)S(1)}, bf16[64,1152]{1,0:T(8,128)(2,1)S(1)}, u32[]{:S(2)}, u32[]{:S(2)}) collective-permute-start(bf16[64,1152]{1,0:T(8,128)(2,1)S(1)} %collective-permute-done.13.rest_3_), channel_id=1, source_target_pairs={{0,1},{1,0},{2,3},{3,2},{4,5},{5,4},{6,7},{7,6},{8,9},{9,8},{10,11... | collective-permute-start | bytes 442376 | tf_op jit(solution)/shard_map/ppermute | solution.py:379
  62.4 8.6 %collective-permute-start.25 = (bf16[128,1152]{1,0:T(8,128)(2,1)S(1)}, bf16[128,1152]{1,0:T(8,128)(2,1)S(1)}, u32[]{:S(2)}, u32[]{:S(2)}) collective-permute-start(bf16[128,1152]{1,0:T(8,128)(2,1)S(1)} %get-tuple-element.78), channel_id=1, source_target_pairs={{1,17},{3,19},{5,21},{7,23},{9,25},{11,27},{13,29},{15,31},{16,0},... | collective-permute-start | bytes 884744 | tf_op jit(solution)/shard_map/ppermute | solution.py:443
  71.1 2.3 %collective-permute-start.26 = (bf16[64,1152]{1,0:T(8,128)(2,1)S(1)}, bf16[64,1152]{1,0:T(8,128)(2,1)S(1)}, u32[]{:S(2)}, u32[]{:S(2)}) collective-permute-start(bf16[64,1152]{1,0:T(8,128)(2,1)S(1)} %slice.29), channel_id=1, source_target_pairs={{0,1},{2,3},{4,5},{6,7},{8,9},{10,11},{12,13},{14,15},{17,16},{19,... | collective-permute-start | bytes 442376 | tf_op jit(solution)/shard_map/ppermute | solution.py:446
  72.4 26.3 %collective-permute-start.42 = (bf16[160,3456]{1,0:T(8,128)(2,1)}, bf16[160,3456]{1,0:T(8,128)(2,1)}, u32[]{:S(2)}, u32[]{:S(2)}) collective-permute-start(bf16[160,3456]{1,0:T(8,128)(2,1)} %features.6), channel_id=1, source_target_pairs={{0,16},{1,17},{2,18},{3,19},{4,20},{5,21},{6,22},{7,23},{8,24},{9,... | collective-permute-start | bytes 3317768 | tf_op jit(solution)/shard_map/ppermute | solution.py:444
  73.4 10.3 %collective-permute-start.30 = (bf16[1,64,1152]{2,1,0:T(8,128)(2,1)S(1)}, bf16[1,64,1152]{2,1,0:T(8,128)(2,1)S(1)}, u32[]{:S(2)}, u32[]{:S(2)}) collective-permute-start(bf16[1,64,1152]{2,1,0:T(8,128)(2,1)S(1)} %bitcast.56), channel_id=1, source_target_pairs={{0,8},{1,9},{2,10},{3,11},{4,12},{5,13},{6,14},{7,15},{8,0},{9,1},... | collective-permute-start | bytes 442376 | tf_op jit(solution)/shard_map/ppermute | solution.py:373
  75.1 9.2 %collective-permute-start.27 = (bf16[1,64,1152]{2,1,0:T(8,128)(2,1)S(1)}, bf16[1,64,1152]{2,1,0:T(8,128)(2,1)S(1)}, u32[]{:S(2)}, u32[]{:S(2)}) collective-permute-start(bf16[1,64,1152]{2,1,0:T(8,128)(2,1)S(1)} %bitcast.57), channel_id=1, source_target_pairs={{0,2},{1,5},{2,0},{3,7},{4,6},{5,1},{6,4},{7,3},{8,10},{9,13},{10,... | collective-permute-start | bytes 442376 | tf_op jit(solution)/shard_map/ppermute | solution.py:376
  76.6 8.3 %collective-permute-start.28 = (bf16[1,64,1152]{2,1,0:T(8,128)(2,1)S(1)}, bf16[1,64,1152]{2,1,0:T(8,128)(2,1)S(1)}, u32[]{:S(2)}, u32[]{:S(2)}) collective-permute-start(bf16[1,64,1152]{2,1,0:T(8,128)(2,1)S(1)} %bitcast.58), channel_id=1, source_target_pairs={{0,4},{1,3},{2,6},{3,1},{4,0},{5,7},{6,2},{7,5},{8,12},{9,11},{10,... | collective-permute-start | bytes 442376 | tf_op jit(solution)/shard_map/ppermute | solution.py:376
  80.7 4.2 %collective-permute-start.34 = (bf16[1,64,1152]{2,1,0:T(8,128)(2,1)S(1)}, bf16[1,64,1152]{2,1,0:T(8,128)(2,1)S(1)}, u32[]{:S(2)}, u32[]{:S(2)}) collective-permute-start(bf16[1,64,1152]{2,1,0:T(8,128)(2,1)S(1)} %bitcast.59), channel_id=1, source_target_pairs={{0,1},{1,0},{2,3},{3,2},{4,5},{5,4},{6,7},{7,6},{8,9},{9,8},{10,11... | collective-permute-start | bytes 442376 | tf_op jit(solution)/shard_map/ppermute | solution.py:379
  83.8 6.5 %collective-permute-start.31 = (bf16[1,64,1152]{2,1,0:T(8,128)(2,1)S(1)}, bf16[1,64,1152]{2,1,0:T(8,128)(2,1)}, u32[]{:S(2)}, u32[]{:S(2)}) collective-permute-start(bf16[1,64,1152]{2,1,0:T(8,128)(2,1)S(1)} %collective-permute-done.30), channel_id=1, source_target_pairs={{0,2},{1,5},{2,0},{3,7},{4,6},{5,1},{6,4},{7,3},{8,10},{9,13},{10,... | collective-permute-start | bytes 442376 | tf_op jit(solution)/shard_map/ppermute | solution.py:376
  84.3 6.0 %collective-permute-start.32 = (bf16[1,64,1152]{2,1,0:T(8,128)(2,1)S(1)}, bf16[1,64,1152]{2,1,0:T(8,128)(2,1)S(1)}, u32[]{:S(2)}, u32[]{:S(2)}) collective-permute-start(bf16[1,64,1152]{2,1,0:T(8,128)(2,1)S(1)} %collective-permute-done.30), channel_id=1, source_target_pairs={{0,4},{1,3},{2,6},{3,1},{4,0},{5,7},{6,2},{7,5},{8,12},{9,11},{10,... | collective-permute-start | bytes 442376 | tf_op jit(solution)/shard_map/ppermute | solution.py:376
  84.9 5.9 %collective-permute-start.38 = (bf16[1,64,1152]{2,1,0:T(8,128)(2,1)S(1)}, bf16[1,64,1152]{2,1,0:T(8,128)(2,1)S(1)}, u32[]{:S(2)}, u32[]{:S(2)}) collective-permute-start(bf16[1,64,1152]{2,1,0:T(8,128)(2,1)S(1)} %collective-permute-done.30), channel_id=1, source_target_pairs={{0,1},{1,0},{2,3},{3,2},{4,5},{5,4},{6,7},{7,6},{8,9},{9,8},{10,11... | collective-permute-start | bytes 442376 | tf_op jit(solution)/shard_map/ppermute | solution.py:379
  85.6 9.9 %collective-permute-start.29 = (bf16[1,64,1152]{2,1,0:T(8,128)(2,1)S(1)}, bf16[1,64,1152]{2,1,0:T(8,128)(2,1)}, u32[]{:S(2)}, u32[]{:S(2)}) collective-permute-start(bf16[1,64,1152]{2,1,0:T(8,128)(2,1)S(1)} %collective-permute-done.27), channel_id=1, source_target_pairs={{0,4},{1,3},{2,6},{3,1},{4,0},{5,7},{6,2},{7,5},{8,12},{9,11},{10,... | collective-permute-start | bytes 442376 | tf_op jit(solution)/shard_map/ppermute | solution.py:376
  90.3 6.3 %collective-permute-start.36 = (bf16[1,64,1152]{2,1,0:T(8,128)(2,1)S(1)}, bf16[1,64,1152]{2,1,0:T(8,128)(2,1)}, u32[]{:S(2)}, u32[]{:S(2)}) collective-permute-start(bf16[1,64,1152]{2,1,0:T(8,128)(2,1)S(1)} %collective-permute-done.27), channel_id=1, source_target_pairs={{0,1},{1,0},{2,3},{3,2},{4,5},{5,4},{6,7},{7,6},{8,9},{9,8},{10,11... | collective-permute-start | bytes 442376 | tf_op jit(solution)/shard_map/ppermute | solution.py:379
  90.3 6.2 %collective-permute-start.35 = (bf16[1,64,1152]{2,1,0:T(8,128)(2,1)S(1)}, bf16[1,64,1152]{2,1,0:T(8,128)(2,1)}, u32[]{:S(2)}, u32[]{:S(2)}) collective-permute-start(bf16[1,64,1152]{2,1,0:T(8,128)(2,1)S(1)} %collective-permute-done.28), channel_id=1, source_target_pairs={{0,1},{1,0},{2,3},{3,2},{4,5},{5,4},{6,7},{7,6},{8,9},{9,8},{10,11... | collective-permute-start | bytes 442376 | tf_op jit(solution)/shard_map/ppermute | solution.py:379
  91.6 5.5 %collective-permute-start.33 = (bf16[1,64,1152]{2,1,0:T(8,128)(2,1)}, bf16[1,64,1152]{2,1,0:T(8,128)(2,1)}, u32[]{:S(2)}, u32[]{:S(2)}) collective-permute-start(bf16[1,64,1152]{2,1,0:T(8,128)(2,1)} %collective-permute-done.31), channel_id=1, source_target_pairs={{0,4},{1,3},{2,6},{3,1},{4,0},{5,7},{6,2},{7,5},{8,12},{9,11},{10,... | collective-permute-start | bytes 442376 | tf_op jit(solution)/shard_map/ppermute | solution.py:376
  95.5 2.6 %collective-permute-start.40 = (bf16[1,64,1152]{2,1,0:T(8,128)(2,1)}, bf16[1,64,1152]{2,1,0:T(8,128)(2,1)S(1)}, u32[]{:S(2)}, u32[]{:S(2)}) collective-permute-start(bf16[1,64,1152]{2,1,0:T(8,128)(2,1)} %collective-permute-done.31), channel_id=1, source_target_pairs={{0,1},{1,0},{2,3},{3,2},{4,5},{5,4},{6,7},{7,6},{8,9},{9,8},{10,11... | collective-permute-start | bytes 442376 | tf_op jit(solution)/shard_map/ppermute | solution.py:379
  96.5 1.6 %collective-permute-start.39 = (bf16[1,64,1152]{2,1,0:T(8,128)(2,1)}, bf16[1,64,1152]{2,1,0:T(8,128)(2,1)S(1)}, u32[]{:S(2)}, u32[]{:S(2)}) collective-permute-start(bf16[1,64,1152]{2,1,0:T(8,128)(2,1)} %copy-done.3), channel_id=1, source_target_pairs={{0,1},{1,0},{2,3},{3,2},{4,5},{5,4},{6,7},{7,6},{8,9},{9,8},{10,11... | collective-permute-start | bytes 442376 | tf_op jit(solution)/shard_map/ppermute | solution.py:379
  96.6 1.7 %collective-permute-start.37 = (bf16[1,64,1152]{2,1,0:T(8,128)(2,1)}, bf16[1,64,1152]{2,1,0:T(8,128)(2,1)S(1)}, u32[]{:S(2)}, u32[]{:S(2)}) collective-permute-start(bf16[1,64,1152]{2,1,0:T(8,128)(2,1)} %collective-permute-done.29), channel_id=1, source_target_pairs={{0,1},{1,0},{2,3},{3,2},{4,5},{5,4},{6,7},{7,6},{8,9},{9,8},{10,11... | collective-permute-start | bytes 442376 | tf_op jit(solution)/shard_map/ppermute | solution.py:379
  97.1 1.6 %collective-permute-start.41 = (bf16[1,64,1152]{2,1,0:T(8,128)(2,1)}, bf16[1,64,1152]{2,1,0:T(8,128)(2,1)S(1)}, u32[]{:S(2)}, u32[]{:S(2)}) collective-permute-start(bf16[1,64,1152]{2,1,0:T(8,128)(2,1)} %collective-permute-done.33), channel_id=1, source_target_pairs={{0,1},{1,0},{2,3},{3,2},{4,5},{5,4},{6,7},{7,6},{8,9},{9,8},{10,11... | collective-permute-start | bytes 442376 | tf_op jit(solution)/shard_map/ppermute | solution.py:379
  106.2 4.6 %collective-permute-start.43 = (bf16[2,160,128]{2,1,0:T(8,128)(2,1)S(1)}, bf16[2,160,128]{2,1,0:T(8,128)(2,1)S(1)}, u32[]{:S(2)}, u32[]{:S(2)}) collective-permute-start(bf16[2,160,128]{2,1,0:T(8,128)(2,1)S(1)} %pad_maximum_fusion), channel_id=1, source_target_pairs={{0,16},{1,17},{2,18},{3,19},{4,20},{5,21},{6,22},{7,23},{8,24},{9,... | collective-permute-start | bytes 245768 | tf_op jit(solution)/shard_map/ppermute | solution.py:462
  111.1 1.2 collective-permute-start.44
  112.3 3.6 %collective-permute-start.45 = (f32[2,1,4]{2,1,0:T(1,128)S(1)}, f32[2,1,4]{2,1,0:T(1,128)S(1)}, u32[]{:S(2)}, u32[]{:S(2)}) collective-permute-start(f32[2,1,4]{2,1,0:T(1,128)S(1)} %pad_maximum_fusion.3), channel_id=1, source_target_pairs={{0,2},{1,3},{2,0},{3,1},{4,6},{5,7},{6,4},{7,5},{8,10},{9,11},{10,... | collective-permute-start | bytes 104 | tf_op jit(solution)/shard_map/ppermute | solution.py:472
  115.8 3.6 %collective-permute-start.46 = (f32[4,1,4]{2,1,0:T(1,128)S(1)}, f32[4,1,4]{2,1,0:T(1,128)S(1)}, u32[]{:S(2)}, u32[]{:S(2)}) collective-permute-start(f32[4,1,4]{2,1,0:T(1,128)S(1)} %pad_maximum_fusion.2), channel_id=1, source_target_pairs={{0,4},{1,5},{2,6},{3,7},{4,0},{5,1},{6,2},{7,3},{8,12},{9,13},{10,... | collective-permute-start | bytes 200 | tf_op jit(solution)/shard_map/ppermute | solution.py:472
  119.4 4.6 %collective-permute-start.47 = (f32[8,1,4]{2,1,0:T(1,128)S(1)}, f32[8,1,4]{2,1,0:T(1,128)S(1)}, u32[]{:S(2)}, u32[]{:S(2)}) collective-permute-start(f32[8,1,4]{2,1,0:T(1,128)S(1)} %pad_maximum_fusion.1), channel_id=1, source_target_pairs={{0,8},{1,9},{2,10},{3,11},{4,12},{5,13},{6,14},{7,15},{8,0},{9,1},... | collective-permute-start | bytes 392 | tf_op jit(solution)/shard_map/ppermute | solution.py:472
  (14 other events, 80.6 us)

commit v4 on v3

--- a/solution.py
+++ b/solution.py
@@ -9,7 +9,7 @@
 EVERYONE = ("parts", "blk")
 NEAR = 4
 CHAINS = 2
-SHARES = (2, 3, 3)
+SHARES = (3, 2, 3)
 MIB = 1024 * 1024
 
 
@@ -116,22 +116,14 @@
     return [outs[chain * NEAR : (chain + 1) * NEAR] for chain in range(CHAINS)]
 
 
-def chunk_copies(number, bases, targets, widths, rows, sems):
-    copies = []
-    for num, (basis, target, width, (begin, end)) in enumerate(zip(bases, targets, widths, rows)):
-        if end > begin:
-            source = basis.at[pl.ds(begin, end - begin), lanes_at(number, width)]
-            copies.append(pltpu.make_async_copy(source, target, sems.at[num]))
-    return copies
-
-
 def stage_bases(part, bases):
-    widths = [basis.shape[1] // (2 * CHAINS) for basis in bases]
-    rows = [(0, basis.shape[0]) for basis in bases]
+    widths = [basis.shape[1] // 2 for basis in bases]
 
     def kernel(where, first, second, first_out, second_out, sems):
-        number = where[0] * CHAINS + CHAINS - 1
-        copy_all(chunk_copies(number, (first, second), (first_out, second_out), widths, rows, sems))
+        copies = []
+        for num, (basis, out, shape) in enumerate(((first, first_out, shapes[0]), (second, second_out, shapes[1]))):
+            copies.append(pltpu.make_async_copy(basis.at[:, lanes_at(where[0], shape[1])], out, sems.at[num]))
+        copy_all(copies)
 
     shapes = [(basis.shape[0], width) for basis, width in zip(bases, widths)]
     return pl.pallas_call(
@@ -214,50 +206,31 @@
     )(jnp.concatenate([part[None], chip_at]), in_hbm(acts), in_hbm(grads))
 
 
-def rotate(part, chunks, chain, factors, bases, rows, total):
+def rotate(chunks, chain, own, sib, bases, total):
     last = chain == CHAINS - 1
-    ranks, wide = factors[0].shape
-    wide_in = bases[0].shape[1] // NEAR if last else bases[0].shape[1] // (2 * CHAINS * NEAR)
+    ranks, wide = own[0].shape
+    wide_in = bases[0].shape[1] // (CHAINS * NEAR)
     widths = (wide_in, wide - wide_in)
-    counts = [end - begin for begin, end in rows]
-    height = sum(counts)
-    spans = [(0, counts[0], 0, wide_in), (counts[0], height, wide_in, wide)]
+    rows_in = bases[0].shape[0]
+    height = rows_in + bases[1].shape[0]
+    spans = ((0, rows_in, 0, wide_in), (rows_in, height, wide_in, wide))
 
     def kernel(where, *rest):
-        own, sib, (basis_in, basis_out), rest = rest[:NEAR], rest[NEAR : 2 * NEAR], rest[2 * NEAR :][:2], rest[2 * NEAR + 2 :]
+        own_here, sib_here, bases_here, rest = rest[:NEAR], rest[NEAR : 2 * NEAR], rest[2 * NEAR :][:2], rest[2 * NEAR + 2 :]
         if total is not None:
             start, rest = rest[0], rest[1:]
-        if last:
-            outs, acc = rest[:-1], rest[-1]
-        else:
-            outs, (buf_in, buf_out, acc, sems) = rest[:-4], rest[-4:]
-            copies = []
-            for spot in range(NEAR):
-                number = (where[0] * CHAINS + chain) * NEAR + where[1 + spot]
-                targets = (buf_in.at[spot], buf_out.at[spot])
-                copies.append(
-                    chunk_copies(number, (basis_in, basis_out), targets, widths, rows, sems.at[spot])
-                )
-                for copy in copies[spot]:
-                    copy.start()
+        outs, acc = rest[:-1], rest[-1]
         for spot in range(NEAR):
-            factor = jnp.concatenate([own[spot][...], sib[SIBLING[spot]][...]], axis=0)
-            if not last:
-                for copy in copies[spot]:
-                    copy.wait()
+            factor = jnp.concatenate([own_here[spot][...], sib_here[SIBLING[spot]][...]], axis=0)
             for num, (from_row, to_row, from_lane, to_lane) in enumerate(spans):
-                if to_row == from_row:
-                    continue
-                if last:
-                    basis = (basis_in, basis_out)[num]
-                    block = basis[rows[num][0] : rows[num][1], lanes_at(where[1 + spot], widths[num])]
-                else:
-                    block = (buf_in, buf_out)[num][spot]
+                block = bases_here[num][:, lanes_at(chain * NEAR + where[spot], widths[num])]
                 value = dot_rows(block, factor[:, from_lane:to_lane])
-                acc[from_row:to_row] = value if spot == 0 else acc[from_row:to_row] + value
+                if spot:
+                    value = value + acc[from_row:to_row]
+                elif total is not None:
+                    value = value + start[from_row:to_row]
+                acc[from_row:to_row] = value
         value = acc[...]
-        if total is not None:
-            value = value + start[...]
         if last:
             value = value.T
             outs[1][...] = value.astype(jnp.bfloat16)
@@ -265,27 +238,20 @@
 
     if last:
         shapes = [jax.ShapeDtypeStruct((2 * ranks, height), kind) for kind in (jnp.float32, jnp.bfloat16)]
-        scratch = []
-        place, operands = VMEM, map(in_vmem, bases)
     else:
         shapes = [jax.ShapeDtypeStruct((height, 2 * ranks), jnp.float32)]
-        scratch = [pltpu.VMEM((NEAR, count, width), jnp.bfloat16) for count, width in zip(counts, widths)]
-        place, operands = HBM, map(in_hbm, bases)
-    scratch.append(pltpu.VMEM((height, 2 * ranks), jnp.float32))
-    if not last:
-        scratch.append(pltpu.SemaphoreType.DMA((NEAR, 2)))
     given = [] if total is None else [total]
-    moved = sum(count * width for count, width in zip(counts, widths))
+    moved = sum((to_row - from_row) * (to_lane - from_lane) for from_row, to_row, from_lane, to_lane in spans)
     results = pl.pallas_call(
         kernel,
-        in_specs=[SMEM] + [VMEM] * (2 * NEAR) + [place] * 2 + [VMEM] * len(given),
+        in_specs=[SMEM] + [VMEM] * (2 * NEAR + 2 + len(given)),
         out_specs=[VMEM] * len(shapes),
         out_shape=shapes,
-        scratch_shapes=scratch,
-        compiler_params=pltpu.CompilerParams(vmem_limit_bytes=(4 if last else 12) * MIB),
+        scratch_shapes=[pltpu.VMEM((height, 2 * ranks), jnp.float32)],
+        compiler_params=pltpu.CompilerParams(vmem_limit_bytes=4 * MIB),
         cost_estimate=estimate(4 * ranks * NEAR * moved, 2 * NEAR * moved),
         name="rotate",
-    )(jnp.concatenate([part[None], chunks]), *factors, *operands, *given)
+    )(chunks, *own, *sib, *map(in_vmem, bases), *given)
     return tuple(results) if last else results[0]
 
 
@@ -302,44 +268,85 @@
             )
             for lanes in (slice(0, wide_in), slice(wide_in, wide))
         ]
-    staged = len(tokens_in) == 1
 
     def kernel(*rest):
         factors, rest = rest[: 2 * chips], rest[2 * chips :]
         held, rest = rest[: len(tokens_in)], rest[len(tokens_in) :]
         outs, acc = rest[:2], rest[2]
-        if not staged:
-            buffer, sems = rest[3:]
-            copies = []
-            for source, (first, last) in zip(held, pieces):
-                for spot in range(first, last):
-                    block = source.at[:, pl.ds((spot - first) * wide, wide)]
-                    copies.append(pltpu.make_async_copy(block, buffer.at[spot], sems.at[spot]))
-                    copies[-1].start()
-        for spot in range(chips):
-            factor = jnp.concatenate([factors[spot][...], factors[chips + spot][...]], axis=0)
-            if not staged:
-                copies[spot].wait()
-            for num, (begin, end) in enumerate(((0, wide_in), (wide_in, wide))):
-                block = held[0][:, spot * wide + begin : spot * wide + end] if staged else buffer[spot, :, begin:end]
-                value = dot_rows(block, factor[:, begin:end])
-                acc[num] = value if spot == 0 else acc[num] + value
+        for source, (first, last) in zip(held, pieces):
+            for spot in range(first, last):
+                factor = jnp.concatenate([factors[spot][...], factors[chips + spot][...]], axis=0)
+                for num, (begin, end) in enumerate(((0, wide_in), (wide_in, wide))):
+                    base = (spot - first) * wide
+                    value = dot_rows(source[:, base + begin : base + end], factor[:, begin:end])
+                    acc[num] = value if spot == 0 else acc[num] + value
         for num, out in enumerate(outs):
             out[...] = acc[num].astype(kind)
 
-    scratch = [pltpu.VMEM((2, tokens, 2 * ranks), jnp.float32)]
-    if not staged:
-        scratch += [pltpu.VMEM((chips, tokens, wide), own[0].dtype), pltpu.SemaphoreType.DMA((chips,))]
-    return pl.pallas_call(
-        kernel,
-        in_specs=[VMEM] * (2 * chips) + [VMEM if staged else HBM] * len(tokens_in),
+    return pl.pallas_call(
+        kernel,
+        in_specs=[VMEM] * (2 * chips + len(tokens_in)),
         out_specs=[VMEM] * 2,
         out_shape=[jax.ShapeDtypeStruct((tokens, 2 * ranks), kind)] * 2,
-        scratch_shapes=scratch,
-        compiler_params=pltpu.CompilerParams(vmem_limit_bytes=(4 if staged else 8) * MIB),
+        scratch_shapes=[pltpu.VMEM((2, tokens, 2 * ranks), jnp.float32)],
+        compiler_params=pltpu.CompilerParams(vmem_limit_bytes=4 * MIB),
         cost_estimate=estimate(4 * tokens * ranks * chips * wide, 4 * ranks * chips * wide),
         name="project",
-    )(*own, *sib, *map(in_vmem if staged else in_hbm, tokens_in))
+    )(*own, *sib, *map(in_vmem, tokens_in))
+
+
+def score(me, lengths, slot_plan, mine, back, queries, rank_count):
+    tokens, columns = mine[0].shape
+    half_rank = rank_count // 2
+    lanes = slot_plan.shape[0] * queries
+
+    def kernel(where, lengths, slot_plan, mine_in, mine_out, back, out):
+        live = lax.broadcasted_iota(jnp.int32, (tokens, columns), 0) < lengths[slot_plan[where[0]]]
+        products = (mine_in[...] + back[0].astype(jnp.float32)) * (mine_out[...] + back[1].astype(jnp.float32))
+        sums = jnp.sum(jnp.where(live, products, 0.0), axis=0, keepdims=True)
+        query_of = lax.broadcasted_iota(jnp.int32, (1, columns), 1) % (queries * half_rank) // half_rank
+        lane = lax.broadcasted_iota(jnp.int32, (1, lanes), 1)
+        row = jnp.zeros((1, lanes), jnp.float32)
+        for query in range(queries):
+            value = jnp.sum(jnp.where(query_of == query, sums, 0.0), axis=1, keepdims=True) / rank_count
+            row = jnp.where(lane == where[0] * queries + query, value, row)
+        out[...] = row
+
+    return pl.pallas_call(
+        kernel,
+        in_specs=[SMEM] * 3 + [VMEM] * 3,
+        out_specs=VMEM,
+        out_shape=jax.ShapeDtypeStruct((1, lanes), jnp.float32),
+        compiler_params=pltpu.CompilerParams(vmem_limit_bytes=4 * MIB),
+        cost_estimate=estimate(6 * tokens * columns, 12 * tokens * columns),
+        name="score",
+    )(me[None], lengths, slot_plan, *mine, back)
+
+
+def own_sequence(me, slot_plan, held, queries):
+    slots = slot_plan.shape[0]
+
+    def kernel(where, slot_plan, held, out):
+        slot = jnp.int32(0)
+        for number in range(slots):
+            slot = jnp.where(slot_plan[number] == where[0], number, slot)
+        lane = lax.broadcasted_iota(jnp.int32, held.shape, 1)
+        out_lane = lax.broadcasted_iota(jnp.int32, (1, queries), 1)
+        row = jnp.zeros((1, queries), jnp.float32)
+        for query in range(queries):
+            value = jnp.sum(jnp.where(lane == slot * queries + query, held[...], 0.0), axis=1, keepdims=True)
+            row = jnp.where(out_lane == query, value, row)
+        out[...] = row
+
+    return pl.pallas_call(
+        kernel,
+        in_specs=[SMEM] * 2 + [VMEM],
+        out_specs=VMEM,
+        out_shape=jax.ShapeDtypeStruct((1, queries), jnp.float32),
+        compiler_params=pltpu.CompilerParams(vmem_limit_bytes=4 * MIB),
+        cost_estimate=estimate(0, 4 * held.size),
+        name="own_sequence",
+    )(me[None], slot_plan, held)
 
 
 def shards(
@@ -412,35 +419,34 @@
         if chain:
             found[chain] = after(found[chain], dense[chain - 1])
         dense.append(choose(spot, found[chain]))
-    bases = stage_bases(part, after((basis_in, basis_out), dense[0]))
+        if chain == 0:
+            second = give_away(1, dense[0])
+            found[1][0], second = lax.optimization_barrier((found[1][0], second))
+    others = [others[0], lax.ppermute(second, EVERYONE, across)]
+    bases = stage_bases(part, after((basis_in, basis_out), dense[-1]))
     for bit in range(bits - 1, 1, -1):
         arrived = [to_chip(dense[chain], 1 << bit) for chain in every]
+        if bit == bits - 1:
+            others[0], arrived[0], *bases = lax.optimization_barrier((others[0], arrived[0], *bases))
         for chain in every:
             if chain:
                 (arrived[chain],) = after((arrived[chain],), dense[chain - 1])
             dense[chain] = dense[chain] + arrived[chain]
-    others.append(lax.ppermute(give_away(1, bases[0]), EVERYONE, across))
-    others[0], dense[0], *bases = lax.optimization_barrier((others[0], dense[0], *bases))
-    gathered = []
+    total = None
     for chain in every:
         own = near_gather(dense[chain][0])
         if chain:
-            own[1:3] = after(own[1:3], gathered[0][0][1])
-        if chain == CHAINS - 1:
-            own[3], others[1] = lax.optimization_barrier((own[3], others[1]))
-        gathered.append((own, [to_core(value) for value in own]))
-
-    rows_in, rows_out = basis_in.shape[0], basis_out.shape[0]
-    rows = ((0, rows_in), (0, rows_out))
-    total = None
-    for chain in range(CHAINS - 1):
-        total = rotate(part, near_at, chain, sum(gathered[chain], []), (basis_in, basis_out), rows, total)
-    partial, sent = rotate(part, near_at, CHAINS - 1, sum(gathered[-1], []), bases, rows, total)
+            own[1:3] = after(own[1:3], first)
+            (own[3],) = after((own[3],), total)
+        first = own[1]
+        total = rotate(near_at, chain, own, [to_core(value) for value in own], bases, total)
+
+    partial, sent = total
     to_sum = [(p * count + i, (1 - p) * count + i) for p in range(2) for i in range(count) if i % 2 != p]
     to_half = [(p * count + i, p * count + (i ^ 1)) for p in range(2) for i in range(count) if i % 2 == p]
     own_tokens = features_of(part, chip_at, *after((acts, grads), sent), [(0, chips)])
     last_piece = give_away(2, sent)
-    arrived, last_piece = lax.optimization_barrier((lax.ppermute(sent, EVERYONE, to_sum), last_piece))
+    arrived, others[1], last_piece = lax.optimization_barrier((lax.ppermute(sent, EVERYONE, to_sum), others[1], last_piece))
     others.append(lax.ppermute(last_piece, EVERYONE, across))
     summed = (partial + arrived.astype(jnp.float32)).astype(jnp.bfloat16)
     given = lax.ppermute(summed[ranks:], EVERYONE, to_half)
@@ -458,22 +464,14 @@
             own += [group[step][entry] for entry in range(source.shape[0])]
             sib += [swapped[SIBLING[step]][entry] for entry in range(source.shape[0])]
 
-    theirs = project(own, sib, rows_in, others, pieces, jnp.bfloat16)
-    back = lax.ppermute(jnp.stack(theirs), EVERYONE, across).astype(jnp.float32)
-    mine = project(own, sib, rows_in, own_tokens, [(0, chips)], jnp.float32)
-    mine_in, mine_out = mine[0] + back[0], mine[1] + back[1]
-    seqs = me * seqs_here + jnp.arange(seqs_here, dtype=jnp.int32)
-    live = jnp.arange(max_length, dtype=jnp.int32)[None, :] < lengths[slot_plan[seqs]][:, None]
-    products = (mine_in * mine_out).reshape(seqs_here, max_length, -1)
-    sums = jnp.sum(jnp.where(live[:, :, None], products, 0.0), axis=1)
-    held = (jnp.sum(sums.reshape(seqs_here, 2, num_queries, half_rank), axis=(1, 3)) / rank_count)[None]
+    theirs = project(own, sib, basis_in.shape[0], others, pieces, jnp.bfloat16)
+    back = lax.ppermute(jnp.stack(theirs), EVERYONE, across)
+    mine = project(own, sib, basis_in.shape[0], own_tokens, [(0, chips)], jnp.float32)
+
+    held = score(me, lengths, slot_plan, mine, back, num_queries, rank_count)
     for bit in range(bits + 1):
-        pairs = [(i, i ^ (1 << bit)) for i in range(count)]
-        held = jnp.concatenate([held, lax.ppermute(held, "blk", pairs)], axis=0)
-    from_device = jnp.arange(count, dtype=jnp.int32) ^ me
-    planned = slot_plan.reshape(count, seqs_here)[from_device]
-    chooser = planned[None, :, :] == seqs[:, None, None]
-    return jnp.sum(jnp.where(chooser[..., None], held[None], 0.0), axis=(1, 2))
+        held = held + lax.ppermute(held, "blk", [(i, i ^ (1 << bit)) for i in range(count)])
+    return own_sequence(me, slot_plan, held, num_queries)
 
 
 def solution(mesh):

time: 125 us -> 111 us (0.89)
  local copies, waits for them, and re-layouts: 7.68 us -> 0.73 us
  Pallas kernels: 30.7 us -> 25.6 us
  starting transfers between devices: 40.2 us -> 43 us
  waiting for transfers between devices: 42 us -> 39.7 us
  between operations: 2.24 us -> 0.31 us
    pallas_call x4 -> x6, Pallas kernels: 15.1 us -> 8.98 us  [the longest x2 5.21 us: rotate(): pl.pallas_call(kernel, in_specs=[SMEM] + [VMEM] * (2 * NEAR + 2 + len(giv...]
    unnamed x28 -> x14, local copies, waits for them, and re-layouts: 5.11 us -> 0.72 us
    ppermute x6, waiting for transfers between devices: 15.5 us -> 12.1 us  [the longest x4 8.34 us: shards(): lax.ppermute(held, 'blk', [(i, i ^ 1 << bit) for i in range(count)])]
    ppermute x1, waiting for transfers between devices: 0.01 us -> 2.94 us  [shards(): others = [lax.ppermute(give_away(0, messages[0][0]), EVERYONE, across)]]
    pallas_call x1, Pallas kernels: 3.03 us -> 5.1 us  [stage_bases(): pl.pallas_call(kernel, in_specs=[SMEM, HBM, HBM], out_specs=[VMEM] * 2, o...]
    gather x3 -> x0, local copies, waits for them, and re-layouts: 1.92 us -> none  [the longest x1 0.66 us: shards(): planned = slot_plan.reshape(count, seqs_here)[from_device]]
    ppermute x9, waiting for transfers between devices: 6.46 us -> 4.73 us  [to_chip(): return lax.ppermute(value, 'blk', [(i, i ^ 2 * mask) for i in range(count)])]
    ppermute x17, waiting for transfers between devices: 2.8 us -> 4.19 us  [to_core(): return lax.ppermute(value, 'blk', [(i, i ^ 1) for i in range(count)])]
  transfers between devices with their start and end apart: 48 -> 48, of which waited for: 22 -> 23; matrix products, arithmetic and copies ran while one was open for 3% -> 1% of each run, Pallas kernels for 17% -> 17%
where the time goes in v4:
time: 111 us
  starting transfers between devices  43 us (39%)
  waiting for transfers between devices  39.7 us (36%)
  Pallas kernels  25.6 us (23%)
  other arithmetic  1.26 us (1%)
    ppermute x9, starting transfers between devices, to_chip(): return lax.ppermute(value, 'blk', [(i, i ^ 2 * mask) for i in range(count)])  14.6 us
    ppermute x12, starting transfers between devices, along(): lax.ppermute(value, 'blk', [(i, i ^ 2 << (second if i % 2 else first)) fo...  11.7 us
    ppermute x12, waiting for transfers between devices, along(): lax.ppermute(value, 'blk', [(i, i ^ 2 << (second if i % 2 else first)) fo...  11.4 us
    ppermute x4, waiting for transfers between devices, shards(): lax.ppermute(held, 'blk', [(i, i ^ 1 << bit) for i in range(count)])  8.34 us
    pallas_call x4, Pallas kernels, features_of(): pl.pallas_call(kernel, in_specs=[SMEM, HBM, HBM], out_specs=[VMEM] * len(...  7.91 us
    pallas_call x2, Pallas kernels, rotate(): pl.pallas_call(kernel, in_specs=[SMEM] + [VMEM] * (2 * NEAR + 2 + len(giv...  5.21 us
    pallas_call x1, Pallas kernels, stage_bases(): pl.pallas_call(kernel, in_specs=[SMEM, HBM, HBM], out_specs=[VMEM] * 2, o...  5.1 us
    ppermute x9, waiting for transfers between devices, to_chip(): return lax.ppermute(value, 'blk', [(i, i ^ 2 * mask) for i in range(count)])  4.73 us
  transfers between devices with their start and end apart: 48, of which 23 were waited for; matrix products, arithmetic and copies ran while one was open for 1% of the time, Pallas kernels for 17%

profile of v4, /device:TPU:0, one launch (start us, length us, event | category | flops | bytes accessed | tf_op | source)
XLA Modules:
  0.0 110.6 jit_solution(9449251504798594851)
XLA Ops:
  0.1 1.9 %rank_halves.1 = (bf16[4,2,16,1152]{3,2,1,0:T(8,128)(2,1)S(1)}, bf16[4,2,16,1152]{3,2,1,0:T(8,128)(2,1)S(1)}) custom-call(s32[2]{0:T(128)S(1)} %pad_add_fusion.where, bf16[1,32,4096]{2,1,0:T(8,128)(2,1)} %left.1, bf16[1,32,14336]{2,1,0:T(8,128)(2,1)} %right.1), custom_call_target="tpu_custom_call" | custom-call | bytes 1179648 | tf_op jit(solution)/shard_map/rank_halves/pallas_call | solution.py:86
  2.6 1.1 %collective-permute-done.received = bf16[4,2,16,1152]{3,2,1,0:T(8,128)(2,1)S(1)} collective-permute-done((bf16[4,2,16,1152]{3,2,1,0:T(8,128)(2,1)S(1)}, bf16[4,2,16,1152]{3,2,1,0:T(8,128)(2,1)S(1)}, u32[]{:S(2)}, u32[]{:S(2)}) %collective-permute-start) | collective-permute-done | bytes 294944 | tf_op jit(solution)/shard_map/ppermute | solution.py:386
  3.8 1.8 %features.5 = bf16[160,3456]{1,0:T(8,128)(2,1)S(1)} custom-call(s32[9]{0:T(128)S(1)} %get-tuple-element.96.where, bf16[160,4096]{1,0:T(8,128)(2,1)} %bitcast.72, bf16[160,14336]{1,0:T(8,128)(2,1)} %bitcast.68), custom_call_target="tpu_custom_call" | custom-call | bytes 2211840 | tf_op jit(solution)/shard_map/features/pallas_call | solution.py:197
  5.7 2.9 %collective-permute-start.8 = (bf16[160,3456]{1,0:T(8,128)(2,1)S(1)}, bf16[160,3456]{1,0:T(8,128)(2,1)S(1)}, u32[]{:S(2)}, u32[]{:S(2)}) collective-permute-start(bf16[160,3456]{1,0:T(8,128)(2,1)S(1)} %features.5), channel_id=1, source_target_pairs={{0,16},{1,17},{2,18},{3,19},{4,20},{5,21},{6,22},{7,23},{8,24},{9,... | collective-permute-start | bytes 3317768 | tf_op jit(solution)/shard_map/ppermute | solution.py:411
  8.6 1.5 %collective-permute-start.1 = (bf16[2,16,1152]{2,1,0:T(8,128)(2,1)S(1)}, bf16[2,16,1152]{2,1,0:T(8,128)(2,1)S(1)}, u32[]{:S(2)}, u32[]{:S(2)}) collective-permute-start(bf16[2,16,1152]{2,1,0:T(8,128)(2,1)S(1)} %get-tuple-element.54), channel_id=1, source_target_pairs={{0,2},{1,3},{2,0},{3,1},{4,6},{5,7},{6,4},{7,5},{8,10},{9,11},{10,... | collective-permute-start | bytes 221192 | tf_op jit(solution)/shard_map/ppermute | solution.py:380
  10.1 1.6 %collective-permute-start.2 = (bf16[2,16,1152]{2,1,0:T(8,128)(2,1)S(1)}, bf16[2,16,1152]{2,1,0:T(8,128)(2,1)S(1)}, u32[]{:S(2)}, u32[]{:S(2)}) collective-permute-start(bf16[2,16,1152]{2,1,0:T(8,128)(2,1)S(1)} %get-tuple-element.55), channel_id=1, source_target_pairs={{0,4},{1,5},{2,6},{3,7},{4,0},{5,1},{6,2},{7,3},{8,12},{9,13},{10,... | collective-permute-start | bytes 221192 | tf_op jit(solution)/shard_map/ppermute | solution.py:380
  12.1 1.5 %collective-permute-start.4 = (bf16[2,16,1152]{2,1,0:T(8,128)(2,1)S(1)}, bf16[2,16,1152]{2,1,0:T(8,128)(2,1)S(1)}, u32[]{:S(2)}, u32[]{:S(2)}) collective-permute-start(bf16[2,16,1152]{2,1,0:T(8,128)(2,1)S(1)} %get-tuple-element.60), channel_id=1, source_target_pairs={{0,2},{1,3},{2,0},{3,1},{4,6},{5,7},{6,4},{7,5},{8,10},{9,11},{10,... | collective-permute-start | bytes 221192 | tf_op jit(solution)/shard_map/ppermute | solution.py:380
  13.6 1.6 %collective-permute-start.5 = (bf16[2,16,1152]{2,1,0:T(8,128)(2,1)S(1)}, bf16[2,16,1152]{2,1,0:T(8,128)(2,1)S(1)}, u32[]{:S(2)}, u32[]{:S(2)}) collective-permute-start(bf16[2,16,1152]{2,1,0:T(8,128)(2,1)S(1)} %get-tuple-element.61), channel_id=1, source_target_pairs={{0,4},{1,5},{2,6},{3,7},{4,0},{5,1},{6,2},{7,3},{8,12},{9,13},{10,... | collective-permute-start | bytes 221192 | tf_op jit(solution)/shard_map/ppermute | solution.py:380
  15.2 1.3 %collective-permute-start.6 = (bf16[2,16,1152]{2,1,0:T(8,128)(2,1)S(1)}, bf16[2,16,1152]{2,1,0:T(8,128)(2,1)S(1)}, u32[]{:S(2)}, u32[]{:S(2)}) collective-permute-start(bf16[2,16,1152]{2,1,0:T(8,128)(2,1)S(1)} %get-tuple-element.62), channel_id=1, source_target_pairs={{0,6},{1,7},{2,4},{3,5},{4,2},{5,3},{6,0},{7,1},{8,14},{9,15},{10,... | collective-permute-start | bytes 221192 | tf_op jit(solution)/shard_map/ppermute | solution.py:380
  17.9 2.7 %collective-permute-start.9 = (bf16[1,64,1152]{2,1,0:T(8,128)(2,1)S(1)}, bf16[1,64,1152]{2,1,0:T(8,128)(2,1)S(1)}, u32[]{:S(2)}, u32[]{:S(2)}) collective-permute-start(bf16[1,64,1152]{2,1,0:T(8,128)(2,1)S(1)} %choose.2), channel_id=1, source_target_pairs={{0,8},{1,9},{2,10},{3,11},{4,12},{5,13},{6,14},{7,15},{8,0},{9,1},... | collective-permute-start | bytes 442376 | tf_op jit(solution)/shard_map/ppermute | solution.py:380
  20.6 1.7 %features.4 = bf16[160,2304]{1,0:T(8,128)(2,1)S(1)} custom-call(s32[9]{0:T(128)S(1)} %get-tuple-element.96.where, bf16[160,4096]{1,0:T(8,128)(2,1)} %bitcast.73, bf16[160,14336]{1,0:T(8,128)(2,1)} %bitcast.69), custom_call_target="tpu_custom_call" | custom-call | bytes 1474560 | tf_op jit(solution)/shard_map/features/pallas_call | solution.py:197
  23.2 1.4 %collective-permute-start.7 = (bf16[1,64,1152]{2,1,0:T(8,128)(2,1)S(1)}, bf16[1,64,1152]{2,1,0:T(8,128)(2,1)S(1)}, u32[]{:S(2)}, u32[]{:S(2)}) collective-permute-start(bf16[1,64,1152]{2,1,0:T(8,128)(2,1)S(1)} %choose.3), channel_id=1, source_target_pairs={{0,8},{1,9},{2,10},{3,11},{4,12},{5,13},{6,14},{7,15},{8,0},{9,1},... | collective-permute-start | bytes 442376 | tf_op jit(solution)/shard_map/ppermute | solution.py:380
  24.6 5.1 %stage_bases.1 = (bf16[256,2048]{1,0:T(8,128)(2,1)S(1)}, bf16[896,7168]{1,0:T(8,128)(2,1)S(1)}) custom-call(s32[1]{0:T(128)} %bitcast.2.where, bf16[256,4096]{1,0:T(8,128)(2,1)} %first, bf16[896,14336]{1,0:T(8,128)(2,1)} %second), custom_call_target="tpu_custom_call" | custom-call | bytes 13893632 | tf_op jit(solution)/shard_map/stage_bases/pallas_call | solution.py:129
  30.3 2.9 %collective-permute-done.8.rest_16_ = bf16[160,3456]{1,0:T(8,128)(2,1)S(1)} collective-permute-done((bf16[160,3456]{1,0:T(8,128)(2,1)S(1)}, bf16[160,3456]{1,0:T(8,128)(2,1)S(1)}, u32[]{:S(2)}, u32[]{:S(2)}) %collective-permute-start.8) | collective-permute-done | bytes 1105952 | tf_op jit(solution)/shard_map/ppermute | solution.py:411
  33.3 1.8 %collective-permute-start.12 = (bf16[64,1152]{1,0:T(8,128)(2,1)S(1)}, bf16[64,1152]{1,0:T(8,128)(2,1)S(1)}, u32[]{:S(2)}, u32[]{:S(2)}) collective-permute-start(bf16[64,1152]{1,0:T(8,128)(2,1)S(1)} %bitcast.32), channel_id=1, source_target_pairs={{0,2},{1,5},{2,0},{3,7},{4,6},{5,1},{6,4},{7,3},{8,10},{9,13},{10,... | collective-permute-start | bytes 442376 | tf_op jit(solution)/shard_map/ppermute | solution.py:383
  35.1 1.6 %collective-permute-start.14 = (bf16[64,1152]{1,0:T(8,128)(2,1)S(1)}, bf16[64,1152]{1,0:T(8,128)(2,1)S(1)}, u32[]{:S(2)}, u32[]{:S(2)}) collective-permute-start(bf16[64,1152]{1,0:T(8,128)(2,1)S(1)} %bitcast.33), channel_id=1, source_target_pairs={{0,4},{1,3},{2,6},{3,1},{4,0},{5,7},{6,2},{7,5},{8,12},{9,11},{10,... | collective-permute-start | bytes 442376 | tf_op jit(solution)/shard_map/ppermute | solution.py:383
  37.5 2.5 %collective-permute-done.12.rest_1_ = bf16[64,1152]{1,0:T(8,128)(2,1)S(1)} collective-permute-done((bf16[64,1152]{1,0:T(8,128)(2,1)S(1)}, bf16[64,1152]{1,0:T(8,128)(2,1)S(1)}, u32[]{:S(2)}, u32[]{:S(2)}) %collective-permute-start.12) | collective-permute-done | bytes 147488 | tf_op jit(solution)/shard_map/ppermute | solution.py:383
  40.9 1.5 %collective-permute-start.25 = (bf16[160,2304]{1,0:T(8,128)(2,1)S(1)}, bf16[160,2304]{1,0:T(8,128)(2,1)S(1)}, u32[]{:S(2)}, u32[]{:S(2)}) collective-permute-start(bf16[160,2304]{1,0:T(8,128)(2,1)S(1)} %features.4), channel_id=1, source_target_pairs={{0,16},{1,17},{2,18},{3,19},{4,20},{5,21},{6,22},{7,23},{8,24},{9,... | collective-permute-start | bytes 2211848 | tf_op jit(solution)/shard_map/ppermute | solution.py:425
  42.4 1.2 %collective-permute-done.10.rest_1_ = bf16[64,1152]{1,0:T(8,128)(2,1)S(1)} collective-permute-done((bf16[64,1152]{1,0:T(8,128)(2,1)S(1)}, bf16[64,1152]{1,0:T(8,128)(2,1)S(1)}, u32[]{:S(2)}, u32[]{:S(2)}) %collective-permute-start.10) | collective-permute-done | bytes 147488 | tf_op jit(solution)/shard_map/ppermute | solution.py:383
  43.5 1.8 %collective-permute-start.13 = (bf16[64,1152]{1,0:T(8,128)(2,1)S(1)}, bf16[64,1152]{1,0:T(8,128)(2,1)S(1)}, u32[]{:S(2)}, u32[]{:S(2)}) collective-permute-start(bf16[64,1152]{1,0:T(8,128)(2,1)S(1)} %collective-permute-done.10.rest_1_), channel_id=1, source_target_pairs={{0,4},{1,3},{2,6},{3,1},{4,0},{5,7},{6,2},{7,5},{8,12},{9,11},{10,... | collective-permute-start | bytes 442376 | tf_op jit(solution)/shard_map/ppermute | solution.py:383
  46.9 2.6 %rotate.2.rest_10_ = f32[1152,128]{1,0:T(8,128)S(1)} custom-call(s32[4]{0:T(128)S(1)} %fusion.where, bf16[64,1152]{1,0:T(8,128)(2,1)S(1)} %bitcast.35, bf16[64,1152]{1,0:T(8,128)(2,1)S(1)} %collective-permute-done.12.rest_1_, bf16[64,1152]{1,0:T(8,128)(2,1)S(1)} %collective-permute-done.14.rest_2_, bf16[64,1152]{1,0:T(8,128)(2,1)S(1)} %collective-permute-done.15.rest_3_, ...), custom_call_target="tpu_custom_call" | custom-call | flops 889192448 | bytes 6946816 | tf_op jit(solution)/shard_map/rotate/pallas_call | solution.py:245
  49.9 1.0 collective-permute-done.23.rest_7_
  50.9 2.7 %rotate.3 = (f32[128,1152]{1,0:T(8,128)S(1)}, bf16[128,1152]{1,0:T(8,128)(2,1)S(1)}) custom-call(s32[4]{0:T(128)S(1)} %fusion.where, bf16[64,1152]{1,0:T(8,128)(2,1)S(1)} %add_bitcast_fusion.rest_0_, bf16[64,1152]{1,0:T(8,128)(2,1)S(1)} %collective-permute-done.10.rest_1_, bf16[64,1152]{1,0:T(8,128)(2,1)S(1)} %collective-permute-done.11.rest_2_, ...), custom_call_target="tpu_custom_call" | custom-call | flops 889192448 | bytes 6946816 | tf_op jit(solution)/shard_map/rotate/pallas_call | solution.py:245
  53.6 1.3 %collective-permute-start.24 = (bf16[128,1152]{1,0:T(8,128)(2,1)S(1)}, bf16[128,1152]{1,0:T(8,128)(2,1)S(1)}, u32[]{:S(2)}, u32[]{:S(2)}) collective-permute-start(bf16[128,1152]{1,0:T(8,128)(2,1)S(1)} %get-tuple-element.81), channel_id=1, source_target_pairs={{1,17},{3,19},{5,21},{7,23},{9,25},{11,27},{13,29},{15,31},{16,0},... | collective-permute-start | bytes 884744 | tf_op jit(solution)/shard_map/ppermute | solution.py:449
  54.9 1.8 %features.6 = bf16[160,3456]{1,0:T(8,128)(2,1)S(1)} custom-call(s32[9]{0:T(128)S(1)} %get-tuple-element.96.where, bf16[160,4096]{1,0:T(8,128)(2,1)} %bitcast.74, bf16[160,14336]{1,0:T(8,128)(2,1)} %bitcast.70), custom_call_target="tpu_custom_call" | custom-call | bytes 2211840 | tf_op jit(solution)/shard_map/features/pallas_call | solution.py:197
  56.7 1.7 %collective-permute-done.25.rest_17_ = bf16[160,2304]{1,0:T(8,128)(2,1)S(1)} collective-permute-done((bf16[160,2304]{1,0:T(8,128)(2,1)S(1)}, bf16[160,2304]{1,0:T(8,128)(2,1)S(1)}, u32[]{:S(2)}, u32[]{:S(2)}) %collective-permute-start.25) | collective-permute-done | bytes 737312 | tf_op jit(solution)/shard_map/ppermute | solution.py:425
  58.4 3.8 %collective-permute-done.24 = bf16[128,1152]{1,0:T(8,128)(2,1)S(1)} collective-permute-done((bf16[128,1152]{1,0:T(8,128)(2,1)S(1)}, bf16[128,1152]{1,0:T(8,128)(2,1)S(1)}, u32[]{:S(2)}, u32[]{:S(2)}) %collective-permute-start.24) | collective-permute-done | bytes 294944 | tf_op jit(solution)/shard_map/ppermute | solution.py:449
  63.0 1.9 %collective-permute-start.26 = (bf16[64,1152]{1,0:T(8,128)(2,1)S(1)}, bf16[64,1152]{1,0:T(8,128)(2,1)}, u32[]{:S(2)}, u32[]{:S(2)}) collective-permute-start(bf16[64,1152]{1,0:T(8,128)(2,1)S(1)} %slice.9), channel_id=1, source_target_pairs={{0,1},{2,3},{4,5},{6,7},{8,9},{10,11},{12,13},{14,15},{17,16},{19,... | collective-permute-start | bytes 442376 | tf_op jit(solution)/shard_map/ppermute | solution.py:452
  66.3 2.7 %collective-permute-start.30 = (bf16[1,64,1152]{2,1,0:T(8,128)(2,1)S(1)}, bf16[1,64,1152]{2,1,0:T(8,128)(2,1)S(1)}, u32[]{:S(2)}, u32[]{:S(2)}) collective-permute-start(bf16[1,64,1152]{2,1,0:T(8,128)(2,1)S(1)} %bitcast.28), channel_id=1, source_target_pairs={{0,8},{1,9},{2,10},{3,11},{4,12},{5,13},{6,14},{7,15},{8,0},{9,1},... | collective-permute-start | bytes 442376 | tf_op jit(solution)/shard_map/ppermute | solution.py:380
  69.0 1.6 %collective-permute-start.27 = (bf16[1,64,1152]{2,1,0:T(8,128)(2,1)S(1)}, bf16[1,64,1152]{2,1,0:T(8,128)(2,1)S(1)}, u32[]{:S(2)}, u32[]{:S(2)}) collective-permute-start(bf16[1,64,1152]{2,1,0:T(8,128)(2,1)S(1)} %bitcast.29), channel_id=1, source_target_pairs={{0,2},{1,5},{2,0},{3,7},{4,6},{5,1},{6,4},{7,3},{8,10},{9,13},{10,... | collective-permute-start | bytes 442376 | tf_op jit(solution)/shard_map/ppermute | solution.py:383
  70.8 2.5 %features.7.rest_16_ = bf16[160,9216]{1,0:T(8,128)(2,1)S(1)} custom-call(s32[9]{0:T(128)S(1)} %get-tuple-element.95.where, bf16[160,4096]{1,0:T(8,128)(2,1)} %bitcast.75, bf16[160,14336]{1,0:T(8,128)(2,1)} %bitcast.71), custom_call_target="tpu_custom_call" | custom-call | bytes 5898240 | tf_op jit(solution)/shard_map/features/pallas_call | solution.py:197
  73.3 3.4 %collective-permute-done.30 = bf16[1,64,1152]{2,1,0:T(8,128)(2,1)S(1)} collective-permute-done((bf16[1,64,1152]{2,1,0:T(8,128)(2,1)S(1)}, bf16[1,64,1152]{2,1,0:T(8,128)(2,1)S(1)}, u32[]{:S(2)}, u32[]{:S(2)}) %collective-permute-start.30) | collective-permute-done | bytes 147488 | tf_op jit(solution)/shard_map/ppermute | solution.py:380
  76.7 1.2 %collective-permute-start.31 = (bf16[1,64,1152]{2,1,0:T(8,128)(2,1)S(1)}, bf16[1,64,1152]{2,1,0:T(8,128)(2,1)S(1)}, u32[]{:S(2)}, u32[]{:S(2)}) collective-permute-start(bf16[1,64,1152]{2,1,0:T(8,128)(2,1)S(1)} %collective-permute-done.30), channel_id=1, source_target_pairs={{0,2},{1,5},{2,0},{3,7},{4,6},{5,1},{6,4},{7,3},{8,10},{9,13},{10,... | collective-permute-start | bytes 442376 | tf_op jit(solution)/shard_map/ppermute | solution.py:383
  78.2 1.9 %collective-permute-start.29 = (bf16[1,64,1152]{2,1,0:T(8,128)(2,1)S(1)}, bf16[1,64,1152]{2,1,0:T(8,128)(2,1)S(1)}, u32[]{:S(2)}, u32[]{:S(2)}) collective-permute-start(bf16[1,64,1152]{2,1,0:T(8,128)(2,1)S(1)} %collective-permute-done.27), channel_id=1, source_target_pairs={{0,4},{1,3},{2,6},{3,1},{4,0},{5,7},{6,2},{7,5},{8,12},{9,11},{10,... | collective-permute-start | bytes 442376 | tf_op jit(solution)/shard_map/ppermute | solution.py:383
  80.1 3.4 %collective-permute-done.31 = bf16[1,64,1152]{2,1,0:T(8,128)(2,1)S(1)} collective-permute-done((bf16[1,64,1152]{2,1,0:T(8,128)(2,1)S(1)}, bf16[1,64,1152]{2,1,0:T(8,128)(2,1)S(1)}, u32[]{:S(2)}, u32[]{:S(2)}) %collective-permute-start.31) | collective-permute-done | bytes 147488 | tf_op jit(solution)/shard_map/ppermute | solution.py:383
  85.4 3.7 %collective-permute-done.33 = bf16[1,64,1152]{2,1,0:T(8,128)(2,1)S(1)} collective-permute-done((bf16[1,64,1152]{2,1,0:T(8,128)(2,1)S(1)}, bf16[1,64,1152]{2,1,0:T(8,128)(2,1)S(1)}, u32[]{:S(2)}, u32[]{:S(2)}) %collective-permute-start.33) | collective-permute-done | bytes 147488 | tf_op jit(solution)/shard_map/ppermute | solution.py:383
  89.1 1.3 %collective-permute-done.41 = bf16[1,64,1152]{2,1,0:T(8,128)(2,1)S(1)} collective-permute-done((bf16[1,64,1152]{2,1,0:T(8,128)(2,1)S(1)}, bf16[1,64,1152]{2,1,0:T(8,128)(2,1)S(1)}, u32[]{:S(2)}, u32[]{:S(2)}) %collective-permute-start.41) | collective-permute-done | bytes 147488 | tf_op jit(solution)/shard_map/ppermute | solution.py:386
  90.5 1.0 project.3
  91.5 1.5 %collective-permute-start.43 = (bf16[2,160,128]{2,1,0:T(8,128)(2,1)S(1)}, bf16[2,160,128]{2,1,0:T(8,128)(2,1)S(1)}, u32[]{:S(2)}, u32[]{:S(2)}) collective-permute-start(bf16[2,160,128]{2,1,0:T(8,128)(2,1)S(1)} %pad_maximum_fusion), channel_id=1, source_target_pairs={{0,16},{1,17},{2,18},{3,19},{4,20},{5,21},{6,22},{7,23},{8,24},{9,... | collective-permute-start | bytes 245768 | tf_op jit(solution)/shard_map/ppermute | solution.py:468
  93.0 1.0 project.2
  94.0 2.1 %collective-permute-done.43.back = bf16[2,160,128]{2,1,0:T(8,128)(2,1)S(1)} collective-permute-done((bf16[2,160,128]{2,1,0:T(8,128)(2,1)S(1)}, bf16[2,160,128]{2,1,0:T(8,128)(2,1)S(1)}, u32[]{:S(2)}, u32[]{:S(2)}) %collective-permute-start.43) | collective-permute-done | bytes 81952 | tf_op jit(solution)/shard_map/ppermute | solution.py:468
  96.8 1.1 %collective-permute-done.44 = f32[1,64]{1,0:T(1,128)S(1)} collective-permute-done((f32[1,64]{1,0:T(1,128)S(1)}, f32[1,64]{1,0:T(1,128)S(1)}, u32[]{:S(2)}, u32[]{:S(2)}) %collective-permute-start.44) | collective-permute-done | bytes 288 | tf_op jit(solution)/shard_map/ppermute | solution.py:473
  97.9 1.2 %collective-permute-start.45 = (f32[1,64]{1,0:T(1,128)S(1)}, f32[1,64]{1,0:T(1,128)S(1)}, u32[]{:S(2)}, u32[]{:S(2)}) collective-permute-start(f32[1,64]{1,0:T(1,128)S(1)} %add.47), channel_id=1, source_target_pairs={{0,2},{1,3},{2,0},{3,1},{4,6},{5,7},{6,4},{7,5},{8,10},{9,11},{10,... | collective-permute-start | bytes 776 | tf_op jit(solution)/shard_map/ppermute | solution.py:473
  99.1 2.4 %collective-permute-done.45 = f32[1,64]{1,0:T(1,128)S(1)} collective-permute-done((f32[1,64]{1,0:T(1,128)S(1)}, f32[1,64]{1,0:T(1,128)S(1)}, u32[]{:S(2)}, u32[]{:S(2)}) %collective-permute-start.45) | collective-permute-done | bytes 288 | tf_op jit(solution)/shard_map/ppermute | solution.py:473
  102.3 2.6 %collective-permute-done.46 = f32[1,64]{1,0:T(1,128)S(1)} collective-permute-done((f32[1,64]{1,0:T(1,128)S(1)}, f32[1,64]{1,0:T(1,128)S(1)}, u32[]{:S(2)}, u32[]{:S(2)}) %collective-permute-start.46) | collective-permute-done | bytes 288 | tf_op jit(solution)/shard_map/ppermute | solution.py:473
  105.0 2.2 %collective-permute-start.47 = (f32[1,64]{1,0:T(1,128)S(1)}, f32[1,64]{1,0:T(1,128)S(1)}, u32[]{:S(2)}, u32[]{:S(2)}) collective-permute-start(f32[1,64]{1,0:T(1,128)S(1)} %add.49), channel_id=1, source_target_pairs={{0,8},{1,9},{2,10},{3,11},{4,12},{5,13},{6,14},{7,15},{8,0},{9,1},... | collective-permute-start | bytes 776 | tf_op jit(solution)/shard_map/ppermute | solution.py:473
  107.2 2.2 %collective-permute-done.47 = f32[1,64]{1,0:T(1,128)S(1)} collective-permute-done((f32[1,64]{1,0:T(1,128)S(1)}, f32[1,64]{1,0:T(1,128)S(1)}, u32[]{:S(2)}, u32[]{:S(2)}) %collective-permute-start.47) | collective-permute-done | bytes 288 | tf_op jit(solution)/shard_map/ppermute | solution.py:473
  109.4 1.1 %own_sequence.1 = f32[1,4]{1,0:T(1,128)} custom-call(s32[1]{0:T(128)} %bitcast.where, s32[16]{0:T(128)S(1)} %copy-done.2, f32[1,64]{1,0:T(1,128)S(1)} %add.50.held), custom_call_target="tpu_custom_call" | custom-call | bytes 256 | tf_op jit(solution)/shard_map/own_sequence/pallas_call | solution.py:341
  (92 shorter events, 14.0 us)
Async XLA Ops:
  2.0 1.7 %collective-permute-start = (bf16[4,2,16,1152]{3,2,1,0:T(8,128)(2,1)S(1)}, bf16[4,2,16,1152]{3,2,1,0:T(8,128)(2,1)S(1)}, u32[]{:S(2)}, u32[]{:S(2)}) collective-permute-start(bf16[4,2,16,1152]{3,2,1,0:T(8,128)(2,1)S(1)} %get-tuple-element.51), channel_id=1, source_target_pairs={{0,1},{1,0},{2,3},{3,2},{4,5},{5,4},{6,7},{7,6},{8,9},{9,8},{10,11... | collective-permute-start | bytes 884744 | tf_op jit(solution)/shard_map/ppermute | solution.py:386
  5.7 27.6 %collective-permute-start.8 = (bf16[160,3456]{1,0:T(8,128)(2,1)S(1)}, bf16[160,3456]{1,0:T(8,128)(2,1)S(1)}, u32[]{:S(2)}, u32[]{:S(2)}) collective-permute-start(bf16[160,3456]{1,0:T(8,128)(2,1)S(1)} %features.5), channel_id=1, source_target_pairs={{0,16},{1,17},{2,18},{3,19},{4,20},{5,21},{6,22},{7,23},{8,24},{9,... | collective-permute-start | bytes 3317768 | tf_op jit(solution)/shard_map/ppermute | solution.py:411
  8.6 5.0 %collective-permute-start.1 = (bf16[2,16,1152]{2,1,0:T(8,128)(2,1)S(1)}, bf16[2,16,1152]{2,1,0:T(8,128)(2,1)S(1)}, u32[]{:S(2)}, u32[]{:S(2)}) collective-permute-start(bf16[2,16,1152]{2,1,0:T(8,128)(2,1)S(1)} %get-tuple-element.54), channel_id=1, source_target_pairs={{0,2},{1,3},{2,0},{3,1},{4,6},{5,7},{6,4},{7,5},{8,10},{9,11},{10,... | collective-permute-start | bytes 221192 | tf_op jit(solution)/shard_map/ppermute | solution.py:380
  10.1 5.1 %collective-permute-start.2 = (bf16[2,16,1152]{2,1,0:T(8,128)(2,1)S(1)}, bf16[2,16,1152]{2,1,0:T(8,128)(2,1)S(1)}, u32[]{:S(2)}, u32[]{:S(2)}) collective-permute-start(bf16[2,16,1152]{2,1,0:T(8,128)(2,1)S(1)} %get-tuple-element.55), channel_id=1, source_target_pairs={{0,4},{1,5},{2,6},{3,7},{4,0},{5,1},{6,2},{7,3},{8,12},{9,13},{10,... | collective-permute-start | bytes 221192 | tf_op jit(solution)/shard_map/ppermute | solution.py:380
  11.7 5.4 %collective-permute-start.3 = (bf16[2,16,1152]{2,1,0:T(8,128)(2,1)S(1)}, bf16[2,16,1152]{2,1,0:T(8,128)(2,1)S(1)}, u32[]{:S(2)}, u32[]{:S(2)}) collective-permute-start(bf16[2,16,1152]{2,1,0:T(8,128)(2,1)S(1)} %get-tuple-element.56), channel_id=1, source_target_pairs={{0,6},{1,7},{2,4},{3,5},{4,2},{5,3},{6,0},{7,1},{8,14},{9,15},{10,... | collective-permute-start | bytes 221192 | tf_op jit(solution)/shard_map/ppermute | solution.py:380
  12.1 10.3 %collective-permute-start.4 = (bf16[2,16,1152]{2,1,0:T(8,128)(2,1)S(1)}, bf16[2,16,1152]{2,1,0:T(8,128)(2,1)S(1)}, u32[]{:S(2)}, u32[]{:S(2)}) collective-permute-start(bf16[2,16,1152]{2,1,0:T(8,128)(2,1)S(1)} %get-tuple-element.60), channel_id=1, source_target_pairs={{0,2},{1,3},{2,0},{3,1},{4,6},{5,7},{6,4},{7,5},{8,10},{9,11},{10,... | collective-permute-start | bytes 221192 | tf_op jit(solution)/shard_map/ppermute | solution.py:380
  13.6 8.7 %collective-permute-start.5 = (bf16[2,16,1152]{2,1,0:T(8,128)(2,1)S(1)}, bf16[2,16,1152]{2,1,0:T(8,128)(2,1)S(1)}, u32[]{:S(2)}, u32[]{:S(2)}) collective-permute-start(bf16[2,16,1152]{2,1,0:T(8,128)(2,1)S(1)} %get-tuple-element.61), channel_id=1, source_target_pairs={{0,4},{1,5},{2,6},{3,7},{4,0},{5,1},{6,2},{7,3},{8,12},{9,13},{10,... | collective-permute-start | bytes 221192 | tf_op jit(solution)/shard_map/ppermute | solution.py:380
  15.2 7.1 %collective-permute-start.6 = (bf16[2,16,1152]{2,1,0:T(8,128)(2,1)S(1)}, bf16[2,16,1152]{2,1,0:T(8,128)(2,1)S(1)}, u32[]{:S(2)}, u32[]{:S(2)}) collective-permute-start(bf16[2,16,1152]{2,1,0:T(8,128)(2,1)S(1)} %get-tuple-element.62), channel_id=1, source_target_pairs={{0,6},{1,7},{2,4},{3,5},{4,2},{5,3},{6,0},{7,1},{8,14},{9,15},{10,... | collective-permute-start | bytes 221192 | tf_op jit(solution)/shard_map/ppermute | solution.py:380
  17.9 12.4 %collective-permute-start.9 = (bf16[1,64,1152]{2,1,0:T(8,128)(2,1)S(1)}, bf16[1,64,1152]{2,1,0:T(8,128)(2,1)S(1)}, u32[]{:S(2)}, u32[]{:S(2)}) collective-permute-start(bf16[1,64,1152]{2,1,0:T(8,128)(2,1)S(1)} %choose.2), channel_id=1, source_target_pairs={{0,8},{1,9},{2,10},{3,11},{4,12},{5,13},{6,14},{7,15},{8,0},{9,1},... | collective-permute-start | bytes 442376 | tf_op jit(solution)/shard_map/ppermute | solution.py:380
  23.2 13.5 %collective-permute-start.7 = (bf16[1,64,1152]{2,1,0:T(8,128)(2,1)S(1)}, bf16[1,64,1152]{2,1,0:T(8,128)(2,1)S(1)}, u32[]{:S(2)}, u32[]{:S(2)}) collective-permute-start(bf16[1,64,1152]{2,1,0:T(8,128)(2,1)S(1)} %choose.3), channel_id=1, source_target_pairs={{0,8},{1,9},{2,10},{3,11},{4,12},{5,13},{6,14},{7,15},{8,0},{9,1},... | collective-permute-start | bytes 442376 | tf_op jit(solution)/shard_map/ppermute | solution.py:380
  33.3 6.7 %collective-permute-start.12 = (bf16[64,1152]{1,0:T(8,128)(2,1)S(1)}, bf16[64,1152]{1,0:T(8,128)(2,1)S(1)}, u32[]{:S(2)}, u32[]{:S(2)}) collective-permute-start(bf16[64,1152]{1,0:T(8,128)(2,1)S(1)} %bitcast.32), channel_id=1, source_target_pairs={{0,2},{1,5},{2,0},{3,7},{4,6},{5,1},{6,4},{7,3},{8,10},{9,13},{10,... | collective-permute-start | bytes 442376 | tf_op jit(solution)/shard_map/ppermute | solution.py:383
  35.1 5.7 %collective-permute-start.14 = (bf16[64,1152]{1,0:T(8,128)(2,1)S(1)}, bf16[64,1152]{1,0:T(8,128)(2,1)S(1)}, u32[]{:S(2)}, u32[]{:S(2)}) collective-permute-start(bf16[64,1152]{1,0:T(8,128)(2,1)S(1)} %bitcast.33), channel_id=1, source_target_pairs={{0,4},{1,3},{2,6},{3,1},{4,0},{5,7},{6,2},{7,5},{8,12},{9,11},{10,... | collective-permute-start | bytes 442376 | tf_op jit(solution)/shard_map/ppermute | solution.py:383
  36.7 5.6 %collective-permute-start.16 = (bf16[64,1152]{1,0:T(8,128)(2,1)S(1)}, bf16[64,1152]{1,0:T(8,128)(2,1)S(1)}, u32[]{:S(2)}, u32[]{:S(2)}) collective-permute-start(bf16[64,1152]{1,0:T(8,128)(2,1)S(1)} %bitcast.34), channel_id=1, source_target_pairs={{0,1},{1,0},{2,3},{3,2},{4,5},{5,4},{6,7},{7,6},{8,9},{9,8},{10,11... | collective-permute-start | bytes 442376 | tf_op jit(solution)/shard_map/ppermute | solution.py:386
  36.8 6.8 %collective-permute-start.10 = (bf16[64,1152]{1,0:T(8,128)(2,1)S(1)}, bf16[64,1152]{1,0:T(8,128)(2,1)S(1)}, u32[]{:S(2)}, u32[]{:S(2)}) collective-permute-start(bf16[64,1152]{1,0:T(8,128)(2,1)S(1)} %add_bitcast_fusion.rest_0_), channel_id=1, source_target_pairs={{0,2},{1,5},{2,0},{3,7},{4,6},{5,1},{6,4},{7,3},{8,10},{9,13},{10,... | collective-permute-start | bytes 442376 | tf_op jit(solution)/shard_map/ppermute | solution.py:383
  37.3 6.2 %collective-permute-start.11 = (bf16[64,1152]{1,0:T(8,128)(2,1)S(1)}, bf16[64,1152]{1,0:T(8,128)(2,1)S(1)}, u32[]{:S(2)}, u32[]{:S(2)}) collective-permute-start(bf16[64,1152]{1,0:T(8,128)(2,1)S(1)} %add_bitcast_fusion.rest_0_), channel_id=1, source_target_pairs={{0,4},{1,3},{2,6},{3,1},{4,0},{5,7},{6,2},{7,5},{8,12},{9,11},{10,... | collective-permute-start | bytes 442376 | tf_op jit(solution)/shard_map/ppermute | solution.py:383
  40.0 5.4 %collective-permute-start.15 = (bf16[64,1152]{1,0:T(8,128)(2,1)S(1)}, bf16[64,1152]{1,0:T(8,128)(2,1)S(1)}, u32[]{:S(2)}, u32[]{:S(2)}) collective-permute-start(bf16[64,1152]{1,0:T(8,128)(2,1)S(1)} %collective-permute-done.12.rest_1_), channel_id=1, source_target_pairs={{0,4},{1,3},{2,6},{3,1},{4,0},{5,7},{6,2},{7,5},{8,12},{9,11},{10,... | collective-permute-start | bytes 442376 | tf_op jit(solution)/shard_map/ppermute | solution.py:383
  40.9 17.5 %collective-permute-start.25 = (bf16[160,2304]{1,0:T(8,128)(2,1)S(1)}, bf16[160,2304]{1,0:T(8,128)(2,1)S(1)}, u32[]{:S(2)}, u32[]{:S(2)}) collective-permute-start(bf16[160,2304]{1,0:T(8,128)(2,1)S(1)} %features.4), channel_id=1, source_target_pairs={{0,16},{1,17},{2,18},{3,19},{4,20},{5,21},{6,22},{7,23},{8,24},{9,... | collective-permute-start | bytes 2211848 | tf_op jit(solution)/shard_map/ppermute | solution.py:425
  42.4 3.0 %collective-permute-start.17 = (bf16[64,1152]{1,0:T(8,128)(2,1)S(1)}, bf16[64,1152]{1,0:T(8,128)(2,1)S(1)}, u32[]{:S(2)}, u32[]{:S(2)}) collective-permute-start(bf16[64,1152]{1,0:T(8,128)(2,1)S(1)} %collective-permute-done.12.rest_1_), channel_id=1, source_target_pairs={{0,1},{1,0},{2,3},{3,2},{4,5},{5,4},{6,7},{7,6},{8,9},{9,8},{10,11... | collective-permute-start | bytes 442376 | tf_op jit(solution)/shard_map/ppermute | solution.py:386
  43.5 2.4 %collective-permute-start.18 = (bf16[64,1152]{1,0:T(8,128)(2,1)S(1)}, bf16[64,1152]{1,0:T(8,128)(2,1)S(1)}, u32[]{:S(2)}, u32[]{:S(2)}) collective-permute-start(bf16[64,1152]{1,0:T(8,128)(2,1)S(1)} %collective-permute-done.14.rest_2_), channel_id=1, source_target_pairs={{0,1},{1,0},{2,3},{3,2},{4,5},{5,4},{6,7},{7,6},{8,9},{9,8},{10,11... | collective-permute-start | bytes 442376 | tf_op jit(solution)/shard_map/ppermute | solution.py:386
  43.5 5.9 %collective-permute-start.13 = (bf16[64,1152]{1,0:T(8,128)(2,1)S(1)}, bf16[64,1152]{1,0:T(8,128)(2,1)S(1)}, u32[]{:S(2)}, u32[]{:S(2)}) collective-permute-start(bf16[64,1152]{1,0:T(8,128)(2,1)S(1)} %collective-permute-done.10.rest_1_), channel_id=1, source_target_pairs={{0,4},{1,3},{2,6},{3,1},{4,0},{5,7},{6,2},{7,5},{8,12},{9,11},{10,... | collective-permute-start | bytes 442376 | tf_op jit(solution)/shard_map/ppermute | solution.py:383
  45.4 1.4 %collective-permute-start.19 = (bf16[64,1152]{1,0:T(8,128)(2,1)S(1)}, bf16[64,1152]{1,0:T(8,128)(2,1)S(1)}, u32[]{:S(2)}, u32[]{:S(2)}) collective-permute-start(bf16[64,1152]{1,0:T(8,128)(2,1)S(1)} %collective-permute-done.15.rest_3_), channel_id=1, source_target_pairs={{0,1},{1,0},{2,3},{3,2},{4,5},{5,4},{6,7},{7,6},{8,9},{9,8},{10,11... | collective-permute-start | bytes 442376 | tf_op jit(solution)/shard_map/ppermute | solution.py:386
  45.4 4.5 %collective-permute-start.20 = (bf16[64,1152]{1,0:T(8,128)(2,1)S(1)}, bf16[64,1152]{1,0:T(8,128)(2,1)S(1)}, u32[]{:S(2)}, u32[]{:S(2)}) collective-permute-start(bf16[64,1152]{1,0:T(8,128)(2,1)S(1)} %add_bitcast_fusion.rest_0_), channel_id=1, source_target_pairs={{0,1},{1,0},{2,3},{3,2},{4,5},{5,4},{6,7},{7,6},{8,9},{9,8},{10,11... | collective-permute-start | bytes 442376 | tf_op jit(solution)/shard_map/ppermute | solution.py:386
  46.0 3.9 %collective-permute-start.21 = (bf16[64,1152]{1,0:T(8,128)(2,1)S(1)}, bf16[64,1152]{1,0:T(8,128)(2,1)S(1)}, u32[]{:S(2)}, u32[]{:S(2)}) collective-permute-start(bf16[64,1152]{1,0:T(8,128)(2,1)S(1)} %collective-permute-done.10.rest_1_), channel_id=1, source_target_pairs={{0,1},{1,0},{2,3},{3,2},{4,5},{5,4},{6,7},{7,6},{8,9},{9,8},{10,11... | collective-permute-start | bytes 442376 | tf_op jit(solution)/shard_map/ppermute | solution.py:386
  46.7 3.2 %collective-permute-start.22 = (bf16[64,1152]{1,0:T(8,128)(2,1)S(1)}, bf16[64,1152]{1,0:T(8,128)(2,1)S(1)}, u32[]{:S(2)}, u32[]{:S(2)}) collective-permute-start(bf16[64,1152]{1,0:T(8,128)(2,1)S(1)} %collective-permute-done.11.rest_2_), channel_id=1, source_target_pairs={{0,1},{1,0},{2,3},{3,2},{4,5},{5,4},{6,7},{7,6},{8,9},{9,8},{10,11... | collective-permute-start | bytes 442376 | tf_op jit(solution)/shard_map/ppermute | solution.py:386
  49.5 1.4 %collective-permute-start.23 = (bf16[64,1152]{1,0:T(8,128)(2,1)S(1)}, bf16[64,1152]{1,0:T(8,128)(2,1)S(1)}, u32[]{:S(2)}, u32[]{:S(2)}) collective-permute-start(bf16[64,1152]{1,0:T(8,128)(2,1)S(1)} %collective-permute-done.13.rest_3_), channel_id=1, source_target_pairs={{0,1},{1,0},{2,3},{3,2},{4,5},{5,4},{6,7},{7,6},{8,9},{9,8},{10,11... | collective-permute-start | bytes 442376 | tf_op jit(solution)/shard_map/ppermute | solution.py:386
  53.6 8.6 %collective-permute-start.24 = (bf16[128,1152]{1,0:T(8,128)(2,1)S(1)}, bf16[128,1152]{1,0:T(8,128)(2,1)S(1)}, u32[]{:S(2)}, u32[]{:S(2)}) collective-permute-start(bf16[128,1152]{1,0:T(8,128)(2,1)S(1)} %get-tuple-element.81), channel_id=1, source_target_pairs={{1,17},{3,19},{5,21},{7,23},{9,25},{11,27},{13,29},{15,31},{16,0},... | collective-permute-start | bytes 884744 | tf_op jit(solution)/shard_map/ppermute | solution.py:449
  63.0 2.4 %collective-permute-start.26 = (bf16[64,1152]{1,0:T(8,128)(2,1)S(1)}, bf16[64,1152]{1,0:T(8,128)(2,1)}, u32[]{:S(2)}, u32[]{:S(2)}) collective-permute-start(bf16[64,1152]{1,0:T(8,128)(2,1)S(1)} %slice.9), channel_id=1, source_target_pairs={{0,1},{2,3},{4,5},{6,7},{8,9},{10,11},{12,13},{14,15},{17,16},{19,... | collective-permute-start | bytes 442376 | tf_op jit(solution)/shard_map/ppermute | solution.py:452
  64.9 25.6 %collective-permute-start.42 = (bf16[160,3456]{1,0:T(8,128)(2,1)S(1)}, bf16[160,3456]{1,0:T(8,128)(2,1)S(1)}, u32[]{:S(2)}, u32[]{:S(2)}) collective-permute-start(bf16[160,3456]{1,0:T(8,128)(2,1)S(1)} %features.6), channel_id=1, source_target_pairs={{0,16},{1,17},{2,18},{3,19},{4,20},{5,21},{6,22},{7,23},{8,24},{9,... | collective-permute-start | bytes 3317768 | tf_op jit(solution)/shard_map/ppermute | solution.py:450
  66.3 10.4 %collective-permute-start.30 = (bf16[1,64,1152]{2,1,0:T(8,128)(2,1)S(1)}, bf16[1,64,1152]{2,1,0:T(8,128)(2,1)S(1)}, u32[]{:S(2)}, u32[]{:S(2)}) collective-permute-start(bf16[1,64,1152]{2,1,0:T(8,128)(2,1)S(1)} %bitcast.28), channel_id=1, source_target_pairs={{0,8},{1,9},{2,10},{3,11},{4,12},{5,13},{6,14},{7,15},{8,0},{9,1},... | collective-permute-start | bytes 442376 | tf_op jit(solution)/shard_map/ppermute | solution.py:380
  69.0 9.0 %collective-permute-start.27 = (bf16[1,64,1152]{2,1,0:T(8,128)(2,1)S(1)}, bf16[1,64,1152]{2,1,0:T(8,128)(2,1)S(1)}, u32[]{:S(2)}, u32[]{:S(2)}) collective-permute-start(bf16[1,64,1152]{2,1,0:T(8,128)(2,1)S(1)} %bitcast.29), channel_id=1, source_target_pairs={{0,2},{1,5},{2,0},{3,7},{4,6},{5,1},{6,4},{7,3},{8,10},{9,13},{10,... | collective-permute-start | bytes 442376 | tf_op jit(solution)/shard_map/ppermute | solution.py:383
  70.6 7.4 %collective-permute-start.28 = (bf16[1,64,1152]{2,1,0:T(8,128)(2,1)S(1)}, bf16[1,64,1152]{2,1,0:T(8,128)(2,1)S(1)}, u32[]{:S(2)}, u32[]{:S(2)}) collective-permute-start(bf16[1,64,1152]{2,1,0:T(8,128)(2,1)S(1)} %bitcast.30), channel_id=1, source_target_pairs={{0,4},{1,3},{2,6},{3,1},{4,0},{5,7},{6,2},{7,5},{8,12},{9,11},{10,... | collective-permute-start | bytes 442376 | tf_op jit(solution)/shard_map/ppermute | solution.py:383
  73.3 4.9 %collective-permute-start.34 = (bf16[1,64,1152]{2,1,0:T(8,128)(2,1)S(1)}, bf16[1,64,1152]{2,1,0:T(8,128)(2,1)S(1)}, u32[]{:S(2)}, u32[]{:S(2)}) collective-permute-start(bf16[1,64,1152]{2,1,0:T(8,128)(2,1)S(1)} %bitcast.31), channel_id=1, source_target_pairs={{0,1},{1,0},{2,3},{3,2},{4,5},{5,4},{6,7},{7,6},{8,9},{9,8},{10,11... | collective-permute-start | bytes 442376 | tf_op jit(solution)/shard_map/ppermute | solution.py:386
  76.7 6.7 %collective-permute-start.31 = (bf16[1,64,1152]{2,1,0:T(8,128)(2,1)S(1)}, bf16[1,64,1152]{2,1,0:T(8,128)(2,1)S(1)}, u32[]{:S(2)}, u32[]{:S(2)}) collective-permute-start(bf16[1,64,1152]{2,1,0:T(8,128)(2,1)S(1)} %collective-permute-done.30), channel_id=1, source_target_pairs={{0,2},{1,5},{2,0},{3,7},{4,6},{5,1},{6,4},{7,3},{8,10},{9,13},{10,... | collective-permute-start | bytes 442376 | tf_op jit(solution)/shard_map/ppermute | solution.py:383
  77.9 5.5 %collective-permute-start.32 = (bf16[1,64,1152]{2,1,0:T(8,128)(2,1)S(1)}, bf16[1,64,1152]{2,1,0:T(8,128)(2,1)S(1)}, u32[]{:S(2)}, u32[]{:S(2)}) collective-permute-start(bf16[1,64,1152]{2,1,0:T(8,128)(2,1)S(1)} %collective-permute-done.30), channel_id=1, source_target_pairs={{0,4},{1,3},{2,6},{3,1},{4,0},{5,7},{6,2},{7,5},{8,12},{9,11},{10,... | collective-permute-start | bytes 442376 | tf_op jit(solution)/shard_map/ppermute | solution.py:383
  78.0 6.0 %collective-permute-start.38 = (bf16[1,64,1152]{2,1,0:T(8,128)(2,1)S(1)}, bf16[1,64,1152]{2,1,0:T(8,128)(2,1)S(1)}, u32[]{:S(2)}, u32[]{:S(2)}) collective-permute-start(bf16[1,64,1152]{2,1,0:T(8,128)(2,1)S(1)} %collective-permute-done.30), channel_id=1, source_target_pairs={{0,1},{1,0},{2,3},{3,2},{4,5},{5,4},{6,7},{7,6},{8,9},{9,8},{10,11... | collective-permute-start | bytes 442376 | tf_op jit(solution)/shard_map/ppermute | solution.py:386
  78.2 6.5 %collective-permute-start.29 = (bf16[1,64,1152]{2,1,0:T(8,128)(2,1)S(1)}, bf16[1,64,1152]{2,1,0:T(8,128)(2,1)S(1)}, u32[]{:S(2)}, u32[]{:S(2)}) collective-permute-start(bf16[1,64,1152]{2,1,0:T(8,128)(2,1)S(1)} %collective-permute-done.27), channel_id=1, source_target_pairs={{0,4},{1,3},{2,6},{3,1},{4,0},{5,7},{6,2},{7,5},{8,12},{9,11},{10,... | collective-permute-start | bytes 442376 | tf_op jit(solution)/shard_map/ppermute | solution.py:383
  83.4 1.5 %collective-permute-start.35 = (bf16[1,64,1152]{2,1,0:T(8,128)(2,1)S(1)}, bf16[1,64,1152]{2,1,0:T(8,128)(2,1)S(1)}, u32[]{:S(2)}, u32[]{:S(2)}) collective-permute-start(bf16[1,64,1152]{2,1,0:T(8,128)(2,1)S(1)} %collective-permute-done.28), channel_id=1, source_target_pairs={{0,1},{1,0},{2,3},{3,2},{4,5},{5,4},{6,7},{7,6},{8,9},{9,8},{10,11... | collective-permute-start | bytes 442376 | tf_op jit(solution)/shard_map/ppermute | solution.py:386
  83.5 1.7 %collective-permute-start.36 = (bf16[1,64,1152]{2,1,0:T(8,128)(2,1)S(1)}, bf16[1,64,1152]{2,1,0:T(8,128)(2,1)S(1)}, u32[]{:S(2)}, u32[]{:S(2)}) collective-permute-start(bf16[1,64,1152]{2,1,0:T(8,128)(2,1)S(1)} %collective-permute-done.27), channel_id=1, source_target_pairs={{0,1},{1,0},{2,3},{3,2},{4,5},{5,4},{6,7},{7,6},{8,9},{9,8},{10,11... | collective-permute-start | bytes 442376 | tf_op jit(solution)/shard_map/ppermute | solution.py:386
  84.0 5.1 %collective-permute-start.33 = (bf16[1,64,1152]{2,1,0:T(8,128)(2,1)S(1)}, bf16[1,64,1152]{2,1,0:T(8,128)(2,1)S(1)}, u32[]{:S(2)}, u32[]{:S(2)}) collective-permute-start(bf16[1,64,1152]{2,1,0:T(8,128)(2,1)S(1)} %collective-permute-done.31), channel_id=1, source_target_pairs={{0,4},{1,3},{2,6},{3,1},{4,0},{5,7},{6,2},{7,5},{8,12},{9,11},{10,... | collective-permute-start | bytes 442376 | tf_op jit(solution)/shard_map/ppermute | solution.py:383
  84.7 4.4 %collective-permute-start.40 = (bf16[1,64,1152]{2,1,0:T(8,128)(2,1)S(1)}, bf16[1,64,1152]{2,1,0:T(8,128)(2,1)S(1)}, u32[]{:S(2)}, u32[]{:S(2)}) collective-permute-start(bf16[1,64,1152]{2,1,0:T(8,128)(2,1)S(1)} %collective-permute-done.31), channel_id=1, source_target_pairs={{0,1},{1,0},{2,3},{3,2},{4,5},{5,4},{6,7},{7,6},{8,9},{9,8},{10,11... | collective-permute-start | bytes 442376 | tf_op jit(solution)/shard_map/ppermute | solution.py:386
  84.9 4.2 %collective-permute-start.39 = (bf16[1,64,1152]{2,1,0:T(8,128)(2,1)S(1)}, bf16[1,64,1152]{2,1,0:T(8,128)(2,1)S(1)}, u32[]{:S(2)}, u32[]{:S(2)}) collective-permute-start(bf16[1,64,1152]{2,1,0:T(8,128)(2,1)S(1)} %collective-permute-done.32), channel_id=1, source_target_pairs={{0,1},{1,0},{2,3},{3,2},{4,5},{5,4},{6,7},{7,6},{8,9},{9,8},{10,11... | collective-permute-start | bytes 442376 | tf_op jit(solution)/shard_map/ppermute | solution.py:386
  85.2 3.9 %collective-permute-start.37 = (bf16[1,64,1152]{2,1,0:T(8,128)(2,1)S(1)}, bf16[1,64,1152]{2,1,0:T(8,128)(2,1)S(1)}, u32[]{:S(2)}, u32[]{:S(2)}) collective-permute-start(bf16[1,64,1152]{2,1,0:T(8,128)(2,1)S(1)} %collective-permute-done.29), channel_id=1, source_target_pairs={{0,1},{1,0},{2,3},{3,2},{4,5},{5,4},{6,7},{7,6},{8,9},{9,8},{10,11... | collective-permute-start | bytes 442376 | tf_op jit(solution)/shard_map/ppermute | solution.py:386
  89.1 1.4 %collective-permute-start.41 = (bf16[1,64,1152]{2,1,0:T(8,128)(2,1)S(1)}, bf16[1,64,1152]{2,1,0:T(8,128)(2,1)S(1)}, u32[]{:S(2)}, u32[]{:S(2)}) collective-permute-start(bf16[1,64,1152]{2,1,0:T(8,128)(2,1)S(1)} %collective-permute-done.33), channel_id=1, source_target_pairs={{0,1},{1,0},{2,3},{3,2},{4,5},{5,4},{6,7},{7,6},{8,9},{9,8},{10,11... | collective-permute-start | bytes 442376 | tf_op jit(solution)/shard_map/ppermute | solution.py:386
  91.5 4.6 %collective-permute-start.43 = (bf16[2,160,128]{2,1,0:T(8,128)(2,1)S(1)}, bf16[2,160,128]{2,1,0:T(8,128)(2,1)S(1)}, u32[]{:S(2)}, u32[]{:S(2)}) collective-permute-start(bf16[2,160,128]{2,1,0:T(8,128)(2,1)S(1)} %pad_maximum_fusion), channel_id=1, source_target_pairs={{0,16},{1,17},{2,18},{3,19},{4,20},{5,21},{6,22},{7,23},{8,24},{9,... | collective-permute-start | bytes 245768 | tf_op jit(solution)/shard_map/ppermute | solution.py:468
  96.8 1.1 %collective-permute-start.44 = (f32[1,64]{1,0:T(1,128)S(1)}, f32[1,64]{1,0:T(1,128)S(1)}, u32[]{:S(2)}, u32[]{:S(2)}) collective-permute-start(f32[1,64]{1,0:T(1,128)S(1)} %score.1), channel_id=1, source_target_pairs={{0,1},{1,0},{2,3},{3,2},{4,5},{5,4},{6,7},{7,6},{8,9},{9,8},{10,11... | collective-permute-start | bytes 776 | tf_op jit(solution)/shard_map/ppermute | solution.py:473
  97.9 3.5 %collective-permute-start.45 = (f32[1,64]{1,0:T(1,128)S(1)}, f32[1,64]{1,0:T(1,128)S(1)}, u32[]{:S(2)}, u32[]{:S(2)}) collective-permute-start(f32[1,64]{1,0:T(1,128)S(1)} %add.47), channel_id=1, source_target_pairs={{0,2},{1,3},{2,0},{3,1},{4,6},{5,7},{6,4},{7,5},{8,10},{9,11},{10,... | collective-permute-start | bytes 776 | tf_op jit(solution)/shard_map/ppermute | solution.py:473
  101.4 3.5 %collective-permute-start.46 = (f32[1,64]{1,0:T(1,128)S(1)}, f32[1,64]{1,0:T(1,128)S(1)}, u32[]{:S(2)}, u32[]{:S(2)}) collective-permute-start(f32[1,64]{1,0:T(1,128)S(1)} %add.48), channel_id=1, source_target_pairs={{0,4},{1,5},{2,6},{3,7},{4,0},{5,1},{6,2},{7,3},{8,12},{9,13},{10,... | collective-permute-start | bytes 776 | tf_op jit(solution)/shard_map/ppermute | solution.py:473
  105.0 4.4 %collective-permute-start.47 = (f32[1,64]{1,0:T(1,128)S(1)}, f32[1,64]{1,0:T(1,128)S(1)}, u32[]{:S(2)}, u32[]{:S(2)}) collective-permute-start(f32[1,64]{1,0:T(1,128)S(1)} %add.49), channel_id=1, source_target_pairs={{0,8},{1,9},{2,10},{3,11},{4,12},{5,13},{6,14},{7,15},{8,0},{9,1},... | collective-permute-start | bytes 776 | tf_op jit(solution)/shard_map/ppermute | solution.py:473
  (7 other events, 68.5 us)

commit v5 on v4

v5 whole, which is shorter than its diff:
```python
import jax
import jax.numpy as jnp
from jax import lax
from jax.experimental import pallas as pl
from jax.experimental.pallas import tpu as pltpu
from jax.sharding import PartitionSpec as P

ROWS = (((1,), (1,)), ((), ()))
EVERYONE = ("parts", "blk")
NEAR = 4
CHAINS = 2
PART, CORE, CHIP, ME, NEAR_AT, CHIP_AT = 0, 1, 2, 3, 4, 8
MIB = 1024 * 1024


def dot_rows(left, right):
    return lax.dot_general(left, right, ROWS, preferred_element_type=jnp.float32)


NEAR_MASKS = ((0, 1, 2, 3), (0, 2, 1, 3))
SIBLING = (0, 2, 1, 3)


def after(values, other):
    return list(lax.optimization_barrier((*values, other)))[:-1]


VMEM = pl.BlockSpec(memory_space=pltpu.VMEM)
SMEM = pl.BlockSpec(memory_space=pltpu.SMEM)
HBM = pl.BlockSpec(memory_space=pltpu.HBM)


def in_hbm(value):
    return pltpu.with_memory_space_constraint(value, pltpu.HBM)


def in_vmem(value):
    return pltpu.with_memory_space_constraint(value, pltpu.VMEM)


def lanes_at(number, width):
    return pl.ds(pl.multiple_of(number * width, 128), width)


def copy_all(copies):
    for copy in copies:
        copy.start()
    for copy in copies:
        copy.wait()


def estimate(flops, moved):
    return pl.CostEstimate(flops=flops, bytes_accessed=moved, transcendentals=0)


class Features:
    def __init__(self, acts, grads, chips):
        self.tokens, self.chips, self.kind = acts.shape[0], chips, acts.dtype
        self.acts, self.grads = acts, grads
        self.wide_in, self.wide_out = acts.shape[1] // 2 // chips, grads.shape[1] // 2 // chips
        self.wide = self.wide_in + self.wide_out
        self.aligned = not (self.wide_in % 128 or self.wide_out % 128)

    def shapes(self, ranges):
        return [pltpu.VMEM((self.tokens, (end - begin) * self.wide), self.kind) for begin, end in ranges]

    def copies(self, sources, outs, ranges, plane, chip_at, sems):
        result = []
        for out, (first, last) in zip(outs, ranges):
            for spot in range(first, last):
                number = 2 * chip_at(spot) + plane
                for source, width, begin in zip(sources, (self.wide_in, self.wide_out), (0, self.wide_in)):
                    result.append(
                        pltpu.make_async_copy(
                            source.at[:, lanes_at(number, width)],
                            out.at[:, pl.ds((spot - first) * self.wide + begin, width)],
                            sems.at[len(result)],
                        )
                    )
        return result

    def plain(self, ranges, plane, chip_at):
        some = [
            jnp.take(jnp.take(value.reshape(self.tokens, self.chips, 2, width), plane, axis=2), chip_at, axis=1)
            for value, width in ((self.acts, self.wide_in), (self.grads, self.wide_out))
        ]
        some = jnp.concatenate(some, axis=2)
        return [some[:, begin:end].reshape(self.tokens, -1) for begin, end in ranges]


def rank_halves(info, left, right):
    half_rank = left.shape[1] // 2
    widths = [factor.shape[2] // (2 * CHAINS * NEAR) for factor in (left, right)]
    wide = sum(widths)

    def kernel(where, left, right, away, kept, sems):
        copies = []
        for side, out in enumerate((away, kept)):
            half = where[CORE] if side else 1 - where[CORE]
            rows = pl.ds(pl.multiple_of(half * half_rank, half_rank), half_rank)
            for chunk in range(NEAR):
                for chain in range(CHAINS):
                    number = (where[PART] * CHAINS + chain) * NEAR + chunk
                    for source, width, begin in zip((left, right), widths, (0, widths[0])):
                        copies.append(
                            pltpu.make_async_copy(
                                source.at[0, rows, lanes_at(number, width)],
                                out.at[chunk, chain, :, pl.ds(begin, width)],
                                sems.at[len(copies)],
                            )
                        )
        copy_all(copies)

    shape = (NEAR, CHAINS, half_rank, wide)
    return pl.pallas_call(
        kernel,
        in_specs=[SMEM] + [HBM] * 2,
        out_specs=[VMEM] * 2,
        out_shape=[pltpu.VMEM(shape, left.dtype)] * 2,
        scratch_shapes=[pltpu.SemaphoreType.DMA((4 * NEAR * CHAINS,))],
        compiler_params=pltpu.CompilerParams(vmem_limit_bytes=4 * MIB),
        cost_estimate=estimate(0, 8 * NEAR * CHAINS * half_rank * wide),
        name="rank_halves",
    )(info, in_hbm(left), in_hbm(right))


def messages_of(info, kept, received):
    def kernel(where, kept, received, *outs):
        for mask, out in enumerate(outs):
            chunk = (where[CHIP] % NEAR) ^ mask
            out[0] = kept[chunk]
            out[1] = received[chunk]

    shape = jax.ShapeDtypeStruct((2,) + kept.shape[1:], kept.dtype)
    return pl.pallas_call(
        kernel,
        in_specs=[SMEM, VMEM, VMEM],
        out_specs=[VMEM] * NEAR,
        out_shape=[shape] * NEAR,
        compiler_params=pltpu.CompilerParams(vmem_limit_bytes=4 * MIB),
        cost_estimate=estimate(0, 4 * 2 * kept.size),
        name="messages",
    )(info, kept, received)


def stage(info, bases, features, given, kept):
    shapes = [(basis.shape[0], basis.shape[1] // 2) for basis in bases]
    ranges = given + kept if features.aligned else []
    total = sum(end - begin for begin, end in ranges)
    plain = []
    if not features.aligned:
        chip_at = info[CHIP_AT : CHIP_AT + features.chips]
        plain = features.plain(given, 1 - info[PART], chip_at) + features.plain(kept, info[PART], chip_at)
        if not bases:
            return plain

    def kernel(where, acts, grads, *rest):
        sources, outs, (sems, more) = rest[: len(bases)], rest[len(bases) : -2], rest[-2:]
        copies = []
        moved = 0
        for num, out in enumerate(outs[len(bases) :]):
            plane = 1 - where[PART] if num < len(given) else where[PART]
            count = 2 * (ranges[num][1] - ranges[num][0])
            copies += features.copies(
                (acts, grads),
                [out],
                ranges[num : num + 1],
                plane,
                lambda spot: where[CHIP_AT + spot],
                more.at[pl.ds(moved, count)],
            )
            moved += count
        for num, (basis, shape) in enumerate(zip(sources, shapes)):
            copies.append(pltpu.make_async_copy(basis.at[:, lanes_at(where[PART], shape[1])], outs[num], sems.at[num]))
        copy_all(copies)

    results = pl.pallas_call(
        kernel,
        in_specs=[SMEM] + [HBM] * (2 + len(bases)),
        out_specs=[VMEM] * (len(bases) + len(ranges)),
        out_shape=[pltpu.VMEM(shape, features.kind) for shape in shapes] + features.shapes(ranges),
        scratch_shapes=[pltpu.SemaphoreType.DMA((2,)), pltpu.SemaphoreType.DMA((max(2 * total, 1),))],
        compiler_params=pltpu.CompilerParams(vmem_limit_bytes=4 * MIB),
        cost_estimate=estimate(0, 2 * sum(shape[0] * shape[1] for shape in shapes)),
        name="stage",
    )(info, *map(in_hbm, (features.acts, features.grads, *bases)))
    return list(results) + plain


def choose(info, queries, found):
    ranks, wide = found[0].shape[2:]
    chips = (info.shape[0] - CHIP_AT - queries) // 5

    def kernel(where, *rest):
        outs = rest[NEAR:]
        for query in range(queries):
            owner = where[CHIP_AT + chips + query]
            place = pl.ds(query * ranks, ranks)
            mask_of = (owner // 2) ^ where[CHIP]
            side = (owner % 2) ^ where[CORE]
            for chain, out in enumerate(outs):
                for mask in range(NEAR):

                    @pl.when(mask_of == mask)
                    def _():
                        out[place] = rest[mask][side, chain]

                @pl.when(mask_of >= NEAR)
                def _():
                    out[place] = jnp.zeros((ranks, wide), out.dtype)

    return pl.pallas_call(
        kernel,
        in_specs=[SMEM] + [VMEM] * NEAR,
        out_specs=[VMEM] * CHAINS,
        out_shape=[jax.ShapeDtypeStruct((queries * ranks, wide), found[0].dtype)] * CHAINS,
        compiler_params=pltpu.CompilerParams(vmem_limit_bytes=4 * MIB),
        cost_estimate=estimate(0, 4 * queries * ranks * wide * CHAINS),
        name="choose",
    )(info, *found)


def meet_halves(info, partial, met, crossed):
    def kernel(where, partial, met, crossed, out):
        @pl.when(where[CORE] == where[PART])
        def _():
            out[...] = (partial[...] + met[...].astype(jnp.float32)).astype(out.dtype)

        @pl.when(where[CORE] != where[PART])
        def _():
            out[...] = (crossed[...].astype(jnp.float32) + met[...].astype(jnp.float32)).astype(out.dtype)

    return pl.pallas_call(
        kernel,
        in_specs=[SMEM] + [VMEM] * 3,
        out_specs=VMEM,
        out_shape=jax.ShapeDtypeStruct(met.shape, met.dtype),
        compiler_params=pltpu.CompilerParams(vmem_limit_bytes=4 * MIB),
        cost_estimate=estimate(2 * partial.size, 10 * partial.size),
        name="meet_halves",
    )(info, partial, met, crossed)


def rotate(info, chain, own, sib, bases, total):
    last = chain == CHAINS - 1
    ranks, wide = own[0].shape
    wide_in = bases[0].shape[1] // (CHAINS * NEAR)
    widths = (wide_in, wide - wide_in)
    rows_in = bases[0].shape[0]
    height = rows_in + bases[1].shape[0]
    spans = ((0, rows_in, 0, wide_in), (rows_in, height, wide_in, wide))

    def kernel(where, *rest):
        own_here, sib_here, bases_here, rest = rest[:NEAR], rest[NEAR : 2 * NEAR], rest[2 * NEAR :][:2], rest[2 * NEAR + 2 :]
        if total is not None:
            start, rest = rest[0], rest[1:]
        outs, acc = rest[:-1], rest[-1]
        for spot in range(NEAR):
            factor = jnp.concatenate([own_here[spot][...], sib_here[SIBLING[spot]][...]], axis=0)
            for num, (from_row, to_row, from_lane, to_lane) in enumerate(spans):
                block = bases_here[num][:, lanes_at(chain * NEAR + where[NEAR_AT + spot], widths[num])]
                value = dot_rows(block, factor[:, from_lane:to_lane])
                if spot:
                    value = value + acc[from_row:to_row]
                elif total is not None:
                    value = value + start[from_row:to_row]
                acc[from_row:to_row] = value
        if last:
            value = acc[...].T
            outs[0][...] = value[:ranks]
            outs[1][...] = jnp.where(where[CORE] == where[PART], value[ranks:], value[:ranks]).astype(jnp.bfloat16)
            outs[2][...] = value[ranks:].astype(jnp.bfloat16)
        else:
            outs[0][...] = acc[...]

    if last:
        shapes = [jax.ShapeDtypeStruct((ranks, height), kind) for kind in (jnp.float32, jnp.bfloat16, jnp.bfloat16)]
    else:
        shapes = [jax.ShapeDtypeStruct((height, 2 * ranks), jnp.float32)]
    given = [] if total is None else [total]
    moved = sum((to_row - from_row) * (to_lane - from_lane) for from_row, to_row, from_lane, to_lane in spans)
    results = pl.pallas_call(
        kernel,
        in_specs=[SMEM] + [VMEM] * (2 * NEAR + 2 + len(given)),
        out_specs=[VMEM] * len(shapes),
        out_shape=shapes,
        scratch_shapes=[pltpu.VMEM((height, 2 * ranks), jnp.float32)],
        compiler_params=pltpu.CompilerParams(vmem_limit_bytes=4 * MIB),
        cost_estimate=estimate(4 * ranks * NEAR * moved, 2 * NEAR * moved),
        name="rotate",
    )(info, *own, *sib, *map(in_vmem, bases), *given)
    return tuple(results) if last else results[0]


def project(arrays, own, sib, wide_in, tokens_in, pieces, kind):
    chips = len(own)
    ranks, wide = arrays[0].shape[1:]
    tokens = tokens_in[0].shape[0]
    if wide_in % 128 or wide % 128:
        both = jnp.stack([jnp.concatenate([arrays[i][m], arrays[j][n]], axis=0) for (i, m), (j, n) in zip(own, sib)])
        held = jnp.concatenate(tokens_in, axis=1).reshape(tokens, chips, wide)
        return [
            jnp.einsum("tgf,gcf->tc", held[:, :, lanes], both[:, :, lanes], preferred_element_type=jnp.float32).astype(
                kind
            )
            for lanes in (slice(0, wide_in), slice(wide_in, wide))
        ]

    def kernel(*rest):
        factors, rest = rest[: len(arrays)], rest[len(arrays) :]
        held, rest = rest[: len(tokens_in)], rest[len(tokens_in) :]
        outs, acc = rest[:2], rest[2]
        for source, (first, last) in zip(held, pieces):
            for spot in range(first, last):
                (i, m), (j, n) = own[spot], sib[spot]
                factor = jnp.concatenate([factors[i][m], factors[j][n]], axis=0)
                for num, (begin, end) in enumerate(((0, wide_in), (wide_in, wide))):
                    base = (spot - first) * wide
                    value = dot_rows(source[:, base + begin : base + end], factor[:, begin:end])
                    acc[num] = value if spot == 0 else acc[num] + value
        for num, out in enumerate(outs):
            out[...] = acc[num].astype(kind)

    return pl.pallas_call(
        kernel,
        in_specs=[VMEM] * (len(arrays) + len(tokens_in)),
        out_specs=[VMEM] * 2,
        out_shape=[jax.ShapeDtypeStruct((tokens, 2 * ranks), kind)] * 2,
        scratch_shapes=[pltpu.VMEM((2, tokens, 2 * ranks), jnp.float32)],
        compiler_params=pltpu.CompilerParams(vmem_limit_bytes=4 * MIB),
        cost_estimate=estimate(4 * tokens * ranks * chips * wide, 4 * ranks * chips * wide),
        name="project",
    )(*arrays, *map(in_vmem, tokens_in))


def score(info, slots, mine, back, queries, rank_count):
    tokens, columns = mine[0].shape
    half_rank = rank_count // 2
    lanes = slots * queries
    lengths_at = info.shape[0] - 2 * slots

    def kernel(where, mine_in, mine_out, back, out):
        live = lax.broadcasted_iota(jnp.int32, (tokens, columns), 0) < where[lengths_at + where[lengths_at + slots + where[ME]]]
        products = (mine_in[...] + back[0].astype(jnp.float32)) * (mine_out[...] + back[1].astype(jnp.float32))
        sums = jnp.sum(jnp.where(live, products, 0.0), axis=0, keepdims=True)
        query_of = lax.broadcasted_iota(jnp.int32, (1, columns), 1) % (queries * half_rank) // half_rank
        lane = lax.broadcasted_iota(jnp.int32, (1, lanes), 1)
        row = jnp.zeros((1, lanes), jnp.float32)
        for query in range(queries):
            value = jnp.sum(jnp.where(query_of == query, sums, 0.0), axis=1, keepdims=True) / rank_count
            row = jnp.where(lane == where[ME] * queries + query, value, row)
        out[...] = row

    return pl.pallas_call(
        kernel,
        in_specs=[SMEM] + [VMEM] * 3,
        out_specs=VMEM,
        out_shape=jax.ShapeDtypeStruct((1, lanes), jnp.float32),
        compiler_params=pltpu.CompilerParams(vmem_limit_bytes=4 * MIB),
        cost_estimate=estimate(6 * tokens * columns, 12 * tokens * columns),
        name="score",
    )(info, *mine, back)


def own_sequence(info, slots, held, queries):
    plan_at = info.shape[0] - slots

    def kernel(where, held, out):
        slot = jnp.int32(0)
        for number in range(slots):
            slot = jnp.where(where[plan_at + number] == where[ME], number, slot)
        lane = lax.broadcasted_iota(jnp.int32, held.shape, 1)
        out_lane = lax.broadcasted_iota(jnp.int32, (1, queries), 1)
        row = jnp.zeros((1, queries), jnp.float32)
        for query in range(queries):
            value = jnp.sum(jnp.where(lane == slot * queries + query, held[...], 0.0), axis=1, keepdims=True)
            row = jnp.where(out_lane == query, value, row)
        out[...] = row

    return pl.pallas_call(
        kernel,
        in_specs=[SMEM, VMEM],
        out_specs=VMEM,
        out_shape=jax.ShapeDtypeStruct((1, queries), jnp.float32),
        compiler_params=pltpu.CompilerParams(vmem_limit_bytes=4 * MIB),
        cost_estimate=estimate(0, 4 * held.size),
        name="own_sequence",
    )(info, held)


def shards(
    activations,
    output_grads,
    basis_in,
    basis_out,
    query_left,
    query_right,
    owners,
    lengths,
    slot_plan,
):
    count = lax.axis_size("blk")
    chips = count // 2
    bits = chips.bit_length() - 1
    me = lax.axis_index("blk")
    part = lax.axis_index("parts")
    core, chip = me % 2, me // 2
    seqs_here, max_length, width_in = activations.shape
    num_queries = owners.shape[0]
    rank_count = query_left.shape[1]
    half_rank = rank_count // 2
    ranks = num_queries * half_rank
    tokens = seqs_here * max_length
    acts = activations.reshape(tokens, width_in)
    grads = output_grads.reshape(tokens, -1)
    across = [(p * count + i, (1 - p) * count + i) for p in range(2) for i in range(count)]

    def to_chip(value, mask):
        return lax.ppermute(value, "blk", [(i, i ^ (2 * mask)) for i in range(count)])

    def along(value, first, second):
        return lax.ppermute(value, "blk", [(i, i ^ (2 << (second if i % 2 else first))) for i in range(count)])

    def to_core(value):
        return lax.ppermute(value, "blk", [(i, i ^ 1) for i in range(count)])

    def near_gather(value, before=None):
        first = along(value, 0, 1)
        if before is not None:
            (first,) = after((first,), before)
        low = jnp.concatenate([value, first], axis=0)
        return low, along(low, 1, 0)

    def near_pieces(value):
        first = along(value, 0, 1)
        second = along(value, 1, 0)
        return [value, first, second, along(first, 1, 0)]

    near_at = jnp.where(core == 0, jnp.array(NEAR_MASKS[0], jnp.int32), jnp.array(NEAR_MASKS[1], jnp.int32)) ^ (
        chip % NEAR
    )
    sources = [[0]]
    for bit in range(2, bits):
        sources.append([mask | (1 << bit) for group in sources for mask in group])
    orders = [[far | near for group in sources for near in NEAR_MASKS[side] for far in group] for side in range(2)]
    chip_at = jnp.where(core == 0, jnp.array(orders[0], jnp.int32), jnp.array(orders[1], jnp.int32)) ^ chip

    (info,) = lax.optimization_barrier((jnp.concatenate([jnp.stack([part, core, chip, me]), near_at, chip_at]),))

    far = (NEAR, chips)

    away, kept = rank_halves(info, query_left, query_right)
    more = jnp.concatenate([info, *after((owners, lengths, slot_plan), away)])
    received, more = lax.optimization_barrier((to_core(away), more))
    messages = messages_of(info, kept, received)

    every = range(CHAINS)
    found = [to_chip(value, mask) if mask else value for mask, value in enumerate(messages)]
    dense = list(choose(more, num_queries, found))
    early = Features(*after((acts, grads), messages[0]), chips)
    (given_away,) = stage(info, [], early, [far], [])
    late = lax.optimization_barrier((acts, grads, basis_in, basis_out, given_away))
    given_away = lax.ppermute(given_away, EVERYONE, across)
    *bases, other_tokens, own_tokens = stage(
        info, late[2:4], Features(late[0], late[1], chips), [(0, NEAR)], [(0, chips)]
    )
    for bit in range(bits - 1, 1, -1):
        arrived = [to_chip(dense[chain], 1 << bit) for chain in every]
        if bit == bits - 1:
            arrived[0], own_tokens, other_tokens, *bases = lax.optimization_barrier(
                (arrived[0], own_tokens, other_tokens, *bases)
            )
        for chain in every:
            if chain:
                (arrived[chain],) = after((arrived[chain],), dense[chain - 1])
            dense[chain] = dense[chain] + arrived[chain]
    total = None
    for chain in every:
        own = near_pieces(dense[chain])
        if chain:
            own[1:3] = after(own[1:3], first)
            (own[3],) = after((own[3],), total)
        first = own[1]
        total = rotate(info, chain, own, [to_core(value) for value in own], bases, total)

    partial, first, second = total

    def number(p, i, q, j):
        return p * count + i, q * count + j

    meet = [number(p, i, *((p, i ^ 1) if i % 2 == p else (1 - p, i))) for p in range(2) for i in range(count)]
    cross = [number(p, i, 1 - p, i ^ 1) for p in range(2) for i in range(count) if i % 2 != p]
    met, crossed = lax.ppermute(first, EVERYONE, meet), lax.ppermute(second, EVERYONE, cross)
    piece = meet_halves(info, partial, met, crossed)

    held = [piece[None]]
    for bit in range(2, bits):
        held.append(to_chip(held[0] if len(held) == 1 else jnp.concatenate(held, axis=0), 1 << bit))
    arrays, own, sib = [], [], []
    for num, source in enumerate(held):
        if num == 1:
            given_away, source = lax.optimization_barrier((given_away, source))
        low, high = near_gather(source)
        if num == 0:
            crossing = [lax.ppermute(value, EVERYONE, across) for value in (low, high)]
        entries = source.shape[0]
        for step in range(NEAR):
            for places, at, base in ((own, step, 0), (sib, SIBLING[step], 2)):
                places += [(4 * num + base + at // 2, at % 2 * entries + entry) for entry in range(entries)]
        sib_high = to_core(high)
        if num == 1:
            early_sib = to_core(crossing[0])
            sib_high, early_sib, *crossing = lax.optimization_barrier((sib_high, early_sib, *crossing))
        arrays += [low, high, to_core(low), sib_high]

    wide_in = basis_in.shape[0]
    theirs = project(arrays, own[NEAR:], sib[NEAR:], wide_in, [given_away], [(0, chips - NEAR)], jnp.bfloat16)
    back = lax.ppermute(jnp.stack(theirs), EVERYONE, across)
    for places, base in ((own, 0), (sib, 2)):
        places += [(len(arrays) + number, place) for number, place in places[:NEAR]]
    late = after(crossing[1:], theirs[0])
    arrays += crossing + [early_sib] + [to_core(value) for value in late]
    kept = [(0, chips), (chips, chips + NEAR)]
    mine = project(arrays, own, sib, wide_in, [own_tokens, other_tokens], kept, jnp.float32)

    held = score(more, count, mine, back, num_queries, rank_count)
    for bit in range(bits + 1):
        held = held + lax.ppermute(held, "blk", [(i, i ^ (1 << bit)) for i in range(count)])
    return own_sequence(more, count, held, num_queries)


def solution(mesh):
    placed = (
        P(("parts", "blk"), None, None),
        P(("parts", "blk"), None, None),
        P("blk", None),
        P("blk", None),
        P("blk", None, None),
        P("blk", None, None),
        P(),
        P("parts"),
        P("parts"),
    )
    return jax.shard_map(
        shards, mesh=mesh, in_specs=placed, out_specs=P(("parts", "blk"), None), check_vma=False
    )
```

time: 111 us -> 107 us (0.964)
  waiting for transfers between devices: 39.7 us -> 48.9 us
  starting transfers between devices: 43 us -> 34.2 us
  Pallas kernels: 25.6 us -> 22.2 us
    ppermute x12 -> x10, waiting for transfers between devices: 11.4 us -> 18.5 us  [along(): lax.ppermute(value, 'blk', [(i, i ^ 2 << (second if i % 2 else first)) fo...]
    ppermute x9 -> x6, starting transfers between devices: 14.6 us -> 7.63 us  [to_chip(): return lax.ppermute(value, 'blk', [(i, i ^ 2 * mask) for i in range(count)])]
    ppermute x9 -> x6, waiting for transfers between devices: 4.73 us -> 10.1 us  [to_chip(): return lax.ppermute(value, 'blk', [(i, i ^ 2 * mask) for i in range(count)])]
    pallas_call x13 -> x10, Pallas kernels: 20.4 us -> 16.9 us  [the longest x2 9.28 us: stage(): pl.pallas_call(kernel, in_specs=[SMEM] + [HBM] * (2 + len(bases)), out_sp...]
    ppermute x5, waiting for transfers between devices: 8.86 us -> 7.05 us  [the longest x1 4.33 us: shards(): lax.ppermute(first, EVERYONE, meet)]
    ppermute x17 -> x15, waiting for transfers between devices: 4.19 us -> 2.45 us  [to_core(): return lax.ppermute(value, 'blk', [(i, i ^ 1) for i in range(count)])]
    ppermute x17 -> x15, starting transfers between devices: 3.29 us -> 4.95 us  [to_core(): return lax.ppermute(value, 'blk', [(i, i ^ 1) for i in range(count)])]
    ppermute x12 -> x10, starting transfers between devices: 11.7 us -> 10.4 us  [along(): lax.ppermute(value, 'blk', [(i, i ^ 2 << (second if i % 2 else first)) fo...]
  transfers between devices with their start and end apart: 48 -> 41, of which waited for: 23 -> 21; matrix products, arithmetic and copies ran while one was open for 1% -> 1% of each run, Pallas kernels for 17% -> 16%
where the time goes in v5:
time: 107 us
  waiting for transfers between devices  48.9 us (46%)
  starting transfers between devices  34.2 us (32%)
  Pallas kernels  22.2 us (21%)
    ppermute x10, waiting for transfers between devices, along(): lax.ppermute(value, 'blk', [(i, i ^ 2 << (second if i % 2 else first)) fo...  18.5 us
    ppermute x10, starting transfers between devices, along(): lax.ppermute(value, 'blk', [(i, i ^ 2 << (second if i % 2 else first)) fo...  10.4 us
    ppermute x6, waiting for transfers between devices, to_chip(): return lax.ppermute(value, 'blk', [(i, i ^ 2 * mask) for i in range(count)])  10.1 us
    pallas_call x2, Pallas kernels, stage(): pl.pallas_call(kernel, in_specs=[SMEM] + [HBM] * (2 + len(bases)), out_sp...  9.28 us
    ppermute x4, waiting for transfers between devices, shards(): lax.ppermute(held, 'blk', [(i, i ^ 1 << bit) for i in range(count)])  8.86 us
    ppermute x6, starting transfers between devices, to_chip(): return lax.ppermute(value, 'blk', [(i, i ^ 2 * mask) for i in range(count)])  7.63 us
    pallas_call x2, Pallas kernels, rotate(): pl.pallas_call(kernel, in_specs=[SMEM] + [VMEM] * (2 * NEAR + 2 + len(giv...  5.23 us
    ppermute x15, starting transfers between devices, to_core(): return lax.ppermute(value, 'blk', [(i, i ^ 1) for i in range(count)])  4.95 us
  transfers between devices with their start and end apart: 41, of which 21 were waited for; matrix products, arithmetic and copies ran while one was open for 1% of the time, Pallas kernels for 16%

profile of v5, /device:TPU:0, one launch (start us, length us, event | category | flops | bytes accessed | tf_op | source)
XLA Modules:
  0.0 106.5 jit_solution(18195588879876419951)
XLA Ops:
  0.1 1.9 %rank_halves.1 = (bf16[4,2,16,1152]{3,2,1,0:T(8,128)(2,1)S(1)}, bf16[4,2,16,1152]{3,2,1,0:T(8,128)(2,1)S(1)}) custom-call(s32[16]{0:T(128)S(1)} %concatenate.12.where, bf16[1,32,4096]{2,1,0:T(8,128)(2,1)} %left.1, bf16[1,32,14336]{2,1,0:T(8,128)(2,1)} %right.1), custom_call_target="tpu_custom_call" | custom-call | bytes 1179648 | tf_op jit(solution)/shard_map/rank_halves/pallas_call | solution.py:115
  2.0 1.8 %collective-permute-start = (bf16[4,2,16,1152]{3,2,1,0:T(8,128)(2,1)S(1)}, bf16[4,2,16,1152]{3,2,1,0:T(8,128)(2,1)S(1)}, u32[]{:S(2)}, u32[]{:S(2)}) collective-permute-start(bf16[4,2,16,1152]{3,2,1,0:T(8,128)(2,1)S(1)} %get-tuple-element.51), channel_id=1, source_target_pairs={{0,1},{1,0},{2,3},{3,2},{4,5},{5,4},{6,7},{7,6},{8,9},{9,8},{10,11... | collective-permute-start | bytes 884744 | tf_op jit(solution)/shard_map/ppermute | solution.py:425
  3.9 0.8 pad_add_fusion.where
  5.7 2.4 %collective-permute-start.1 = (bf16[2,2,16,1152]{3,2,1,0:T(8,128)(2,1)S(1)}, bf16[2,2,16,1152]{3,2,1,0:T(8,128)(2,1)S(1)}, u32[]{:S(2)}, u32[]{:S(2)}) collective-permute-start(bf16[2,2,16,1152]{3,2,1,0:T(8,128)(2,1)S(1)} %get-tuple-element.59), channel_id=1, source_target_pairs={{0,2},{1,3},{2,0},{3,1},{4,6},{5,7},{6,4},{7,5},{8,10},{9,11},{10,... | collective-permute-start | bytes 442376 | tf_op jit(solution)/shard_map/ppermute | solution.py:419
  8.1 1.6 %collective-permute-start.2 = (bf16[2,2,16,1152]{3,2,1,0:T(8,128)(2,1)S(1)}, bf16[2,2,16,1152]{3,2,1,0:T(8,128)(2,1)S(1)}, u32[]{:S(2)}, u32[]{:S(2)}) collective-permute-start(bf16[2,2,16,1152]{3,2,1,0:T(8,128)(2,1)S(1)} %get-tuple-element.60), channel_id=1, source_target_pairs={{0,4},{1,5},{2,6},{3,7},{4,0},{5,1},{6,2},{7,3},{8,12},{9,13},{10,... | collective-permute-start | bytes 442376 | tf_op jit(solution)/shard_map/ppermute | solution.py:419
  9.7 2.0 %stage.2 = bf16[160,4608]{1,0:T(8,128)(2,1)S(1)} custom-call(s32[16]{0:T(128)S(1)} %concatenate.12.where, bf16[160,4096]{1,0:T(8,128)(2,1)} %bitcast.16, bf16[160,14336]{1,0:T(8,128)(2,1)} %bitcast.14), custom_call_target="tpu_custom_call" | custom-call | tf_op jit(solution)/shard_map/stage/pallas_call | solution.py:177
  11.7 1.9 %collective-permute-start.26 = (bf16[160,4608]{1,0:T(8,128)(2,1)S(1)}, bf16[160,4608]{1,0:T(8,128)(2,1)S(1)}, u32[]{:S(2)}, u32[]{:S(2)}) collective-permute-start(bf16[160,4608]{1,0:T(8,128)(2,1)S(1)} %stage.2), channel_id=1, source_target_pairs={{0,16},{1,17},{2,18},{3,19},{4,20},{5,21},{6,22},{7,23},{8,24},{9,... | collective-permute-start | bytes 4423688 | tf_op jit(solution)/shard_map/ppermute | solution.py:463
  13.6 1.2 %collective-permute-done.2.rest_2_ = bf16[2,2,16,1152]{3,2,1,0:T(8,128)(2,1)S(1)} collective-permute-done((bf16[2,2,16,1152]{3,2,1,0:T(8,128)(2,1)S(1)}, bf16[2,2,16,1152]{3,2,1,0:T(8,128)(2,1)S(1)}, u32[]{:S(2)}, u32[]{:S(2)}) %collective-permute-start.2) | collective-permute-done | bytes 147488 | tf_op jit(solution)/shard_map/ppermute | solution.py:419
  14.8 2.1 %collective-permute-done.3.rest_3_ = bf16[2,2,16,1152]{3,2,1,0:T(8,128)(2,1)S(1)} collective-permute-done((bf16[2,2,16,1152]{3,2,1,0:T(8,128)(2,1)S(1)}, bf16[2,2,16,1152]{3,2,1,0:T(8,128)(2,1)S(1)}, u32[]{:S(2)}, u32[]{:S(2)}) %collective-permute-start.3) | collective-permute-done | bytes 147488 | tf_op jit(solution)/shard_map/ppermute | solution.py:419
  16.9 0.8 choose.1
  17.7 2.8 %collective-permute-start.5 = (bf16[64,1152]{1,0:T(8,128)(2,1)S(1)}, bf16[64,1152]{1,0:T(8,128)(2,1)S(1)}, u32[]{:S(2)}, u32[]{:S(2)}) collective-permute-start(bf16[64,1152]{1,0:T(8,128)(2,1)S(1)} %get-tuple-element.63), channel_id=1, source_target_pairs={{0,8},{1,9},{2,10},{3,11},{4,12},{5,13},{6,14},{7,15},{8,0},{9,1},... | collective-permute-start | bytes 442376 | tf_op jit(solution)/shard_map/ppermute | solution.py:419
  20.5 7.3 %stage.3 = (bf16[256,2048]{1,0:T(8,128)(2,1)S(1)}, bf16[896,7168]{1,0:T(8,128)(2,1)S(1)}, bf16[160,4608]{1,0:T(8,128)(2,1)S(1)}, bf16[160,9216]{1,0:T(8,128)(2,1)S(1)}) custom-call(s32[16]{0:T(128)S(1)} %concatenate.12.where, bf16[160,4096]{1,0:T(8,128)(2,1)} %bitcast.17, bf16[160,14336]{1,0:T(8,128)(2,1)} %bitcast.15, bf16[256,4096]{1,0:T(8,128)(2,1)} %rest_0_, ...), custom_call_target="tpu_custom_call" | custom-call | bytes 13893632 | tf_op jit(solution)/shard_map/stage/pallas_call | solution.py:177
  28.2 1.7 %collective-permute-start.8 = (bf16[64,1152]{1,0:T(8,128)(2,1)S(1)}, bf16[64,1152]{1,0:T(8,128)(2,1)S(1)}, u32[]{:S(2)}, u32[]{:S(2)}) collective-permute-start(bf16[64,1152]{1,0:T(8,128)(2,1)S(1)} %add.28.rest_0_), channel_id=1, source_target_pairs={{0,2},{1,5},{2,0},{3,7},{4,6},{5,1},{6,4},{7,3},{8,10},{9,13},{10,... | collective-permute-start | bytes 442376 | tf_op jit(solution)/shard_map/ppermute | solution.py:422
  29.9 1.6 %collective-permute-start.10 = (bf16[64,1152]{1,0:T(8,128)(2,1)S(1)}, bf16[64,1152]{1,0:T(8,128)(2,1)S(1)}, u32[]{:S(2)}, u32[]{:S(2)}) collective-permute-start(bf16[64,1152]{1,0:T(8,128)(2,1)S(1)} %add.28.rest_0_), channel_id=1, source_target_pairs={{0,4},{1,3},{2,6},{3,1},{4,0},{5,7},{6,2},{7,5},{8,12},{9,11},{10,... | collective-permute-start | bytes 442376 | tf_op jit(solution)/shard_map/ppermute | solution.py:422
  31.5 5.2 %collective-permute-done.4 = bf16[64,1152]{1,0:T(8,128)(2,1)S(1)} collective-permute-done((bf16[64,1152]{1,0:T(8,128)(2,1)S(1)}, bf16[64,1152]{1,0:T(8,128)(2,1)S(1)}, u32[]{:S(2)}, u32[]{:S(2)}) %collective-permute-start.4) | collective-permute-done | bytes 147488 | tf_op jit(solution)/shard_map/ppermute | solution.py:419
  36.7 1.5 %collective-permute-start.6 = (bf16[64,1152]{1,0:T(8,128)(2,1)S(1)}, bf16[64,1152]{1,0:T(8,128)(2,1)S(1)}, u32[]{:S(2)}, u32[]{:S(2)}) collective-permute-start(bf16[64,1152]{1,0:T(8,128)(2,1)S(1)} %add.29.rest_0_), channel_id=1, source_target_pairs={{0,2},{1,5},{2,0},{3,7},{4,6},{5,1},{6,4},{7,3},{8,10},{9,13},{10,... | collective-permute-start | bytes 442376 | tf_op jit(solution)/shard_map/ppermute | solution.py:422
  38.3 2.0 %collective-permute-start.7 = (bf16[64,1152]{1,0:T(8,128)(2,1)S(1)}, bf16[64,1152]{1,0:T(8,128)(2,1)S(1)}, u32[]{:S(2)}, u32[]{:S(2)}) collective-permute-start(bf16[64,1152]{1,0:T(8,128)(2,1)S(1)} %add.29.rest_0_), channel_id=1, source_target_pairs={{0,4},{1,3},{2,6},{3,1},{4,0},{5,7},{6,2},{7,5},{8,12},{9,11},{10,... | collective-permute-start | bytes 442376 | tf_op jit(solution)/shard_map/ppermute | solution.py:422
  40.3 1.9 %collective-permute-done.6.rest_1_ = bf16[64,1152]{1,0:T(8,128)(2,1)S(1)} collective-permute-done((bf16[64,1152]{1,0:T(8,128)(2,1)S(1)}, bf16[64,1152]{1,0:T(8,128)(2,1)S(1)}, u32[]{:S(2)}, u32[]{:S(2)}) %collective-permute-start.6) | collective-permute-done | bytes 147488 | tf_op jit(solution)/shard_map/ppermute | solution.py:422
  42.2 1.2 %collective-permute-done.11.rest_3_ = bf16[64,1152]{1,0:T(8,128)(2,1)S(1)} collective-permute-done((bf16[64,1152]{1,0:T(8,128)(2,1)S(1)}, bf16[64,1152]{1,0:T(8,128)(2,1)S(1)}, u32[]{:S(2)}, u32[]{:S(2)}) %collective-permute-start.11) | collective-permute-done | bytes 147488 | tf_op jit(solution)/shard_map/ppermute | solution.py:422
  43.4 1.6 %collective-permute-done.7.rest_2_ = bf16[64,1152]{1,0:T(8,128)(2,1)S(1)} collective-permute-done((bf16[64,1152]{1,0:T(8,128)(2,1)S(1)}, bf16[64,1152]{1,0:T(8,128)(2,1)S(1)}, u32[]{:S(2)}, u32[]{:S(2)}) %collective-permute-start.7) | collective-permute-done | bytes 147488 | tf_op jit(solution)/shard_map/ppermute | solution.py:422
  46.0 2.6 %rotate.2.rest_10_ = f32[1152,128]{1,0:T(8,128)S(1)} custom-call(s32[16]{0:T(128)S(1)} %concatenate.12.where, bf16[64,1152]{1,0:T(8,128)(2,1)S(1)} %add.28.rest_0_, bf16[64,1152]{1,0:T(8,128)(2,1)S(1)} %collective-permute-done.8.rest_1_, bf16[64,1152]{1,0:T(8,128)(2,1)S(1)} %collective-permute-done.10.rest_2_, ...), custom_call_target="tpu_custom_call" | custom-call | flops 889192448 | bytes 6946816 | tf_op jit(solution)/shard_map/rotate/pallas_call | solution.py:282
  48.6 1.5 %collective-permute-done.9.rest_3_ = bf16[64,1152]{1,0:T(8,128)(2,1)S(1)} collective-permute-done((bf16[64,1152]{1,0:T(8,128)(2,1)S(1)}, bf16[64,1152]{1,0:T(8,128)(2,1)S(1)}, u32[]{:S(2)}, u32[]{:S(2)}) %collective-permute-start.9) | collective-permute-done | bytes 147488 | tf_op jit(solution)/shard_map/ppermute | solution.py:422
  50.2 1.3 %collective-permute-done.19.rest_7_ = bf16[64,1152]{1,0:T(8,128)(2,1)S(1)} collective-permute-done((bf16[64,1152]{1,0:T(8,128)(2,1)S(1)}, bf16[64,1152]{1,0:T(8,128)(2,1)S(1)}, u32[]{:S(2)}, u32[]{:S(2)}) %collective-permute-start.19) | collective-permute-done | bytes 147488 | tf_op jit(solution)/shard_map/ppermute | solution.py:425
  51.5 2.7 %rotate.3 = (f32[64,1152]{1,0:T(8,128)S(1)}, bf16[64,1152]{1,0:T(8,128)(2,1)S(1)}, bf16[64,1152]{1,0:T(8,128)(2,1)S(1)}) custom-call(s32[16]{0:T(128)S(1)} %concatenate.12.where, bf16[64,1152]{1,0:T(8,128)(2,1)S(1)} %add.29.rest_0_, bf16[64,1152]{1,0:T(8,128)(2,1)S(1)} %collective-permute-done.6.rest_1_, ...), custom_call_target="tpu_custom_call" | custom-call | flops 889192448 | bytes 6946816 | tf_op jit(solution)/shard_map/rotate/pallas_call | solution.py:282
  54.4 0.7 collective-permute-start.21
  55.0 4.3 %collective-permute-done.20.met = bf16[64,1152]{1,0:T(8,128)(2,1)S(1)} collective-permute-done((bf16[64,1152]{1,0:T(8,128)(2,1)S(1)}, bf16[64,1152]{1,0:T(8,128)(2,1)S(1)}, u32[]{:S(2)}, u32[]{:S(2)}) %collective-permute-start.20) | collective-permute-done | bytes 147488 | tf_op jit(solution)/shard_map/ppermute | solution.py:493
  59.9 0.7 collective-permute-start.22
  61.0 4.1 %collective-permute-done.22 = bf16[1,64,1152]{2,1,0:T(8,128)(2,1)S(1)} collective-permute-done((bf16[1,64,1152]{2,1,0:T(8,128)(2,1)S(1)}, bf16[1,64,1152]{2,1,0:T(8,128)(2,1)S(1)}, u32[]{:S(2)}, u32[]{:S(2)}) %collective-permute-start.22) | collective-permute-done | bytes 147488 | tf_op jit(solution)/shard_map/ppermute | solution.py:422
  65.2 3.4 %collective-permute-start.32 = (bf16[2,64,1152]{2,1,0:T(8,128)(2,1)S(1)}, bf16[2,64,1152]{2,1,0:T(8,128)(2,1)S(1)}, u32[]{:S(2)}, u32[]{:S(2)}) collective-permute-start(bf16[2,64,1152]{2,1,0:T(8,128)(2,1)S(1)} %pad_maximum_fusion.rest_0_), channel_id=1, source_target_pairs={{0,16},{1,17},{2,18},{3,19},{4,20},{5,21},{6,22},{7,23},{8,24},{9,... | collective-permute-start | bytes 884744 | tf_op jit(solution)/shard_map/ppermute | solution.py:505
  69.1 1.7 %collective-permute-done.27 = bf16[1,64,1152]{2,1,0:T(8,128)(2,1)S(1)} collective-permute-done((bf16[1,64,1152]{2,1,0:T(8,128)(2,1)S(1)}, bf16[1,64,1152]{2,1,0:T(8,128)(2,1)S(1)}, u32[]{:S(2)}, u32[]{:S(2)}) %collective-permute-start.27) | collective-permute-done | bytes 147488 | tf_op jit(solution)/shard_map/ppermute | solution.py:419
  70.7 1.9 %collective-permute-start.28 = (bf16[1,64,1152]{2,1,0:T(8,128)(2,1)S(1)}, bf16[1,64,1152]{2,1,0:T(8,128)(2,1)S(1)}, u32[]{:S(2)}, u32[]{:S(2)}) collective-permute-start(bf16[1,64,1152]{2,1,0:T(8,128)(2,1)S(1)} %collective-permute-done.27), channel_id=1, source_target_pairs={{0,2},{1,5},{2,0},{3,7},{4,6},{5,1},{6,4},{7,3},{8,10},{9,13},{10,... | collective-permute-start | bytes 442376 | tf_op jit(solution)/shard_map/ppermute | solution.py:422
  72.6 3.2 %collective-permute-done.28 = bf16[1,64,1152]{2,1,0:T(8,128)(2,1)S(1)} collective-permute-done((bf16[1,64,1152]{2,1,0:T(8,128)(2,1)S(1)}, bf16[1,64,1152]{2,1,0:T(8,128)(2,1)S(1)}, u32[]{:S(2)}, u32[]{:S(2)}) %collective-permute-start.28) | collective-permute-done | bytes 147488 | tf_op jit(solution)/shard_map/ppermute | solution.py:422
  76.0 1.5 %collective-permute-start.33 = (bf16[2,64,1152]{2,1,0:T(8,128)(2,1)S(1)}, bf16[2,64,1152]{2,1,0:T(8,128)(2,1)S(1)}, u32[]{:S(2)}, u32[]{:S(2)}) collective-permute-start(bf16[2,64,1152]{2,1,0:T(8,128)(2,1)S(1)} %collective-permute-done.32.rest_8_), channel_id=1, source_target_pairs={{0,1},{1,0},{2,3},{3,2},{4,5},{5,4},{6,7},{7,6},{8,9},{9,8},{10,11... | collective-permute-start | bytes 884744 | tf_op jit(solution)/shard_map/ppermute | solution.py:425
  77.8 4.9 %collective-permute-done.29.rest_5_ = bf16[2,64,1152]{2,1,0:T(8,128)(2,1)S(1)} collective-permute-done((bf16[2,64,1152]{2,1,0:T(8,128)(2,1)S(1)}, bf16[2,64,1152]{2,1,0:T(8,128)(2,1)S(1)}, u32[]{:S(2)}, u32[]{:S(2)}) %collective-permute-start.29) | collective-permute-done | bytes 294944 | tf_op jit(solution)/shard_map/ppermute | solution.py:422
  83.7 2.7 %collective-permute-done.34.rest_9_ = bf16[2,64,1152]{2,1,0:T(8,128)(2,1)S(1)} collective-permute-done((bf16[2,64,1152]{2,1,0:T(8,128)(2,1)S(1)}, bf16[2,64,1152]{2,1,0:T(8,128)(2,1)S(1)}, u32[]{:S(2)}, u32[]{:S(2)}) %collective-permute-start.34) | collective-permute-done | bytes 294944 | tf_op jit(solution)/shard_map/ppermute | solution.py:505
  87.1 0.9 collective-permute-start.36
  88.1 0.6 collective-permute-done.35.rest_11_
  88.7 1.4 %project.3 = (f32[160,128]{1,0:T(8,128)S(1)}, f32[160,128]{1,0:T(8,128)S(1)}) custom-call(bf16[2,64,1152]{2,1,0:T(8,128)(2,1)S(1)} %pad_maximum_fusion.rest_0_, bf16[2,64,1152]{2,1,0:T(8,128)(2,1)S(1)} %collective-permute-done.23.rest_1_, bf16[2,64,1152]{2,1,0:T(8,128)(2,1)S(1)} %collective-permute-done.24.rest_2_, ...), custom_call_target="tpu_custom_call" | custom-call | flops 566231040 | bytes 3538944 | tf_op jit(solution)/shard_map/project/pallas_call | solution.py:324
  90.1 1.9 %collective-permute-done.36.back = bf16[2,160,128]{2,1,0:T(8,128)(2,1)S(1)} collective-permute-done((bf16[2,160,128]{2,1,0:T(8,128)(2,1)S(1)}, bf16[2,160,128]{2,1,0:T(8,128)(2,1)S(1)}, u32[]{:S(2)}, u32[]{:S(2)}) %collective-permute-start.36) | collective-permute-done | bytes 81952 | tf_op jit(solution)/shard_map/ppermute | solution.py:518
  92.0 0.7 score.1
  92.7 1.1 %collective-permute-done.37 = f32[1,64]{1,0:T(1,128)S(1)} collective-permute-done((f32[1,64]{1,0:T(1,128)S(1)}, f32[1,64]{1,0:T(1,128)S(1)}, u32[]{:S(2)}, u32[]{:S(2)}) %collective-permute-start.37) | collective-permute-done | bytes 288 | tf_op jit(solution)/shard_map/ppermute | solution.py:528
  93.8 1.3 %collective-permute-start.38 = (f32[1,64]{1,0:T(1,128)S(1)}, f32[1,64]{1,0:T(1,128)S(1)}, u32[]{:S(2)}, u32[]{:S(2)}) collective-permute-start(f32[1,64]{1,0:T(1,128)S(1)} %add.30), channel_id=1, source_target_pairs={{0,2},{1,3},{2,0},{3,1},{4,6},{5,7},{6,4},{7,5},{8,10},{9,11},{10,... | collective-permute-start | bytes 776 | tf_op jit(solution)/shard_map/ppermute | solution.py:528
  95.2 2.2 %collective-permute-done.38 = f32[1,64]{1,0:T(1,128)S(1)} collective-permute-done((f32[1,64]{1,0:T(1,128)S(1)}, f32[1,64]{1,0:T(1,128)S(1)}, u32[]{:S(2)}, u32[]{:S(2)}) %collective-permute-start.38) | collective-permute-done | bytes 288 | tf_op jit(solution)/shard_map/ppermute | solution.py:528
  97.4 1.0 collective-permute-start.39
  98.4 2.5 %collective-permute-done.39 = f32[1,64]{1,0:T(1,128)S(1)} collective-permute-done((f32[1,64]{1,0:T(1,128)S(1)}, f32[1,64]{1,0:T(1,128)S(1)}, u32[]{:S(2)}, u32[]{:S(2)}) %collective-permute-start.39) | collective-permute-done | bytes 288 | tf_op jit(solution)/shard_map/ppermute | solution.py:528
  100.9 1.4 %collective-permute-start.40 = (f32[1,64]{1,0:T(1,128)S(1)}, f32[1,64]{1,0:T(1,128)S(1)}, u32[]{:S(2)}, u32[]{:S(2)}) collective-permute-start(f32[1,64]{1,0:T(1,128)S(1)} %add.32), channel_id=1, source_target_pairs={{0,8},{1,9},{2,10},{3,11},{4,12},{5,13},{6,14},{7,15},{8,0},{9,1},... | collective-permute-start | bytes 776 | tf_op jit(solution)/shard_map/ppermute | solution.py:528
  102.4 3.0 %collective-permute-done.40 = f32[1,64]{1,0:T(1,128)S(1)} collective-permute-done((f32[1,64]{1,0:T(1,128)S(1)}, f32[1,64]{1,0:T(1,128)S(1)}, u32[]{:S(2)}, u32[]{:S(2)}) %collective-permute-start.40) | collective-permute-done | bytes 288 | tf_op jit(solution)/shard_map/ppermute | solution.py:528
  105.4 1.1 %own_sequence.1 = f32[1,4]{1,0:T(1,128)} custom-call(s32[52]{0:T(128)S(1)} %pad_add_fusion.where, f32[1,64]{1,0:T(1,128)S(1)} %add.33.held), custom_call_target="tpu_custom_call" | custom-call | bytes 256 | tf_op jit(solution)/shard_map/own_sequence/pallas_call | solution.py:380
  (60 shorter events, 6.5 us)
Async XLA Ops:
  2.0 3.0 %collective-permute-start = (bf16[4,2,16,1152]{3,2,1,0:T(8,128)(2,1)S(1)}, bf16[4,2,16,1152]{3,2,1,0:T(8,128)(2,1)S(1)}, u32[]{:S(2)}, u32[]{:S(2)}) collective-permute-start(bf16[4,2,16,1152]{3,2,1,0:T(8,128)(2,1)S(1)} %get-tuple-element.51), channel_id=1, source_target_pairs={{0,1},{1,0},{2,3},{3,2},{4,5},{5,4},{6,7},{7,6},{8,9},{9,8},{10,11... | collective-permute-start | bytes 884744 | tf_op jit(solution)/shard_map/ppermute | solution.py:425
  5.7 8.0 %collective-permute-start.1 = (bf16[2,2,16,1152]{3,2,1,0:T(8,128)(2,1)S(1)}, bf16[2,2,16,1152]{3,2,1,0:T(8,128)(2,1)S(1)}, u32[]{:S(2)}, u32[]{:S(2)}) collective-permute-start(bf16[2,2,16,1152]{3,2,1,0:T(8,128)(2,1)S(1)} %get-tuple-element.59), channel_id=1, source_target_pairs={{0,2},{1,3},{2,0},{3,1},{4,6},{5,7},{6,4},{7,5},{8,10},{9,11},{10,... | collective-permute-start | bytes 442376 | tf_op jit(solution)/shard_map/ppermute | solution.py:419
  8.1 6.7 %collective-permute-start.2 = (bf16[2,2,16,1152]{3,2,1,0:T(8,128)(2,1)S(1)}, bf16[2,2,16,1152]{3,2,1,0:T(8,128)(2,1)S(1)}, u32[]{:S(2)}, u32[]{:S(2)}) collective-permute-start(bf16[2,2,16,1152]{3,2,1,0:T(8,128)(2,1)S(1)} %get-tuple-element.60), channel_id=1, source_target_pairs={{0,4},{1,5},{2,6},{3,7},{4,0},{5,1},{6,2},{7,3},{8,12},{9,13},{10,... | collective-permute-start | bytes 442376 | tf_op jit(solution)/shard_map/ppermute | solution.py:419
  9.7 7.2 %collective-permute-start.3 = (bf16[2,2,16,1152]{3,2,1,0:T(8,128)(2,1)S(1)}, bf16[2,2,16,1152]{3,2,1,0:T(8,128)(2,1)S(1)}, u32[]{:S(2)}, u32[]{:S(2)}) collective-permute-start(bf16[2,2,16,1152]{3,2,1,0:T(8,128)(2,1)S(1)} %get-tuple-element.61), channel_id=1, source_target_pairs={{0,6},{1,7},{2,4},{3,5},{4,2},{5,3},{6,0},{7,1},{8,14},{9,15},{10,... | collective-permute-start | bytes 442376 | tf_op jit(solution)/shard_map/ppermute | solution.py:419
  11.7 59.0 %collective-permute-start.26 = (bf16[160,4608]{1,0:T(8,128)(2,1)S(1)}, bf16[160,4608]{1,0:T(8,128)(2,1)S(1)}, u32[]{:S(2)}, u32[]{:S(2)}) collective-permute-start(bf16[160,4608]{1,0:T(8,128)(2,1)S(1)} %stage.2), channel_id=1, source_target_pairs={{0,16},{1,17},{2,18},{3,19},{4,20},{5,21},{6,22},{7,23},{8,24},{9,... | collective-permute-start | bytes 4423688 | tf_op jit(solution)/shard_map/ppermute | solution.py:463
  17.7 10.5 %collective-permute-start.5 = (bf16[64,1152]{1,0:T(8,128)(2,1)S(1)}, bf16[64,1152]{1,0:T(8,128)(2,1)S(1)}, u32[]{:S(2)}, u32[]{:S(2)}) collective-permute-start(bf16[64,1152]{1,0:T(8,128)(2,1)S(1)} %get-tuple-element.63), channel_id=1, source_target_pairs={{0,8},{1,9},{2,10},{3,11},{4,12},{5,13},{6,14},{7,15},{8,0},{9,1},... | collective-permute-start | bytes 442376 | tf_op jit(solution)/shard_map/ppermute | solution.py:419
  27.8 8.9 %collective-permute-start.4 = (bf16[64,1152]{1,0:T(8,128)(2,1)S(1)}, bf16[64,1152]{1,0:T(8,128)(2,1)S(1)}, u32[]{:S(2)}, u32[]{:S(2)}) collective-permute-start(bf16[64,1152]{1,0:T(8,128)(2,1)S(1)} %get-tuple-element.62), channel_id=1, source_target_pairs={{0,8},{1,9},{2,10},{3,11},{4,12},{5,13},{6,14},{7,15},{8,0},{9,1},... | collective-permute-start | bytes 442376 | tf_op jit(solution)/shard_map/ppermute | solution.py:419
  28.2 10.1 %collective-permute-start.8 = (bf16[64,1152]{1,0:T(8,128)(2,1)S(1)}, bf16[64,1152]{1,0:T(8,128)(2,1)S(1)}, u32[]{:S(2)}, u32[]{:S(2)}) collective-permute-start(bf16[64,1152]{1,0:T(8,128)(2,1)S(1)} %add.28.rest_0_), channel_id=1, source_target_pairs={{0,2},{1,5},{2,0},{3,7},{4,6},{5,1},{6,4},{7,3},{8,10},{9,13},{10,... | collective-permute-start | bytes 442376 | tf_op jit(solution)/shard_map/ppermute | solution.py:422
  29.9 8.4 %collective-permute-start.10 = (bf16[64,1152]{1,0:T(8,128)(2,1)S(1)}, bf16[64,1152]{1,0:T(8,128)(2,1)S(1)}, u32[]{:S(2)}, u32[]{:S(2)}) collective-permute-start(bf16[64,1152]{1,0:T(8,128)(2,1)S(1)} %add.28.rest_0_), channel_id=1, source_target_pairs={{0,4},{1,3},{2,6},{3,1},{4,0},{5,7},{6,2},{7,5},{8,12},{9,11},{10,... | collective-permute-start | bytes 442376 | tf_op jit(solution)/shard_map/ppermute | solution.py:422
  31.5 8.8 %collective-permute-start.12 = (bf16[64,1152]{1,0:T(8,128)(2,1)S(1)}, bf16[64,1152]{1,0:T(8,128)(2,1)S(1)}, u32[]{:S(2)}, u32[]{:S(2)}) collective-permute-start(bf16[64,1152]{1,0:T(8,128)(2,1)S(1)} %add.28.rest_0_), channel_id=1, source_target_pairs={{0,1},{1,0},{2,3},{3,2},{4,5},{5,4},{6,7},{7,6},{8,9},{9,8},{10,11... | collective-permute-start | bytes 442376 | tf_op jit(solution)/shard_map/ppermute | solution.py:425
  36.7 5.5 %collective-permute-start.6 = (bf16[64,1152]{1,0:T(8,128)(2,1)S(1)}, bf16[64,1152]{1,0:T(8,128)(2,1)S(1)}, u32[]{:S(2)}, u32[]{:S(2)}) collective-permute-start(bf16[64,1152]{1,0:T(8,128)(2,1)S(1)} %add.29.rest_0_), channel_id=1, source_target_pairs={{0,2},{1,5},{2,0},{3,7},{4,6},{5,1},{6,4},{7,3},{8,10},{9,13},{10,... | collective-permute-start | bytes 442376 | tf_op jit(solution)/shard_map/ppermute | solution.py:422
  38.3 5.1 %collective-permute-start.11 = (bf16[64,1152]{1,0:T(8,128)(2,1)S(1)}, bf16[64,1152]{1,0:T(8,128)(2,1)S(1)}, u32[]{:S(2)}, u32[]{:S(2)}) collective-permute-start(bf16[64,1152]{1,0:T(8,128)(2,1)S(1)} %collective-permute-done.8.rest_1_), channel_id=1, source_target_pairs={{0,4},{1,3},{2,6},{3,1},{4,0},{5,7},{6,2},{7,5},{8,12},{9,11},{10,... | collective-permute-start | bytes 442376 | tf_op jit(solution)/shard_map/ppermute | solution.py:422
  38.3 6.7 %collective-permute-start.7 = (bf16[64,1152]{1,0:T(8,128)(2,1)S(1)}, bf16[64,1152]{1,0:T(8,128)(2,1)S(1)}, u32[]{:S(2)}, u32[]{:S(2)}) collective-permute-start(bf16[64,1152]{1,0:T(8,128)(2,1)S(1)} %add.29.rest_0_), channel_id=1, source_target_pairs={{0,4},{1,3},{2,6},{3,1},{4,0},{5,7},{6,2},{7,5},{8,12},{9,11},{10,... | collective-permute-start | bytes 442376 | tf_op jit(solution)/shard_map/ppermute | solution.py:422
  40.3 5.1 %collective-permute-start.13 = (bf16[64,1152]{1,0:T(8,128)(2,1)S(1)}, bf16[64,1152]{1,0:T(8,128)(2,1)S(1)}, u32[]{:S(2)}, u32[]{:S(2)}) collective-permute-start(bf16[64,1152]{1,0:T(8,128)(2,1)S(1)} %collective-permute-done.8.rest_1_), channel_id=1, source_target_pairs={{0,1},{1,0},{2,3},{3,2},{4,5},{5,4},{6,7},{7,6},{8,9},{9,8},{10,11... | collective-permute-start | bytes 442376 | tf_op jit(solution)/shard_map/ppermute | solution.py:425
  42.2 3.2 %collective-permute-start.14 = (bf16[64,1152]{1,0:T(8,128)(2,1)S(1)}, bf16[64,1152]{1,0:T(8,128)(2,1)S(1)}, u32[]{:S(2)}, u32[]{:S(2)}) collective-permute-start(bf16[64,1152]{1,0:T(8,128)(2,1)S(1)} %collective-permute-done.10.rest_2_), channel_id=1, source_target_pairs={{0,1},{1,0},{2,3},{3,2},{4,5},{5,4},{6,7},{7,6},{8,9},{9,8},{10,11... | collective-permute-start | bytes 442376 | tf_op jit(solution)/shard_map/ppermute | solution.py:425
  43.4 2.6 %collective-permute-start.15 = (bf16[64,1152]{1,0:T(8,128)(2,1)S(1)}, bf16[64,1152]{1,0:T(8,128)(2,1)S(1)}, u32[]{:S(2)}, u32[]{:S(2)}) collective-permute-start(bf16[64,1152]{1,0:T(8,128)(2,1)S(1)} %collective-permute-done.11.rest_3_), channel_id=1, source_target_pairs={{0,1},{1,0},{2,3},{3,2},{4,5},{5,4},{6,7},{7,6},{8,9},{9,8},{10,11... | collective-permute-start | bytes 442376 | tf_op jit(solution)/shard_map/ppermute | solution.py:425
  45.0 5.1 %collective-permute-start.9 = (bf16[64,1152]{1,0:T(8,128)(2,1)S(1)}, bf16[64,1152]{1,0:T(8,128)(2,1)S(1)}, u32[]{:S(2)}, u32[]{:S(2)}) collective-permute-start(bf16[64,1152]{1,0:T(8,128)(2,1)S(1)} %collective-permute-done.6.rest_1_), channel_id=1, source_target_pairs={{0,4},{1,3},{2,6},{3,1},{4,0},{5,7},{6,2},{7,5},{8,12},{9,11},{10,... | collective-permute-start | bytes 442376 | tf_op jit(solution)/shard_map/ppermute | solution.py:422
  45.5 4.7 %collective-permute-start.16 = (bf16[64,1152]{1,0:T(8,128)(2,1)S(1)}, bf16[64,1152]{1,0:T(8,128)(2,1)S(1)}, u32[]{:S(2)}, u32[]{:S(2)}) collective-permute-start(bf16[64,1152]{1,0:T(8,128)(2,1)S(1)} %add.29.rest_0_), channel_id=1, source_target_pairs={{0,1},{1,0},{2,3},{3,2},{4,5},{5,4},{6,7},{7,6},{8,9},{9,8},{10,11... | collective-permute-start | bytes 442376 | tf_op jit(solution)/shard_map/ppermute | solution.py:425
  45.5 4.7 %collective-permute-start.17 = (bf16[64,1152]{1,0:T(8,128)(2,1)S(1)}, bf16[64,1152]{1,0:T(8,128)(2,1)S(1)}, u32[]{:S(2)}, u32[]{:S(2)}) collective-permute-start(bf16[64,1152]{1,0:T(8,128)(2,1)S(1)} %collective-permute-done.6.rest_1_), channel_id=1, source_target_pairs={{0,1},{1,0},{2,3},{3,2},{4,5},{5,4},{6,7},{7,6},{8,9},{9,8},{10,11... | collective-permute-start | bytes 442376 | tf_op jit(solution)/shard_map/ppermute | solution.py:425
  46.0 4.2 %collective-permute-start.18 = (bf16[64,1152]{1,0:T(8,128)(2,1)S(1)}, bf16[64,1152]{1,0:T(8,128)(2,1)S(1)}, u32[]{:S(2)}, u32[]{:S(2)}) collective-permute-start(bf16[64,1152]{1,0:T(8,128)(2,1)S(1)} %collective-permute-done.7.rest_2_), channel_id=1, source_target_pairs={{0,1},{1,0},{2,3},{3,2},{4,5},{5,4},{6,7},{7,6},{8,9},{9,8},{10,11... | collective-permute-start | bytes 442376 | tf_op jit(solution)/shard_map/ppermute | solution.py:425
  50.1 1.4 %collective-permute-start.19 = (bf16[64,1152]{1,0:T(8,128)(2,1)S(1)}, bf16[64,1152]{1,0:T(8,128)(2,1)S(1)}, u32[]{:S(2)}, u32[]{:S(2)}) collective-permute-start(bf16[64,1152]{1,0:T(8,128)(2,1)S(1)} %collective-permute-done.9.rest_3_), channel_id=1, source_target_pairs={{0,1},{1,0},{2,3},{3,2},{4,5},{5,4},{6,7},{7,6},{8,9},{9,8},{10,11... | collective-permute-start | bytes 442376 | tf_op jit(solution)/shard_map/ppermute | solution.py:425
  54.2 5.2 %collective-permute-start.20 = (bf16[64,1152]{1,0:T(8,128)(2,1)S(1)}, bf16[64,1152]{1,0:T(8,128)(2,1)S(1)}, u32[]{:S(2)}, u32[]{:S(2)}) collective-permute-start(bf16[64,1152]{1,0:T(8,128)(2,1)S(1)} %get-tuple-element.82), channel_id=1, source_target_pairs={{0,1},{1,17},{2,3},{3,19},{4,5},{5,21},{6,7},{7,23},{8,9},{9,25},{... | collective-permute-start | bytes 442376 | tf_op jit(solution)/shard_map/ppermute | solution.py:493
  54.4 5.0 %collective-permute-start.21 = (bf16[64,1152]{1,0:T(8,128)(2,1)S(1)}, bf16[64,1152]{1,0:T(8,128)(2,1)S(1)}, u32[]{:S(2)}, u32[]{:S(2)}) collective-permute-start(bf16[64,1152]{1,0:T(8,128)(2,1)S(1)} %get-tuple-element.83), channel_id=1, source_target_pairs={{1,16},{3,18},{5,20},{7,22},{9,24},{11,26},{13,28},{15,30},{16,1},... | collective-permute-start | bytes 442376 | tf_op jit(solution)/shard_map/ppermute | solution.py:493
  59.9 5.2 %collective-permute-start.22 = (bf16[1,64,1152]{2,1,0:T(8,128)(2,1)S(1)}, bf16[1,64,1152]{2,1,0:T(8,128)(2,1)S(1)}, u32[]{:S(2)}, u32[]{:S(2)}) collective-permute-start(bf16[1,64,1152]{2,1,0:T(8,128)(2,1)S(1)} %bitcast.9), channel_id=1, source_target_pairs={{0,2},{1,5},{2,0},{3,7},{4,6},{5,1},{6,4},{7,3},{8,10},{9,13},{10,... | collective-permute-start | bytes 442376 | tf_op jit(solution)/shard_map/ppermute | solution.py:422
  60.6 10.1 %collective-permute-start.27 = (bf16[1,64,1152]{2,1,0:T(8,128)(2,1)S(1)}, bf16[1,64,1152]{2,1,0:T(8,128)(2,1)S(1)}, u32[]{:S(2)}, u32[]{:S(2)}) collective-permute-start(bf16[1,64,1152]{2,1,0:T(8,128)(2,1)S(1)} %bitcast.10), channel_id=1, source_target_pairs={{0,8},{1,9},{2,10},{3,11},{4,12},{5,13},{6,14},{7,15},{8,0},{9,1},... | collective-permute-start | bytes 442376 | tf_op jit(solution)/shard_map/ppermute | solution.py:419
  65.2 10.8 %collective-permute-start.32 = (bf16[2,64,1152]{2,1,0:T(8,128)(2,1)S(1)}, bf16[2,64,1152]{2,1,0:T(8,128)(2,1)S(1)}, u32[]{:S(2)}, u32[]{:S(2)}) collective-permute-start(bf16[2,64,1152]{2,1,0:T(8,128)(2,1)S(1)} %pad_maximum_fusion.rest_0_), channel_id=1, source_target_pairs={{0,16},{1,17},{2,18},{3,19},{4,20},{5,21},{6,22},{7,23},{8,24},{9,... | collective-permute-start | bytes 884744 | tf_op jit(solution)/shard_map/ppermute | solution.py:505
  68.6 8.8 %collective-permute-start.23 = (bf16[2,64,1152]{2,1,0:T(8,128)(2,1)S(1)}, bf16[2,64,1152]{2,1,0:T(8,128)(2,1)S(1)}, u32[]{:S(2)}, u32[]{:S(2)}) collective-permute-start(bf16[2,64,1152]{2,1,0:T(8,128)(2,1)S(1)} %pad_maximum_fusion.rest_0_), channel_id=1, source_target_pairs={{0,4},{1,3},{2,6},{3,1},{4,0},{5,7},{6,2},{7,5},{8,12},{9,11},{10,... | collective-permute-start | bytes 884744 | tf_op jit(solution)/shard_map/ppermute | solution.py:422
  70.7 5.1 %collective-permute-start.28 = (bf16[1,64,1152]{2,1,0:T(8,128)(2,1)S(1)}, bf16[1,64,1152]{2,1,0:T(8,128)(2,1)S(1)}, u32[]{:S(2)}, u32[]{:S(2)}) collective-permute-start(bf16[1,64,1152]{2,1,0:T(8,128)(2,1)S(1)} %collective-permute-done.27), channel_id=1, source_target_pairs={{0,2},{1,5},{2,0},{3,7},{4,6},{5,1},{6,4},{7,3},{8,10},{9,13},{10,... | collective-permute-start | bytes 442376 | tf_op jit(solution)/shard_map/ppermute | solution.py:422
  75.9 6.8 %collective-permute-start.29 = (bf16[2,64,1152]{2,1,0:T(8,128)(2,1)S(1)}, bf16[2,64,1152]{2,1,0:T(8,128)(2,1)S(1)}, u32[]{:S(2)}, u32[]{:S(2)}) collective-permute-start(bf16[2,64,1152]{2,1,0:T(8,128)(2,1)S(1)} %constant_dynamic-update-slice_fusion.rest_4_), channel_id=1, source_target_pairs={{0,4},{1,3},{2,6},{3,1},{4,0},{5,7},{6,2},{7,5},{8,12},{9,11},{10,... | collective-permute-start | bytes 884744 | tf_op jit(solution)/shard_map/ppermute | solution.py:422
  76.0 7.4 %collective-permute-start.33 = (bf16[2,64,1152]{2,1,0:T(8,128)(2,1)S(1)}, bf16[2,64,1152]{2,1,0:T(8,128)(2,1)S(1)}, u32[]{:S(2)}, u32[]{:S(2)}) collective-permute-start(bf16[2,64,1152]{2,1,0:T(8,128)(2,1)S(1)} %collective-permute-done.32.rest_8_), channel_id=1, source_target_pairs={{0,1},{1,0},{2,3},{3,2},{4,5},{5,4},{6,7},{7,6},{8,9},{9,8},{10,11... | collective-permute-start | bytes 884744 | tf_op jit(solution)/shard_map/ppermute | solution.py:425
  77.4 9.0 %collective-permute-start.34 = (bf16[2,64,1152]{2,1,0:T(8,128)(2,1)S(1)}, bf16[2,64,1152]{2,1,0:T(8,128)(2,1)S(1)}, u32[]{:S(2)}, u32[]{:S(2)}) collective-permute-start(bf16[2,64,1152]{2,1,0:T(8,128)(2,1)S(1)} %collective-permute-done.23.rest_1_), channel_id=1, source_target_pairs={{0,16},{1,17},{2,18},{3,19},{4,20},{5,21},{6,22},{7,23},{8,24},{9,... | collective-permute-start | bytes 884744 | tf_op jit(solution)/shard_map/ppermute | solution.py:505
  82.7 3.7 %collective-permute-start.31 = (bf16[2,64,1152]{2,1,0:T(8,128)(2,1)S(1)}, bf16[2,64,1152]{2,1,0:T(8,128)(2,1)S(1)}, u32[]{:S(2)}, u32[]{:S(2)}) collective-permute-start(bf16[2,64,1152]{2,1,0:T(8,128)(2,1)S(1)} %collective-permute-done.29.rest_5_), channel_id=1, source_target_pairs={{0,1},{1,0},{2,3},{3,2},{4,5},{5,4},{6,7},{7,6},{8,9},{9,8},{10,11... | collective-permute-start | bytes 884744 | tf_op jit(solution)/shard_map/ppermute | solution.py:425
  82.9 3.5 %collective-permute-start.24 = (bf16[2,64,1152]{2,1,0:T(8,128)(2,1)S(1)}, bf16[2,64,1152]{2,1,0:T(8,128)(2,1)S(1)}, u32[]{:S(2)}, u32[]{:S(2)}) collective-permute-start(bf16[2,64,1152]{2,1,0:T(8,128)(2,1)S(1)} %pad_maximum_fusion.rest_0_), channel_id=1, source_target_pairs={{0,1},{1,0},{2,3},{3,2},{4,5},{5,4},{6,7},{7,6},{8,9},{9,8},{10,11... | collective-permute-start | bytes 884744 | tf_op jit(solution)/shard_map/ppermute | solution.py:425
  83.2 3.2 %collective-permute-start.25 = (bf16[2,64,1152]{2,1,0:T(8,128)(2,1)S(1)}, bf16[2,64,1152]{2,1,0:T(8,128)(2,1)S(1)}, u32[]{:S(2)}, u32[]{:S(2)}) collective-permute-start(bf16[2,64,1152]{2,1,0:T(8,128)(2,1)S(1)} %collective-permute-done.23.rest_1_), channel_id=1, source_target_pairs={{0,1},{1,0},{2,3},{3,2},{4,5},{5,4},{6,7},{7,6},{8,9},{9,8},{10,11... | collective-permute-start | bytes 884744 | tf_op jit(solution)/shard_map/ppermute | solution.py:425
  83.4 3.0 %collective-permute-start.30 = (bf16[2,64,1152]{2,1,0:T(8,128)(2,1)S(1)}, bf16[2,64,1152]{2,1,0:T(8,128)(2,1)S(1)}, u32[]{:S(2)}, u32[]{:S(2)}) collective-permute-start(bf16[2,64,1152]{2,1,0:T(8,128)(2,1)S(1)} %constant_dynamic-update-slice_fusion.rest_4_), channel_id=1, source_target_pairs={{0,1},{1,0},{2,3},{3,2},{4,5},{5,4},{6,7},{7,6},{8,9},{9,8},{10,11... | collective-permute-start | bytes 884744 | tf_op jit(solution)/shard_map/ppermute | solution.py:425
  87.0 1.6 %collective-permute-start.35 = (bf16[2,64,1152]{2,1,0:T(8,128)(2,1)S(1)}, bf16[2,64,1152]{2,1,0:T(8,128)(2,1)S(1)}, u32[]{:S(2)}, u32[]{:S(2)}) collective-permute-start(bf16[2,64,1152]{2,1,0:T(8,128)(2,1)S(1)} %collective-permute-done.34.rest_9_), channel_id=1, source_target_pairs={{0,1},{1,0},{2,3},{3,2},{4,5},{5,4},{6,7},{7,6},{8,9},{9,8},{10,11... | collective-permute-start | bytes 884744 | tf_op jit(solution)/shard_map/ppermute | solution.py:425
  87.1 4.9 %collective-permute-start.36 = (bf16[2,160,128]{2,1,0:T(8,128)(2,1)S(1)}, bf16[2,160,128]{2,1,0:T(8,128)(2,1)S(1)}, u32[]{:S(2)}, u32[]{:S(2)}) collective-permute-start(bf16[2,160,128]{2,1,0:T(8,128)(2,1)S(1)} %pad_maximum_fusion.1), channel_id=1, source_target_pairs={{0,16},{1,17},{2,18},{3,19},{4,20},{5,21},{6,22},{7,23},{8,24},{9,... | collective-permute-start | bytes 245768 | tf_op jit(solution)/shard_map/ppermute | solution.py:518
  92.7 1.1 %collective-permute-start.37 = (f32[1,64]{1,0:T(1,128)S(1)}, f32[1,64]{1,0:T(1,128)S(1)}, u32[]{:S(2)}, u32[]{:S(2)}) collective-permute-start(f32[1,64]{1,0:T(1,128)S(1)} %score.1), channel_id=1, source_target_pairs={{0,1},{1,0},{2,3},{3,2},{4,5},{5,4},{6,7},{7,6},{8,9},{9,8},{10,11... | collective-permute-start | bytes 776 | tf_op jit(solution)/shard_map/ppermute | solution.py:528
  93.8 3.5 %collective-permute-start.38 = (f32[1,64]{1,0:T(1,128)S(1)}, f32[1,64]{1,0:T(1,128)S(1)}, u32[]{:S(2)}, u32[]{:S(2)}) collective-permute-start(f32[1,64]{1,0:T(1,128)S(1)} %add.30), channel_id=1, source_target_pairs={{0,2},{1,3},{2,0},{3,1},{4,6},{5,7},{6,4},{7,5},{8,10},{9,11},{10,... | collective-permute-start | bytes 776 | tf_op jit(solution)/shard_map/ppermute | solution.py:528
  97.4 3.5 %collective-permute-start.39 = (f32[1,64]{1,0:T(1,128)S(1)}, f32[1,64]{1,0:T(1,128)S(1)}, u32[]{:S(2)}, u32[]{:S(2)}) collective-permute-start(f32[1,64]{1,0:T(1,128)S(1)} %add.31), channel_id=1, source_target_pairs={{0,4},{1,5},{2,6},{3,7},{4,0},{5,1},{6,2},{7,3},{8,12},{9,13},{10,... | collective-permute-start | bytes 776 | tf_op jit(solution)/shard_map/ppermute | solution.py:528
  100.9 4.4 %collective-permute-start.40 = (f32[1,64]{1,0:T(1,128)S(1)}, f32[1,64]{1,0:T(1,128)S(1)}, u32[]{:S(2)}, u32[]{:S(2)}) collective-permute-start(f32[1,64]{1,0:T(1,128)S(1)} %add.32), channel_id=1, source_target_pairs={{0,8},{1,9},{2,10},{3,11},{4,12},{5,13},{6,14},{7,15},{8,0},{9,1},... | collective-permute-start | bytes 776 | tf_op jit(solution)/shard_map/ppermute | solution.py:528

commit v6 on v5

--- a/solution.py
+++ b/solution.py
@@ -336,11 +336,12 @@
 def score(info, slots, mine, back, queries, rank_count):
     tokens, columns = mine[0].shape
     half_rank = rank_count // 2
-    lanes = slots * queries
+    lanes = -(-slots * queries // 128) * 128
     lengths_at = info.shape[0] - 2 * slots
 
     def kernel(where, mine_in, mine_out, back, out):
-        live = lax.broadcasted_iota(jnp.int32, (tokens, columns), 0) < where[lengths_at + where[lengths_at + slots + where[ME]]]
+        sequence = where[lengths_at + slots + where[ME]]
+        live = lax.broadcasted_iota(jnp.int32, (tokens, columns), 0) < where[lengths_at + sequence]
         products = (mine_in[...] + back[0].astype(jnp.float32)) * (mine_out[...] + back[1].astype(jnp.float32))
         sums = jnp.sum(jnp.where(live, products, 0.0), axis=0, keepdims=True)
         query_of = lax.broadcasted_iota(jnp.int32, (1, columns), 1) % (queries * half_rank) // half_rank
@@ -348,7 +349,7 @@
         row = jnp.zeros((1, lanes), jnp.float32)
         for query in range(queries):
             value = jnp.sum(jnp.where(query_of == query, sums, 0.0), axis=1, keepdims=True) / rank_count
-            row = jnp.where(lane == where[ME] * queries + query, value, row)
+            row = jnp.where(lane == sequence * queries + query, value, row)
         out[...] = row
 
     return pl.pallas_call(
@@ -362,20 +363,12 @@
     )(info, *mine, back)
 
 
-def own_sequence(info, slots, held, queries):
-    plan_at = info.shape[0] - slots
+def own_sequence(info, held, queries):
+
+    lanes = held.shape[1]
 
     def kernel(where, held, out):
-        slot = jnp.int32(0)
-        for number in range(slots):
-            slot = jnp.where(where[plan_at + number] == where[ME], number, slot)
-        lane = lax.broadcasted_iota(jnp.int32, held.shape, 1)
-        out_lane = lax.broadcasted_iota(jnp.int32, (1, queries), 1)
-        row = jnp.zeros((1, queries), jnp.float32)
-        for query in range(queries):
-            value = jnp.sum(jnp.where(lane == slot * queries + query, held[...], 0.0), axis=1, keepdims=True)
-            row = jnp.where(out_lane == query, value, row)
-        out[...] = row
+        out[...] = pltpu.roll(held[...], lanes - where[ME] * queries, 1)[:, :queries]
 
     return pl.pallas_call(
         kernel,
@@ -461,15 +454,11 @@
     (given_away,) = stage(info, [], early, [far], [])
     late = lax.optimization_barrier((acts, grads, basis_in, basis_out, given_away))
     given_away = lax.ppermute(given_away, EVERYONE, across)
-    *bases, other_tokens, own_tokens = stage(
-        info, late[2:4], Features(late[0], late[1], chips), [(0, NEAR)], [(0, chips)]
-    )
+    bases = stage(info, late[2:4], Features(*late[:2], chips), [], [])
     for bit in range(bits - 1, 1, -1):
         arrived = [to_chip(dense[chain], 1 << bit) for chain in every]
         if bit == bits - 1:
-            arrived[0], own_tokens, other_tokens, *bases = lax.optimization_barrier(
-                (arrived[0], own_tokens, other_tokens, *bases)
-            )
+            arrived[0], *bases = lax.optimization_barrier((arrived[0], *bases))
         for chain in every:
             if chain:
                 (arrived[chain],) = after((arrived[chain],), dense[chain - 1])
@@ -491,6 +480,9 @@
     meet = [number(p, i, *((p, i ^ 1) if i % 2 == p else (1 - p, i))) for p in range(2) for i in range(count)]
     cross = [number(p, i, 1 - p, i ^ 1) for p in range(2) for i in range(count) if i % 2 != p]
     met, crossed = lax.ppermute(first, EVERYONE, meet), lax.ppermute(second, EVERYONE, cross)
+    late = Features(*after((acts, grads), first), chips)
+    other_tokens, own_tokens = stage(info, [], late, [(0, NEAR)], [(0, chips)])
+    met, other_tokens, own_tokens = lax.optimization_barrier((met, other_tokens, own_tokens))
     piece = meet_halves(info, partial, met, crossed)
 
     held = [piece[None]]
@@ -526,7 +518,7 @@
     held = score(more, count, mine, back, num_queries, rank_count)
     for bit in range(bits + 1):
         held = held + lax.ppermute(held, "blk", [(i, i ^ (1 << bit)) for i in range(count)])
-    return own_sequence(more, count, held, num_queries)
+    return own_sequence(info, held, num_queries)
 
 
 def solution(mesh):

time: 107 us -> 105 us (0.981)
  waiting for transfers between devices: 48.9 us -> 43.4 us
  starting transfers between devices: 34.2 us -> 36.7 us
  Pallas kernels: 22.2 us -> 23.6 us
    ppermute x1, waiting for transfers between devices: 4.33 us -> 1.27 us  [shards(): lax.ppermute(first, EVERYONE, meet)]
    ppermute x10, waiting for transfers between devices: 18.5 us -> 16.8 us  [along(): lax.ppermute(value, 'blk', [(i, i ^ 2 << (second if i % 2 else first)) fo...]
    ppermute x6, starting transfers between devices: 7.63 us -> 9.31 us  [to_chip(): return lax.ppermute(value, 'blk', [(i, i ^ 2 * mask) for i in range(count)])]
    pallas_call x2 -> x3, Pallas kernels: 9.28 us -> 10.7 us  [stage(): pl.pallas_call(kernel, in_specs=[SMEM] + [HBM] * (2 + len(bases)), out_sp...]
  transfers between devices with their start and end apart: 41 -> 41, of which waited for: 21 -> 22; matrix products, arithmetic and copies ran while one was open for 1% -> 1% of each run, Pallas kernels for 16% -> 18%
where the time goes in v6:
time: 105 us
  waiting for transfers between devices  43.4 us (41%)
  starting transfers between devices  36.7 us (35%)
  Pallas kernels  23.6 us (22%)
    ppermute x10, waiting for transfers between devices, along(): lax.ppermute(value, 'blk', [(i, i ^ 2 << (second if i % 2 else first)) fo...  16.8 us
    ppermute x10, starting transfers between devices, along(): lax.ppermute(value, 'blk', [(i, i ^ 2 << (second if i % 2 else first)) fo...  11.2 us
    pallas_call x3, Pallas kernels, stage(): pl.pallas_call(kernel, in_specs=[SMEM] + [HBM] * (2 + len(bases)), out_sp...  10.7 us
    ppermute x6, waiting for transfers between devices, to_chip(): return lax.ppermute(value, 'blk', [(i, i ^ 2 * mask) for i in range(count)])  9.74 us
    ppermute x6, starting transfers between devices, to_chip(): return lax.ppermute(value, 'blk', [(i, i ^ 2 * mask) for i in range(count)])  9.31 us
    ppermute x4, waiting for transfers between devices, shards(): lax.ppermute(held, 'blk', [(i, i ^ 1 << bit) for i in range(count)])  7.81 us
    pallas_call x2, Pallas kernels, rotate(): pl.pallas_call(kernel, in_specs=[SMEM] + [VMEM] * (2 * NEAR + 2 + len(giv...  5.23 us
    ppermute x15, starting transfers between devices, to_core(): return lax.ppermute(value, 'blk', [(i, i ^ 1) for i in range(count)])  4.84 us
  transfers between devices with their start and end apart: 41, of which 22 were waited for; matrix products, arithmetic and copies ran while one was open for 1% of the time, Pallas kernels for 18%

profile of v6, /device:TPU:0, one launch (start us, length us, event | category | flops | bytes accessed | tf_op | source)
XLA Modules:
  0.0 104.9 jit_solution(536876029439158880)
XLA Ops:
  0.1 1.9 %rank_halves.1 = (bf16[4,2,16,1152]{3,2,1,0:T(8,128)(2,1)S(1)}, bf16[4,2,16,1152]{3,2,1,0:T(8,128)(2,1)S(1)}) custom-call(s32[16]{0:T(128)S(1)} %concatenate.12.where, bf16[1,32,4096]{2,1,0:T(8,128)(2,1)} %left.1, bf16[1,32,14336]{2,1,0:T(8,128)(2,1)} %right.1), custom_call_target="tpu_custom_call" | custom-call | bytes 1179648 | tf_op jit(solution)/shard_map/rank_halves/pallas_call | solution.py:115
  2.0 1.8 %collective-permute-start = (bf16[4,2,16,1152]{3,2,1,0:T(8,128)(2,1)S(1)}, bf16[4,2,16,1152]{3,2,1,0:T(8,128)(2,1)S(1)}, u32[]{:S(2)}, u32[]{:S(2)}) collective-permute-start(bf16[4,2,16,1152]{3,2,1,0:T(8,128)(2,1)S(1)} %get-tuple-element.54), channel_id=1, source_target_pairs={{0,1},{1,0},{2,3},{3,2},{4,5},{5,4},{6,7},{7,6},{8,9},{9,8},{10,11... | collective-permute-start | bytes 884744 | tf_op jit(solution)/shard_map/ppermute | solution.py:418
  3.9 0.8 pad_add_fusion.where
  5.7 2.4 %collective-permute-start.1 = (bf16[2,2,16,1152]{3,2,1,0:T(8,128)(2,1)S(1)}, bf16[2,2,16,1152]{3,2,1,0:T(8,128)(2,1)S(1)}, u32[]{:S(2)}, u32[]{:S(2)}) collective-permute-start(bf16[2,2,16,1152]{3,2,1,0:T(8,128)(2,1)S(1)} %get-tuple-element.62), channel_id=1, source_target_pairs={{0,2},{1,3},{2,0},{3,1},{4,6},{5,7},{6,4},{7,5},{8,10},{9,11},{10,... | collective-permute-start | bytes 442376 | tf_op jit(solution)/shard_map/ppermute | solution.py:412
  8.1 1.6 %collective-permute-start.2 = (bf16[2,2,16,1152]{3,2,1,0:T(8,128)(2,1)S(1)}, bf16[2,2,16,1152]{3,2,1,0:T(8,128)(2,1)S(1)}, u32[]{:S(2)}, u32[]{:S(2)}) collective-permute-start(bf16[2,2,16,1152]{3,2,1,0:T(8,128)(2,1)S(1)} %get-tuple-element.63), channel_id=1, source_target_pairs={{0,4},{1,5},{2,6},{3,7},{4,0},{5,1},{6,2},{7,3},{8,12},{9,13},{10,... | collective-permute-start | bytes 442376 | tf_op jit(solution)/shard_map/ppermute | solution.py:412
  9.7 2.0 %stage.3 = bf16[160,4608]{1,0:T(8,128)(2,1)S(1)} custom-call(s32[16]{0:T(128)S(1)} %concatenate.12.where, bf16[160,4096]{1,0:T(8,128)(2,1)} %bitcast.17, bf16[160,14336]{1,0:T(8,128)(2,1)} %bitcast.14), custom_call_target="tpu_custom_call" | custom-call | tf_op jit(solution)/shard_map/stage/pallas_call | solution.py:177
  11.7 1.9 %collective-permute-start.26 = (bf16[160,4608]{1,0:T(8,128)(2,1)S(1)}, bf16[160,4608]{1,0:T(8,128)(2,1)S(1)}, u32[]{:S(2)}, u32[]{:S(2)}) collective-permute-start(bf16[160,4608]{1,0:T(8,128)(2,1)S(1)} %stage.3), channel_id=1, source_target_pairs={{0,16},{1,17},{2,18},{3,19},{4,20},{5,21},{6,22},{7,23},{8,24},{9,... | collective-permute-start | bytes 4423688 | tf_op jit(solution)/shard_map/ppermute | solution.py:456
  13.6 1.2 %collective-permute-done.2.rest_2_ = bf16[2,2,16,1152]{3,2,1,0:T(8,128)(2,1)S(1)} collective-permute-done((bf16[2,2,16,1152]{3,2,1,0:T(8,128)(2,1)S(1)}, bf16[2,2,16,1152]{3,2,1,0:T(8,128)(2,1)S(1)}, u32[]{:S(2)}, u32[]{:S(2)}) %collective-permute-start.2) | collective-permute-done | bytes 147488 | tf_op jit(solution)/shard_map/ppermute | solution.py:412
  14.8 2.1 %collective-permute-done.3.rest_3_ = bf16[2,2,16,1152]{3,2,1,0:T(8,128)(2,1)S(1)} collective-permute-done((bf16[2,2,16,1152]{3,2,1,0:T(8,128)(2,1)S(1)}, bf16[2,2,16,1152]{3,2,1,0:T(8,128)(2,1)S(1)}, u32[]{:S(2)}, u32[]{:S(2)}) %collective-permute-start.3) | collective-permute-done | bytes 147488 | tf_op jit(solution)/shard_map/ppermute | solution.py:412
  16.9 0.8 choose.1
  17.7 2.8 %collective-permute-start.5 = (bf16[64,1152]{1,0:T(8,128)(2,1)S(1)}, bf16[64,1152]{1,0:T(8,128)(2,1)S(1)}, u32[]{:S(2)}, u32[]{:S(2)}) collective-permute-start(bf16[64,1152]{1,0:T(8,128)(2,1)S(1)} %get-tuple-element.66), channel_id=1, source_target_pairs={{0,8},{1,9},{2,10},{3,11},{4,12},{5,13},{6,14},{7,15},{8,0},{9,1},... | collective-permute-start | bytes 442376 | tf_op jit(solution)/shard_map/ppermute | solution.py:412
  20.5 5.7 %stage.4 = (bf16[256,2048]{1,0:T(8,128)(2,1)S(1)}, bf16[896,7168]{1,0:T(8,128)(2,1)S(1)}) custom-call(s32[16]{0:T(128)S(1)} %concatenate.12.where, bf16[160,4096]{1,0:T(8,128)(2,1)} %bitcast.18, bf16[160,14336]{1,0:T(8,128)(2,1)} %bitcast.15, bf16[256,4096]{1,0:T(8,128)(2,1)} %rest_0_, bf16[896,14336]{1,0:T(8,128)(2,1)} %rest_1_), custom_call_target="tpu_custom_call" | custom-call | bytes 13893632 | tf_op jit(solution)/shard_map/stage/pallas_call | solution.py:177
  26.4 0.7 collective-permute-done.5
  27.1 1.4 %collective-permute-start.8 = (bf16[64,1152]{1,0:T(8,128)(2,1)S(1)}, bf16[64,1152]{1,0:T(8,128)(2,1)S(1)}, u32[]{:S(2)}, u32[]{:S(2)}) collective-permute-start(bf16[64,1152]{1,0:T(8,128)(2,1)S(1)} %add.28.rest_0_), channel_id=1, source_target_pairs={{0,2},{1,5},{2,0},{3,7},{4,6},{5,1},{6,4},{7,3},{8,10},{9,13},{10,... | collective-permute-start | bytes 442376 | tf_op jit(solution)/shard_map/ppermute | solution.py:415
  28.5 2.3 %collective-permute-start.10 = (bf16[64,1152]{1,0:T(8,128)(2,1)S(1)}, bf16[64,1152]{1,0:T(8,128)(2,1)S(1)}, u32[]{:S(2)}, u32[]{:S(2)}) collective-permute-start(bf16[64,1152]{1,0:T(8,128)(2,1)S(1)} %add.28.rest_0_), channel_id=1, source_target_pairs={{0,4},{1,3},{2,6},{3,1},{4,0},{5,7},{6,2},{7,5},{8,12},{9,11},{10,... | collective-permute-start | bytes 442376 | tf_op jit(solution)/shard_map/ppermute | solution.py:415
  30.8 4.2 %collective-permute-done.4 = bf16[64,1152]{1,0:T(8,128)(2,1)S(1)} collective-permute-done((bf16[64,1152]{1,0:T(8,128)(2,1)S(1)}, bf16[64,1152]{1,0:T(8,128)(2,1)S(1)}, u32[]{:S(2)}, u32[]{:S(2)}) %collective-permute-start.4) | collective-permute-done | bytes 147488 | tf_op jit(solution)/shard_map/ppermute | solution.py:412
  35.1 1.6 %collective-permute-start.6 = (bf16[64,1152]{1,0:T(8,128)(2,1)S(1)}, bf16[64,1152]{1,0:T(8,128)(2,1)S(1)}, u32[]{:S(2)}, u32[]{:S(2)}) collective-permute-start(bf16[64,1152]{1,0:T(8,128)(2,1)S(1)} %add.29.rest_0_), channel_id=1, source_target_pairs={{0,2},{1,5},{2,0},{3,7},{4,6},{5,1},{6,4},{7,3},{8,10},{9,13},{10,... | collective-permute-start | bytes 442376 | tf_op jit(solution)/shard_map/ppermute | solution.py:415
  36.7 2.0 %collective-permute-start.7 = (bf16[64,1152]{1,0:T(8,128)(2,1)S(1)}, bf16[64,1152]{1,0:T(8,128)(2,1)S(1)}, u32[]{:S(2)}, u32[]{:S(2)}) collective-permute-start(bf16[64,1152]{1,0:T(8,128)(2,1)S(1)} %add.29.rest_0_), channel_id=1, source_target_pairs={{0,4},{1,3},{2,6},{3,1},{4,0},{5,7},{6,2},{7,5},{8,12},{9,11},{10,... | collective-permute-start | bytes 442376 | tf_op jit(solution)/shard_map/ppermute | solution.py:415
  38.7 2.7 %collective-permute-done.6.rest_1_ = bf16[64,1152]{1,0:T(8,128)(2,1)S(1)} collective-permute-done((bf16[64,1152]{1,0:T(8,128)(2,1)S(1)}, bf16[64,1152]{1,0:T(8,128)(2,1)S(1)}, u32[]{:S(2)}, u32[]{:S(2)}) %collective-permute-start.6) | collective-permute-done | bytes 147488 | tf_op jit(solution)/shard_map/ppermute | solution.py:415
  41.9 1.5 %collective-permute-done.7.rest_2_ = bf16[64,1152]{1,0:T(8,128)(2,1)S(1)} collective-permute-done((bf16[64,1152]{1,0:T(8,128)(2,1)S(1)}, bf16[64,1152]{1,0:T(8,128)(2,1)S(1)}, u32[]{:S(2)}, u32[]{:S(2)}) %collective-permute-start.7) | collective-permute-done | bytes 147488 | tf_op jit(solution)/shard_map/ppermute | solution.py:415
  44.5 2.6 %rotate.2.rest_10_ = f32[1152,128]{1,0:T(8,128)S(1)} custom-call(s32[16]{0:T(128)S(1)} %concatenate.12.where, bf16[64,1152]{1,0:T(8,128)(2,1)S(1)} %add.28.rest_0_, bf16[64,1152]{1,0:T(8,128)(2,1)S(1)} %collective-permute-done.8.rest_1_, bf16[64,1152]{1,0:T(8,128)(2,1)S(1)} %collective-permute-done.10.rest_2_, ...), custom_call_target="tpu_custom_call" | custom-call | flops 889192448 | bytes 6946816 | tf_op jit(solution)/shard_map/rotate/pallas_call | solution.py:282
  47.0 1.5 %collective-permute-done.9.rest_3_ = bf16[64,1152]{1,0:T(8,128)(2,1)S(1)} collective-permute-done((bf16[64,1152]{1,0:T(8,128)(2,1)S(1)}, bf16[64,1152]{1,0:T(8,128)(2,1)S(1)}, u32[]{:S(2)}, u32[]{:S(2)}) %collective-permute-start.9) | collective-permute-done | bytes 147488 | tf_op jit(solution)/shard_map/ppermute | solution.py:415
  48.6 1.3 %collective-permute-done.19.rest_7_ = bf16[64,1152]{1,0:T(8,128)(2,1)S(1)} collective-permute-done((bf16[64,1152]{1,0:T(8,128)(2,1)S(1)}, bf16[64,1152]{1,0:T(8,128)(2,1)S(1)}, u32[]{:S(2)}, u32[]{:S(2)}) %collective-permute-start.19) | collective-permute-done | bytes 147488 | tf_op jit(solution)/shard_map/ppermute | solution.py:418
  49.9 2.7 %rotate.3 = (f32[64,1152]{1,0:T(8,128)S(1)}, bf16[64,1152]{1,0:T(8,128)(2,1)S(1)}, bf16[64,1152]{1,0:T(8,128)(2,1)S(1)}) custom-call(s32[16]{0:T(128)S(1)} %concatenate.12.where, bf16[64,1152]{1,0:T(8,128)(2,1)S(1)} %add.29.rest_0_, bf16[64,1152]{1,0:T(8,128)(2,1)S(1)} %collective-permute-done.6.rest_1_, ...), custom_call_target="tpu_custom_call" | custom-call | flops 889192448 | bytes 6946816 | tf_op jit(solution)/shard_map/rotate/pallas_call | solution.py:282
  52.8 0.7 collective-permute-start.21
  53.5 3.0 %stage.5 = (bf16[160,4608]{1,0:T(8,128)(2,1)S(1)}, bf16[160,9216]{1,0:T(8,128)(2,1)S(1)}) custom-call(s32[16]{0:T(128)S(1)} %concatenate.12.where, bf16[160,4096]{1,0:T(8,128)(2,1)} %bitcast.19, bf16[160,14336]{1,0:T(8,128)(2,1)} %bitcast.16), custom_call_target="tpu_custom_call" | custom-call | tf_op jit(solution)/shard_map/stage/pallas_call | solution.py:177
  56.5 1.3 %collective-permute-done.20.met = bf16[64,1152]{1,0:T(8,128)(2,1)S(1)} collective-permute-done((bf16[64,1152]{1,0:T(8,128)(2,1)S(1)}, bf16[64,1152]{1,0:T(8,128)(2,1)S(1)}, u32[]{:S(2)}, u32[]{:S(2)}) %collective-permute-start.20) | collective-permute-done | bytes 147488 | tf_op jit(solution)/shard_map/ppermute | solution.py:482
  59.0 2.2 %collective-permute-start.27 = (bf16[1,64,1152]{2,1,0:T(8,128)(2,1)S(1)}, bf16[1,64,1152]{2,1,0:T(8,128)(2,1)S(1)}, u32[]{:S(2)}, u32[]{:S(2)}) collective-permute-start(bf16[1,64,1152]{2,1,0:T(8,128)(2,1)S(1)} %bitcast.10), channel_id=1, source_target_pairs={{0,8},{1,9},{2,10},{3,11},{4,12},{5,13},{6,14},{7,15},{8,0},{9,1},... | collective-permute-start | bytes 442376 | tf_op jit(solution)/shard_map/ppermute | solution.py:412
  61.2 2.4 %collective-permute-done.22 = bf16[1,64,1152]{2,1,0:T(8,128)(2,1)S(1)} collective-permute-done((bf16[1,64,1152]{2,1,0:T(8,128)(2,1)S(1)}, bf16[1,64,1152]{2,1,0:T(8,128)(2,1)S(1)}, u32[]{:S(2)}, u32[]{:S(2)}) %collective-permute-start.22) | collective-permute-done | bytes 147488 | tf_op jit(solution)/shard_map/ppermute | solution.py:415
  63.6 3.4 %collective-permute-start.32 = (bf16[2,64,1152]{2,1,0:T(8,128)(2,1)S(1)}, bf16[2,64,1152]{2,1,0:T(8,128)(2,1)S(1)}, u32[]{:S(2)}, u32[]{:S(2)}) collective-permute-start(bf16[2,64,1152]{2,1,0:T(8,128)(2,1)S(1)} %pad_maximum_fusion.rest_0_), channel_id=1, source_target_pairs={{0,16},{1,17},{2,18},{3,19},{4,20},{5,21},{6,22},{7,23},{8,24},{9,... | collective-permute-start | bytes 884744 | tf_op jit(solution)/shard_map/ppermute | solution.py:497
  67.5 1.5 %collective-permute-done.27 = bf16[1,64,1152]{2,1,0:T(8,128)(2,1)S(1)} collective-permute-done((bf16[1,64,1152]{2,1,0:T(8,128)(2,1)S(1)}, bf16[1,64,1152]{2,1,0:T(8,128)(2,1)S(1)}, u32[]{:S(2)}, u32[]{:S(2)}) %collective-permute-start.27) | collective-permute-done | bytes 147488 | tf_op jit(solution)/shard_map/ppermute | solution.py:412
  69.0 2.0 %collective-permute-start.28 = (bf16[1,64,1152]{2,1,0:T(8,128)(2,1)S(1)}, bf16[1,64,1152]{2,1,0:T(8,128)(2,1)S(1)}, u32[]{:S(2)}, u32[]{:S(2)}) collective-permute-start(bf16[1,64,1152]{2,1,0:T(8,128)(2,1)S(1)} %collective-permute-done.27), channel_id=1, source_target_pairs={{0,2},{1,5},{2,0},{3,7},{4,6},{5,1},{6,4},{7,3},{8,10},{9,13},{10,... | collective-permute-start | bytes 442376 | tf_op jit(solution)/shard_map/ppermute | solution.py:415
  71.1 3.1 %collective-permute-done.28 = bf16[1,64,1152]{2,1,0:T(8,128)(2,1)S(1)} collective-permute-done((bf16[1,64,1152]{2,1,0:T(8,128)(2,1)S(1)}, bf16[1,64,1152]{2,1,0:T(8,128)(2,1)S(1)}, u32[]{:S(2)}, u32[]{:S(2)}) %collective-permute-start.28) | collective-permute-done | bytes 147488 | tf_op jit(solution)/shard_map/ppermute | solution.py:415
  74.6 1.2 %collective-permute-start.33 = (bf16[2,64,1152]{2,1,0:T(8,128)(2,1)S(1)}, bf16[2,64,1152]{2,1,0:T(8,128)(2,1)S(1)}, u32[]{:S(2)}, u32[]{:S(2)}) collective-permute-start(bf16[2,64,1152]{2,1,0:T(8,128)(2,1)S(1)} %collective-permute-done.32.rest_8_), channel_id=1, source_target_pairs={{0,1},{1,0},{2,3},{3,2},{4,5},{5,4},{6,7},{7,6},{8,9},{9,8},{10,11... | collective-permute-start | bytes 884744 | tf_op jit(solution)/shard_map/ppermute | solution.py:418
  75.8 5.1 %collective-permute-done.29.rest_5_ = bf16[2,64,1152]{2,1,0:T(8,128)(2,1)S(1)} collective-permute-done((bf16[2,64,1152]{2,1,0:T(8,128)(2,1)S(1)}, bf16[2,64,1152]{2,1,0:T(8,128)(2,1)S(1)}, u32[]{:S(2)}, u32[]{:S(2)}) %collective-permute-start.29) | collective-permute-done | bytes 294944 | tf_op jit(solution)/shard_map/ppermute | solution.py:415
  82.0 2.8 %collective-permute-done.34.rest_9_ = bf16[2,64,1152]{2,1,0:T(8,128)(2,1)S(1)} collective-permute-done((bf16[2,64,1152]{2,1,0:T(8,128)(2,1)S(1)}, bf16[2,64,1152]{2,1,0:T(8,128)(2,1)S(1)}, u32[]{:S(2)}, u32[]{:S(2)}) %collective-permute-start.34) | collective-permute-done | bytes 294944 | tf_op jit(solution)/shard_map/ppermute | solution.py:497
  85.9 1.2 %collective-permute-done.35.rest_11_ = bf16[2,64,1152]{2,1,0:T(8,128)(2,1)S(1)} collective-permute-done((bf16[2,64,1152]{2,1,0:T(8,128)(2,1)S(1)}, bf16[2,64,1152]{2,1,0:T(8,128)(2,1)S(1)}, u32[]{:S(2)}, u32[]{:S(2)}) %collective-permute-start.35) | collective-permute-done | bytes 294944 | tf_op jit(solution)/shard_map/ppermute | solution.py:418
  87.1 1.4 %project.3 = (f32[160,128]{1,0:T(8,128)S(1)}, f32[160,128]{1,0:T(8,128)S(1)}) custom-call(bf16[2,64,1152]{2,1,0:T(8,128)(2,1)S(1)} %pad_maximum_fusion.rest_0_, bf16[2,64,1152]{2,1,0:T(8,128)(2,1)S(1)} %collective-permute-done.23.rest_1_, bf16[2,64,1152]{2,1,0:T(8,128)(2,1)S(1)} %collective-permute-done.24.rest_2_, ...), custom_call_target="tpu_custom_call" | custom-call | flops 566231040 | bytes 3538944 | tf_op jit(solution)/shard_map/project/pallas_call | solution.py:324
  88.5 1.9 %collective-permute-done.36.back = bf16[2,160,128]{2,1,0:T(8,128)(2,1)S(1)} collective-permute-done((bf16[2,160,128]{2,1,0:T(8,128)(2,1)S(1)}, bf16[2,160,128]{2,1,0:T(8,128)(2,1)S(1)}, u32[]{:S(2)}, u32[]{:S(2)}) %collective-permute-start.36) | collective-permute-done | bytes 81952 | tf_op jit(solution)/shard_map/ppermute | solution.py:510
  90.5 0.7 score.1
  91.1 1.1 %collective-permute-done.37 = f32[1,128]{1,0:T(1,128)S(1)} collective-permute-done((f32[1,128]{1,0:T(1,128)S(1)}, f32[1,128]{1,0:T(1,128)S(1)}, u32[]{:S(2)}, u32[]{:S(2)}) %collective-permute-start.37) | collective-permute-done | bytes 544 | tf_op jit(solution)/shard_map/ppermute | solution.py:520
  92.2 1.4 %collective-permute-start.38 = (f32[1,128]{1,0:T(1,128)S(1)}, f32[1,128]{1,0:T(1,128)S(1)}, u32[]{:S(2)}, u32[]{:S(2)}) collective-permute-start(f32[1,128]{1,0:T(1,128)S(1)} %add.30), channel_id=1, source_target_pairs={{0,2},{1,3},{2,0},{3,1},{4,6},{5,7},{6,4},{7,5},{8,10},{9,11},{10,... | collective-permute-start | bytes 1544 | tf_op jit(solution)/shard_map/ppermute | solution.py:520
  93.6 2.2 %collective-permute-done.38 = f32[1,128]{1,0:T(1,128)S(1)} collective-permute-done((f32[1,128]{1,0:T(1,128)S(1)}, f32[1,128]{1,0:T(1,128)S(1)}, u32[]{:S(2)}, u32[]{:S(2)}) %collective-permute-start.38) | collective-permute-done | bytes 544 | tf_op jit(solution)/shard_map/ppermute | solution.py:520
  95.8 0.9 collective-permute-start.39
  96.7 2.7 %collective-permute-done.39 = f32[1,128]{1,0:T(1,128)S(1)} collective-permute-done((f32[1,128]{1,0:T(1,128)S(1)}, f32[1,128]{1,0:T(1,128)S(1)}, u32[]{:S(2)}, u32[]{:S(2)}) %collective-permute-start.39) | collective-permute-done | bytes 544 | tf_op jit(solution)/shard_map/ppermute | solution.py:520
  99.3 2.6 %collective-permute-start.40 = (f32[1,128]{1,0:T(1,128)S(1)}, f32[1,128]{1,0:T(1,128)S(1)}, u32[]{:S(2)}, u32[]{:S(2)}) collective-permute-start(f32[1,128]{1,0:T(1,128)S(1)} %add.32), channel_id=1, source_target_pairs={{0,8},{1,9},{2,10},{3,11},{4,12},{5,13},{6,14},{7,15},{8,0},{9,1},... | collective-permute-start | bytes 1544 | tf_op jit(solution)/shard_map/ppermute | solution.py:520
  101.9 1.9 %collective-permute-done.40 = f32[1,128]{1,0:T(1,128)S(1)} collective-permute-done((f32[1,128]{1,0:T(1,128)S(1)}, f32[1,128]{1,0:T(1,128)S(1)}, u32[]{:S(2)}, u32[]{:S(2)}) %collective-permute-start.40) | collective-permute-done | bytes 544 | tf_op jit(solution)/shard_map/ppermute | solution.py:520
  103.8 1.1 %own_sequence.1 = f32[1,4]{1,0:T(1,128)} custom-call(s32[16]{0:T(128)S(1)} %concatenate.12.where, f32[1,128]{1,0:T(1,128)S(1)} %add.33.held), custom_call_target="tpu_custom_call" | custom-call | bytes 512 | tf_op jit(solution)/shard_map/own_sequence/pallas_call | solution.py:373
  (61 shorter events, 7.4 us)
Async XLA Ops:
  2.0 3.0 %collective-permute-start = (bf16[4,2,16,1152]{3,2,1,0:T(8,128)(2,1)S(1)}, bf16[4,2,16,1152]{3,2,1,0:T(8,128)(2,1)S(1)}, u32[]{:S(2)}, u32[]{:S(2)}) collective-permute-start(bf16[4,2,16,1152]{3,2,1,0:T(8,128)(2,1)S(1)} %get-tuple-element.54), channel_id=1, source_target_pairs={{0,1},{1,0},{2,3},{3,2},{4,5},{5,4},{6,7},{7,6},{8,9},{9,8},{10,11... | collective-permute-start | bytes 884744 | tf_op jit(solution)/shard_map/ppermute | solution.py:418
  5.7 8.0 %collective-permute-start.1 = (bf16[2,2,16,1152]{3,2,1,0:T(8,128)(2,1)S(1)}, bf16[2,2,16,1152]{3,2,1,0:T(8,128)(2,1)S(1)}, u32[]{:S(2)}, u32[]{:S(2)}) collective-permute-start(bf16[2,2,16,1152]{3,2,1,0:T(8,128)(2,1)S(1)} %get-tuple-element.62), channel_id=1, source_target_pairs={{0,2},{1,3},{2,0},{3,1},{4,6},{5,7},{6,4},{7,5},{8,10},{9,11},{10,... | collective-permute-start | bytes 442376 | tf_op jit(solution)/shard_map/ppermute | solution.py:412
  8.1 6.7 %collective-permute-start.2 = (bf16[2,2,16,1152]{3,2,1,0:T(8,128)(2,1)S(1)}, bf16[2,2,16,1152]{3,2,1,0:T(8,128)(2,1)S(1)}, u32[]{:S(2)}, u32[]{:S(2)}) collective-permute-start(bf16[2,2,16,1152]{3,2,1,0:T(8,128)(2,1)S(1)} %get-tuple-element.63), channel_id=1, source_target_pairs={{0,4},{1,5},{2,6},{3,7},{4,0},{5,1},{6,2},{7,3},{8,12},{9,13},{10,... | collective-permute-start | bytes 442376 | tf_op jit(solution)/shard_map/ppermute | solution.py:412
  9.7 7.2 %collective-permute-start.3 = (bf16[2,2,16,1152]{3,2,1,0:T(8,128)(2,1)S(1)}, bf16[2,2,16,1152]{3,2,1,0:T(8,128)(2,1)S(1)}, u32[]{:S(2)}, u32[]{:S(2)}) collective-permute-start(bf16[2,2,16,1152]{3,2,1,0:T(8,128)(2,1)S(1)} %get-tuple-element.64), channel_id=1, source_target_pairs={{0,6},{1,7},{2,4},{3,5},{4,2},{5,3},{6,0},{7,1},{8,14},{9,15},{10,... | collective-permute-start | bytes 442376 | tf_op jit(solution)/shard_map/ppermute | solution.py:412
  11.7 57.3 %collective-permute-start.26 = (bf16[160,4608]{1,0:T(8,128)(2,1)S(1)}, bf16[160,4608]{1,0:T(8,128)(2,1)S(1)}, u32[]{:S(2)}, u32[]{:S(2)}) collective-permute-start(bf16[160,4608]{1,0:T(8,128)(2,1)S(1)} %stage.3), channel_id=1, source_target_pairs={{0,16},{1,17},{2,18},{3,19},{4,20},{5,21},{6,22},{7,23},{8,24},{9,... | collective-permute-start | bytes 4423688 | tf_op jit(solution)/shard_map/ppermute | solution.py:456
  17.7 9.4 %collective-permute-start.5 = (bf16[64,1152]{1,0:T(8,128)(2,1)S(1)}, bf16[64,1152]{1,0:T(8,128)(2,1)S(1)}, u32[]{:S(2)}, u32[]{:S(2)}) collective-permute-start(bf16[64,1152]{1,0:T(8,128)(2,1)S(1)} %get-tuple-element.66), channel_id=1, source_target_pairs={{0,8},{1,9},{2,10},{3,11},{4,12},{5,13},{6,14},{7,15},{8,0},{9,1},... | collective-permute-start | bytes 442376 | tf_op jit(solution)/shard_map/ppermute | solution.py:412
  26.1 8.9 %collective-permute-start.4 = (bf16[64,1152]{1,0:T(8,128)(2,1)S(1)}, bf16[64,1152]{1,0:T(8,128)(2,1)S(1)}, u32[]{:S(2)}, u32[]{:S(2)}) collective-permute-start(bf16[64,1152]{1,0:T(8,128)(2,1)S(1)} %get-tuple-element.65), channel_id=1, source_target_pairs={{0,8},{1,9},{2,10},{3,11},{4,12},{5,13},{6,14},{7,15},{8,0},{9,1},... | collective-permute-start | bytes 442376 | tf_op jit(solution)/shard_map/ppermute | solution.py:412
  27.1 9.6 %collective-permute-start.8 = (bf16[64,1152]{1,0:T(8,128)(2,1)S(1)}, bf16[64,1152]{1,0:T(8,128)(2,1)S(1)}, u32[]{:S(2)}, u32[]{:S(2)}) collective-permute-start(bf16[64,1152]{1,0:T(8,128)(2,1)S(1)} %add.28.rest_0_), channel_id=1, source_target_pairs={{0,2},{1,5},{2,0},{3,7},{4,6},{5,1},{6,4},{7,3},{8,10},{9,13},{10,... | collective-permute-start | bytes 442376 | tf_op jit(solution)/shard_map/ppermute | solution.py:415
  28.5 8.2 %collective-permute-start.10 = (bf16[64,1152]{1,0:T(8,128)(2,1)S(1)}, bf16[64,1152]{1,0:T(8,128)(2,1)S(1)}, u32[]{:S(2)}, u32[]{:S(2)}) collective-permute-start(bf16[64,1152]{1,0:T(8,128)(2,1)S(1)} %add.28.rest_0_), channel_id=1, source_target_pairs={{0,4},{1,3},{2,6},{3,1},{4,0},{5,7},{6,2},{7,5},{8,12},{9,11},{10,... | collective-permute-start | bytes 442376 | tf_op jit(solution)/shard_map/ppermute | solution.py:415
  30.8 7.9 %collective-permute-start.12 = (bf16[64,1152]{1,0:T(8,128)(2,1)S(1)}, bf16[64,1152]{1,0:T(8,128)(2,1)S(1)}, u32[]{:S(2)}, u32[]{:S(2)}) collective-permute-start(bf16[64,1152]{1,0:T(8,128)(2,1)S(1)} %add.28.rest_0_), channel_id=1, source_target_pairs={{0,1},{1,0},{2,3},{3,2},{4,5},{5,4},{6,7},{7,6},{8,9},{9,8},{10,11... | collective-permute-start | bytes 442376 | tf_op jit(solution)/shard_map/ppermute | solution.py:418
  35.1 6.3 %collective-permute-start.6 = (bf16[64,1152]{1,0:T(8,128)(2,1)S(1)}, bf16[64,1152]{1,0:T(8,128)(2,1)S(1)}, u32[]{:S(2)}, u32[]{:S(2)}) collective-permute-start(bf16[64,1152]{1,0:T(8,128)(2,1)S(1)} %add.29.rest_0_), channel_id=1, source_target_pairs={{0,2},{1,5},{2,0},{3,7},{4,6},{5,1},{6,4},{7,3},{8,10},{9,13},{10,... | collective-permute-start | bytes 442376 | tf_op jit(solution)/shard_map/ppermute | solution.py:415
  36.7 5.1 %collective-permute-start.11 = (bf16[64,1152]{1,0:T(8,128)(2,1)S(1)}, bf16[64,1152]{1,0:T(8,128)(2,1)S(1)}, u32[]{:S(2)}, u32[]{:S(2)}) collective-permute-start(bf16[64,1152]{1,0:T(8,128)(2,1)S(1)} %collective-permute-done.8.rest_1_), channel_id=1, source_target_pairs={{0,4},{1,3},{2,6},{3,1},{4,0},{5,7},{6,2},{7,5},{8,12},{9,11},{10,... | collective-permute-start | bytes 442376 | tf_op jit(solution)/shard_map/ppermute | solution.py:415
  36.7 6.7 %collective-permute-start.7 = (bf16[64,1152]{1,0:T(8,128)(2,1)S(1)}, bf16[64,1152]{1,0:T(8,128)(2,1)S(1)}, u32[]{:S(2)}, u32[]{:S(2)}) collective-permute-start(bf16[64,1152]{1,0:T(8,128)(2,1)S(1)} %add.29.rest_0_), channel_id=1, source_target_pairs={{0,4},{1,3},{2,6},{3,1},{4,0},{5,7},{6,2},{7,5},{8,12},{9,11},{10,... | collective-permute-start | bytes 442376 | tf_op jit(solution)/shard_map/ppermute | solution.py:415
  38.7 5.1 %collective-permute-start.13 = (bf16[64,1152]{1,0:T(8,128)(2,1)S(1)}, bf16[64,1152]{1,0:T(8,128)(2,1)S(1)}, u32[]{:S(2)}, u32[]{:S(2)}) collective-permute-start(bf16[64,1152]{1,0:T(8,128)(2,1)S(1)} %collective-permute-done.8.rest_1_), channel_id=1, source_target_pairs={{0,1},{1,0},{2,3},{3,2},{4,5},{5,4},{6,7},{7,6},{8,9},{9,8},{10,11... | collective-permute-start | bytes 442376 | tf_op jit(solution)/shard_map/ppermute | solution.py:418
  41.4 2.5 %collective-permute-start.14 = (bf16[64,1152]{1,0:T(8,128)(2,1)S(1)}, bf16[64,1152]{1,0:T(8,128)(2,1)S(1)}, u32[]{:S(2)}, u32[]{:S(2)}) collective-permute-start(bf16[64,1152]{1,0:T(8,128)(2,1)S(1)} %collective-permute-done.10.rest_2_), channel_id=1, source_target_pairs={{0,1},{1,0},{2,3},{3,2},{4,5},{5,4},{6,7},{7,6},{8,9},{9,8},{10,11... | collective-permute-start | bytes 442376 | tf_op jit(solution)/shard_map/ppermute | solution.py:418
  41.8 2.6 %collective-permute-start.15 = (bf16[64,1152]{1,0:T(8,128)(2,1)S(1)}, bf16[64,1152]{1,0:T(8,128)(2,1)S(1)}, u32[]{:S(2)}, u32[]{:S(2)}) collective-permute-start(bf16[64,1152]{1,0:T(8,128)(2,1)S(1)} %collective-permute-done.11.rest_3_), channel_id=1, source_target_pairs={{0,1},{1,0},{2,3},{3,2},{4,5},{5,4},{6,7},{7,6},{8,9},{9,8},{10,11... | collective-permute-start | bytes 442376 | tf_op jit(solution)/shard_map/ppermute | solution.py:418
  43.4 5.1 %collective-permute-start.9 = (bf16[64,1152]{1,0:T(8,128)(2,1)S(1)}, bf16[64,1152]{1,0:T(8,128)(2,1)S(1)}, u32[]{:S(2)}, u32[]{:S(2)}) collective-permute-start(bf16[64,1152]{1,0:T(8,128)(2,1)S(1)} %collective-permute-done.6.rest_1_), channel_id=1, source_target_pairs={{0,4},{1,3},{2,6},{3,1},{4,0},{5,7},{6,2},{7,5},{8,12},{9,11},{10,... | collective-permute-start | bytes 442376 | tf_op jit(solution)/shard_map/ppermute | solution.py:415
  43.9 4.7 %collective-permute-start.16 = (bf16[64,1152]{1,0:T(8,128)(2,1)S(1)}, bf16[64,1152]{1,0:T(8,128)(2,1)S(1)}, u32[]{:S(2)}, u32[]{:S(2)}) collective-permute-start(bf16[64,1152]{1,0:T(8,128)(2,1)S(1)} %add.29.rest_0_), channel_id=1, source_target_pairs={{0,1},{1,0},{2,3},{3,2},{4,5},{5,4},{6,7},{7,6},{8,9},{9,8},{10,11... | collective-permute-start | bytes 442376 | tf_op jit(solution)/shard_map/ppermute | solution.py:418
  43.9 4.7 %collective-permute-start.17 = (bf16[64,1152]{1,0:T(8,128)(2,1)S(1)}, bf16[64,1152]{1,0:T(8,128)(2,1)S(1)}, u32[]{:S(2)}, u32[]{:S(2)}) collective-permute-start(bf16[64,1152]{1,0:T(8,128)(2,1)S(1)} %collective-permute-done.6.rest_1_), channel_id=1, source_target_pairs={{0,1},{1,0},{2,3},{3,2},{4,5},{5,4},{6,7},{7,6},{8,9},{9,8},{10,11... | collective-permute-start | bytes 442376 | tf_op jit(solution)/shard_map/ppermute | solution.py:418
  44.4 4.2 %collective-permute-start.18 = (bf16[64,1152]{1,0:T(8,128)(2,1)S(1)}, bf16[64,1152]{1,0:T(8,128)(2,1)S(1)}, u32[]{:S(2)}, u32[]{:S(2)}) collective-permute-start(bf16[64,1152]{1,0:T(8,128)(2,1)S(1)} %collective-permute-done.7.rest_2_), channel_id=1, source_target_pairs={{0,1},{1,0},{2,3},{3,2},{4,5},{5,4},{6,7},{7,6},{8,9},{9,8},{10,11... | collective-permute-start | bytes 442376 | tf_op jit(solution)/shard_map/ppermute | solution.py:418
  48.6 1.4 %collective-permute-start.19 = (bf16[64,1152]{1,0:T(8,128)(2,1)S(1)}, bf16[64,1152]{1,0:T(8,128)(2,1)S(1)}, u32[]{:S(2)}, u32[]{:S(2)}) collective-permute-start(bf16[64,1152]{1,0:T(8,128)(2,1)S(1)} %collective-permute-done.9.rest_3_), channel_id=1, source_target_pairs={{0,1},{1,0},{2,3},{3,2},{4,5},{5,4},{6,7},{7,6},{8,9},{9,8},{10,11... | collective-permute-start | bytes 442376 | tf_op jit(solution)/shard_map/ppermute | solution.py:418
  52.6 5.2 %collective-permute-start.20 = (bf16[64,1152]{1,0:T(8,128)(2,1)S(1)}, bf16[64,1152]{1,0:T(8,128)(2,1)S(1)}, u32[]{:S(2)}, u32[]{:S(2)}) collective-permute-start(bf16[64,1152]{1,0:T(8,128)(2,1)S(1)} %get-tuple-element.83), channel_id=1, source_target_pairs={{0,1},{1,17},{2,3},{3,19},{4,5},{5,21},{6,7},{7,23},{8,9},{9,25},{... | collective-permute-start | bytes 442376 | tf_op jit(solution)/shard_map/ppermute | solution.py:482
  52.8 5.0 %collective-permute-start.21 = (bf16[64,1152]{1,0:T(8,128)(2,1)S(1)}, bf16[64,1152]{1,0:T(8,128)(2,1)S(1)}, u32[]{:S(2)}, u32[]{:S(2)}) collective-permute-start(bf16[64,1152]{1,0:T(8,128)(2,1)S(1)} %get-tuple-element.89), channel_id=1, source_target_pairs={{1,16},{3,18},{5,20},{7,22},{9,24},{11,26},{13,28},{15,30},{16,1},... | collective-permute-start | bytes 442376 | tf_op jit(solution)/shard_map/ppermute | solution.py:482
  58.4 5.2 %collective-permute-start.22 = (bf16[1,64,1152]{2,1,0:T(8,128)(2,1)S(1)}, bf16[1,64,1152]{2,1,0:T(8,128)(2,1)S(1)}, u32[]{:S(2)}, u32[]{:S(2)}) collective-permute-start(bf16[1,64,1152]{2,1,0:T(8,128)(2,1)S(1)} %bitcast.9), channel_id=1, source_target_pairs={{0,2},{1,5},{2,0},{3,7},{4,6},{5,1},{6,4},{7,3},{8,10},{9,13},{10,... | collective-permute-start | bytes 442376 | tf_op jit(solution)/shard_map/ppermute | solution.py:415
  59.0 10.1 %collective-permute-start.27 = (bf16[1,64,1152]{2,1,0:T(8,128)(2,1)S(1)}, bf16[1,64,1152]{2,1,0:T(8,128)(2,1)S(1)}, u32[]{:S(2)}, u32[]{:S(2)}) collective-permute-start(bf16[1,64,1152]{2,1,0:T(8,128)(2,1)S(1)} %bitcast.10), channel_id=1, source_target_pairs={{0,8},{1,9},{2,10},{3,11},{4,12},{5,13},{6,14},{7,15},{8,0},{9,1},... | collective-permute-start | bytes 442376 | tf_op jit(solution)/shard_map/ppermute | solution.py:412
  63.6 11.0 %collective-permute-start.32 = (bf16[2,64,1152]{2,1,0:T(8,128)(2,1)S(1)}, bf16[2,64,1152]{2,1,0:T(8,128)(2,1)S(1)}, u32[]{:S(2)}, u32[]{:S(2)}) collective-permute-start(bf16[2,64,1152]{2,1,0:T(8,128)(2,1)S(1)} %pad_maximum_fusion.rest_0_), channel_id=1, source_target_pairs={{0,16},{1,17},{2,18},{3,19},{4,20},{5,21},{6,22},{7,23},{8,24},{9,... | collective-permute-start | bytes 884744 | tf_op jit(solution)/shard_map/ppermute | solution.py:497
  67.0 8.8 %collective-permute-start.23 = (bf16[2,64,1152]{2,1,0:T(8,128)(2,1)S(1)}, bf16[2,64,1152]{2,1,0:T(8,128)(2,1)S(1)}, u32[]{:S(2)}, u32[]{:S(2)}) collective-permute-start(bf16[2,64,1152]{2,1,0:T(8,128)(2,1)S(1)} %pad_maximum_fusion.rest_0_), channel_id=1, source_target_pairs={{0,4},{1,3},{2,6},{3,1},{4,0},{5,7},{6,2},{7,5},{8,12},{9,11},{10,... | collective-permute-start | bytes 884744 | tf_op jit(solution)/shard_map/ppermute | solution.py:415
  69.0 5.1 %collective-permute-start.28 = (bf16[1,64,1152]{2,1,0:T(8,128)(2,1)S(1)}, bf16[1,64,1152]{2,1,0:T(8,128)(2,1)S(1)}, u32[]{:S(2)}, u32[]{:S(2)}) collective-permute-start(bf16[1,64,1152]{2,1,0:T(8,128)(2,1)S(1)} %collective-permute-done.27), channel_id=1, source_target_pairs={{0,2},{1,5},{2,0},{3,7},{4,6},{5,1},{6,4},{7,3},{8,10},{9,13},{10,... | collective-permute-start | bytes 442376 | tf_op jit(solution)/shard_map/ppermute | solution.py:415
  74.2 6.8 %collective-permute-start.29 = (bf16[2,64,1152]{2,1,0:T(8,128)(2,1)S(1)}, bf16[2,64,1152]{2,1,0:T(8,128)(2,1)S(1)}, u32[]{:S(2)}, u32[]{:S(2)}) collective-permute-start(bf16[2,64,1152]{2,1,0:T(8,128)(2,1)S(1)} %constant_dynamic-update-slice_fusion.rest_4_), channel_id=1, source_target_pairs={{0,4},{1,3},{2,6},{3,1},{4,0},{5,7},{6,2},{7,5},{8,12},{9,11},{10,... | collective-permute-start | bytes 884744 | tf_op jit(solution)/shard_map/ppermute | solution.py:415
  74.6 7.3 %collective-permute-start.33 = (bf16[2,64,1152]{2,1,0:T(8,128)(2,1)S(1)}, bf16[2,64,1152]{2,1,0:T(8,128)(2,1)S(1)}, u32[]{:S(2)}, u32[]{:S(2)}) collective-permute-start(bf16[2,64,1152]{2,1,0:T(8,128)(2,1)S(1)} %collective-permute-done.32.rest_8_), channel_id=1, source_target_pairs={{0,1},{1,0},{2,3},{3,2},{4,5},{5,4},{6,7},{7,6},{8,9},{9,8},{10,11... | collective-permute-start | bytes 884744 | tf_op jit(solution)/shard_map/ppermute | solution.py:418
  75.8 9.0 %collective-permute-start.34 = (bf16[2,64,1152]{2,1,0:T(8,128)(2,1)S(1)}, bf16[2,64,1152]{2,1,0:T(8,128)(2,1)S(1)}, u32[]{:S(2)}, u32[]{:S(2)}) collective-permute-start(bf16[2,64,1152]{2,1,0:T(8,128)(2,1)S(1)} %collective-permute-done.23.rest_1_), channel_id=1, source_target_pairs={{0,16},{1,17},{2,18},{3,19},{4,20},{5,21},{6,22},{7,23},{8,24},{9,... | collective-permute-start | bytes 884744 | tf_op jit(solution)/shard_map/ppermute | solution.py:497
  81.0 3.9 %collective-permute-start.31 = (bf16[2,64,1152]{2,1,0:T(8,128)(2,1)S(1)}, bf16[2,64,1152]{2,1,0:T(8,128)(2,1)S(1)}, u32[]{:S(2)}, u32[]{:S(2)}) collective-permute-start(bf16[2,64,1152]{2,1,0:T(8,128)(2,1)S(1)} %collective-permute-done.29.rest_5_), channel_id=1, source_target_pairs={{0,1},{1,0},{2,3},{3,2},{4,5},{5,4},{6,7},{7,6},{8,9},{9,8},{10,11... | collective-permute-start | bytes 884744 | tf_op jit(solution)/shard_map/ppermute | solution.py:418
  81.3 3.5 %collective-permute-start.24 = (bf16[2,64,1152]{2,1,0:T(8,128)(2,1)S(1)}, bf16[2,64,1152]{2,1,0:T(8,128)(2,1)S(1)}, u32[]{:S(2)}, u32[]{:S(2)}) collective-permute-start(bf16[2,64,1152]{2,1,0:T(8,128)(2,1)S(1)} %pad_maximum_fusion.rest_0_), channel_id=1, source_target_pairs={{0,1},{1,0},{2,3},{3,2},{4,5},{5,4},{6,7},{7,6},{8,9},{9,8},{10,11... | collective-permute-start | bytes 884744 | tf_op jit(solution)/shard_map/ppermute | solution.py:418
  81.5 3.3 %collective-permute-start.25 = (bf16[2,64,1152]{2,1,0:T(8,128)(2,1)S(1)}, bf16[2,64,1152]{2,1,0:T(8,128)(2,1)S(1)}, u32[]{:S(2)}, u32[]{:S(2)}) collective-permute-start(bf16[2,64,1152]{2,1,0:T(8,128)(2,1)S(1)} %collective-permute-done.23.rest_1_), channel_id=1, source_target_pairs={{0,1},{1,0},{2,3},{3,2},{4,5},{5,4},{6,7},{7,6},{8,9},{9,8},{10,11... | collective-permute-start | bytes 884744 | tf_op jit(solution)/shard_map/ppermute | solution.py:418
  81.9 3.0 %collective-permute-start.30 = (bf16[2,64,1152]{2,1,0:T(8,128)(2,1)S(1)}, bf16[2,64,1152]{2,1,0:T(8,128)(2,1)S(1)}, u32[]{:S(2)}, u32[]{:S(2)}) collective-permute-start(bf16[2,64,1152]{2,1,0:T(8,128)(2,1)S(1)} %constant_dynamic-update-slice_fusion.rest_4_), channel_id=1, source_target_pairs={{0,1},{1,0},{2,3},{3,2},{4,5},{5,4},{6,7},{7,6},{8,9},{9,8},{10,11... | collective-permute-start | bytes 884744 | tf_op jit(solution)/shard_map/ppermute | solution.py:418
  85.5 1.6 %collective-permute-start.35 = (bf16[2,64,1152]{2,1,0:T(8,128)(2,1)S(1)}, bf16[2,64,1152]{2,1,0:T(8,128)(2,1)S(1)}, u32[]{:S(2)}, u32[]{:S(2)}) collective-permute-start(bf16[2,64,1152]{2,1,0:T(8,128)(2,1)S(1)} %collective-permute-done.34.rest_9_), channel_id=1, source_target_pairs={{0,1},{1,0},{2,3},{3,2},{4,5},{5,4},{6,7},{7,6},{8,9},{9,8},{10,11... | collective-permute-start | bytes 884744 | tf_op jit(solution)/shard_map/ppermute | solution.py:418
  85.5 4.9 %collective-permute-start.36 = (bf16[2,160,128]{2,1,0:T(8,128)(2,1)S(1)}, bf16[2,160,128]{2,1,0:T(8,128)(2,1)S(1)}, u32[]{:S(2)}, u32[]{:S(2)}) collective-permute-start(bf16[2,160,128]{2,1,0:T(8,128)(2,1)S(1)} %pad_maximum_fusion.1), channel_id=1, source_target_pairs={{0,16},{1,17},{2,18},{3,19},{4,20},{5,21},{6,22},{7,23},{8,24},{9,... | collective-permute-start | bytes 245768 | tf_op jit(solution)/shard_map/ppermute | solution.py:510
  91.1 1.1 %collective-permute-start.37 = (f32[1,128]{1,0:T(1,128)S(1)}, f32[1,128]{1,0:T(1,128)S(1)}, u32[]{:S(2)}, u32[]{:S(2)}) collective-permute-start(f32[1,128]{1,0:T(1,128)S(1)} %score.1), channel_id=1, source_target_pairs={{0,1},{1,0},{2,3},{3,2},{4,5},{5,4},{6,7},{7,6},{8,9},{9,8},{10,11... | collective-permute-start | bytes 1544 | tf_op jit(solution)/shard_map/ppermute | solution.py:520
  92.2 3.5 %collective-permute-start.38 = (f32[1,128]{1,0:T(1,128)S(1)}, f32[1,128]{1,0:T(1,128)S(1)}, u32[]{:S(2)}, u32[]{:S(2)}) collective-permute-start(f32[1,128]{1,0:T(1,128)S(1)} %add.30), channel_id=1, source_target_pairs={{0,2},{1,3},{2,0},{3,1},{4,6},{5,7},{6,4},{7,5},{8,10},{9,11},{10,... | collective-permute-start | bytes 1544 | tf_op jit(solution)/shard_map/ppermute | solution.py:520
  95.8 3.5 %collective-permute-start.39 = (f32[1,128]{1,0:T(1,128)S(1)}, f32[1,128]{1,0:T(1,128)S(1)}, u32[]{:S(2)}, u32[]{:S(2)}) collective-permute-start(f32[1,128]{1,0:T(1,128)S(1)} %add.31), channel_id=1, source_target_pairs={{0,4},{1,5},{2,6},{3,7},{4,0},{5,1},{6,2},{7,3},{8,12},{9,13},{10,... | collective-permute-start | bytes 1544 | tf_op jit(solution)/shard_map/ppermute | solution.py:520
  99.3 4.4 %collective-permute-start.40 = (f32[1,128]{1,0:T(1,128)S(1)}, f32[1,128]{1,0:T(1,128)S(1)}, u32[]{:S(2)}, u32[]{:S(2)}) collective-permute-start(f32[1,128]{1,0:T(1,128)S(1)} %add.32), channel_id=1, source_target_pairs={{0,8},{1,9},{2,10},{3,11},{4,12},{5,13},{6,14},{7,15},{8,0},{9,1},... | collective-permute-start | bytes 1544 | tf_op jit(solution)/shard_map/ppermute | solution.py:520
